TPU v7x, 128 devices: a whole 4x4x4 slice. The times are simulated.
128 devices in a mesh: tm: 32 (over y, x, core), head: 4 (over z).
Axes of the slice: x: 4, y: 4, z: 4, core: 2. Of those that a mesh axis runs over, the one named last changes fastest.
Arguments:
- tokens: bfloat16 [65536, 2240], P('tm'), may hold values from -6 to 6
- qkv_weight: bfloat16 [2240, 6720], P('tm', 'head'), may hold values from -0.125 to 0.125
- block_mask: int32 [128], P('tm'), may hold values from 0 to 268435455
- head_scale: float32 [20], P('head'), may hold values from 0.8 to 3.75, as said below
- norm_gain: float32 [2240], P('head'), may hold values from 0.25 to 1.75
Outputs:
- attended: bfloat16 [65536, 2240], P('tm', 'head')
Inputs may be any that keep to these rules, and one draw needn't show every extreme that they name: `head_scale`: a per-head positive scale.
All inputs are finite; a program needn't handle non-finite values.
Results may differ from a plain program's by a relative error of at most 0.0055.
Values may be sent and summed in bfloat16 or wider, within the bound.
No kernel may reach another device: no remote copies, remote signals or barrier semaphores. Data moves between devices by JAX's collectives and lax.ppermute only.
A program may use at most 128 MiB of HBM per device.

v0:
```python
import jax
import jax.numpy as jnp
from jax import lax
from jax.sharding import PartitionSpec as P

H = 20
DH = 112
BLOCK = 64
GROUP = 512


def prefix_2(shard, axis, join, neutral):
    place = lax.axis_index(axis)
    gathered = jax.tree.map(
        lambda a, kind: lax.all_gather(a.astype(kind), axis), shard, (jnp.bfloat16, jnp.bfloat16)
    )
    state = jax.tree.map(lambda a, e: jnp.zeros_like(a) + jnp.asarray(e, a.dtype), shard, neutral)

    def one(turn, state):
        return join(
            state,
            jax.tree.map(
                lambda a, own: lax.dynamic_index_in_dim(a, turn, 0, False).astype(own.dtype),
                gathered,
                shard,
            ),
        )

    return lax.fori_loop(0, place, one, state)


def token_mask(codes, block):
    row = jnp.arange(8)[:, None]
    col = jnp.arange(8)[None, :]
    bits = jnp.where(row > col, row * (row - 1) // 2 + col, 0)
    shifted = jnp.right_shift(codes[:, None, None], bits[None])
    block_ok = (row > col)[None] & (jnp.bitwise_and(shifted, 1) == 1)
    wide = jnp.repeat(jnp.repeat(block_ok, block, axis=1), block, axis=2)
    pos = jnp.arange(8 * block)
    same = (pos[:, None] // block == pos[None, :] // block) & (pos[:, None] >= pos[None, :])
    return wide | same[None]


def body(tokens, qkv_weight, block_mask, head_scale, norm_gain):
    tok_rows = tokens.shape[0]
    local_heads = head_scale.shape[0]
    blocks_here = tok_rows // GROUP
    qkv = jnp.dot(
        tokens,
        lax.all_gather(qkv_weight, "tm", axis=0, tiled=True),
        preferred_element_type=jnp.float32,
    )
    qkv = qkv.astype(jnp.bfloat16).reshape(blocks_here, GROUP, local_heads, 3, DH)
    fq = (jax.nn.elu(qkv[:, :, :, 0].astype(jnp.float32)) + 1.0).astype(jnp.bfloat16)
    fk = (jax.nn.elu(qkv[:, :, :, 1].astype(jnp.float32)) + 1.0).astype(jnp.bfloat16)
    vals = qkv[:, :, :, 2]
    state = jnp.einsum("ncht,nchu->nhtu", fk, vals, preferred_element_type=jnp.float32)
    norm_state = jnp.sum(fk.astype(jnp.float32), axis=1)
    dev_state = jnp.sum(state, axis=0)
    dev_norm = jnp.sum(norm_state, axis=0)

    def combine(earlier, later):
        return (earlier[0] + later[0], earlier[1] + later[1])

    ident = (jnp.zeros_like(dev_state), jnp.zeros_like(dev_norm))
    before, norm_before = prefix_2((dev_state, dev_norm), "tm", combine, ident)
    prefix = before[None] + jnp.cumsum(state, axis=0) - state
    norm_prefix = norm_before[None] + jnp.cumsum(norm_state, axis=0) - norm_state
    allowed = token_mask(block_mask, BLOCK)
    scores = jnp.einsum("ncht,nsht->nhcs", fq, fk, preferred_element_type=jnp.float32)
    scores = jnp.where(allowed[:, None], scores, 0.0)
    weights = scores.astype(jnp.bfloat16)
    fq32 = fq.astype(jnp.float32)
    numer = jnp.einsum("nhcs,nshu->nchu", weights, vals, preferred_element_type=jnp.float32)
    numer = numer + jnp.einsum("ncht,nhtu->nchu", fq32, prefix, precision=lax.Precision.HIGHEST)
    denom = jnp.transpose(jnp.sum(scores, axis=3), (0, 2, 1)) + jnp.sum(
        fq32 * norm_prefix[:, None], axis=3
    )
    out = (numer / denom[..., None]).reshape(tok_rows, local_heads, DH) * head_scale[None, :, None]
    squares = lax.psum(jnp.sum(out * out, axis=(1, 2)), "head")
    mean_square = squares / (H * DH)
    normed = (
        out
        / jnp.sqrt(mean_square + 1e-06)[:, None, None]
        * norm_gain.reshape(local_heads, DH)[None]
    )
    return normed.reshape(tok_rows, local_heads * DH).astype(jnp.bfloat16)


def solution(mesh):
    in_specs = (P("tm", None), P("tm", "head"), P("tm"), P("head"), P("head"))
    out_specs = P("tm", "head")
    return jax.shard_map(body, mesh=mesh, in_specs=in_specs, out_specs=out_specs, check_vma=False)
```

profile of v0, /device:TPU:30, one launch (start us, length us, event | category | flops | bytes accessed | tf_op | source)
XLA Modules:
  0.0 236.3 jit_solution(10714894027891418296)
XLA Ops:
  7.3 55.0 %all-gather.9.cloned.1.call-done = bf16[32,70,1680]{2,1,0:T(8,128)(2,1)} async-done(((bf16[1,70,1680]{2,1,0:T(8,128)(2,1)}), bf16[32,70,1680]{2,1,0:T(8,128)(2,1)}) %all-gather.9.cloned.1.call-update) | async-done | bytes 7526416 | tf_op jit(solution)/shard_map/all_gather | solution.py:50
  62.3 10.3 %reshape.264 = bf16[2240,1680]{1,0:T(8,128)(2,1)} reshape(bf16[32,70,1680]{2,1,0:T(8,128)(2,1)} %all-gather.9.cloned.1.call-done) | data formatting | bytes 15052800
  72.6 22.5 %convolution_convert_fusion = bf16[2048,1680]{0,1:T(8,128)(2,1)} fusion(bf16[2048,2240]{0,1:T(8,128)(2,1)} %param.7, bf16[2240,1680]{1,0:T(8,128)(2,1)} %reshape.264), kind=kOutput, calls=%fused_computation.11 | convolution fusion | flops 15417507840 | bytes 23582720 | tf_op jit(solution)/shard_map/dot_general | solution.py:48
  95.0 15.1 %reshape.253 = bf16[4,512,5,3,112]{1,0,4,3,2:T(4,128)(2,1)} reshape(bf16[2048,1680]{0,1:T(8,128)(2,1)} %convolution_convert_fusion) | data formatting | bytes 13762560 | tf_op jit(solution)/shard_map/reshape | solution.py:53
  110.1 5.9 %fusion.24 = (bf16[4,512,5,1,112]{1,0,4,3,2:T(4,128)(2,1)S(1)}, bf16[4,512,5,1,112]{1,0,4,3,2:T(4,128)(2,1)}, bf16[4,512,5,1,112]{1,0,4,3,2:T(4,128)(2,1)S(1)}) fusion(bf16[4,512,5,3,112]{1,0,4,3,2:T(4,128)(2,1)} %reshape.253), kind=kLoop, calls=%fused_computation.55 | loop fusion | bytes 13762560 | tf_op jit(solution)/shard_map/slice | solution.py:56
  116.1 3.6 %fusion.25 = (bf16[5,112,112]{2,1,0:T(8,128)(2,1)}, f32[4,5,112,112]{3,2,1,0:T(8,128)S(1)}) fusion(bf16[4,512,5,1,112]{1,0,4,3,2:T(4,128)(2,1)S(1)} %get-tuple-element.53, bf16[4,512,5,1,112]{1,0,4,3,2:T(4,128)(2,1)S(1)} %get-tuple-element.55), kind=kOutput, calls=%fused_computation.56 | convolution fusion | flops 263970560 | bytes 5716480 | tf_op jit(solution)/shard_map/ncht,nchu->nhtu/dot_general | solution.py:57
  120.9 2.2 fusion.21
  123.1 23.7 %all-gather.3 = bf16[32,5,112]{2,1,0:T(8,128)(2,1)S(1)} all-gather(bf16[1,5,112]{2,1,0:T(8,128)(2,1)S(1)} %bitcast.77), channel_id=3, replica_groups=mesh['tm'=32,'head'=4] {'tm'}, dimensions={0}, use_global_device_ids=true | all-gather | bytes 36960 | tf_op jit(solution)/shard_map/all_gather | solution.py:15
  146.8 2.3 convert_reduce_fusion
  149.1 9.0 %select_reduce_fusion = (f32[4,5,512]{2,1,0:T(8,128)}, bf16[4,5,512,512]{2,3,1,0:T(8,128)(2,1)S(1)}) fusion(pred[4,512,512]{1,2,0:T(8,128)(4,1)S(1)} %bitcast_or_fusion, bf16[4,512,5,1,112]{1,0,4,3,2:T(4,128)(2,1)S(1)} %get-tuple-element.55, bf16[4,512,5,1,112]{1,0,4,3,2:T(4,128)(2,1)S(1)} %copy-done), kind=kOutput, calls=%fused_computation.2 | convolution fusion | flops 1203886080 | bytes 16162816 | tf_op jit(solution)/shard_map/ncht,nsht->nhcs/dot_general | solution.py:70
  158.1 3.8 %fusion = f32[4,5,112,512]{3,2,1,0:T(8,128)} fusion(bf16[4,5,512,512]{2,3,1,0:T(8,128)(2,1)S(1)} %get-tuple-element.59, pred[4,512,512]{1,2,0:T(8,128)(4,1)S(1)} %bitcast_or_fusion, bf16[4,512,5,1,112]{1,0,4,3,2:T(4,128)(2,1)S(1)} %copy-done.3), kind=kOutput, calls=%fused_computation.8 | convolution fusion | flops 1179648000 | bytes 18415616 | tf_op jit(solution)/shard_map/nhcs,nshu->nchu/dot_general | solution.py:74
  161.9 3.9 %all-gather.7.cloned.1.call-done = bf16[160,112,112]{2,1,0:T(8,128)(2,1)} async-done(((bf16[5,112,112]{2,1,0:T(8,128)(2,1)}), bf16[160,112,112]{2,1,0:T(8,128)(2,1)}) %all-gather.7.cloned.1.call-update) | async-done | bytes 4014096 | tf_op jit(solution)/shard_map/all_gather | solution.py:15
  165.8 30.6 %while.12 = (s32[]{:T(128)}, f32[5,112,112]{2,1,0:T(8,128)S(1)}, f32[5,112]{1,0:T(8,128)S(1)}, s32[]{:T(128)}, bf16[32,5,112,112]{3,2,1,0:T(8,128)(2,1)}, /*inde...) while((s32[]{:T(128)}, f32[5,112,112]{2,1,0:T(8,128)S(1)}, f32[5,112]{1,0:T(8,128)S(1)}, ...), condition=%wide.region_3.4_spmd, body=%wide.region_2.3_spmd.sunk | while | flops 126565 | bytes 632935 | solution.py:29
  165.8 1.0 convert_add_fusion.4
  166.8 1.0 convert_add_fusion.4
  167.8 1.0 convert_add_fusion.4
  168.9 1.0 convert_add_fusion.4
  169.9 1.0 convert_add_fusion.4
  170.9 1.0 convert_add_fusion.4
  173.9 1.0 convert_add_fusion.4
  174.9 1.0 convert_add_fusion.4
  175.9 1.0 convert_add_fusion.4
  177.0 1.0 convert_add_fusion.4
  178.0 1.0 convert_add_fusion.4
  179.0 1.0 convert_add_fusion.4
  180.0 1.0 convert_add_fusion.4
  196.5 4.0 %multiply_reduce_fusion.1 = f32[4,512,5]{1,2,0:T(8,128)S(1)} fusion(f32[4,5,112]{2,1,0:T(8,128)S(1)} %fusion.11, bf16[4,512,5,1,112]{1,0,4,3,2:T(4,128)(2,1)} %get-tuple-element.54), kind=kLoop, calls=%fused_computation.21 | loop fusion | flops 10311680 | bytes 2343680 | tf_op jit(solution)/shard_map/reduce_sum | solution.py:76
  200.8 6.3 %multiply_reduce_fusion = (f32[4,512]{1,0:T(4,128)S(1)}, f32[4,512,5,112]{1,3,2,0:T(8,128)S(1)}) fusion(f32[5]{0:T(128)S(1)} %copy-done.7, f32[4,512,5]{1,2,0:T(8,128)S(1)} %bitcast_add_fusion, f32[4,5,112,512]{3,2,1,0:T(8,128)} %fusion, f32[4,5,112,112]{3,2,1,0:T(8,128)S(1)} %fusion.10, bf16[4,512,5,1,112]{1,0,4,3,2:T(4,128)(2,1)S(1)} %copy-done.1), kind=kOutput, calls=%fused_computation.20 | convolution fusion | flops 1554020352 | bytes 12521492 | tf_op jit(solution)/shard_map/ncht,nhtu->nchu/dot_general | solution.py:75
  207.1 3.0 %copy.22 = f32[4,512,5,112]{1,0,3,2:T(4,128)S(1)} copy(f32[4,512,5,112]{1,3,2,0:T(8,128)S(1)} %get-tuple-element.61) | data formatting | bytes 9175040 | tf_op jit(solution)/shard_map/div | solution.py:79
  210.1 4.2 %copy.28 = f32[70,8,4,512]{3,1,2,0:T(8,128)} copy(f32[70,8,4,512]{3,2,1,0:T(4,128)S(1)} %bitcast.72) | data formatting | bytes 9175040
  214.3 10.8 %psum.7 = f32[2048]{0:T(1024)S(1)} all-reduce(f32[2048]{0:T(1024)S(1)} %bitcast.75), channel_id=1, replica_groups=mesh['tm'=32,'head'=4] {'head'}, use_global_device_ids=true, to_apply=%region_10.11 | all-reduce | flops 2048 | bytes 16384 | tf_op jit(solution)/shard_map/psum | solution.py:80
  225.1 4.3 %multiply_convert_fusion = bf16[2048,560]{0,1:T(8,128)(2,1)} fusion(f32[2048,560]{0,1:T(8,128)} %bitcast.71, f32[560]{0:T(1024)S(1)} %copy-done.5, f32[2048]{0:T(1024)S(1)} %add_sqrt_fusion, f32[560]{0:T(1024)S(1)} %mul.51), kind=kLoop, calls=%fused_computation.19 | loop fusion | flops 4587520 | bytes 6893952 | tf_op jit(solution)/shard_map/convert_element_type | solution.py:87
  (85 shorter events, 19.2 us)
Async XLA Ops:
  6.5 55.8 %all-gather.9.cloned.1.call-start = ((), (), s32[]{:S(2)}) async-start(), calls=%async_computation.1 | async-start | bytes 8515584 | tf_op jit(solution)/shard_map/all_gather | solution.py:50
  7.3 158.5 %all-gather.7.cloned.1.call-start = ((), (), s32[]{:S(2)}) async-start(), calls=%async_computation | async-start | bytes 4730880 | tf_op jit(solution)/shard_map/all_gather | solution.py:15
  116.1 3.6 %copy-start.2 = (bf16[4,512,5,1,112]{1,0,4,3,2:T(4,128)(2,1)}, bf16[4,512,5,1,112]{1,0,4,3,2:T(4,128)(2,1)S(1)}, u32[]{:S(2)}) copy-start(bf16[4,512,5,1,112]{1,0,4,3,2:T(4,128)(2,1)S(1)} %get-tuple-element.53) | copy-start | bytes 6881284
  116.1 3.6 %copy-start.6 = (s32[4]{0:T(128)S(1)}, s32[4]{0:T(128)}, u32[]{:S(2)}) copy-start(s32[4]{0:T(128)} %param.9) | copy-start | bytes 52
  116.1 4.0 %copy-start.7 = (f32[5]{0:T(128)S(1)}, f32[5]{0:T(128)}, u32[]{:S(2)}) copy-start(f32[5]{0:T(128)} %param.10) | copy-start | bytes 64
  120.2 28.9 %copy-start = (bf16[4,512,5,1,112]{1,0,4,3,2:T(4,128)(2,1)S(1)}, bf16[4,512,5,1,112]{1,0,4,3,2:T(4,128)(2,1)}, u32[]{:S(2)}) copy-start(bf16[4,512,5,1,112]{1,0,4,3,2:T(4,128)(2,1)} %get-tuple-element.54) | copy-start | bytes 6881284
  149.1 9.0 %copy-start.3 = (bf16[4,512,5,1,112]{1,0,4,3,2:T(4,128)(2,1)S(1)}, bf16[4,512,5,1,112]{1,0,4,3,2:T(4,128)(2,1)}, u32[]{:S(2)}) copy-start(bf16[4,512,5,1,112]{1,0,4,3,2:T(4,128)(2,1)} %copy-done.2) | copy-start | bytes 6881284
  161.9 38.7 %copy-start.4 = (f32[4,5,512]{2,1,0:T(8,128)S(1)}, f32[4,5,512]{2,1,0:T(8,128)}, u32[]{:S(2)}) copy-start(f32[4,5,512]{2,1,0:T(8,128)} %get-tuple-element.58) | copy-start | bytes 122884
  196.4 4.4 %copy-start.1 = (bf16[4,512,5,1,112]{1,0,4,3,2:T(4,128)(2,1)S(1)}, bf16[4,512,5,1,112]{1,0,4,3,2:T(4,128)(2,1)}, u32[]{:S(2)}) copy-start(bf16[4,512,5,1,112]{1,0,4,3,2:T(4,128)(2,1)} %get-tuple-element.54) | copy-start | bytes 6881284
  210.1 15.0 %copy-start.5 = (f32[560]{0:T(1024)S(1)}, f32[560]{0:T(1024)}, u32[]{:S(2)}) copy-start(f32[560]{0:T(1024)} %param.11) | copy-start | bytes 6724
Sparse Core Ops, SparseCore 0:
  9.7 52.5 all-gather.8
  119.8 45.9 all-gather.6
where the time goes:
time: 238 us; the launch traced here: 236 us
  waiting for transfers between devices  59.6 us (25%)
  matrix products  45.1 us (19%)
  other arithmetic  43.3 us (18%)
  local copies, waits for them, and re-layouts  38.9 us (16%)
  blocking collectives  34.5 us (14%)
  between operations  13.6 us (6%)
    all_gather x1, waiting for transfers between devices, body(): lax.all_gather(qkv_weight, 'tm', axis=0, tiled=True)  55 us
    add x60, other arithmetic, combine(): return (earlier[0] + later[0], earlier[1] + later[1])  29.4 us
    all_gather x1, blocking collectives, prefix_2(): lax.all_gather(a.astype(kind), axis)  23.7 us
    dot_general x1, matrix products, body(): jnp.dot(tokens, lax.all_gather(qkv_weight, 'tm', axis=0, tiled=True), pre...  22.5 us
    reshape x1, local copies, waits for them, and re-layouts, body(): qkv.astype(jnp.bfloat16).reshape(blocks_here, GROUP, local_heads, 3, DH)  15.1 us
    unnamed x19, local copies, waits for them, and re-layouts  14.5 us
    psum x1, blocking collectives, body(): squares = lax.psum(jnp.sum(out * out, axis=(1, 2)), 'head')  10.8 us
    dot_general x1, matrix products, body(): jnp.einsum('ncht,nsht->nhcs', fq, fk, preferred_element_type=jnp.float32)  8.96 us
  transfers between devices with their start and end apart: 2, of which 2 were waited for; matrix products, arithmetic and copies ran while one was open for 8% of the time, Pallas kernels for 0%

commit v1 on v0

v1 whole, which is shorter than its diff:
```python
import jax
import jax.numpy as jnp
from jax import lax
from jax.experimental import pallas as pl
from jax.experimental.pallas import tpu as pltpu
from jax.sharding import PartitionSpec as P

H = 20
DH = 112
GROUP = 512
D = 2240
HL = 5
CHIPS = 16
SHARD = 70
ROWS = 144
K = CHIPS * ROWS
VA = 128
C1 = 640
C2 = 256
BF = jnp.bfloat16
F32 = jnp.float32
MIB = 1 << 20


def place(y, x, c):
    return (y % 4) * 8 + (x % 4) * 2 + c


def perm(move):
    return [
        (place(y, x, c), place(*move(y, x, c)))
        for y in range(4)
        for x in range(4)
        for c in range(2)
    ]


SIBLING = perm(lambda y, x, c: (y, x, 1 - c))


def first_leg(d):
    return perm(lambda y, x, c: (y, x + d, c) if c == 0 else (y + d, x, c))


def second_leg(d):
    return perm(lambda y, x, c: (y + d, x, c) if c == 0 else (y, x + d, c))


def along_x(d):
    return perm(lambda y, x, c: (y, x + d, c))


def later_y(d):
    return [
        (place(y, x, c), place(y + d, x, c))
        for y in range(4 - d)
        for x in range(4)
        for c in range(2)
    ]


def shift(a, moves):
    return lax.ppermute(a, "tm", moves)


def column_sets(w):
    heads = w.reshape(w.shape[0], HL, 3, DH)
    q, k, v = (heads[:, :, i].reshape(w.shape[0], HL * DH) for i in range(3))
    zero = jnp.zeros((w.shape[0], 64), w.dtype)
    one = jnp.concatenate([k, q[:, :80], q[:, 160:368], zero[:, :48]], axis=1)
    two = jnp.concatenate([v, q[:, 80:160], q[:, 368:], zero], axis=1)
    return one, two


def spread_kernel(x_ref, o_ref):
    for i in range(CHIPS):
        o_ref[i * ROWS : i * ROWS + 2 * SHARD, :] = x_ref[i * 2 * SHARD : (i + 1) * 2 * SHARD, :]
        o_ref[i * ROWS + 2 * SHARD : (i + 1) * ROWS, :] = jnp.zeros(
            (ROWS - 2 * SHARD, x_ref.shape[1]), BF
        )


def spread(xt):
    n = xt.shape[1]
    blk = 256
    return pl.pallas_call(
        spread_kernel,
        grid=(n // blk,),
        in_specs=[pl.BlockSpec((D, blk), lambda g: (0, g))],
        out_specs=pl.BlockSpec((K, blk), lambda g: (0, g)),
        out_shape=jax.ShapeDtypeStruct((K, n), BF),
        compiler_params=pltpu.CompilerParams(vmem_limit_bytes=24 * MIB),
        cost_estimate=pl.CostEstimate(flops=0, bytes_accessed=2 * n * K * 2, transcendentals=0),
        name="spread",
    )(xt)


def load_weights(pos, own, sib, wbuf, wt, sem, cols):
    y, x, c = pos[0], pos[1], pos[2]
    copies = []
    for side, blocks in enumerate((own, sib)):
        which = c if side == 0 else 1 - c
        for d in range(4):
            for r in range(4):
                dy = jnp.where(which == 0, d, r)
                dx = jnp.where(which == 0, r, d)
                chip = ((y + 4 - dy) & 3) * 4 + ((x + 4 - dx) & 3)
                at = pl.multiple_of(chip * ROWS, ROWS)
                copies.append(
                    pltpu.make_async_copy(
                        blocks[d].at[r],
                        wbuf.at[which, pl.ds(at, ROWS)],
                        sem.at[len(copies)],
                    )
                )
    for copy in copies:
        copy.start()
    for copy in copies:
        copy.wait()
    for which in range(2):
        for kb in range(K // 256):
            wt[which * cols : (which + 1) * cols, kb * 256 : (kb + 1) * 256] = wbuf[
                which, kb * 256 : (kb + 1) * 256, :
            ].T


def feature(raw):
    a = raw.astype(BF).astype(F32)
    return jnp.where(a > 0, a + 1.0, jnp.exp(jnp.minimum(a, 0.0))).astype(BF)


def kv_kernel(pos, *refs):
    own, sib = refs[:4], refs[4:8]
    x_ref, fk_ref, v_ref, q_ref, pre_ref, tot_ref, wbuf, wt, run, sem = refs[8:]
    g = pl.program_id(0)

    @pl.when(g == 0)
    def _():
        load_weights(pos, own, sib, wbuf, wt, sem, C1)
        run[...] = jnp.zeros_like(run)

    x = x_ref[...]
    one = jnp.dot(wt[:C1, :], x, preferred_element_type=F32)
    fk = feature(one)
    q_ref[:80, :] = fk[HL * DH :, :]
    two = jnp.dot(wt[C1:, :], x, preferred_element_type=F32)
    q_ref[80:, :] = feature(two[HL * DH :, :])
    tail = (lax.broadcasted_iota(jnp.int32, (VA - DH, GROUP), 0) == 0).astype(F32).astype(BF)
    for h in range(HL):
        kn = fk[h * DH : (h + 1) * DH, :].T
        fk_ref[h] = kn
        va = jnp.concatenate([two[h * DH : (h + 1) * DH, :].astype(BF), tail], axis=0)
        v_ref[h] = va
        state = jnp.dot(va, kn, preferred_element_type=F32)
        before = run[h]
        pre_ref[0, h] = before
        run[h] = before + state

    @pl.when(g == pl.num_programs(0) - 1)
    def _():
        tot_ref[...] = run[...].astype(BF)


def kv_call(pos, own, sib, xp):
    n = xp.shape[1]
    groups = n // GROUP
    anywhere = pl.BlockSpec(memory_space=pl.ANY)
    return pl.pallas_call(
        kv_kernel,
        grid_spec=pltpu.PrefetchScalarGridSpec(
            num_scalar_prefetch=1,
            grid=(groups,),
            in_specs=[anywhere] * 8 + [pl.BlockSpec((K, GROUP), lambda g, p: (0, g))],
            out_specs=[
                pl.BlockSpec((HL, GROUP, DH), lambda g, p: (0, g, 0)),
                pl.BlockSpec((HL, VA, GROUP), lambda g, p: (0, 0, g)),
                pl.BlockSpec((160, GROUP), lambda g, p: (0, g)),
                pl.BlockSpec((1, HL, VA, DH), lambda g, p: (g, 0, 0, 0)),
                pl.BlockSpec((HL, VA, DH), lambda g, p: (0, 0, 0)),
            ],
            scratch_shapes=[
                pltpu.VMEM((2, K, C1), BF),
                pltpu.VMEM((2 * C1, K), BF),
                pltpu.VMEM((HL, VA, DH), F32),
                pltpu.SemaphoreType.DMA((32,)),
            ],
        ),
        out_shape=[
            jax.ShapeDtypeStruct((HL, n, DH), BF),
            jax.ShapeDtypeStruct((HL, VA, n), BF),
            jax.ShapeDtypeStruct((160, n), BF),
            jax.ShapeDtypeStruct((groups, HL, VA, DH), F32),
            jax.ShapeDtypeStruct((HL, VA, DH), BF),
        ],
        compiler_params=pltpu.CompilerParams(vmem_limit_bytes=40 * MIB),
        cost_estimate=pl.CostEstimate(
            flops=2 * n * K * 2 * C1, bytes_accessed=n * K * 2 + 2 * K * C1 * 2, transcendentals=0
        ),
        name="keys_values",
    )(pos, *own, *sib, xp)


def mask_rows(code, j0, rows, t0, cols):
    parts = []
    for j in range(j0, j0 + rows // 64):
        t = lax.broadcasted_iota(jnp.int32, (64, cols), 1) + t0
        s = lax.broadcasted_iota(jnp.int32, (64, cols), 0)
        i = t >> 6
        bit = (jnp.full((64, cols), code, jnp.int32) >> (((i * (i - 1)) >> 1) + j)) & 1
        same = jnp.where(s <= (t & 63), 1, 0)
        keep = jnp.where(i > j, bit, jnp.where(i == j, same, 0))
        parts.append(keep.astype(F32).astype(BF))
    return jnp.concatenate(parts, axis=0)


def q_kernel(pos, codes, *refs):
    own, sib = refs[:4], refs[4:8]
    x_ref, fk_ref, v_ref, q_ref, fq_ref, num_ref, wbuf, wt, sem = refs[8:]
    g = pl.program_id(0)

    @pl.when(g == 0)
    def _():
        load_weights(pos, own, sib, wbuf, wt, sem, C2)

    raw = jnp.dot(wt[...], x_ref[...], preferred_element_type=F32)
    fq_ref[:160, :] = q_ref[...]
    fq_ref[160:368, :] = feature(raw[:208, :])
    fq_ref[368:, :] = feature(raw[C2 : C2 + 192, :])
    code = codes[g]
    half = GROUP // 2
    upper = mask_rows(code, 0, half, 0, GROUP)
    lower = mask_rows(code, 4, half, half, half)
    for h in range(HL):
        fq = fq_ref[h * DH : (h + 1) * DH, :]
        top = jnp.dot(fk_ref[h, :half, :], fq, preferred_element_type=F32)
        top = top.astype(BF) * upper
        low = jnp.dot(fk_ref[h, half:, :], fq[:, half:], preferred_element_type=F32)
        low = low.astype(BF) * lower
        num = jnp.dot(v_ref[h, :, :half], top, preferred_element_type=F32)
        more = jnp.dot(v_ref[h, :, half:], low, preferred_element_type=F32)
        num_ref[h, :, :half] = num[:, :half]
        num_ref[h, :, half:] = num[:, half:] + more


def q_call(pos, codes, own, sib, xp, fk, v, q):
    n = xp.shape[1]
    groups = n // GROUP
    anywhere = pl.BlockSpec(memory_space=pl.ANY)
    return pl.pallas_call(
        q_kernel,
        grid_spec=pltpu.PrefetchScalarGridSpec(
            num_scalar_prefetch=2,
            grid=(groups,),
            in_specs=[anywhere] * 8
            + [
                pl.BlockSpec((K, GROUP), lambda g, p, m: (0, g)),
                pl.BlockSpec((HL, GROUP, DH), lambda g, p, m: (0, g, 0)),
                pl.BlockSpec((HL, VA, GROUP), lambda g, p, m: (0, 0, g)),
                pl.BlockSpec((160, GROUP), lambda g, p, m: (0, g)),
            ],
            out_specs=[
                pl.BlockSpec((HL * DH, GROUP), lambda g, p, m: (0, g)),
                pl.BlockSpec((HL, VA, GROUP), lambda g, p, m: (0, 0, g)),
            ],
            scratch_shapes=[
                pltpu.VMEM((2, K, C2), BF),
                pltpu.VMEM((2 * C2, K), BF),
                pltpu.SemaphoreType.DMA((32,)),
            ],
        ),
        out_shape=[
            jax.ShapeDtypeStruct((HL * DH, n), BF),
            jax.ShapeDtypeStruct((HL, VA, n), F32),
        ],
        compiler_params=pltpu.CompilerParams(vmem_limit_bytes=40 * MIB),
        cost_estimate=pl.CostEstimate(
            flops=2 * n * K * 2 * C2 + 2 * n * GROUP * 256 * 2 * HL,
            bytes_accessed=n * K * 2 + 2 * K * C2 * 2,
            transcendentals=0,
        ),
        name="queries",
    )(pos, codes, *own, *sib, xp, fk, v, q)


def join_kernel(scale, dev_ref, pre_ref, fq_ref, num_ref, out_ref, sq_ref):
    total = jnp.zeros((1, GROUP), F32)
    for h in range(HL):
        prefix = (dev_ref[h] + pre_ref[0, h]).astype(BF)
        fq = fq_ref[h * DH : (h + 1) * DH, :]
        num = num_ref[h] + jnp.dot(prefix, fq, preferred_element_type=F32)
        out = num[:DH, :] * (scale[h] / num[DH : DH + 1, :])
        out_ref[h * DH : (h + 1) * DH, :] = out
        total = total + jnp.sum(out * out, axis=0, keepdims=True)
    sq_ref[...] = total


def join_call(scale, dev, pre, fq, num):
    n = fq.shape[1]
    groups = n // GROUP
    return pl.pallas_call(
        join_kernel,
        grid_spec=pltpu.PrefetchScalarGridSpec(
            num_scalar_prefetch=1,
            grid=(groups,),
            in_specs=[
                pl.BlockSpec((HL, VA, DH), lambda g, s: (0, 0, 0)),
                pl.BlockSpec((1, HL, VA, DH), lambda g, s: (g, 0, 0, 0)),
                pl.BlockSpec((HL * DH, GROUP), lambda g, s: (0, g)),
                pl.BlockSpec((HL, VA, GROUP), lambda g, s: (0, 0, g)),
            ],
            out_specs=[
                pl.BlockSpec((HL * DH, GROUP), lambda g, s: (0, g)),
                pl.BlockSpec((1, GROUP), lambda g, s: (0, g)),
            ],
        ),
        out_shape=[
            jax.ShapeDtypeStruct((HL * DH, n), F32),
            jax.ShapeDtypeStruct((1, n), F32),
        ],
        compiler_params=pltpu.CompilerParams(vmem_limit_bytes=24 * MIB),
        cost_estimate=pl.CostEstimate(
            flops=2 * n * 256 * VA * HL, bytes_accessed=n * 560 * 12, transcendentals=0
        ),
        name="join",
    )(scale, dev, pre, fq, num)


def norm_kernel(out_ref, sq_ref, gain_ref, o_ref):
    inv = lax.rsqrt(sq_ref[...] * (1.0 / (H * DH)) + 1e-06)
    o_ref[...] = (out_ref[...] * inv * gain_ref[...]).astype(BF)


def norm_call(out, squares, gain):
    n = out.shape[1]
    return pl.pallas_call(
        norm_kernel,
        grid=(n // GROUP,),
        in_specs=[
            pl.BlockSpec((HL * DH, GROUP), lambda g: (0, g)),
            pl.BlockSpec((1, GROUP), lambda g: (0, g)),
            pl.BlockSpec((HL * DH, 1), lambda g: (0, 0)),
        ],
        out_specs=pl.BlockSpec((HL * DH, GROUP), lambda g: (0, g)),
        out_shape=jax.ShapeDtypeStruct((HL * DH, n), BF),
        compiler_params=pltpu.CompilerParams(vmem_limit_bytes=24 * MIB),
        cost_estimate=pl.CostEstimate(flops=0, bytes_accessed=n * 560 * 6, transcendentals=0),
        name="norm",
    )(out, squares, gain)


def gather(own):
    near = jnp.stack([own] + [shift(own, first_leg(d)) for d in (1, 2, 3)])
    return near


def body(tokens, qkv_weight, block_mask, head_scale, norm_gain):
    me = lax.axis_index("tm")
    core = me % 2
    pos = jnp.stack([me // 8, (me // 2) % 4, core]).astype(jnp.int32)
    one, two = column_sets(qkv_weight)
    theirs = shift(jnp.where(core == 0, two, one), SIBLING)
    mine = jnp.where(core == 0, one, two)
    rows = jnp.concatenate(
        [
            jnp.where(core == 0, mine, theirs),
            jnp.where(core == 0, theirs, mine),
            jnp.zeros((ROWS - 2 * SHARD, C1 + C2), BF),
        ]
    )
    near1 = gather(rows[:, :C1])
    near2 = gather(rows[:, C1:])
    near1, near2 = lax.optimization_barrier((near1, near2))
    own1 = [near1] + [shift(near1, second_leg(d)) for d in (1, 2, 3)]
    own2 = [near2] + [shift(near2, second_leg(d)) for d in (1, 2, 3)]
    sib1 = [shift(a, SIBLING) for a in own1]
    sib2 = [shift(a, SIBLING) for a in own2]

    xp = spread(tokens.T)
    fk, v, q, pre, tot = kv_call(pos, own1, sib1, xp)

    other = shift(tot, SIBLING).astype(F32)
    before = jnp.where(core == 1, other, 0.0)
    chip = (tot.astype(F32) + other).astype(BF)
    row = chip.astype(F32)
    for d in (1, 2, 3):
        got = shift(chip, along_x(d)).astype(F32)
        row = row + got
        before = before + jnp.where(pos[1] >= d, got, 0.0)
    row = row.astype(BF)
    for d in (1, 2, 3):
        before = before + shift(row, later_y(d)).astype(F32)

    fq, num = q_call(pos, block_mask, own2, sib2, xp, fk, v, q)
    out, squares = join_call(head_scale, before, pre, fq, num)
    squares = squares + sum(
        lax.ppermute(squares, "head", [(i, (i + d) % 4) for i in range(4)]) for d in (1, 2, 3)
    )
    return norm_call(out, squares, norm_gain.reshape(HL * DH, 1)).T


def solution(mesh):
    in_specs = (P("tm", None), P("tm", "head"), P("tm"), P("head"), P("head"))
    out_specs = P("tm", "head")
    return jax.shard_map(body, mesh=mesh, in_specs=in_specs, out_specs=out_specs, check_vma=False)
```

time: 238 us -> 156 us (0.66)
  the two profiles are of different devices: /device:TPU:30 before, /device:TPU:0 now
where the time goes in v1:
time: 156 us; the launch traced here: 155 us
  Pallas kernels  53.4 us (34%)
  starting transfers between devices  41.6 us (27%)
  waiting for transfers between devices  32.5 us (21%)
  local copies, waits for them, and re-layouts  23.3 us (15%)
  other arithmetic  3.82 us (2%)
    ppermute x28, starting transfers between devices, shift(): return lax.ppermute(a, 'tm', moves)  35 us
    ppermute x28, waiting for transfers between devices, shift(): return lax.ppermute(a, 'tm', moves)  30 us
    pallas_call x1, Pallas kernels, kv_call(): pl.pallas_call(kv_kernel, grid_spec=pltpu.PrefetchScalarGridSpec(num_scal...  24.5 us
    pallas_call x1, Pallas kernels, q_call(): pl.pallas_call(q_kernel, grid_spec=pltpu.PrefetchScalarGridSpec(num_scala...  20 us
    unnamed x32, local copies, waits for them, and re-layouts  19.2 us
    ppermute x3, starting transfers between devices, body(): lax.ppermute(squares, 'head', [(i, (i + d) % 4) for i in range(4)])  6.58 us
    pallas_call x1, Pallas kernels, spread(): pl.pallas_call(spread_kernel, grid=(n // blk,), in_specs=[pl.BlockSpec((D...  3.39 us
    pallas_call x1, Pallas kernels, join_call(): pl.pallas_call(join_kernel, grid_spec=pltpu.PrefetchScalarGridSpec(num_sc...  3.18 us
  transfers between devices with their start and end apart: 31, of which 12 were waited for; matrix products, arithmetic and copies ran while one was open for 1% of the time, Pallas kernels for 15%

profile of v1, /device:TPU:0, one launch (start us, length us, event | category | flops | bytes accessed | tf_op | source)
XLA Modules:
  0.0 155.0 jit_solution(1407390330733081769)
XLA Ops:
  1.5 1.6 %slice_reduce_fusion.2 = (bf16[70,5,112]{2,1,0:T(8,128)(2,1)S(1)}, bf16[70,5,112]{2,1,0:T(8,128)(2,1)S(1)}, bf16[70,5,112]{2,1,0:T(8,128)(2,1)S(1)}) fusion(bf16[70,5,3,112]{3,2,1,0:T(4,128)(2,1)S(1)} %reshape.6), kind=kLoop, calls=%fused_computation.21 | loop fusion | bytes 470400 | tf_op jit(solution)/shard_map/slice | solution.py:68
  5.8 2.9 %collective-permute-start.6 = (bf16[144,256]{1,0:T(8,128)(2,1)S(1)}, bf16[144,256]{1,0:T(8,128)(2,1)S(1)}, u32[]{:S(2)}, u32[]{:S(2)}) collective-permute-start(bf16[144,256]{1,0:T(8,128)(2,1)S(1)} %get-tuple-element.33), channel_id=1, source_target_pairs={{0,24},{4,100},{8,0},{12,108},{16,8},{20,116},{24,16},{28,124},{32... | collective-permute-start | bytes 221192 | tf_op jit(solution)/shard_map/ppermute | solution.py:63
  8.7 2.3 %collective-permute-start.5 = (bf16[144,256]{1,0:T(8,128)(2,1)S(1)}, bf16[144,256]{1,0:T(8,128)(2,1)S(1)}, u32[]{:S(2)}, u32[]{:S(2)}) collective-permute-start(bf16[144,256]{1,0:T(8,128)(2,1)S(1)} %get-tuple-element.33), channel_id=1, source_target_pairs={{0,16},{4,68},{8,24},{12,76},{16,0},{20,84},{24,8},{28,92},{32,48}... | collective-permute-start | bytes 221192 | tf_op jit(solution)/shard_map/ppermute | solution.py:63
  11.0 1.9 %collective-permute-start.1 = (bf16[144,640]{1,0:T(8,128)(2,1)S(1)}, bf16[144,640]{1,0:T(8,128)(2,1)S(1)}, u32[]{:S(2)}, u32[]{:S(2)}) collective-permute-start(bf16[144,640]{1,0:T(8,128)(2,1)S(1)} %get-tuple-element.35), channel_id=1, source_target_pairs={{0,8},{4,36},{8,16},{12,44},{16,24},{20,52},{24,0},{28,60},{32,40}... | collective-permute-start | bytes 552968 | tf_op jit(solution)/shard_map/ppermute | solution.py:63
  13.7 2.0 %collective-permute-start.3 = (bf16[144,640]{1,0:T(8,128)(2,1)S(1)}, bf16[144,640]{1,0:T(8,128)(2,1)S(1)}, u32[]{:S(2)}, u32[]{:S(2)}) collective-permute-start(bf16[144,640]{1,0:T(8,128)(2,1)S(1)} %get-tuple-element.35), channel_id=1, source_target_pairs={{0,24},{4,100},{8,0},{12,108},{16,8},{20,116},{24,16},{28,124},{32... | collective-permute-start | bytes 552968 | tf_op jit(solution)/shard_map/ppermute | solution.py:63
  15.7 2.1 %collective-permute-done.1 = bf16[144,640]{1,0:T(8,128)(2,1)S(1)} collective-permute-done((bf16[144,640]{1,0:T(8,128)(2,1)S(1)}, bf16[144,640]{1,0:T(8,128)(2,1)S(1)}, u32[]{:S(2)}, u32[]{:S(2)}) %collective-permute-start.1) | collective-permute-done | bytes 184352 | tf_op jit(solution)/shard_map/ppermute | solution.py:63
  17.8 2.1 %collective-permute-done.2 = bf16[144,640]{1,0:T(8,128)(2,1)S(1)} collective-permute-done((bf16[144,640]{1,0:T(8,128)(2,1)S(1)}, bf16[144,640]{1,0:T(8,128)(2,1)S(1)}, u32[]{:S(2)}, u32[]{:S(2)}) %collective-permute-start.2) | collective-permute-done | bytes 184352 | tf_op jit(solution)/shard_map/ppermute | solution.py:63
  20.8 1.6 %collective-permute-start.7 = (bf16[4,144,640]{2,1,0:T(8,128)(2,1)S(1)}, bf16[4,144,640]{2,1,0:T(8,128)(2,1)S(1)}, u32[]{:S(2)}, u32[]{:S(2)}) collective-permute-start(bf16[4,144,640]{2,1,0:T(8,128)(2,1)S(1)} %pad_maximum_fusion.refs_0_), channel_id=1, source_target_pairs={{0,32},{4,12},{8,40},{12,20},{16,48},{20,28},{24,56},{28,4},{32,64... | collective-permute-start | bytes 2211848 | tf_op jit(solution)/shard_map/ppermute | solution.py:63
  22.4 2.9 %collective-permute-start.8 = (bf16[4,144,640]{2,1,0:T(8,128)(2,1)S(1)}, bf16[4,144,640]{2,1,0:T(8,128)(2,1)S(1)}, u32[]{:S(2)}, u32[]{:S(2)}) collective-permute-start(bf16[4,144,640]{2,1,0:T(8,128)(2,1)S(1)} %pad_maximum_fusion.refs_0_), channel_id=1, source_target_pairs={{0,64},{4,20},{8,72},{12,28},{16,80},{20,4},{24,88},{28,12},{32,96... | collective-permute-start | bytes 2211848 | tf_op jit(solution)/shard_map/ppermute | solution.py:63
  26.7 6.8 %collective-permute-done.7.refs_1_ = bf16[4,144,640]{2,1,0:T(8,128)(2,1)S(1)} collective-permute-done((bf16[4,144,640]{2,1,0:T(8,128)(2,1)S(1)}, bf16[4,144,640]{2,1,0:T(8,128)(2,1)S(1)}, u32[]{:S(2)}, u32[]{:S(2)}) %collective-permute-start.7) | collective-permute-done | bytes 737312 | tf_op jit(solution)/shard_map/ppermute | solution.py:63
  33.5 9.1 %collective-permute-done.8.refs_2_ = bf16[4,144,640]{2,1,0:T(8,128)(2,1)S(1)} collective-permute-done((bf16[4,144,640]{2,1,0:T(8,128)(2,1)S(1)}, bf16[4,144,640]{2,1,0:T(8,128)(2,1)S(1)}, u32[]{:S(2)}, u32[]{:S(2)}) %collective-permute-start.8) | collective-permute-done | bytes 737312 | tf_op jit(solution)/shard_map/ppermute | solution.py:63
  43.2 3.6 %copy-done.1 = bf16[2048,2240]{0,1:T(8,128)(2,1)S(1)} copy-done((bf16[2048,2240]{0,1:T(8,128)(2,1)S(1)}, bf16[2048,2240]{0,1:T(8,128)(2,1)}, u32[]{:S(2)}) %copy-start.1) | copy-done | bytes 9175064
  46.8 3.4 %spread.1.refs_8_ = bf16[2304,2048]{1,0:T(8,128)(2,1)S(1)} custom-call(bf16[2240,2048]{1,0:T(8,128)(2,1)S(1)} %bitcast.15), custom_call_target="tpu_custom_call" | custom-call | bytes 18874368 | tf_op jit(solution)/shard_map/spread/pallas_call | solution.py:86
  50.2 3.6 %copy-done = bf16[2304,2048]{1,0:T(8,128)(2,1)} copy-done((bf16[2304,2048]{1,0:T(8,128)(2,1)}, bf16[2304,2048]{1,0:T(8,128)(2,1)S(1)}, u32[]{:S(2)}) %copy-start) | copy-done | bytes 9437208
  55.0 24.5 %keys_values.1 = (bf16[5,2048,112]{2,1,0:T(8,128)(2,1)S(1)}, bf16[5,128,2048]{2,1,0:T(8,128)(2,1)S(1)}, bf16[160,2048]{1,0:T(8,128)(2,1)S(1)}, f32[4,5,128,112]{3,2,1,0:T(8,128)S(1)}, bf16[5,128,112]{2,1,0:T(8,128)(2,1)S(1)}) custom-call(s32[3]{0:T(128)S(1)} %pad_add_fusion.pos, bf16[4,144,640]{2,1,0:T(8,128)(2,1)S(1)} %pad_maximum_fusion.refs_0_, ...), custom_call_target="tpu_custom_call" | custom-call | flops 12079595520 | bytes 15335424 | tf_op jit(solution)/shard_map/keys_values/pallas_call | solution.py:168
  85.1 2.1 %collective-permute-start.22 = (bf16[4,144,256]{2,1,0:T(8,128)(2,1)S(1)}, bf16[4,144,256]{2,1,0:T(8,128)(2,1)S(1)}, u32[]{:S(2)}, u32[]{:S(2)}) collective-permute-start(bf16[4,144,256]{2,1,0:T(8,128)(2,1)S(1)} %pad_maximum_fusion.1.refs_0_), channel_id=1, source_target_pairs={{0,64},{4,20},{8,72},{12,28},{16,80},{20,4},{24,88},{28,12},{32,96... | collective-permute-start | bytes 884744 | tf_op jit(solution)/shard_map/ppermute | solution.py:63
  87.2 1.7 %collective-permute-start.23 = (bf16[4,144,256]{2,1,0:T(8,128)(2,1)S(1)}, bf16[4,144,256]{2,1,0:T(8,128)(2,1)S(1)}, u32[]{:S(2)}, u32[]{:S(2)}) collective-permute-start(bf16[4,144,256]{2,1,0:T(8,128)(2,1)S(1)} %pad_maximum_fusion.1.refs_0_), channel_id=1, source_target_pairs={{0,96},{4,28},{8,104},{12,4},{16,112},{20,12},{24,120},{28,20},{32... | collective-permute-start | bytes 884744 | tf_op jit(solution)/shard_map/ppermute | solution.py:63
  91.0 2.8 %collective-permute-start.16 = (bf16[5,128,112]{2,1,0:T(8,128)(2,1)}, bf16[5,128,112]{2,1,0:T(8,128)(2,1)}, u32[]{:S(2)}, u32[]{:S(2)}) collective-permute-start(bf16[5,128,112]{2,1,0:T(8,128)(2,1)} %fusion.6), channel_id=1, source_target_pairs={{0,16},{4,20},{8,24},{12,28},{16,0},{20,4},{24,8},{28,12},{32,48},... | collective-permute-start | bytes 430088 | tf_op jit(solution)/shard_map/ppermute | solution.py:63
  95.6 3.6 %collective-permute-done.15 = bf16[5,128,112]{2,1,0:T(8,128)(2,1)} collective-permute-done((bf16[5,128,112]{2,1,0:T(8,128)(2,1)}, bf16[5,128,112]{2,1,0:T(8,128)(2,1)}, u32[]{:S(2)}, u32[]{:S(2)}) %collective-permute-start.15) | collective-permute-done | bytes 143392 | tf_op jit(solution)/shard_map/ppermute | solution.py:63
  99.2 2.9 %collective-permute-done.16 = bf16[5,128,112]{2,1,0:T(8,128)(2,1)} collective-permute-done((bf16[5,128,112]{2,1,0:T(8,128)(2,1)}, bf16[5,128,112]{2,1,0:T(8,128)(2,1)}, u32[]{:S(2)}, u32[]{:S(2)}) %collective-permute-start.16) | collective-permute-done | bytes 143392 | tf_op jit(solution)/shard_map/ppermute | solution.py:63
  103.3 3.0 %collective-permute-start.18 = (bf16[5,128,112]{2,1,0:T(8,128)(2,1)S(1)}, bf16[5,128,112]{2,1,0:T(8,128)(2,1)S(1)}, u32[]{:S(2)}, u32[]{:S(2)}) collective-permute-start(bf16[5,128,112]{2,1,0:T(8,128)(2,1)S(1)} %fusion.7), channel_id=1, source_target_pairs={{0,32},{4,36},{8,40},{12,44},{16,48},{20,52},{24,56},{28,60},{32,6... | collective-permute-start | bytes 430088 | tf_op jit(solution)/shard_map/ppermute | solution.py:63
  106.4 3.9 %collective-permute-start.19 = (bf16[5,128,112]{2,1,0:T(8,128)(2,1)S(1)}, bf16[5,128,112]{2,1,0:T(8,128)(2,1)S(1)}, u32[]{:S(2)}, u32[]{:S(2)}) collective-permute-start(bf16[5,128,112]{2,1,0:T(8,128)(2,1)S(1)} %fusion.7), channel_id=1, source_target_pairs={{0,64},{4,68},{8,72},{12,76},{16,80},{20,84},{24,88},{28,92},{32,9... | collective-permute-start | bytes 430088 | tf_op jit(solution)/shard_map/ppermute | solution.py:63
  110.3 1.5 collective-permute-start.20
  111.9 1.7 %copy-done.8 = bf16[5,2048,112]{2,1,0:T(8,128)(2,1)S(1)} copy-done((bf16[5,2048,112]{2,1,0:T(8,128)(2,1)S(1)}, bf16[5,2048,112]{2,1,0:T(8,128)(2,1)}, u32[]{:S(2)}) %copy-start.8) | copy-done | bytes 2293784
  113.6 1.7 %copy-done.10 = bf16[5,128,2048]{2,1,0:T(8,128)(2,1)S(1)} copy-done((bf16[5,128,2048]{2,1,0:T(8,128)(2,1)S(1)}, bf16[5,128,2048]{2,1,0:T(8,128)(2,1)}, u32[]{:S(2)}) %copy-start.10) | copy-done | bytes 2621464
  116.5 20.0 %queries.1 = (bf16[560,2048]{1,0:T(8,128)(2,1)S(1)}, f32[5,128,2048]{2,1,0:T(8,128)}) custom-call(s32[3]{0:T(128)S(1)} %pad_add_fusion.pos, s32[4]{0:T(128)S(1)} %copy-done.6, bf16[4,144,256]{2,1,0:T(8,128)(2,1)S(1)} %pad_maximum_fusion.1.refs_0_, bf16[4,144,256]{2,1,0:T(8,128)(2,1)S(1)} %collective-permute-done.21.refs_1_, ...), custom_call_target="tpu_custom_call" | custom-call | flops 10200547328 | bytes 11796480 | tf_op jit(solution)/shard_map/queries/pallas_call | solution.py:249
  137.7 2.5 %copy-done.2 = f32[5,128,2048]{2,1,0:T(8,128)S(1)} copy-done((f32[5,128,2048]{2,1,0:T(8,128)S(1)}, f32[5,128,2048]{2,1,0:T(8,128)}, u32[]{:S(2)}) %copy-start.2) | copy-done | bytes 5242904
  140.2 3.2 %join.1 = (f32[560,2048]{1,0:T(8,128)S(1)}, f32[1,2048]{1,0:T(1,128)S(1)}) custom-call(f32[5]{0:T(128)S(1)} %copy-done.3, f32[5,128,112]{2,1,0:T(8,128)S(1)} %fusion.5.dev_ref, f32[4,5,128,112]{3,2,1,0:T(8,128)S(1)} %get-tuple-element.18.pre_ref, bf16[560,2048]{1,0:T(8,128)(2,1)S(1)} %get-tuple-element.23.fq_ref, f32[5,128,2048]{2,1,0:T(8,128)S(1)} %copy-done.2), custom_call_target="tpu_custom_call" | custom-call | flops 671088640 | bytes 13762560 | tf_op jit(solution)/shard_map/join/pallas_call | solution.py:300
  143.4 2.0 %collective-permute-start.28 = (f32[1,2048]{1,0:T(1,128)S(1)}, f32[1,2048]{1,0:T(1,128)S(1)}, u32[]{:S(2)}, u32[]{:S(2)}) collective-permute-start(f32[1,2048]{1,0:T(1,128)S(1)} %get-tuple-element.26), channel_id=1, source_target_pairs={{0,1},{1,2},{2,3},{3,0},{4,5},{5,6},{6,7},{7,4},{8,9},{9,10},{10,1... | collective-permute-start | bytes 24584 | tf_op jit(solution)/shard_map/ppermute | solution.py:396
  145.4 3.6 %collective-permute-start.29 = (f32[1,2048]{1,0:T(1,128)S(1)}, f32[1,2048]{1,0:T(1,128)S(1)}, u32[]{:S(2)}, u32[]{:S(2)}) collective-permute-start(f32[1,2048]{1,0:T(1,128)S(1)} %get-tuple-element.26), channel_id=1, source_target_pairs={{0,2},{1,3},{2,0},{3,1},{4,6},{5,7},{6,4},{7,5},{8,10},{9,11},{10,... | collective-permute-start | bytes 24584 | tf_op jit(solution)/shard_map/ppermute | solution.py:396
  150.7 1.9 %collective-permute-done.30 = f32[1,2048]{1,0:T(1,128)S(1)} collective-permute-done((f32[1,2048]{1,0:T(1,128)S(1)}, f32[1,2048]{1,0:T(1,128)S(1)}, u32[]{:S(2)}, u32[]{:S(2)}) %collective-permute-start.30) | collective-permute-done | bytes 8224 | tf_op jit(solution)/shard_map/ppermute | solution.py:396
  152.6 2.4 %norm.1 = bf16[560,2048]{1,0:T(8,128)(2,1)} custom-call(f32[560,2048]{1,0:T(8,128)S(1)} %get-tuple-element.25.out_ref, f32[1,2048]{1,0:T(1,128)S(1)} %add_add_fusion.sq_ref, f32[560,1]{1,0:T(8,128)S(1)} %reshape.8.gain_ref), custom_call_target="tpu_custom_call" | custom-call | bytes 6881280 | tf_op jit(solution)/shard_map/norm/pallas_call | solution.py:335
  (94 shorter events, 23.6 us)
Async XLA Ops:
  4.1 1.4 collective-permute-start
  5.8 7.9 %collective-permute-start.6 = (bf16[144,256]{1,0:T(8,128)(2,1)S(1)}, bf16[144,256]{1,0:T(8,128)(2,1)S(1)}, u32[]{:S(2)}, u32[]{:S(2)}) collective-permute-start(bf16[144,256]{1,0:T(8,128)(2,1)S(1)} %get-tuple-element.33), channel_id=1, source_target_pairs={{0,24},{4,100},{8,0},{12,108},{16,8},{20,116},{24,16},{28,124},{32... | collective-permute-start | bytes 221192 | tf_op jit(solution)/shard_map/ppermute | solution.py:63
  8.7 7.0 %collective-permute-start.4 = (bf16[144,256]{1,0:T(8,128)(2,1)S(1)}, bf16[144,256]{1,0:T(8,128)(2,1)S(1)}, u32[]{:S(2)}, u32[]{:S(2)}) collective-permute-start(bf16[144,256]{1,0:T(8,128)(2,1)S(1)} %get-tuple-element.33), channel_id=1, source_target_pairs={{0,8},{4,36},{8,16},{12,44},{16,24},{20,52},{24,0},{28,60},{32,40}... | collective-permute-start | bytes 221192 | tf_op jit(solution)/shard_map/ppermute | solution.py:63
  8.7 7.0 %collective-permute-start.5 = (bf16[144,256]{1,0:T(8,128)(2,1)S(1)}, bf16[144,256]{1,0:T(8,128)(2,1)S(1)}, u32[]{:S(2)}, u32[]{:S(2)}) collective-permute-start(bf16[144,256]{1,0:T(8,128)(2,1)S(1)} %get-tuple-element.33), channel_id=1, source_target_pairs={{0,16},{4,68},{8,24},{12,76},{16,0},{20,84},{24,8},{28,92},{32,48}... | collective-permute-start | bytes 221192 | tf_op jit(solution)/shard_map/ppermute | solution.py:63
  11.0 6.8 %collective-permute-start.1 = (bf16[144,640]{1,0:T(8,128)(2,1)S(1)}, bf16[144,640]{1,0:T(8,128)(2,1)S(1)}, u32[]{:S(2)}, u32[]{:S(2)}) collective-permute-start(bf16[144,640]{1,0:T(8,128)(2,1)S(1)} %get-tuple-element.35), channel_id=1, source_target_pairs={{0,8},{4,36},{8,16},{12,44},{16,24},{20,52},{24,0},{28,60},{32,40}... | collective-permute-start | bytes 552968 | tf_op jit(solution)/shard_map/ppermute | solution.py:63
  12.9 7.0 %collective-permute-start.2 = (bf16[144,640]{1,0:T(8,128)(2,1)S(1)}, bf16[144,640]{1,0:T(8,128)(2,1)S(1)}, u32[]{:S(2)}, u32[]{:S(2)}) collective-permute-start(bf16[144,640]{1,0:T(8,128)(2,1)S(1)} %get-tuple-element.35), channel_id=1, source_target_pairs={{0,16},{4,68},{8,24},{12,76},{16,0},{20,84},{24,8},{28,92},{32,48}... | collective-permute-start | bytes 552968 | tf_op jit(solution)/shard_map/ppermute | solution.py:63
  13.7 7.0 %collective-permute-start.3 = (bf16[144,640]{1,0:T(8,128)(2,1)S(1)}, bf16[144,640]{1,0:T(8,128)(2,1)S(1)}, u32[]{:S(2)}, u32[]{:S(2)}) collective-permute-start(bf16[144,640]{1,0:T(8,128)(2,1)S(1)} %get-tuple-element.35), channel_id=1, source_target_pairs={{0,24},{4,100},{8,0},{12,108},{16,8},{20,116},{24,16},{28,124},{32... | collective-permute-start | bytes 552968 | tf_op jit(solution)/shard_map/ppermute | solution.py:63
  20.8 12.7 %collective-permute-start.7 = (bf16[4,144,640]{2,1,0:T(8,128)(2,1)S(1)}, bf16[4,144,640]{2,1,0:T(8,128)(2,1)S(1)}, u32[]{:S(2)}, u32[]{:S(2)}) collective-permute-start(bf16[4,144,640]{2,1,0:T(8,128)(2,1)S(1)} %pad_maximum_fusion.refs_0_), channel_id=1, source_target_pairs={{0,32},{4,12},{8,40},{12,20},{16,48},{20,28},{24,56},{28,4},{32,64... | collective-permute-start | bytes 2211848 | tf_op jit(solution)/shard_map/ppermute | solution.py:63
  22.4 20.2 %collective-permute-start.8 = (bf16[4,144,640]{2,1,0:T(8,128)(2,1)S(1)}, bf16[4,144,640]{2,1,0:T(8,128)(2,1)S(1)}, u32[]{:S(2)}, u32[]{:S(2)}) collective-permute-start(bf16[4,144,640]{2,1,0:T(8,128)(2,1)S(1)} %pad_maximum_fusion.refs_0_), channel_id=1, source_target_pairs={{0,64},{4,20},{8,72},{12,28},{16,80},{20,4},{24,88},{28,12},{32,96... | collective-permute-start | bytes 2211848 | tf_op jit(solution)/shard_map/ppermute | solution.py:63
  25.3 17.3 %collective-permute-start.9 = (bf16[4,144,640]{2,1,0:T(8,128)(2,1)S(1)}, bf16[4,144,640]{2,1,0:T(8,128)(2,1)}, u32[]{:S(2)}, u32[]{:S(2)}) collective-permute-start(bf16[4,144,640]{2,1,0:T(8,128)(2,1)S(1)} %pad_maximum_fusion.refs_0_), channel_id=1, source_target_pairs={{0,96},{4,28},{8,104},{12,4},{16,112},{20,12},{24,120},{28,20},{32... | collective-permute-start | bytes 2211848 | tf_op jit(solution)/shard_map/ppermute | solution.py:63
  26.6 27.2 %collective-permute-start.10 = (bf16[4,144,640]{2,1,0:T(8,128)(2,1)S(1)}, bf16[4,144,640]{2,1,0:T(8,128)(2,1)}, u32[]{:S(2)}, u32[]{:S(2)}) collective-permute-start(bf16[4,144,640]{2,1,0:T(8,128)(2,1)S(1)} %pad_maximum_fusion.refs_0_), channel_id=1, source_target_pairs={{0,4},{4,0},{8,12},{12,8},{16,20},{20,16},{24,28},{28,24},{32,36},... | collective-permute-start | bytes 2211848 | tf_op jit(solution)/shard_map/ppermute | solution.py:63
  33.5 20.4 %collective-permute-start.11 = (bf16[4,144,640]{2,1,0:T(8,128)(2,1)S(1)}, bf16[4,144,640]{2,1,0:T(8,128)(2,1)}, u32[]{:S(2)}, u32[]{:S(2)}) collective-permute-start(bf16[4,144,640]{2,1,0:T(8,128)(2,1)S(1)} %collective-permute-done.7.refs_1_), channel_id=1, source_target_pairs={{0,4},{4,0},{8,12},{12,8},{16,20},{20,16},{24,28},{28,24},{32,36},... | collective-permute-start | bytes 2211848 | tf_op jit(solution)/shard_map/ppermute | solution.py:63
  42.6 11.2 %collective-permute-start.12 = (bf16[4,144,640]{2,1,0:T(8,128)(2,1)S(1)}, bf16[4,144,640]{2,1,0:T(8,128)(2,1)}, u32[]{:S(2)}, u32[]{:S(2)}) collective-permute-start(bf16[4,144,640]{2,1,0:T(8,128)(2,1)S(1)} %collective-permute-done.8.refs_2_), channel_id=1, source_target_pairs={{0,4},{4,0},{8,12},{12,8},{16,20},{20,16},{24,28},{28,24},{32,36},... | collective-permute-start | bytes 2211848 | tf_op jit(solution)/shard_map/ppermute | solution.py:63
  42.6 11.2 %collective-permute-start.13 = (bf16[4,144,640]{2,1,0:T(8,128)(2,1)}, bf16[4,144,640]{2,1,0:T(8,128)(2,1)}, u32[]{:S(2)}, u32[]{:S(2)}) collective-permute-start(bf16[4,144,640]{2,1,0:T(8,128)(2,1)} %collective-permute-done.9.refs_3_), channel_id=1, source_target_pairs={{0,4},{4,0},{8,12},{12,8},{16,20},{20,16},{24,28},{28,24},{32,36},... | collective-permute-start | bytes 2211848 | tf_op jit(solution)/shard_map/ppermute | solution.py:63
  53.8 58.1 %copy-start.6 = (s32[4]{0:T(128)S(1)}, s32[4]{0:T(128)}, u32[]{:S(2)}) copy-start(s32[4]{0:T(128)} %codes.1) | copy-start | bytes 52
  83.4 5.6 %collective-permute-start.14 = (bf16[5,128,112]{2,1,0:T(8,128)(2,1)S(1)}, bf16[5,128,112]{2,1,0:T(8,128)(2,1)S(1)}, u32[]{:S(2)}, u32[]{:S(2)}) collective-permute-start(bf16[5,128,112]{2,1,0:T(8,128)(2,1)S(1)} %get-tuple-element.17), channel_id=1, source_target_pairs={{0,4},{4,0},{8,12},{12,8},{16,20},{20,16},{24,28},{28,24},{32,36},... | collective-permute-start | bytes 430088 | tf_op jit(solution)/shard_map/ppermute | solution.py:63
  83.6 10.2 %collective-permute-start.21 = (bf16[4,144,256]{2,1,0:T(8,128)(2,1)S(1)}, bf16[4,144,256]{2,1,0:T(8,128)(2,1)S(1)}, u32[]{:S(2)}, u32[]{:S(2)}) collective-permute-start(bf16[4,144,256]{2,1,0:T(8,128)(2,1)S(1)} %pad_maximum_fusion.1.refs_0_), channel_id=1, source_target_pairs={{0,32},{4,12},{8,40},{12,20},{16,48},{20,28},{24,56},{28,4},{32,64... | collective-permute-start | bytes 884744 | tf_op jit(solution)/shard_map/ppermute | solution.py:63
  85.1 10.0 %collective-permute-start.22 = (bf16[4,144,256]{2,1,0:T(8,128)(2,1)S(1)}, bf16[4,144,256]{2,1,0:T(8,128)(2,1)S(1)}, u32[]{:S(2)}, u32[]{:S(2)}) collective-permute-start(bf16[4,144,256]{2,1,0:T(8,128)(2,1)S(1)} %pad_maximum_fusion.1.refs_0_), channel_id=1, source_target_pairs={{0,64},{4,20},{8,72},{12,28},{16,80},{20,4},{24,88},{28,12},{32,96... | collective-permute-start | bytes 884744 | tf_op jit(solution)/shard_map/ppermute | solution.py:63
  87.2 8.4 %collective-permute-start.23 = (bf16[4,144,256]{2,1,0:T(8,128)(2,1)S(1)}, bf16[4,144,256]{2,1,0:T(8,128)(2,1)S(1)}, u32[]{:S(2)}, u32[]{:S(2)}) collective-permute-start(bf16[4,144,256]{2,1,0:T(8,128)(2,1)S(1)} %pad_maximum_fusion.1.refs_0_), channel_id=1, source_target_pairs={{0,96},{4,28},{8,104},{12,4},{16,112},{20,12},{24,120},{28,20},{32... | collective-permute-start | bytes 884744 | tf_op jit(solution)/shard_map/ppermute | solution.py:63
  89.7 9.5 %collective-permute-start.15 = (bf16[5,128,112]{2,1,0:T(8,128)(2,1)}, bf16[5,128,112]{2,1,0:T(8,128)(2,1)}, u32[]{:S(2)}, u32[]{:S(2)}) collective-permute-start(bf16[5,128,112]{2,1,0:T(8,128)(2,1)} %fusion.6), channel_id=1, source_target_pairs={{0,8},{4,12},{8,16},{12,20},{16,24},{20,28},{24,0},{28,4},{32,40},... | collective-permute-start | bytes 430088 | tf_op jit(solution)/shard_map/ppermute | solution.py:63
  91.0 11.0 %collective-permute-start.16 = (bf16[5,128,112]{2,1,0:T(8,128)(2,1)}, bf16[5,128,112]{2,1,0:T(8,128)(2,1)}, u32[]{:S(2)}, u32[]{:S(2)}) collective-permute-start(bf16[5,128,112]{2,1,0:T(8,128)(2,1)} %fusion.6), channel_id=1, source_target_pairs={{0,16},{4,20},{8,24},{12,28},{16,0},{20,4},{24,8},{28,12},{32,48},... | collective-permute-start | bytes 430088 | tf_op jit(solution)/shard_map/ppermute | solution.py:63
  93.8 8.3 %collective-permute-start.17 = (bf16[5,128,112]{2,1,0:T(8,128)(2,1)}, bf16[5,128,112]{2,1,0:T(8,128)(2,1)}, u32[]{:S(2)}, u32[]{:S(2)}) collective-permute-start(bf16[5,128,112]{2,1,0:T(8,128)(2,1)} %fusion.6), channel_id=1, source_target_pairs={{0,24},{4,28},{8,0},{12,4},{16,8},{20,12},{24,16},{28,20},{32,56},... | collective-permute-start | bytes 430088 | tf_op jit(solution)/shard_map/ppermute | solution.py:63
  95.1 11.3 %collective-permute-start.24 = (bf16[4,144,256]{2,1,0:T(8,128)(2,1)S(1)}, bf16[4,144,256]{2,1,0:T(8,128)(2,1)S(1)}, u32[]{:S(2)}, u32[]{:S(2)}) collective-permute-start(bf16[4,144,256]{2,1,0:T(8,128)(2,1)S(1)} %pad_maximum_fusion.1.refs_0_), channel_id=1, source_target_pairs={{0,4},{4,0},{8,12},{12,8},{16,20},{20,16},{24,28},{28,24},{32,36},... | collective-permute-start | bytes 884744 | tf_op jit(solution)/shard_map/ppermute | solution.py:63
  95.6 14.7 %collective-permute-start.25 = (bf16[4,144,256]{2,1,0:T(8,128)(2,1)S(1)}, bf16[4,144,256]{2,1,0:T(8,128)(2,1)S(1)}, u32[]{:S(2)}, u32[]{:S(2)}) collective-permute-start(bf16[4,144,256]{2,1,0:T(8,128)(2,1)S(1)} %collective-permute-done.21.refs_1_), channel_id=1, source_target_pairs={{0,4},{4,0},{8,12},{12,8},{16,20},{20,16},{24,28},{28,24},{32,36},... | collective-permute-start | bytes 884744 | tf_op jit(solution)/shard_map/ppermute | solution.py:63
  99.2 12.7 %collective-permute-start.26 = (bf16[4,144,256]{2,1,0:T(8,128)(2,1)S(1)}, bf16[4,144,256]{2,1,0:T(8,128)(2,1)S(1)}, u32[]{:S(2)}, u32[]{:S(2)}) collective-permute-start(bf16[4,144,256]{2,1,0:T(8,128)(2,1)S(1)} %collective-permute-done.22.refs_2_), channel_id=1, source_target_pairs={{0,4},{4,0},{8,12},{12,8},{16,20},{20,16},{24,28},{28,24},{32,36},... | collective-permute-start | bytes 884744 | tf_op jit(solution)/shard_map/ppermute | solution.py:63
  102.1 9.8 %collective-permute-start.27 = (bf16[4,144,256]{2,1,0:T(8,128)(2,1)S(1)}, bf16[4,144,256]{2,1,0:T(8,128)(2,1)}, u32[]{:S(2)}, u32[]{:S(2)}) collective-permute-start(bf16[4,144,256]{2,1,0:T(8,128)(2,1)S(1)} %collective-permute-done.23.refs_3_), channel_id=1, source_target_pairs={{0,4},{4,0},{8,12},{12,8},{16,20},{20,16},{24,28},{28,24},{32,36},... | collective-permute-start | bytes 884744 | tf_op jit(solution)/shard_map/ppermute | solution.py:63
  103.3 33.1 %collective-permute-start.18 = (bf16[5,128,112]{2,1,0:T(8,128)(2,1)S(1)}, bf16[5,128,112]{2,1,0:T(8,128)(2,1)S(1)}, u32[]{:S(2)}, u32[]{:S(2)}) collective-permute-start(bf16[5,128,112]{2,1,0:T(8,128)(2,1)S(1)} %fusion.7), channel_id=1, source_target_pairs={{0,32},{4,36},{8,40},{12,44},{16,48},{20,52},{24,56},{28,60},{32,6... | collective-permute-start | bytes 430088 | tf_op jit(solution)/shard_map/ppermute | solution.py:63
  106.4 30.1 %collective-permute-start.19 = (bf16[5,128,112]{2,1,0:T(8,128)(2,1)S(1)}, bf16[5,128,112]{2,1,0:T(8,128)(2,1)S(1)}, u32[]{:S(2)}, u32[]{:S(2)}) collective-permute-start(bf16[5,128,112]{2,1,0:T(8,128)(2,1)S(1)} %fusion.7), channel_id=1, source_target_pairs={{0,64},{4,68},{8,72},{12,76},{16,80},{20,84},{24,88},{28,92},{32,9... | collective-permute-start | bytes 430088 | tf_op jit(solution)/shard_map/ppermute | solution.py:63
  110.3 26.1 %collective-permute-start.20 = (bf16[5,128,112]{2,1,0:T(8,128)(2,1)S(1)}, bf16[5,128,112]{2,1,0:T(8,128)(2,1)S(1)}, u32[]{:S(2)}, u32[]{:S(2)}) collective-permute-start(bf16[5,128,112]{2,1,0:T(8,128)(2,1)S(1)} %fusion.7), channel_id=1, source_target_pairs={{0,96},{4,100},{8,104},{12,108},{16,112},{20,116},{24,120},{28,124... | collective-permute-start | bytes 430088 | tf_op jit(solution)/shard_map/ppermute | solution.py:63
  143.4 6.7 %collective-permute-start.28 = (f32[1,2048]{1,0:T(1,128)S(1)}, f32[1,2048]{1,0:T(1,128)S(1)}, u32[]{:S(2)}, u32[]{:S(2)}) collective-permute-start(f32[1,2048]{1,0:T(1,128)S(1)} %get-tuple-element.26), channel_id=1, source_target_pairs={{0,1},{1,2},{2,3},{3,0},{4,5},{5,6},{6,7},{7,4},{8,9},{9,10},{10,1... | collective-permute-start | bytes 24584 | tf_op jit(solution)/shard_map/ppermute | solution.py:396
  145.4 5.3 %collective-permute-start.29 = (f32[1,2048]{1,0:T(1,128)S(1)}, f32[1,2048]{1,0:T(1,128)S(1)}, u32[]{:S(2)}, u32[]{:S(2)}) collective-permute-start(f32[1,2048]{1,0:T(1,128)S(1)} %get-tuple-element.26), channel_id=1, source_target_pairs={{0,2},{1,3},{2,0},{3,1},{4,6},{5,7},{6,4},{7,5},{8,10},{9,11},{10,... | collective-permute-start | bytes 24584 | tf_op jit(solution)/shard_map/ppermute | solution.py:396
  149.0 3.7 %collective-permute-start.30 = (f32[1,2048]{1,0:T(1,128)S(1)}, f32[1,2048]{1,0:T(1,128)S(1)}, u32[]{:S(2)}, u32[]{:S(2)}) collective-permute-start(f32[1,2048]{1,0:T(1,128)S(1)} %get-tuple-element.26), channel_id=1, source_target_pairs={{0,3},{1,0},{2,1},{3,2},{4,7},{5,4},{6,5},{7,6},{8,11},{9,8},{10,9... | collective-permute-start | bytes 24584 | tf_op jit(solution)/shard_map/ppermute | solution.py:396
  (15 other events, 83.1 us)

commit v2 on v1

v2 whole, which is shorter than its diff:
```python
import jax
import jax.numpy as jnp
from jax import lax
from jax.experimental import pallas as pl
from jax.experimental.pallas import tpu as pltpu
from jax.sharding import PartitionSpec as P

H = 20
DH = 112
GROUP = 512
D = 2240
HL = 5
SHARD = 70
PAD = 72
BLK = 4 * PAD
VA = 128
QCOL = 1152
COLS = 1792
BF = jnp.bfloat16
F32 = jnp.float32
MIB = 1 << 20
VMEM = 60 * MIB


def place(y, x, c):
    return (y % 4) * 8 + (x % 4) * 2 + c


def perm(move):
    return [
        (place(y, x, c), place(*move(y, x, c)))
        for y in range(4)
        for x in range(4)
        for c in range(2)
    ]


SIBLING = perm(lambda y, x, c: (y, x, 1 - c))


def first_leg(d):
    return perm(lambda y, x, c: (y, x + d, c) if c == 0 else (y + d, x, c))


def second_leg(d):
    return perm(lambda y, x, c: (y + d, x, c) if c == 0 else (y, x + d, c))


def along_x(d):
    return perm(lambda y, x, c: (y, x + d, c))


def later_y(d):
    return [
        (place(y, x, c), place(y + d, x, c))
        for y in range(4 - d)
        for x in range(4)
        for c in range(2)
    ]


def shift(a, moves):
    return lax.ppermute(a, "tm", moves)


def pack_kernel(pos, a0, a1, a2, a3, g_ref, parts, wide, sem):
    coord = jnp.where(pos[2] == 0, pos[1], pos[0])
    copies = [
        pltpu.make_async_copy(a, parts.at[(coord + 4 - r) & 3], sem.at[r])
        for r, a in enumerate((a0, a1, a2, a3))
    ]
    for copy in copies:
        copy.start()
    wide[...] = jnp.zeros_like(wide)
    for copy in copies:
        copy.wait()
    for p in range(4):
        shard = parts[p].astype(F32)
        for kind, base in ((0, QCOL), (1, 0), (2, HL * DH)):
            for h in range(HL):
                at = h * 3 * DH + kind * DH
                to = base + h * DH
                wide[p * PAD : p * PAD + SHARD, to : to + DH] = shard[:, at : at + DH]
    g_ref[...] = wide[...].astype(BF)


def pack(pos, shards):
    return pl.pallas_call(
        pack_kernel,
        grid_spec=pltpu.PrefetchScalarGridSpec(
            num_scalar_prefetch=1,
            grid=(1,),
            in_specs=[pl.BlockSpec(memory_space=pl.ANY)] * 4,
            out_specs=pl.BlockSpec((BLK, COLS), lambda g, p: (0, 0)),
            scratch_shapes=[
                pltpu.VMEM((4, SHARD, 3 * HL * DH), BF),
                pltpu.VMEM((BLK, COLS), F32),
                pltpu.SemaphoreType.DMA((4,)),
            ],
        ),
        out_shape=jax.ShapeDtypeStruct((BLK, COLS), BF),
        compiler_params=pltpu.CompilerParams(vmem_limit_bytes=VMEM),
        cost_estimate=pl.CostEstimate(flops=0, bytes_accessed=4 * MIB, transcendentals=0),
        name="pack",
    )(pos, *shards)


def spread_kernel(x_ref, o_ref):
    gap = jnp.zeros((PAD - SHARD, x_ref.shape[1]), BF)
    for y in range(4):
        for x in range(4):
            for c in range(2):
                block, slot = (y, x) if c == 0 else (4 + x, y)
                dev = place(y, x, c)
                at = slot * PAD
                o_ref[block, at : at + SHARD, :] = x_ref[dev * SHARD : (dev + 1) * SHARD, :]
                o_ref[block, at + SHARD : at + PAD, :] = gap


def spread(xt):
    n = xt.shape[1]
    blk = 256
    return pl.pallas_call(
        spread_kernel,
        grid=(n // blk,),
        in_specs=[pl.BlockSpec((D, blk), lambda g: (0, g))],
        out_specs=pl.BlockSpec((8, BLK, blk), lambda g: (0, 0, g)),
        out_shape=jax.ShapeDtypeStruct((8, BLK, n), BF),
        compiler_params=pltpu.CompilerParams(vmem_limit_bytes=VMEM),
        cost_estimate=pl.CostEstimate(flops=0, bytes_accessed=4 * n * D, transcendentals=0),
        name="spread",
    )(xt)


def product(w, x):
    return lax.dot_general(w, x, (((0,), (0,)), ((), ())), preferred_element_type=F32)


def fetch(pieces, wbuf, sem, first, cols):
    copies = [
        pltpu.make_async_copy(
            piece.at[:, pl.ds(first, cols)], wbuf.at[pl.ds(i * BLK, BLK)], sem.at[i]
        )
        for i, piece in enumerate(pieces)
    ]
    for copy in copies:
        copy.start()
    for copy in copies:
        copy.wait()


def rows_of(x_refs):
    return jnp.concatenate([x[0] for x in x_refs], axis=0)


def x_specs(n):
    return [
        pl.BlockSpec((1, BLK, GROUP), lambda g, b, *_, i=i: (b[i], 0, g)) for i in range(n)
    ]


def part_kernel(count, more, blocks, *refs):
    pieces, x_refs = refs[:count], refs[count : 2 * count]
    rest = refs[2 * count :]
    kv_in, q_in = rest[:2] if more else (None, None)
    kv_ref, q_ref, wbuf, sem = rest[2 * more :]

    @pl.when(pl.program_id(0) == 0)
    def _():
        fetch(pieces, wbuf, sem, 0, COLS)

    x = rows_of(x_refs)
    kv = product(wbuf[:, : 2 * HL * DH], x)
    kv_ref[...] = kv + kv_in[...] if more else kv
    q = product(wbuf[:, QCOL : QCOL + HL * DH], x)
    q_ref[...] = q + q_in[...] if more else q


def part_call(blocks, pieces, xp, sums=()):
    count, n = len(pieces), xp.shape[2]
    kv_spec = pl.BlockSpec((2 * HL * DH, GROUP), lambda g, b: (0, g))
    q_spec = pl.BlockSpec((HL * DH, GROUP), lambda g, b: (0, g))
    return pl.pallas_call(
        lambda *refs: part_kernel(count, 1 if sums else 0, *refs),
        grid_spec=pltpu.PrefetchScalarGridSpec(
            num_scalar_prefetch=1,
            grid=(n // GROUP,),
            in_specs=[pl.BlockSpec(memory_space=pl.ANY)] * count
            + x_specs(count)
            + ([kv_spec, q_spec] if sums else []),
            out_specs=[kv_spec, q_spec],
            scratch_shapes=[
                pltpu.VMEM((count * BLK, COLS), BF),
                pltpu.SemaphoreType.DMA((count,)),
            ],
        ),
        out_shape=[
            jax.ShapeDtypeStruct((2 * HL * DH, n), F32),
            jax.ShapeDtypeStruct((HL * DH, n), F32),
        ],
        compiler_params=pltpu.CompilerParams(vmem_limit_bytes=VMEM),
        cost_estimate=pl.CostEstimate(
            flops=2 * n * 768 * 1680, bytes_accessed=8 * n * 1680, transcendentals=0
        ),
        name="part_more" if sums else "part_first",
    )(blocks, *pieces, *([xp] * count), *sums)


def feature(raw):
    a = raw.astype(BF).astype(F32)
    return jnp.where(a > 0, a + 1.0, jnp.exp(jnp.minimum(a, 0.0))).astype(BF)


def kv_kernel(count, blocks, *refs):
    pieces, x_refs = refs[:count], refs[count : 2 * count]
    sum_ref, fk_ref, v_ref, pre_ref, tot_ref, wbuf, run, sem = refs[2 * count :]
    g = pl.program_id(0)

    @pl.when(g == 0)
    def _():
        fetch(pieces, wbuf, sem, 0, QCOL)
        run[...] = jnp.zeros_like(run)

    x = rows_of(x_refs)
    raw = product(wbuf[:, : 2 * HL * DH], x) + sum_ref[...]
    fk = feature(raw[: HL * DH, :])
    tail = (lax.broadcasted_iota(jnp.int32, (VA - DH, GROUP), 0) == 0).astype(F32).astype(BF)
    for h in range(HL):
        kn = fk[h * DH : (h + 1) * DH, :].T
        fk_ref[h] = kn
        at = (HL + h) * DH
        va = jnp.concatenate([raw[at : at + DH, :].astype(BF), tail], axis=0)
        v_ref[h] = va
        state = jnp.dot(va, kn, preferred_element_type=F32)
        before = run[h]
        pre_ref[0, h] = before
        run[h] = before + state

    @pl.when(g == pl.num_programs(0) - 1)
    def _():
        tot_ref[...] = run[...].astype(BF)


def kv_call(blocks, pieces, xp, sums):
    count, n = len(pieces), xp.shape[2]
    groups = n // GROUP
    return pl.pallas_call(
        lambda *refs: kv_kernel(count, *refs),
        grid_spec=pltpu.PrefetchScalarGridSpec(
            num_scalar_prefetch=1,
            grid=(groups,),
            in_specs=[pl.BlockSpec(memory_space=pl.ANY)] * count
            + x_specs(count)
            + [pl.BlockSpec((2 * HL * DH, GROUP), lambda g, p: (0, g))],
            out_specs=[
                pl.BlockSpec((HL, GROUP, DH), lambda g, p: (0, g, 0)),
                pl.BlockSpec((HL, VA, GROUP), lambda g, p: (0, 0, g)),
                pl.BlockSpec((1, HL, VA, DH), lambda g, p: (g, 0, 0, 0)),
                pl.BlockSpec((HL, VA, DH), lambda g, p: (0, 0, 0)),
            ],
            scratch_shapes=[
                pltpu.VMEM((count * BLK, QCOL), BF),
                pltpu.VMEM((HL, VA, DH), F32),
                pltpu.SemaphoreType.DMA((count,)),
            ],
        ),
        out_shape=[
            jax.ShapeDtypeStruct((HL, n, DH), BF),
            jax.ShapeDtypeStruct((HL, VA, n), BF),
            jax.ShapeDtypeStruct((groups, HL, VA, DH), F32),
            jax.ShapeDtypeStruct((HL, VA, DH), BF),
        ],
        compiler_params=pltpu.CompilerParams(vmem_limit_bytes=VMEM),
        cost_estimate=pl.CostEstimate(
            flops=2 * n * 1280 * 1120, bytes_accessed=4 * n * 1120, transcendentals=0
        ),
        name="keys_values",
    )(blocks, *pieces, *([xp] * count), sums)


def q_kernel(count, blocks, *refs):
    pieces, x_refs = refs[:count], refs[count : 2 * count]
    sum_ref, fq_ref, wbuf, sem = refs[2 * count :]

    @pl.when(pl.program_id(0) == 0)
    def _():
        fetch(pieces, wbuf, sem, QCOL, COLS - QCOL)

    x = rows_of(x_refs)
    fq_ref[...] = feature(product(wbuf[:, : HL * DH], x) + sum_ref[...])


def q_call(blocks, pieces, xp, sums):
    count, n = len(pieces), xp.shape[2]
    spec = pl.BlockSpec((HL * DH, GROUP), lambda g, p: (0, g))
    return pl.pallas_call(
        lambda *refs: q_kernel(count, *refs),
        grid_spec=pltpu.PrefetchScalarGridSpec(
            num_scalar_prefetch=1,
            grid=(n // GROUP,),
            in_specs=[pl.BlockSpec(memory_space=pl.ANY)] * count + x_specs(count) + [spec],
            out_specs=spec,
            scratch_shapes=[
                pltpu.VMEM((count * BLK, COLS - QCOL), BF),
                pltpu.SemaphoreType.DMA((count,)),
            ],
        ),
        out_shape=jax.ShapeDtypeStruct((HL * DH, n), BF),
        compiler_params=pltpu.CompilerParams(vmem_limit_bytes=VMEM),
        cost_estimate=pl.CostEstimate(
            flops=2 * n * 1280 * 560, bytes_accessed=4 * n * 560, transcendentals=0
        ),
        name="queries",
    )(blocks, *pieces, *([xp] * count), sums)


def mask_rows(code, j0, rows, t0, cols):
    parts = []
    for j in range(j0, j0 + rows // 64):
        t = lax.broadcasted_iota(jnp.int32, (64, cols), 1) + t0
        s = lax.broadcasted_iota(jnp.int32, (64, cols), 0)
        i = t >> 6
        bit = (jnp.full((64, cols), code, jnp.int32) >> (((i * (i - 1)) >> 1) + j)) & 1
        same = jnp.where(s <= (t & 63), 1, 0)
        keep = jnp.where(i > j, bit, jnp.where(i == j, same, 0))
        parts.append(keep.astype(F32).astype(BF))
    return jnp.concatenate(parts, axis=0)


def attend_kernel(codes, fk_ref, v_ref, fq_ref, num_ref):
    code = codes[pl.program_id(0)]
    half = GROUP // 2
    upper = mask_rows(code, 0, half, 0, GROUP)
    lower = mask_rows(code, 4, half, half, half)
    for h in range(HL):
        fq = fq_ref[h * DH : (h + 1) * DH, :]
        top = jnp.dot(fk_ref[h, :half, :], fq, preferred_element_type=F32)
        top = top.astype(BF) * upper
        low = jnp.dot(fk_ref[h, half:, :], fq[:, half:], preferred_element_type=F32)
        low = low.astype(BF) * lower
        num = jnp.dot(v_ref[h, :, :half], top, preferred_element_type=F32)
        more = jnp.dot(v_ref[h, :, half:], low, preferred_element_type=F32)
        num_ref[h, :, :half] = num[:, :half]
        num_ref[h, :, half:] = num[:, half:] + more


def attend_call(codes, fk, v, fq):
    n = fq.shape[1]
    return pl.pallas_call(
        attend_kernel,
        grid_spec=pltpu.PrefetchScalarGridSpec(
            num_scalar_prefetch=1,
            grid=(n // GROUP,),
            in_specs=[
                pl.BlockSpec((HL, GROUP, DH), lambda g, m: (0, g, 0)),
                pl.BlockSpec((HL, VA, GROUP), lambda g, m: (0, 0, g)),
                pl.BlockSpec((HL * DH, GROUP), lambda g, m: (0, g)),
            ],
            out_specs=pl.BlockSpec((HL, VA, GROUP), lambda g, m: (0, 0, g)),
        ),
        out_shape=jax.ShapeDtypeStruct((HL, VA, n), F32),
        compiler_params=pltpu.CompilerParams(vmem_limit_bytes=VMEM),
        cost_estimate=pl.CostEstimate(
            flops=2 * n * GROUP * 512 * 2 * HL, bytes_accessed=8 * n * 560, transcendentals=0
        ),
        name="attend",
    )(codes, fk, v, fq)


def join_kernel(scale, dev_ref, pre_ref, fq_ref, num_ref, out_ref, sq_ref):
    total = jnp.zeros((1, GROUP), F32)
    for h in range(HL):
        prefix = (dev_ref[h] + pre_ref[0, h]).astype(BF)
        fq = fq_ref[h * DH : (h + 1) * DH, :]
        num = num_ref[h] + jnp.dot(prefix, fq, preferred_element_type=F32)
        out = num[:DH, :] * (scale[h] / num[DH : DH + 1, :])
        out_ref[h * DH : (h + 1) * DH, :] = out
        total = total + jnp.sum(out * out, axis=0, keepdims=True)
    sq_ref[...] = total


def join_call(scale, dev, pre, fq, num):
    n = fq.shape[1]
    groups = n // GROUP
    return pl.pallas_call(
        join_kernel,
        grid_spec=pltpu.PrefetchScalarGridSpec(
            num_scalar_prefetch=1,
            grid=(groups,),
            in_specs=[
                pl.BlockSpec((HL, VA, DH), lambda g, s: (0, 0, 0)),
                pl.BlockSpec((1, HL, VA, DH), lambda g, s: (g, 0, 0, 0)),
                pl.BlockSpec((HL * DH, GROUP), lambda g, s: (0, g)),
                pl.BlockSpec((HL, VA, GROUP), lambda g, s: (0, 0, g)),
            ],
            out_specs=[
                pl.BlockSpec((HL * DH, GROUP), lambda g, s: (0, g)),
                pl.BlockSpec((1, GROUP), lambda g, s: (0, g)),
            ],
        ),
        out_shape=[
            jax.ShapeDtypeStruct((HL * DH, n), F32),
            jax.ShapeDtypeStruct((1, n), F32),
        ],
        compiler_params=pltpu.CompilerParams(vmem_limit_bytes=VMEM),
        cost_estimate=pl.CostEstimate(
            flops=2 * n * 256 * VA * HL, bytes_accessed=n * 560 * 12, transcendentals=0
        ),
        name="join",
    )(scale, dev, pre, fq, num)


def norm_kernel(out_ref, sq_ref, gain_ref, o_ref):
    inv = lax.rsqrt(sq_ref[...] * (1.0 / (H * DH)) + 1e-06)
    o_ref[...] = (out_ref[...] * inv * gain_ref[...]).astype(BF)


def norm_call(out, squares, gain):
    n = out.shape[1]
    return pl.pallas_call(
        norm_kernel,
        grid=(n // GROUP,),
        in_specs=[
            pl.BlockSpec((HL * DH, GROUP), lambda g: (0, g)),
            pl.BlockSpec((1, GROUP), lambda g: (0, g)),
            pl.BlockSpec((HL * DH, 1), lambda g: (0, 0)),
        ],
        out_specs=pl.BlockSpec((HL * DH, GROUP), lambda g: (0, g)),
        out_shape=jax.ShapeDtypeStruct((HL * DH, n), BF),
        compiler_params=pltpu.CompilerParams(vmem_limit_bytes=VMEM),
        cost_estimate=pl.CostEstimate(flops=0, bytes_accessed=n * 560 * 6, transcendentals=0),
        name="norm",
    )(out, squares, gain)


def body(tokens, qkv_weight, block_mask, head_scale, norm_gain):
    me = lax.axis_index("tm").astype(jnp.int32)
    y, x, core = me // 8, (me // 2) % 4, me % 2
    pos = jnp.stack([y, x, core])
    shards = [qkv_weight] + [shift(qkv_weight, first_leg(d)) for d in (1, 2, 3)]
    xp = spread(tokens.T)
    *shards, xp = lax.optimization_barrier((*shards, xp))
    near = pack(pos, shards)
    own = [near] + [shift(near, second_leg(d)) for d in (1, 2, 3)]
    sib = [shift(a, SIBLING) for a in own]

    def block(mine, d):
        which = core if mine else 1 - core
        return which * 4 + (jnp.where(which == 0, y, x) + 4 - d) % 4

    def blocks(steps):
        return jnp.stack([block(mine, d) for d in steps for mine in (True, False)])

    def pieces(steps):
        return [a[d] for d in steps for a in (own, sib)]

    sums = part_call(blocks([0]), pieces([0]), xp)
    kv_sum, q_sum = part_call(blocks([1]), pieces([1]), xp, sums)
    last = [2, 3]
    fk, v, pre, tot = kv_call(blocks(last), pieces(last), xp, kv_sum)

    other = shift(tot, SIBLING).astype(F32)
    before = jnp.where(core == 1, other, 0.0)
    chip = (tot.astype(F32) + other).astype(BF)
    chip, q_sum = lax.optimization_barrier((chip, q_sum))
    fq = q_call(blocks(last), pieces(last), xp, q_sum)
    row = chip.astype(F32)
    for d in (1, 2, 3):
        got = shift(chip, along_x(d)).astype(F32)
        row = row + got
        before = before + jnp.where(x >= d, got, 0.0)
    row, fq = lax.optimization_barrier((row.astype(BF), fq))
    num = attend_call(block_mask, fk, v, fq)
    for d in (1, 2, 3):
        before = before + shift(row, later_y(d)).astype(F32)

    out, squares = join_call(head_scale, before, pre, fq, num)
    squares = squares + sum(
        lax.ppermute(squares, "head", [(i, (i + d) % 4) for i in range(4)]) for d in (1, 2, 3)
    )
    return norm_call(out, squares, norm_gain.reshape(HL * DH, 1)).T


def solution(mesh):
    in_specs = (P("tm", None), P("tm", "head"), P("tm"), P("head"), P("head"))
    out_specs = P("tm", "head")
    return jax.shard_map(body, mesh=mesh, in_specs=in_specs, out_specs=out_specs, check_vma=False)
```

time: 156 us -> 154 us (0.987)
  Pallas kernels: 53.4 us -> 87.1 us
  local copies, waits for them, and re-layouts: 23.3 us -> 4.32 us
  starting transfers between devices: 41.6 us -> 31 us
  waiting for transfers between devices: 32.5 us -> 24.7 us
  other arithmetic: 3.82 us -> 5.88 us
    pallas_call x2 -> x6, Pallas kernels: 44.5 us -> 64.9 us  [the longest x2 26 us: part_call(): pl.pallas_call(lambda *refs: part_kernel(count, 1 if sums else 0, *refs),...]
    unnamed x32 -> x16, local copies, waits for them, and re-layouts: 19.2 us -> 3.47 us
    ppermute x28 -> x17, starting transfers between devices: 35 us -> 24.5 us  [shift(): return lax.ppermute(a, 'tm', moves)]
    ppermute x28 -> x17, waiting for transfers between devices: 30 us -> 22.7 us  [shift(): return lax.ppermute(a, 'tm', moves)]
    pallas_call x1, Pallas kernels: 3.39 us -> 9.73 us  [spread(): pl.pallas_call(spread_kernel, grid=(n // blk,), in_specs=[pl.BlockSpec((D...]
    pallas_call x1, Pallas kernels: 3.18 us -> 7.92 us  [join_call(): pl.pallas_call(join_kernel, grid_spec=pltpu.PrefetchScalarGridSpec(num_sc...]
    another operation x3 -> x4, other arithmetic: 0.23 us -> 2.59 us  [the longest x3 1.94 us: blocks(): return jnp.stack([block(mine, d) for d in steps for mine in (True, False)])]
    pallas_call x1, Pallas kernels: 2.38 us -> 4.59 us  [norm_call(): pl.pallas_call(norm_kernel, grid=(n // GROUP,), in_specs=[pl.BlockSpec((H...]
  transfers between devices with their start and end apart: 31 -> 20, of which waited for: 12 -> 5; matrix products, arithmetic and copies ran while one was open for 1% -> 2% of each run, Pallas kernels for 15% -> 36%
where the time goes in v2:
time: 154 us; the launch traced here: 153 us
  Pallas kernels  87.1 us (57%)
  starting transfers between devices  31 us (20%)
  waiting for transfers between devices  24.7 us (16%)
  other arithmetic  5.88 us (4%)
  local copies, waits for them, and re-layouts  4.32 us (3%)
    pallas_call x2, Pallas kernels, part_call(): pl.pallas_call(lambda *refs: part_kernel(count, 1 if sums else 0, *refs),...  26 us
    ppermute x17, starting transfers between devices, shift(): return lax.ppermute(a, 'tm', moves)  24.5 us
    ppermute x17, waiting for transfers between devices, shift(): return lax.ppermute(a, 'tm', moves)  22.7 us
    pallas_call x1, Pallas kernels, kv_call(): pl.pallas_call(lambda *refs: kv_kernel(count, *refs), grid_spec=pltpu.Pre...  15.4 us
    pallas_call x1, Pallas kernels, q_call(): pl.pallas_call(lambda *refs: q_kernel(count, *refs), grid_spec=pltpu.Pref...  10.1 us
    pallas_call x1, Pallas kernels, attend_call(): pl.pallas_call(attend_kernel, grid_spec=pltpu.PrefetchScalarGridSpec(num_...  9.74 us
    pallas_call x1, Pallas kernels, spread(): pl.pallas_call(spread_kernel, grid=(n // blk,), in_specs=[pl.BlockSpec((D...  9.73 us
    pallas_call x1, Pallas kernels, join_call(): pl.pallas_call(join_kernel, grid_spec=pltpu.PrefetchScalarGridSpec(num_sc...  7.92 us
  transfers between devices with their start and end apart: 20, of which 5 were waited for; matrix products, arithmetic and copies ran while one was open for 2% of the time, Pallas kernels for 36%

profile of v2, /device:TPU:0, one launch (start us, length us, event | category | flops | bytes accessed | tf_op | source)
XLA Modules:
  0.0 153.2 jit_solution(6399720942034503028)
XLA Ops:
  0.0 1.6 %collective-permute-start = (bf16[70,1680]{1,0:T(8,128)(2,1)}, bf16[70,1680]{1,0:T(8,128)(2,1)S(1)}, u32[]{:S(2)}, u32[]{:S(2)}) collective-permute-start(bf16[70,1680]{1,0:T(8,128)(2,1)} %a0), channel_id=1, source_target_pairs={{0,8},{4,36},{8,16},{12,44},{16,24},{20,52},{24,0},{28,60},{32,40}... | collective-permute-start | bytes 705608 | tf_op jit(solution)/shard_map/ppermute | solution.py:63
  1.6 2.7 %collective-permute-start.1 = (bf16[70,1680]{1,0:T(8,128)(2,1)}, bf16[70,1680]{1,0:T(8,128)(2,1)S(1)}, u32[]{:S(2)}, u32[]{:S(2)}) collective-permute-start(bf16[70,1680]{1,0:T(8,128)(2,1)} %a0), channel_id=1, source_target_pairs={{0,16},{4,68},{8,24},{12,76},{16,0},{20,84},{24,8},{28,92},{32,48}... | collective-permute-start | bytes 705608 | tf_op jit(solution)/shard_map/ppermute | solution.py:63
  4.3 1.4 collective-permute-start.2
  5.7 9.7 %spread.1.refs_3_.refs_4_.refs_5_.refs_6_.refs_7_.refs_8_ = bf16[8,288,2048]{2,1,0:T(8,128)(2,1)} custom-call(bf16[2240,2048]{1,0:T(8,128)(2,1)} %bitcast.13), custom_call_target="tpu_custom_call" | custom-call | bytes 18350080 | tf_op jit(solution)/shard_map/spread/pallas_call | solution.py:123
  17.6 3.6 %pack.1.refs_1_ = bf16[288,1792]{1,0:T(8,128)(2,1)} custom-call(s32[3]{0:T(128)} %pad_add_fusion.1.pos, bf16[70,1680]{1,0:T(8,128)(2,1)} %a0, bf16[70,1680]{1,0:T(8,128)(2,1)} %copy-done.4, bf16[70,1680]{1,0:T(8,128)(2,1)} %copy-done.5, bf16[70,1680]{1,0:T(8,128)(2,1)} %copy-done.6), custom_call_target="tpu_custom_call" | custom-call | bytes 4194304 | tf_op jit(solution)/shard_map/pack/pallas_call | solution.py:88
  21.3 1.6 %collective-permute-start.7 = (bf16[288,1792]{1,0:T(8,128)(2,1)}, bf16[288,1792]{1,0:T(8,128)(2,1)}, u32[]{:S(2)}, u32[]{:S(2)}) collective-permute-start(bf16[288,1792]{1,0:T(8,128)(2,1)} %pack.1.refs_1_), channel_id=1, source_target_pairs={{0,32},{4,12},{8,40},{12,20},{16,48},{20,28},{24,56},{28,4},{32,64... | collective-permute-start | bytes 3096584 | tf_op jit(solution)/shard_map/ppermute | solution.py:63
  22.9 2.9 %collective-permute-start.3 = (bf16[288,1792]{1,0:T(8,128)(2,1)}, bf16[288,1792]{1,0:T(8,128)(2,1)S(1)}, u32[]{:S(2)}, u32[]{:S(2)}) collective-permute-start(bf16[288,1792]{1,0:T(8,128)(2,1)} %pack.1.refs_1_), channel_id=1, source_target_pairs={{0,64},{4,20},{8,72},{12,28},{16,80},{20,4},{24,88},{28,12},{32,96... | collective-permute-start | bytes 3096584 | tf_op jit(solution)/shard_map/ppermute | solution.py:63
  25.8 1.3 collective-permute-start.5
  27.2 10.3 %collective-permute-done.7.refs_1_ = bf16[288,1792]{1,0:T(8,128)(2,1)} collective-permute-done((bf16[288,1792]{1,0:T(8,128)(2,1)}, bf16[288,1792]{1,0:T(8,128)(2,1)}, u32[]{:S(2)}, u32[]{:S(2)}) %collective-permute-start.7) | collective-permute-done | bytes 1032224 | tf_op jit(solution)/shard_map/ppermute | solution.py:63
  38.8 10.9 %collective-permute-done.3.refs_1_ = bf16[288,1792]{1,0:T(8,128)(2,1)S(1)} collective-permute-done((bf16[288,1792]{1,0:T(8,128)(2,1)}, bf16[288,1792]{1,0:T(8,128)(2,1)S(1)}, u32[]{:S(2)}, u32[]{:S(2)}) %collective-permute-start.3) | collective-permute-done | bytes 1032224 | tf_op jit(solution)/shard_map/ppermute | solution.py:63
  50.9 1.0 copy-done.3
  51.9 10.9 %part_first.1 = (f32[1120,2048]{1,0:T(8,128)}, f32[560,2048]{1,0:T(8,128)}) custom-call(s32[2]{0:T(128)} %pad_add_fusion.3.refs_0_, bf16[288,1792]{1,0:T(8,128)(2,1)} %pack.1.refs_1_, bf16[288,1792]{1,0:T(8,128)(2,1)} %copy-done.3, bf16[8,288,2048]{2,1,0:T(8,128)(2,1)} %spread.1.refs_3_.refs_4_.refs_5_.refs_6_.refs_7_.refs_8_, ...), custom_call_target="tpu_custom_call" | custom-call | flops 5284823040 | bytes 27525120 | tf_op jit(solution)/shard_map/part_first/pallas_call | solution.py:183
  62.8 15.0 %part_more.1 = (f32[1120,2048]{1,0:T(8,128)}, f32[560,2048]{1,0:T(8,128)}) custom-call(s32[2]{0:T(128)} %pad_add_fusion.2.refs_0_, bf16[288,1792]{1,0:T(8,128)(2,1)} %collective-permute-done.7.refs_1_, bf16[288,1792]{1,0:T(8,128)(2,1)} %collective-permute-done.8.refs_2_, bf16[8,288,2048]{2,1,0:T(8,128)(2,1)} %spread.1.refs_3_.refs_4_.refs_5_.refs_6_.refs_7_.refs_8_, ...), custom_call_target="tpu_custom_call" | custom-call | flops 5284823040 | bytes 27525120 | tf_op jit(solution)/shard_map/part_more/pallas_call | solution.py:183
  77.9 1.0 copy-done.2
  78.9 15.4 %keys_values.1 = (bf16[5,2048,112]{2,1,0:T(8,128)(2,1)}, bf16[5,128,2048]{2,1,0:T(8,128)(2,1)}, f32[4,5,128,112]{3,2,1,0:T(8,128)}, bf16[5,128,112]{2,1,0:T(8,128)(2,1)}) custom-call(s32[4]{0:T(128)} %pad_add_fusion.refs_0_, bf16[288,1792]{1,0:T(8,128)(2,1)} %copy-done, bf16[288,1792]{1,0:T(8,128)(2,1)} %copy-done.2, bf16[288,1792]{1,0:T(8,128)(2,1)} %copy-done.1, ...), custom_call_target="tpu_custom_call" | custom-call | flops 5872025600 | bytes 9175040 | tf_op jit(solution)/shard_map/keys_values/pallas_call | solution.py:247
  94.6 1.4 collective-permute-done.10
  96.0 1.0 fusion.6
  97.7 0.9 collective-permute-start.12
  98.5 1.9 %collective-permute-start.13 = (bf16[5,128,112]{2,1,0:T(8,128)(2,1)S(1)}, bf16[5,128,112]{2,1,0:T(8,128)(2,1)S(1)}, u32[]{:S(2)}, u32[]{:S(2)}) collective-permute-start(bf16[5,128,112]{2,1,0:T(8,128)(2,1)S(1)} %fusion.6), channel_id=1, source_target_pairs={{0,24},{4,28},{8,0},{12,4},{16,8},{20,12},{24,16},{28,20},{32,56},... | collective-permute-start | bytes 430088 | tf_op jit(solution)/shard_map/ppermute | solution.py:63
  100.4 10.1 %queries.1.fq_ref = bf16[560,2048]{1,0:T(8,128)(2,1)} custom-call(s32[4]{0:T(128)} %pad_add_fusion.refs_0_, bf16[288,1792]{1,0:T(8,128)(2,1)} %copy-done, bf16[288,1792]{1,0:T(8,128)(2,1)} %copy-done.2, bf16[288,1792]{1,0:T(8,128)(2,1)} %copy-done.1, bf16[288,1792]{1,0:T(8,128)(2,1)} %collective-permute-done.6.refs_4_, ...), custom_call_target="tpu_custom_call" | custom-call | flops 2936012800 | bytes 4587520 | tf_op jit(solution)/shard_map/queries/pallas_call | solution.py:296
  110.7 3.2 %collective-permute-start.14 = (bf16[5,128,112]{2,1,0:T(8,128)(2,1)S(1)}, bf16[5,128,112]{2,1,0:T(8,128)(2,1)S(1)}, u32[]{:S(2)}, u32[]{:S(2)}) collective-permute-start(bf16[5,128,112]{2,1,0:T(8,128)(2,1)S(1)} %fusion.7), channel_id=1, source_target_pairs={{0,32},{4,36},{8,40},{12,44},{16,48},{20,52},{24,56},{28,60},{32,6... | collective-permute-start | bytes 430088 | tf_op jit(solution)/shard_map/ppermute | solution.py:63
  113.9 4.0 %collective-permute-start.15 = (bf16[5,128,112]{2,1,0:T(8,128)(2,1)S(1)}, bf16[5,128,112]{2,1,0:T(8,128)(2,1)S(1)}, u32[]{:S(2)}, u32[]{:S(2)}) collective-permute-start(bf16[5,128,112]{2,1,0:T(8,128)(2,1)S(1)} %fusion.7), channel_id=1, source_target_pairs={{0,64},{4,68},{8,72},{12,76},{16,80},{20,84},{24,88},{28,92},{32,9... | collective-permute-start | bytes 430088 | tf_op jit(solution)/shard_map/ppermute | solution.py:63
  117.9 1.5 collective-permute-start.16
  119.4 9.7 %attend.1.num_ref = f32[5,128,2048]{2,1,0:T(8,128)} custom-call(s32[4]{0:T(128)} %codes.1, bf16[5,2048,112]{2,1,0:T(8,128)(2,1)} %get-tuple-element.39.fk_ref, bf16[5,128,2048]{2,1,0:T(8,128)(2,1)} %get-tuple-element.40.v_ref, bf16[560,2048]{1,0:T(8,128)(2,1)} %queries.1.fq_ref), custom_call_target="tpu_custom_call" | custom-call | flops 10737418240 | bytes 9175040 | tf_op jit(solution)/shard_map/attend/pallas_call | solution.py:349
  129.1 0.9 fusion.5.dev_ref
  130.1 7.9 %join.1 = (f32[560,2048]{1,0:T(8,128)}, f32[1,2048]{1,0:T(1,128)}) custom-call(f32[5]{0:T(128)} %scale.1, f32[5,128,112]{2,1,0:T(8,128)} %fusion.5.dev_ref, f32[4,5,128,112]{3,2,1,0:T(8,128)} %get-tuple-element.37.pre_ref, bf16[560,2048]{1,0:T(8,128)(2,1)} %queries.1.fq_ref, f32[5,128,2048]{2,1,0:T(8,128)} %attend.1.num_ref), custom_call_target="tpu_custom_call" | custom-call | flops 671088640 | bytes 13762560 | tf_op jit(solution)/shard_map/join/pallas_call | solution.py:385
  138.0 1.9 %collective-permute-start.17 = (f32[1,2048]{1,0:T(1,128)}, f32[1,2048]{1,0:T(1,128)S(1)}, u32[]{:S(2)}, u32[]{:S(2)}) collective-permute-start(f32[1,2048]{1,0:T(1,128)} %get-tuple-element.42), channel_id=1, source_target_pairs={{0,1},{1,2},{2,3},{3,0},{4,5},{5,6},{6,7},{7,4},{8,9},{9,10},{10,1... | collective-permute-start | bytes 24584 | tf_op jit(solution)/shard_map/ppermute | solution.py:479
  139.9 3.6 %collective-permute-start.18 = (f32[1,2048]{1,0:T(1,128)}, f32[1,2048]{1,0:T(1,128)S(1)}, u32[]{:S(2)}, u32[]{:S(2)}) collective-permute-start(f32[1,2048]{1,0:T(1,128)} %get-tuple-element.42), channel_id=1, source_target_pairs={{0,2},{1,3},{2,0},{3,1},{4,6},{5,7},{6,4},{7,5},{8,10},{9,11},{10,... | collective-permute-start | bytes 24584 | tf_op jit(solution)/shard_map/ppermute | solution.py:479
  143.5 1.0 collective-permute-start.19
  145.4 1.9 %collective-permute-done.19 = f32[1,2048]{1,0:T(1,128)S(1)} collective-permute-done((f32[1,2048]{1,0:T(1,128)}, f32[1,2048]{1,0:T(1,128)S(1)}, u32[]{:S(2)}, u32[]{:S(2)}) %collective-permute-start.19) | collective-permute-done | bytes 8224 | tf_op jit(solution)/shard_map/ppermute | solution.py:479
  147.3 1.3 add_add_fusion.sq_ref
  148.7 4.6 %norm.1 = bf16[560,2048]{1,0:T(8,128)(2,1)} custom-call(f32[560,2048]{1,0:T(8,128)} %get-tuple-element.41.out_ref, f32[1,2048]{1,0:T(1,128)} %add_add_fusion.sq_ref, f32[560,1]{1,0:T(8,128)} %reshape.4.gain_ref), custom_call_target="tpu_custom_call" | custom-call | bytes 6881280 | tf_op jit(solution)/shard_map/norm/pallas_call | solution.py:420
  (42 shorter events, 6.6 us)
Async XLA Ops:
  0.0 16.1 %collective-permute-start = (bf16[70,1680]{1,0:T(8,128)(2,1)}, bf16[70,1680]{1,0:T(8,128)(2,1)S(1)}, u32[]{:S(2)}, u32[]{:S(2)}) collective-permute-start(bf16[70,1680]{1,0:T(8,128)(2,1)} %a0), channel_id=1, source_target_pairs={{0,8},{4,36},{8,16},{12,44},{16,24},{20,52},{24,0},{28,60},{32,40}... | collective-permute-start | bytes 705608 | tf_op jit(solution)/shard_map/ppermute | solution.py:63
  1.6 14.6 %collective-permute-start.1 = (bf16[70,1680]{1,0:T(8,128)(2,1)}, bf16[70,1680]{1,0:T(8,128)(2,1)S(1)}, u32[]{:S(2)}, u32[]{:S(2)}) collective-permute-start(bf16[70,1680]{1,0:T(8,128)(2,1)} %a0), channel_id=1, source_target_pairs={{0,16},{4,68},{8,24},{12,76},{16,0},{20,84},{24,8},{28,92},{32,48}... | collective-permute-start | bytes 705608 | tf_op jit(solution)/shard_map/ppermute | solution.py:63
  4.3 11.8 %collective-permute-start.2 = (bf16[70,1680]{1,0:T(8,128)(2,1)}, bf16[70,1680]{1,0:T(8,128)(2,1)S(1)}, u32[]{:S(2)}, u32[]{:S(2)}) collective-permute-start(bf16[70,1680]{1,0:T(8,128)(2,1)} %a0), channel_id=1, source_target_pairs={{0,24},{4,100},{8,0},{12,108},{16,8},{20,116},{24,16},{28,124},{32... | collective-permute-start | bytes 705608 | tf_op jit(solution)/shard_map/ppermute | solution.py:63
  16.1 0.7 copy-start.4
  16.1 0.8 copy-start.5
  16.9 0.7 copy-start.6
  21.3 16.2 %collective-permute-start.7 = (bf16[288,1792]{1,0:T(8,128)(2,1)}, bf16[288,1792]{1,0:T(8,128)(2,1)}, u32[]{:S(2)}, u32[]{:S(2)}) collective-permute-start(bf16[288,1792]{1,0:T(8,128)(2,1)} %pack.1.refs_1_), channel_id=1, source_target_pairs={{0,32},{4,12},{8,40},{12,20},{16,48},{20,28},{24,56},{28,4},{32,64... | collective-permute-start | bytes 3096584 | tf_op jit(solution)/shard_map/ppermute | solution.py:63
  22.9 26.8 %collective-permute-start.3 = (bf16[288,1792]{1,0:T(8,128)(2,1)}, bf16[288,1792]{1,0:T(8,128)(2,1)S(1)}, u32[]{:S(2)}, u32[]{:S(2)}) collective-permute-start(bf16[288,1792]{1,0:T(8,128)(2,1)} %pack.1.refs_1_), channel_id=1, source_target_pairs={{0,64},{4,20},{8,72},{12,28},{16,80},{20,4},{24,88},{28,12},{32,96... | collective-permute-start | bytes 3096584 | tf_op jit(solution)/shard_map/ppermute | solution.py:63
  25.8 23.9 %collective-permute-start.5 = (bf16[288,1792]{1,0:T(8,128)(2,1)}, bf16[288,1792]{1,0:T(8,128)(2,1)S(1)}, u32[]{:S(2)}, u32[]{:S(2)}) collective-permute-start(bf16[288,1792]{1,0:T(8,128)(2,1)} %pack.1.refs_1_), channel_id=1, source_target_pairs={{0,96},{4,28},{8,104},{12,4},{16,112},{20,12},{24,120},{28,20},{32... | collective-permute-start | bytes 3096584 | tf_op jit(solution)/shard_map/ppermute | solution.py:63
  27.2 23.7 %collective-permute-start.9 = (bf16[288,1792]{1,0:T(8,128)(2,1)}, bf16[288,1792]{1,0:T(8,128)(2,1)S(1)}, u32[]{:S(2)}, u32[]{:S(2)}) collective-permute-start(bf16[288,1792]{1,0:T(8,128)(2,1)} %pack.1.refs_1_), channel_id=1, source_target_pairs={{0,4},{4,0},{8,12},{12,8},{16,20},{20,16},{24,28},{28,24},{32,36},... | collective-permute-start | bytes 3096584 | tf_op jit(solution)/shard_map/ppermute | solution.py:63
  37.5 25.3 %collective-permute-start.8 = (bf16[288,1792]{1,0:T(8,128)(2,1)}, bf16[288,1792]{1,0:T(8,128)(2,1)}, u32[]{:S(2)}, u32[]{:S(2)}) collective-permute-start(bf16[288,1792]{1,0:T(8,128)(2,1)} %collective-permute-done.7.refs_1_), channel_id=1, source_target_pairs={{0,4},{4,0},{8,12},{12,8},{16,20},{20,16},{24,28},{28,24},{32,36},... | collective-permute-start | bytes 3096584 | tf_op jit(solution)/shard_map/ppermute | solution.py:63
  49.7 13.1 %copy-start = (bf16[288,1792]{1,0:T(8,128)(2,1)}, bf16[288,1792]{1,0:T(8,128)(2,1)S(1)}, u32[]{:S(2)}) copy-start(bf16[288,1792]{1,0:T(8,128)(2,1)S(1)} %collective-permute-done.3.refs_1_) | copy-start | bytes 3096580
  49.7 28.2 %collective-permute-start.4 = (bf16[288,1792]{1,0:T(8,128)(2,1)S(1)}, bf16[288,1792]{1,0:T(8,128)(2,1)S(1)}, u32[]{:S(2)}, u32[]{:S(2)}) collective-permute-start(bf16[288,1792]{1,0:T(8,128)(2,1)S(1)} %collective-permute-done.3.refs_1_), channel_id=1, source_target_pairs={{0,4},{4,0},{8,12},{12,8},{16,20},{20,16},{24,28},{28,24},{32,36},... | collective-permute-start | bytes 3096584 | tf_op jit(solution)/shard_map/ppermute | solution.py:63
  49.7 13.1 %copy-start.1 = (bf16[288,1792]{1,0:T(8,128)(2,1)}, bf16[288,1792]{1,0:T(8,128)(2,1)S(1)}, u32[]{:S(2)}) copy-start(bf16[288,1792]{1,0:T(8,128)(2,1)S(1)} %collective-permute-done.5.refs_3_) | copy-start | bytes 3096580
  49.7 28.2 %collective-permute-start.6 = (bf16[288,1792]{1,0:T(8,128)(2,1)S(1)}, bf16[288,1792]{1,0:T(8,128)(2,1)}, u32[]{:S(2)}, u32[]{:S(2)}) collective-permute-start(bf16[288,1792]{1,0:T(8,128)(2,1)S(1)} %collective-permute-done.5.refs_3_), channel_id=1, source_target_pairs={{0,4},{4,0},{8,12},{12,8},{16,20},{20,16},{24,28},{28,24},{32,36},... | collective-permute-start | bytes 3096584 | tf_op jit(solution)/shard_map/ppermute | solution.py:63
  50.9 1.0 copy-start.3
  77.9 1.0 copy-start.2
  94.3 1.7 %collective-permute-start.10 = (bf16[5,128,112]{2,1,0:T(8,128)(2,1)}, bf16[5,128,112]{2,1,0:T(8,128)(2,1)S(1)}, u32[]{:S(2)}, u32[]{:S(2)}) collective-permute-start(bf16[5,128,112]{2,1,0:T(8,128)(2,1)} %get-tuple-element.32), channel_id=1, source_target_pairs={{0,4},{4,0},{8,12},{12,8},{16,20},{20,16},{24,28},{28,24},{32,36},... | collective-permute-start | bytes 430088 | tf_op jit(solution)/shard_map/ppermute | solution.py:63
  97.0 13.5 %collective-permute-start.11 = (bf16[5,128,112]{2,1,0:T(8,128)(2,1)S(1)}, bf16[5,128,112]{2,1,0:T(8,128)(2,1)S(1)}, u32[]{:S(2)}, u32[]{:S(2)}) collective-permute-start(bf16[5,128,112]{2,1,0:T(8,128)(2,1)S(1)} %fusion.6), channel_id=1, source_target_pairs={{0,8},{4,12},{8,16},{12,20},{16,24},{20,28},{24,0},{28,4},{32,40},... | collective-permute-start | bytes 430088 | tf_op jit(solution)/shard_map/ppermute | solution.py:63
  97.7 12.9 %collective-permute-start.12 = (bf16[5,128,112]{2,1,0:T(8,128)(2,1)S(1)}, bf16[5,128,112]{2,1,0:T(8,128)(2,1)S(1)}, u32[]{:S(2)}, u32[]{:S(2)}) collective-permute-start(bf16[5,128,112]{2,1,0:T(8,128)(2,1)S(1)} %fusion.6), channel_id=1, source_target_pairs={{0,16},{4,20},{8,24},{12,28},{16,0},{20,4},{24,8},{28,12},{32,48},... | collective-permute-start | bytes 430088 | tf_op jit(solution)/shard_map/ppermute | solution.py:63
  98.5 12.0 %collective-permute-start.13 = (bf16[5,128,112]{2,1,0:T(8,128)(2,1)S(1)}, bf16[5,128,112]{2,1,0:T(8,128)(2,1)S(1)}, u32[]{:S(2)}, u32[]{:S(2)}) collective-permute-start(bf16[5,128,112]{2,1,0:T(8,128)(2,1)S(1)} %fusion.6), channel_id=1, source_target_pairs={{0,24},{4,28},{8,0},{12,4},{16,8},{20,12},{24,16},{28,20},{32,56},... | collective-permute-start | bytes 430088 | tf_op jit(solution)/shard_map/ppermute | solution.py:63
  110.7 18.4 %collective-permute-start.14 = (bf16[5,128,112]{2,1,0:T(8,128)(2,1)S(1)}, bf16[5,128,112]{2,1,0:T(8,128)(2,1)S(1)}, u32[]{:S(2)}, u32[]{:S(2)}) collective-permute-start(bf16[5,128,112]{2,1,0:T(8,128)(2,1)S(1)} %fusion.7), channel_id=1, source_target_pairs={{0,32},{4,36},{8,40},{12,44},{16,48},{20,52},{24,56},{28,60},{32,6... | collective-permute-start | bytes 430088 | tf_op jit(solution)/shard_map/ppermute | solution.py:63
  113.9 15.3 %collective-permute-start.15 = (bf16[5,128,112]{2,1,0:T(8,128)(2,1)S(1)}, bf16[5,128,112]{2,1,0:T(8,128)(2,1)S(1)}, u32[]{:S(2)}, u32[]{:S(2)}) collective-permute-start(bf16[5,128,112]{2,1,0:T(8,128)(2,1)S(1)} %fusion.7), channel_id=1, source_target_pairs={{0,64},{4,68},{8,72},{12,76},{16,80},{20,84},{24,88},{28,92},{32,9... | collective-permute-start | bytes 430088 | tf_op jit(solution)/shard_map/ppermute | solution.py:63
  117.9 11.2 %collective-permute-start.16 = (bf16[5,128,112]{2,1,0:T(8,128)(2,1)S(1)}, bf16[5,128,112]{2,1,0:T(8,128)(2,1)S(1)}, u32[]{:S(2)}, u32[]{:S(2)}) collective-permute-start(bf16[5,128,112]{2,1,0:T(8,128)(2,1)S(1)} %fusion.7), channel_id=1, source_target_pairs={{0,96},{4,100},{8,104},{12,108},{16,112},{20,116},{24,120},{28,124... | collective-permute-start | bytes 430088 | tf_op jit(solution)/shard_map/ppermute | solution.py:63
  130.1 14.4 %copy-start.7 = (f32[560]{0:T(1024)S(1)}, f32[560]{0:T(1024)}, u32[]{:S(2)}) copy-start(f32[560]{0:T(1024)} %param.9) | copy-start | bytes 6724
  138.0 7.4 %collective-permute-start.17 = (f32[1,2048]{1,0:T(1,128)}, f32[1,2048]{1,0:T(1,128)S(1)}, u32[]{:S(2)}, u32[]{:S(2)}) collective-permute-start(f32[1,2048]{1,0:T(1,128)} %get-tuple-element.42), channel_id=1, source_target_pairs={{0,1},{1,2},{2,3},{3,0},{4,5},{5,6},{6,7},{7,4},{8,9},{9,10},{10,1... | collective-permute-start | bytes 24584 | tf_op jit(solution)/shard_map/ppermute | solution.py:479
  139.9 5.5 %collective-permute-start.18 = (f32[1,2048]{1,0:T(1,128)}, f32[1,2048]{1,0:T(1,128)S(1)}, u32[]{:S(2)}, u32[]{:S(2)}) collective-permute-start(f32[1,2048]{1,0:T(1,128)} %get-tuple-element.42), channel_id=1, source_target_pairs={{0,2},{1,3},{2,0},{3,1},{4,6},{5,7},{6,4},{7,5},{8,10},{9,11},{10,... | collective-permute-start | bytes 24584 | tf_op jit(solution)/shard_map/ppermute | solution.py:479
  143.5 3.9 %collective-permute-start.19 = (f32[1,2048]{1,0:T(1,128)}, f32[1,2048]{1,0:T(1,128)S(1)}, u32[]{:S(2)}, u32[]{:S(2)}) collective-permute-start(f32[1,2048]{1,0:T(1,128)} %get-tuple-element.42), channel_id=1, source_target_pairs={{0,3},{1,0},{2,1},{3,2},{4,7},{5,4},{6,5},{7,6},{8,11},{9,8},{10,9... | collective-permute-start | bytes 24584 | tf_op jit(solution)/shard_map/ppermute | solution.py:479

commit v3 on v2

--- a/solution.py
+++ b/solution.py
@@ -20,6 +20,7 @@
 F32 = jnp.float32
 MIB = 1 << 20
 VMEM = 60 * MIB
+QUICK = pl.CostEstimate(flops=1, bytes_accessed=1, transcendentals=0)
 
 
 def place(y, x, c):
@@ -100,7 +101,7 @@
         ),
         out_shape=jax.ShapeDtypeStruct((BLK, COLS), BF),
         compiler_params=pltpu.CompilerParams(vmem_limit_bytes=VMEM),
-        cost_estimate=pl.CostEstimate(flops=0, bytes_accessed=4 * MIB, transcendentals=0),
+        cost_estimate=QUICK,
         name="pack",
     )(pos, *shards)
 
@@ -127,7 +128,7 @@
         out_specs=pl.BlockSpec((8, BLK, blk), lambda g: (0, 0, g)),
         out_shape=jax.ShapeDtypeStruct((8, BLK, n), BF),
         compiler_params=pltpu.CompilerParams(vmem_limit_bytes=VMEM),
-        cost_estimate=pl.CostEstimate(flops=0, bytes_accessed=4 * n * D, transcendentals=0),
+        cost_estimate=QUICK,
         name="spread",
     )(xt)
 
@@ -159,36 +160,31 @@
     ]
 
 
-def part_kernel(count, more, blocks, *refs):
+def part_kernel(count, blocks, *refs):
     pieces, x_refs = refs[:count], refs[count : 2 * count]
-    rest = refs[2 * count :]
-    kv_in, q_in = rest[:2] if more else (None, None)
-    kv_ref, q_ref, wbuf, sem = rest[2 * more :]
+    kv_ref, q_ref, wbuf, sem = refs[2 * count :]
 
     @pl.when(pl.program_id(0) == 0)
     def _():
         fetch(pieces, wbuf, sem, 0, COLS)
 
     x = rows_of(x_refs)
-    kv = product(wbuf[:, : 2 * HL * DH], x)
-    kv_ref[...] = kv + kv_in[...] if more else kv
-    q = product(wbuf[:, QCOL : QCOL + HL * DH], x)
-    q_ref[...] = q + q_in[...] if more else q
-
-
-def part_call(blocks, pieces, xp, sums=()):
+    kv_ref[...] = product(wbuf[:, : 2 * HL * DH], x)
+    q_ref[...] = product(wbuf[:, QCOL : QCOL + HL * DH], x)
+
+
+def part_call(blocks, pieces, xp):
     count, n = len(pieces), xp.shape[2]
-    kv_spec = pl.BlockSpec((2 * HL * DH, GROUP), lambda g, b: (0, g))
-    q_spec = pl.BlockSpec((HL * DH, GROUP), lambda g, b: (0, g))
-    return pl.pallas_call(
-        lambda *refs: part_kernel(count, 1 if sums else 0, *refs),
+    return pl.pallas_call(
+        lambda *refs: part_kernel(count, *refs),
         grid_spec=pltpu.PrefetchScalarGridSpec(
             num_scalar_prefetch=1,
             grid=(n // GROUP,),
-            in_specs=[pl.BlockSpec(memory_space=pl.ANY)] * count
-            + x_specs(count)
-            + ([kv_spec, q_spec] if sums else []),
-            out_specs=[kv_spec, q_spec],
+            in_specs=[pl.BlockSpec(memory_space=pl.ANY)] * count + x_specs(count),
+            out_specs=[
+                pl.BlockSpec((2 * HL * DH, GROUP), lambda g, b: (0, g)),
+                pl.BlockSpec((HL * DH, GROUP), lambda g, b: (0, g)),
+            ],
             scratch_shapes=[
                 pltpu.VMEM((count * BLK, COLS), BF),
                 pltpu.SemaphoreType.DMA((count,)),
@@ -199,11 +195,43 @@
             jax.ShapeDtypeStruct((HL * DH, n), F32),
         ],
         compiler_params=pltpu.CompilerParams(vmem_limit_bytes=VMEM),
-        cost_estimate=pl.CostEstimate(
-            flops=2 * n * 768 * 1680, bytes_accessed=8 * n * 1680, transcendentals=0
-        ),
-        name="part_more" if sums else "part_first",
-    )(blocks, *pieces, *([xp] * count), *sums)
+        cost_estimate=QUICK,
+        name="part_first",
+    )(blocks, *pieces, *([xp] * count))
+
+
+def more_kernel(count, blocks, *refs):
+    pieces, x_refs = refs[:count], refs[count : 2 * count]
+    sum_ref, kv_ref, wbuf, sem = refs[2 * count :]
+
+    @pl.when(pl.program_id(0) == 0)
+    def _():
+        fetch(pieces, wbuf, sem, 0, QCOL)
+
+    x = rows_of(x_refs)
+    kv_ref[...] = product(wbuf[:, : 2 * HL * DH], x) + sum_ref[...]
+
+
+def more_call(blocks, pieces, xp, sums):
+    count, n = len(pieces), xp.shape[2]
+    spec = pl.BlockSpec((2 * HL * DH, GROUP), lambda g, b: (0, g))
+    return pl.pallas_call(
+        lambda *refs: more_kernel(count, *refs),
+        grid_spec=pltpu.PrefetchScalarGridSpec(
+            num_scalar_prefetch=1,
+            grid=(n // GROUP,),
+            in_specs=[pl.BlockSpec(memory_space=pl.ANY)] * count + x_specs(count) + [spec],
+            out_specs=spec,
+            scratch_shapes=[
+                pltpu.VMEM((count * BLK, QCOL), BF),
+                pltpu.SemaphoreType.DMA((count,)),
+            ],
+        ),
+        out_shape=jax.ShapeDtypeStruct((2 * HL * DH, n), F32),
+        compiler_params=pltpu.CompilerParams(vmem_limit_bytes=VMEM),
+        cost_estimate=QUICK,
+        name="part_more",
+    )(blocks, *pieces, *([xp] * count), sums)
 
 
 def feature(raw):
@@ -222,14 +250,14 @@
         run[...] = jnp.zeros_like(run)
 
     x = rows_of(x_refs)
-    raw = product(wbuf[:, : 2 * HL * DH], x) + sum_ref[...]
-    fk = feature(raw[: HL * DH, :])
+    half = HL * DH
+    fk = feature(product(wbuf[:, :half], x) + sum_ref[:half, :])
+    vals = (product(wbuf[:, half : 2 * half], x) + sum_ref[half:, :]).astype(BF)
     tail = (lax.broadcasted_iota(jnp.int32, (VA - DH, GROUP), 0) == 0).astype(F32).astype(BF)
     for h in range(HL):
         kn = fk[h * DH : (h + 1) * DH, :].T
         fk_ref[h] = kn
-        at = (HL + h) * DH
-        va = jnp.concatenate([raw[at : at + DH, :].astype(BF), tail], axis=0)
+        va = jnp.concatenate([vals[h * DH : (h + 1) * DH, :], tail], axis=0)
         v_ref[h] = va
         state = jnp.dot(va, kn, preferred_element_type=F32)
         before = run[h]
@@ -271,9 +299,7 @@
             jax.ShapeDtypeStruct((HL, VA, DH), BF),
         ],
         compiler_params=pltpu.CompilerParams(vmem_limit_bytes=VMEM),
-        cost_estimate=pl.CostEstimate(
-            flops=2 * n * 1280 * 1120, bytes_accessed=4 * n * 1120, transcendentals=0
-        ),
+        cost_estimate=QUICK,
         name="keys_values",
     )(blocks, *pieces, *([xp] * count), sums)
 
@@ -307,9 +333,7 @@
         ),
         out_shape=jax.ShapeDtypeStruct((HL * DH, n), BF),
         compiler_params=pltpu.CompilerParams(vmem_limit_bytes=VMEM),
-        cost_estimate=pl.CostEstimate(
-            flops=2 * n * 1280 * 560, bytes_accessed=4 * n * 560, transcendentals=0
-        ),
+        cost_estimate=QUICK,
         name="queries",
     )(blocks, *pieces, *([xp] * count), sums)
 
@@ -359,10 +383,8 @@
             out_specs=pl.BlockSpec((HL, VA, GROUP), lambda g, m: (0, 0, g)),
         ),
         out_shape=jax.ShapeDtypeStruct((HL, VA, n), F32),
-        compiler_params=pltpu.CompilerParams(vmem_limit_bytes=VMEM),
-        cost_estimate=pl.CostEstimate(
-            flops=2 * n * GROUP * 512 * 2 * HL, bytes_accessed=8 * n * 560, transcendentals=0
-        ),
+        compiler_params=pltpu.CompilerParams(vmem_limit_bytes=20 * MIB),
+        cost_estimate=QUICK,
         name="attend",
     )(codes, fk, v, fq)
 
@@ -402,10 +424,8 @@
             jax.ShapeDtypeStruct((HL * DH, n), F32),
             jax.ShapeDtypeStruct((1, n), F32),
         ],
-        compiler_params=pltpu.CompilerParams(vmem_limit_bytes=VMEM),
-        cost_estimate=pl.CostEstimate(
-            flops=2 * n * 256 * VA * HL, bytes_accessed=n * 560 * 12, transcendentals=0
-        ),
+        compiler_params=pltpu.CompilerParams(vmem_limit_bytes=20 * MIB),
+        cost_estimate=QUICK,
         name="join",
     )(scale, dev, pre, fq, num)
 
@@ -427,8 +447,8 @@
         ],
         out_specs=pl.BlockSpec((HL * DH, GROUP), lambda g: (0, g)),
         out_shape=jax.ShapeDtypeStruct((HL * DH, n), BF),
-        compiler_params=pltpu.CompilerParams(vmem_limit_bytes=VMEM),
-        cost_estimate=pl.CostEstimate(flops=0, bytes_accessed=n * 560 * 6, transcendentals=0),
+        compiler_params=pltpu.CompilerParams(vmem_limit_bytes=20 * MIB),
+        cost_estimate=QUICK,
         name="norm",
     )(out, squares, gain)
 
@@ -438,32 +458,36 @@
     y, x, core = me // 8, (me // 2) % 4, me % 2
     pos = jnp.stack([y, x, core])
     shards = [qkv_weight] + [shift(qkv_weight, first_leg(d)) for d in (1, 2, 3)]
-    xp = spread(tokens.T)
-    *shards, xp = lax.optimization_barrier((*shards, xp))
     near = pack(pos, shards)
+    near, xt = lax.optimization_barrier((near, tokens.T))
     own = [near] + [shift(near, second_leg(d)) for d in (1, 2, 3)]
-    sib = [shift(a, SIBLING) for a in own]
+    sib = [shift(near, SIBLING)]
+    xp = spread(xt)
 
     def block(mine, d):
         which = core if mine else 1 - core
         return which * 4 + (jnp.where(which == 0, y, x) + 4 - d) % 4
 
-    def blocks(steps):
-        return jnp.stack([block(mine, d) for d in steps for mine in (True, False)])
-
-    def pieces(steps):
-        return [a[d] for d in steps for a in (own, sib)]
-
-    sums = part_call(blocks([0]), pieces([0]), xp)
-    kv_sum, q_sum = part_call(blocks([1]), pieces([1]), xp, sums)
-    last = [2, 3]
+    def blocks(which):
+        return jnp.stack([block(mine, d) for mine, d in which])
+
+    def pieces(which):
+        return [(own if mine else sib)[d] for mine, d in which]
+
+    first = [(True, 0), (False, 0)]
+    mine = [(True, d) for d in (1, 2, 3)]
+    last = [(False, d) for d in (1, 2, 3)]
+    kv_sum, q_sum = part_call(blocks(first), pieces(first), xp)
+    *own, kv_sum = lax.optimization_barrier((*own, kv_sum))
+    sib += [shift(a, SIBLING) for a in own[1:]]
+    kv_sum = more_call(blocks(mine), pieces(mine), xp, kv_sum)
     fk, v, pre, tot = kv_call(blocks(last), pieces(last), xp, kv_sum)
 
     other = shift(tot, SIBLING).astype(F32)
     before = jnp.where(core == 1, other, 0.0)
     chip = (tot.astype(F32) + other).astype(BF)
     chip, q_sum = lax.optimization_barrier((chip, q_sum))
-    fq = q_call(blocks(last), pieces(last), xp, q_sum)
+    fq = q_call(blocks(mine + last), pieces(mine + last), xp, q_sum)
     row = chip.astype(F32)
     for d in (1, 2, 3):
         got = shift(chip, along_x(d)).astype(F32)

time: 154 us -> 133 us (0.86)
  waiting for transfers between devices: 24.7 us -> 10.1 us
  Pallas kernels: 87.1 us -> 76.4 us
  starting transfers between devices: 31 us -> 34.5 us
    ppermute x17, waiting for transfers between devices: 22.7 us -> 7.56 us  [shift(): return lax.ppermute(a, 'tm', moves)]
    pallas_call x1, Pallas kernels: 7.92 us -> 3.18 us  [join_call(): pl.pallas_call(join_kernel, grid_spec=pltpu.PrefetchScalarGridSpec(num_sc...]
    ppermute x17, starting transfers between devices: 24.5 us -> 27.9 us  [shift(): return lax.ppermute(a, 'tm', moves)]
    pallas_call x1, Pallas kernels: 9.74 us -> 7.16 us  [attend_call(): pl.pallas_call(attend_kernel, grid_spec=pltpu.PrefetchScalarGridSpec(num_...]
    pallas_call x1, Pallas kernels: 4.59 us -> 2.38 us  [norm_call(): pl.pallas_call(norm_kernel, grid=(n // GROUP,), in_specs=[pl.BlockSpec((H...]
    pallas_call x1, Pallas kernels: 10.1 us -> 11.8 us  [q_call(): pl.pallas_call(lambda *refs: q_kernel(count, *refs), grid_spec=pltpu.Pref...]
    unnamed x16 -> x26, local copies, waits for them, and re-layouts: 3.47 us -> 4.81 us
  transfers between devices with their start and end apart: 20 -> 20, of which waited for: 5 -> 6; matrix products, arithmetic and copies ran while one was open for 2% -> 3% of each run, Pallas kernels for 36% -> 40%
where the time goes in v3:
time: 133 us; the launch traced here: 132 us
  Pallas kernels  76.4 us (57%)
  starting transfers between devices  34.5 us (26%)
  waiting for transfers between devices  10.1 us (8%)
  local copies, waits for them, and re-layouts  5.6 us (4%)
  other arithmetic  5.48 us (4%)
    ppermute x17, starting transfers between devices, shift(): return lax.ppermute(a, 'tm', moves)  27.9 us
    pallas_call x1, Pallas kernels, kv_call(): pl.pallas_call(lambda *refs: kv_kernel(count, *refs), grid_spec=pltpu.Pre...  13.9 us
    pallas_call x1, Pallas kernels, more_call(): pl.pallas_call(lambda *refs: more_kernel(count, *refs), grid_spec=pltpu.P...  13.6 us
    pallas_call x1, Pallas kernels, q_call(): pl.pallas_call(lambda *refs: q_kernel(count, *refs), grid_spec=pltpu.Pref...  11.8 us
    pallas_call x1, Pallas kernels, part_call(): pl.pallas_call(lambda *refs: part_kernel(count, *refs), grid_spec=pltpu.P...  11 us
    pallas_call x1, Pallas kernels, spread(): pl.pallas_call(spread_kernel, grid=(n // blk,), in_specs=[pl.BlockSpec((D...  9.74 us
    ppermute x17, waiting for transfers between devices, shift(): return lax.ppermute(a, 'tm', moves)  7.56 us
    pallas_call x1, Pallas kernels, attend_call(): pl.pallas_call(attend_kernel, grid_spec=pltpu.PrefetchScalarGridSpec(num_...  7.16 us
  transfers between devices with their start and end apart: 20, of which 6 were waited for; matrix products, arithmetic and copies ran while one was open for 3% of the time, Pallas kernels for 40%

profile of v3, /device:TPU:0, one launch (start us, length us, event | category | flops | bytes accessed | tf_op | source)
XLA Modules:
  0.0 132.3 jit_solution(754599230225861805)
XLA Ops:
  0.0 1.6 %collective-permute-start = (bf16[70,1680]{1,0:T(8,128)(2,1)}, bf16[70,1680]{1,0:T(8,128)(2,1)S(1)}, u32[]{:S(2)}, u32[]{:S(2)}) collective-permute-start(bf16[70,1680]{1,0:T(8,128)(2,1)} %a0.1), channel_id=1, source_target_pairs={{0,8},{4,36},{8,16},{12,44},{16,24},{20,52},{24,0},{28,60},{32,40}... | collective-permute-start | bytes 705608 | tf_op jit(solution)/shard_map/ppermute | solution.py:64
  1.6 2.7 %collective-permute-start.1 = (bf16[70,1680]{1,0:T(8,128)(2,1)}, bf16[70,1680]{1,0:T(8,128)(2,1)S(1)}, u32[]{:S(2)}, u32[]{:S(2)}) collective-permute-start(bf16[70,1680]{1,0:T(8,128)(2,1)} %a0.1), channel_id=1, source_target_pairs={{0,16},{4,68},{8,24},{12,76},{16,0},{20,84},{24,8},{28,92},{32,48}... | collective-permute-start | bytes 705608 | tf_op jit(solution)/shard_map/ppermute | solution.py:64
  4.3 1.4 %collective-permute-start.2 = (bf16[70,1680]{1,0:T(8,128)(2,1)}, bf16[70,1680]{1,0:T(8,128)(2,1)S(1)}, u32[]{:S(2)}, u32[]{:S(2)}) collective-permute-start(bf16[70,1680]{1,0:T(8,128)(2,1)} %a0.1), channel_id=1, source_target_pairs={{0,24},{4,100},{8,0},{12,108},{16,8},{20,116},{24,16},{28,124},{32... | collective-permute-start | bytes 705608 | tf_op jit(solution)/shard_map/ppermute | solution.py:64
  6.4 1.4 %collective-permute-done.a1 = bf16[70,1680]{1,0:T(8,128)(2,1)S(1)} collective-permute-done((bf16[70,1680]{1,0:T(8,128)(2,1)}, bf16[70,1680]{1,0:T(8,128)(2,1)S(1)}, u32[]{:S(2)}, u32[]{:S(2)}) %collective-permute-start) | collective-permute-done | bytes 235232 | tf_op jit(solution)/shard_map/ppermute | solution.py:64
  7.8 3.8 %collective-permute-done.1.a2 = bf16[70,1680]{1,0:T(8,128)(2,1)S(1)} collective-permute-done((bf16[70,1680]{1,0:T(8,128)(2,1)}, bf16[70,1680]{1,0:T(8,128)(2,1)S(1)}, u32[]{:S(2)}, u32[]{:S(2)}) %collective-permute-start.1) | collective-permute-done | bytes 235232 | tf_op jit(solution)/shard_map/ppermute | solution.py:64
  13.0 3.6 %pack.1.refs_1_ = bf16[288,1792]{1,0:T(8,128)(2,1)} custom-call(s32[3]{0:T(128)} %pad_add_fusion.1.pos, bf16[70,1680]{1,0:T(8,128)(2,1)} %a0.1, bf16[70,1680]{1,0:T(8,128)(2,1)} %copy-done.9, bf16[70,1680]{1,0:T(8,128)(2,1)} %copy-done.10, bf16[70,1680]{1,0:T(8,128)(2,1)} %copy-done.11), custom_call_target="tpu_custom_call" | custom-call | flops 1 | bytes 1 | tf_op jit(solution)/shard_map/pack/pallas_call | solution.py:89
  16.7 1.6 %collective-permute-start.3 = (bf16[288,1792]{1,0:T(8,128)(2,1)}, bf16[288,1792]{1,0:T(8,128)(2,1)S(1)}, u32[]{:S(2)}, u32[]{:S(2)}) collective-permute-start(bf16[288,1792]{1,0:T(8,128)(2,1)} %pack.1.refs_1_), channel_id=1, source_target_pairs={{0,32},{4,12},{8,40},{12,20},{16,48},{20,28},{24,56},{28,4},{32,64... | collective-permute-start | bytes 3096584 | tf_op jit(solution)/shard_map/ppermute | solution.py:64
  18.4 2.9 %collective-permute-start.4 = (bf16[288,1792]{1,0:T(8,128)(2,1)}, bf16[288,1792]{1,0:T(8,128)(2,1)S(1)}, u32[]{:S(2)}, u32[]{:S(2)}) collective-permute-start(bf16[288,1792]{1,0:T(8,128)(2,1)} %pack.1.refs_1_), channel_id=1, source_target_pairs={{0,64},{4,20},{8,72},{12,28},{16,80},{20,4},{24,88},{28,12},{32,96... | collective-permute-start | bytes 3096584 | tf_op jit(solution)/shard_map/ppermute | solution.py:64
  21.3 1.3 %collective-permute-start.5 = (bf16[288,1792]{1,0:T(8,128)(2,1)}, bf16[288,1792]{1,0:T(8,128)(2,1)S(1)}, u32[]{:S(2)}, u32[]{:S(2)}) collective-permute-start(bf16[288,1792]{1,0:T(8,128)(2,1)} %pack.1.refs_1_), channel_id=1, source_target_pairs={{0,96},{4,28},{8,104},{12,4},{16,112},{20,12},{24,120},{28,20},{32... | collective-permute-start | bytes 3096584 | tf_op jit(solution)/shard_map/ppermute | solution.py:64
  23.3 9.7 %spread.1.refs_3_.refs_4_.refs_5_.refs_6_.refs_7_.refs_8_.refs_9_.refs_10_.refs_11_.refs_12_ = bf16[8,288,2048]{2,1,0:T(8,128)(2,1)} custom-call(bf16[2240,2048]{1,0:T(8,128)(2,1)} %bitcast.13), custom_call_target="tpu_custom_call" | custom-call | flops 1 | bytes 1 | tf_op jit(solution)/shard_map/spread/pallas_call | solution.py:124
  33.0 11.0 %part_first.1 = (f32[1120,2048]{1,0:T(8,128)}, f32[560,2048]{1,0:T(8,128)}) custom-call(s32[2]{0:T(128)} %pad_add_fusion.2.refs_0_, bf16[288,1792]{1,0:T(8,128)(2,1)} %pack.1.refs_1_, bf16[288,1792]{1,0:T(8,128)(2,1)} %collective-permute-done.6.refs_2_, ...), custom_call_target="tpu_custom_call" | custom-call | flops 1 | bytes 1 | tf_op jit(solution)/shard_map/part_first/pallas_call | solution.py:178
  44.0 1.1 collective-permute-done.4.refs_2_
  47.1 13.6 %part_more.1.refs_7_ = f32[1120,2048]{1,0:T(8,128)} custom-call(s32[3]{0:T(128)} %pad_add_fusion.3.refs_0_, bf16[288,1792]{1,0:T(8,128)(2,1)} %copy-done.6, bf16[288,1792]{1,0:T(8,128)(2,1)} %copy-done.7, bf16[288,1792]{1,0:T(8,128)(2,1)} %copy-done.8, ...), custom_call_target="tpu_custom_call" | custom-call | flops 1 | bytes 1 | tf_op jit(solution)/shard_map/part_more/pallas_call | solution.py:218
  60.7 13.9 %keys_values.1 = (bf16[5,2048,112]{2,1,0:T(8,128)(2,1)}, bf16[5,128,2048]{2,1,0:T(8,128)(2,1)}, f32[4,5,128,112]{3,2,1,0:T(8,128)}, bf16[5,128,112]{2,1,0:T(8,128)(2,1)}) custom-call(s32[3]{0:T(128)} %pad_add_fusion.refs_0_, bf16[288,1792]{1,0:T(8,128)(2,1)} %collective-permute-done.7.refs_1_.refs_4_, ...), custom_call_target="tpu_custom_call" | custom-call | flops 1 | bytes 1 | tf_op jit(solution)/shard_map/keys_values/pallas_call | solution.py:275
  75.1 1.2 collective-permute-done.10
  77.3 1.3 collective-permute-start.11
  78.6 2.1 %collective-permute-start.12 = (bf16[5,128,112]{2,1,0:T(8,128)(2,1)S(1)}, bf16[5,128,112]{2,1,0:T(8,128)(2,1)S(1)}, u32[]{:S(2)}, u32[]{:S(2)}) collective-permute-start(bf16[5,128,112]{2,1,0:T(8,128)(2,1)S(1)} %fusion.6), channel_id=1, source_target_pairs={{0,16},{4,20},{8,24},{12,28},{16,0},{20,4},{24,8},{28,12},{32,48},... | collective-permute-start | bytes 430088 | tf_op jit(solution)/shard_map/ppermute | solution.py:64
  80.7 1.6 %collective-permute-start.13 = (bf16[5,128,112]{2,1,0:T(8,128)(2,1)S(1)}, bf16[5,128,112]{2,1,0:T(8,128)(2,1)S(1)}, u32[]{:S(2)}, u32[]{:S(2)}) collective-permute-start(bf16[5,128,112]{2,1,0:T(8,128)(2,1)S(1)} %fusion.6), channel_id=1, source_target_pairs={{0,24},{4,28},{8,0},{12,4},{16,8},{20,12},{24,16},{28,20},{32,56},... | collective-permute-start | bytes 430088 | tf_op jit(solution)/shard_map/ppermute | solution.py:64
  83.0 11.8 %queries.1.fq_ref = bf16[560,2048]{1,0:T(8,128)(2,1)} custom-call(s32[6]{0:T(128)} %stack.69.refs_0_, bf16[288,1792]{1,0:T(8,128)(2,1)} %copy-done.6, bf16[288,1792]{1,0:T(8,128)(2,1)} %copy-done.7, bf16[288,1792]{1,0:T(8,128)(2,1)} %copy-done.8, bf16[288,1792]{1,0:T(8,128)(2,1)} %collective-permute-done.7.refs_1_.refs_4_, ...), custom_call_target="tpu_custom_call" | custom-call | flops 1 | bytes 1 | tf_op jit(solution)/shard_map/queries/pallas_call | solution.py:322
  95.6 3.5 %collective-permute-start.14 = (bf16[5,128,112]{2,1,0:T(8,128)(2,1)}, bf16[5,128,112]{2,1,0:T(8,128)(2,1)S(1)}, u32[]{:S(2)}, u32[]{:S(2)}) collective-permute-start(bf16[5,128,112]{2,1,0:T(8,128)(2,1)} %fusion.7), channel_id=1, source_target_pairs={{0,32},{4,36},{8,40},{12,44},{16,48},{20,52},{24,56},{28,60},{32,6... | collective-permute-start | bytes 430088 | tf_op jit(solution)/shard_map/ppermute | solution.py:64
  99.0 4.7 %collective-permute-start.15 = (bf16[5,128,112]{2,1,0:T(8,128)(2,1)}, bf16[5,128,112]{2,1,0:T(8,128)(2,1)}, u32[]{:S(2)}, u32[]{:S(2)}) collective-permute-start(bf16[5,128,112]{2,1,0:T(8,128)(2,1)} %fusion.7), channel_id=1, source_target_pairs={{0,64},{4,68},{8,72},{12,76},{16,80},{20,84},{24,88},{28,92},{32,9... | collective-permute-start | bytes 430088 | tf_op jit(solution)/shard_map/ppermute | solution.py:64
  103.7 1.9 %collective-permute-start.16 = (bf16[5,128,112]{2,1,0:T(8,128)(2,1)}, bf16[5,128,112]{2,1,0:T(8,128)(2,1)}, u32[]{:S(2)}, u32[]{:S(2)}) collective-permute-start(bf16[5,128,112]{2,1,0:T(8,128)(2,1)} %fusion.7), channel_id=1, source_target_pairs={{0,96},{4,100},{8,104},{12,108},{16,112},{20,116},{24,120},{28,124... | collective-permute-start | bytes 430088 | tf_op jit(solution)/shard_map/ppermute | solution.py:64
  105.7 1.6 %copy-done = bf16[560,2048]{1,0:T(8,128)(2,1)S(1)} copy-done((bf16[560,2048]{1,0:T(8,128)(2,1)S(1)}, bf16[560,2048]{1,0:T(8,128)(2,1)}, u32[]{:S(2)}) %copy-start) | copy-done | bytes 2293784
  107.3 1.7 %copy-done.2 = bf16[5,128,2048]{2,1,0:T(8,128)(2,1)S(1)} copy-done((bf16[5,128,2048]{2,1,0:T(8,128)(2,1)S(1)}, bf16[5,128,2048]{2,1,0:T(8,128)(2,1)}, u32[]{:S(2)}) %copy-start.2) | copy-done | bytes 2621464
  109.1 7.2 %attend.1.num_ref = f32[5,128,2048]{2,1,0:T(8,128)S(1)} custom-call(s32[4]{0:T(128)S(1)} %copy-done.4, bf16[5,2048,112]{2,1,0:T(8,128)(2,1)S(1)} %copy-done.1, bf16[5,128,2048]{2,1,0:T(8,128)(2,1)S(1)} %copy-done.2, bf16[560,2048]{1,0:T(8,128)(2,1)S(1)} %copy-done), custom_call_target="tpu_custom_call" | custom-call | flops 1 | bytes 1 | tf_op jit(solution)/shard_map/attend/pallas_call | solution.py:373
  116.3 1.2 fusion.5.dev_ref
  117.5 3.2 %join.1 = (f32[560,2048]{1,0:T(8,128)S(1)}, f32[1,2048]{1,0:T(1,128)S(1)}) custom-call(f32[5]{0:T(128)S(1)} %copy-done.5, f32[5,128,112]{2,1,0:T(8,128)S(1)} %fusion.5.dev_ref, f32[4,5,128,112]{3,2,1,0:T(8,128)S(1)} %copy-done.3, bf16[560,2048]{1,0:T(8,128)(2,1)S(1)} %copy-done, f32[5,128,2048]{2,1,0:T(8,128)S(1)} %attend.1.num_ref), custom_call_target="tpu_custom_call" | custom-call | flops 1 | bytes 1 | tf_op jit(solution)/shard_map/join/pallas_call | solution.py:407
  120.7 2.0 %collective-permute-start.17 = (f32[1,2048]{1,0:T(1,128)S(1)}, f32[1,2048]{1,0:T(1,128)S(1)}, u32[]{:S(2)}, u32[]{:S(2)}) collective-permute-start(f32[1,2048]{1,0:T(1,128)S(1)} %get-tuple-element.40), channel_id=1, source_target_pairs={{0,1},{1,2},{2,3},{3,0},{4,5},{5,6},{6,7},{7,4},{8,9},{9,10},{10,1... | collective-permute-start | bytes 24584 | tf_op jit(solution)/shard_map/ppermute | solution.py:503
  122.7 3.6 %collective-permute-start.18 = (f32[1,2048]{1,0:T(1,128)S(1)}, f32[1,2048]{1,0:T(1,128)S(1)}, u32[]{:S(2)}, u32[]{:S(2)}) collective-permute-start(f32[1,2048]{1,0:T(1,128)S(1)} %get-tuple-element.40), channel_id=1, source_target_pairs={{0,2},{1,3},{2,0},{3,1},{4,6},{5,7},{6,4},{7,5},{8,10},{9,11},{10,... | collective-permute-start | bytes 24584 | tf_op jit(solution)/shard_map/ppermute | solution.py:503
  126.3 1.0 collective-permute-start.19
  128.0 1.9 %collective-permute-done.19 = f32[1,2048]{1,0:T(1,128)S(1)} collective-permute-done((f32[1,2048]{1,0:T(1,128)S(1)}, f32[1,2048]{1,0:T(1,128)S(1)}, u32[]{:S(2)}, u32[]{:S(2)}) %collective-permute-start.19) | collective-permute-done | bytes 8224 | tf_op jit(solution)/shard_map/ppermute | solution.py:503
  129.9 2.4 %norm.1 = bf16[560,2048]{1,0:T(8,128)(2,1)} custom-call(f32[560,2048]{1,0:T(8,128)S(1)} %get-tuple-element.39.out_ref, f32[1,2048]{1,0:T(1,128)S(1)} %add_add_fusion.sq_ref, f32[560,1]{1,0:T(8,128)S(1)} %reshape.4.gain_ref), custom_call_target="tpu_custom_call" | custom-call | flops 1 | bytes 1 | tf_op jit(solution)/shard_map/norm/pallas_call | solution.py:440
  (53 shorter events, 8.3 us)
Async XLA Ops:
  0.0 7.7 %collective-permute-start = (bf16[70,1680]{1,0:T(8,128)(2,1)}, bf16[70,1680]{1,0:T(8,128)(2,1)S(1)}, u32[]{:S(2)}, u32[]{:S(2)}) collective-permute-start(bf16[70,1680]{1,0:T(8,128)(2,1)} %a0.1), channel_id=1, source_target_pairs={{0,8},{4,36},{8,16},{12,44},{16,24},{20,52},{24,0},{28,60},{32,40}... | collective-permute-start | bytes 705608 | tf_op jit(solution)/shard_map/ppermute | solution.py:64
  1.6 10.0 %collective-permute-start.1 = (bf16[70,1680]{1,0:T(8,128)(2,1)}, bf16[70,1680]{1,0:T(8,128)(2,1)S(1)}, u32[]{:S(2)}, u32[]{:S(2)}) collective-permute-start(bf16[70,1680]{1,0:T(8,128)(2,1)} %a0.1), channel_id=1, source_target_pairs={{0,16},{4,68},{8,24},{12,76},{16,0},{20,84},{24,8},{28,92},{32,48}... | collective-permute-start | bytes 705608 | tf_op jit(solution)/shard_map/ppermute | solution.py:64
  4.3 7.3 %collective-permute-start.2 = (bf16[70,1680]{1,0:T(8,128)(2,1)}, bf16[70,1680]{1,0:T(8,128)(2,1)S(1)}, u32[]{:S(2)}, u32[]{:S(2)}) collective-permute-start(bf16[70,1680]{1,0:T(8,128)(2,1)} %a0.1), channel_id=1, source_target_pairs={{0,24},{4,100},{8,0},{12,108},{16,8},{20,116},{24,16},{28,124},{32... | collective-permute-start | bytes 705608 | tf_op jit(solution)/shard_map/ppermute | solution.py:64
  7.8 3.8 %copy-start.9 = (bf16[70,1680]{1,0:T(8,128)(2,1)}, bf16[70,1680]{1,0:T(8,128)(2,1)S(1)}, u32[]{:S(2)}) copy-start(bf16[70,1680]{1,0:T(8,128)(2,1)S(1)} %collective-permute-done.a1) | copy-start | bytes 705604
  12.3 0.7 copy-start.11
  16.6 16.4 %collective-permute-start.6 = (bf16[288,1792]{1,0:T(8,128)(2,1)}, bf16[288,1792]{1,0:T(8,128)(2,1)}, u32[]{:S(2)}, u32[]{:S(2)}) collective-permute-start(bf16[288,1792]{1,0:T(8,128)(2,1)} %pack.1.refs_1_), channel_id=1, source_target_pairs={{0,4},{4,0},{8,12},{12,8},{16,20},{20,16},{24,28},{28,24},{32,36},... | collective-permute-start | bytes 3096584 | tf_op jit(solution)/shard_map/ppermute | solution.py:64
  16.7 27.3 %collective-permute-start.3 = (bf16[288,1792]{1,0:T(8,128)(2,1)}, bf16[288,1792]{1,0:T(8,128)(2,1)S(1)}, u32[]{:S(2)}, u32[]{:S(2)}) collective-permute-start(bf16[288,1792]{1,0:T(8,128)(2,1)} %pack.1.refs_1_), channel_id=1, source_target_pairs={{0,32},{4,12},{8,40},{12,20},{16,48},{20,28},{24,56},{28,4},{32,64... | collective-permute-start | bytes 3096584 | tf_op jit(solution)/shard_map/ppermute | solution.py:64
  18.4 26.8 %collective-permute-start.4 = (bf16[288,1792]{1,0:T(8,128)(2,1)}, bf16[288,1792]{1,0:T(8,128)(2,1)S(1)}, u32[]{:S(2)}, u32[]{:S(2)}) collective-permute-start(bf16[288,1792]{1,0:T(8,128)(2,1)} %pack.1.refs_1_), channel_id=1, source_target_pairs={{0,64},{4,20},{8,72},{12,28},{16,80},{20,4},{24,88},{28,12},{32,96... | collective-permute-start | bytes 3096584 | tf_op jit(solution)/shard_map/ppermute | solution.py:64
  21.3 23.9 %collective-permute-start.5 = (bf16[288,1792]{1,0:T(8,128)(2,1)}, bf16[288,1792]{1,0:T(8,128)(2,1)S(1)}, u32[]{:S(2)}, u32[]{:S(2)}) collective-permute-start(bf16[288,1792]{1,0:T(8,128)(2,1)} %pack.1.refs_1_), channel_id=1, source_target_pairs={{0,96},{4,28},{8,104},{12,4},{16,112},{20,12},{24,120},{28,20},{32... | collective-permute-start | bytes 3096584 | tf_op jit(solution)/shard_map/ppermute | solution.py:64
  44.0 3.1 %copy-start.6 = (bf16[288,1792]{1,0:T(8,128)(2,1)}, bf16[288,1792]{1,0:T(8,128)(2,1)S(1)}, u32[]{:S(2)}) copy-start(bf16[288,1792]{1,0:T(8,128)(2,1)S(1)} %collective-permute-done.3.refs_1_) | copy-start | bytes 3096580
  45.1 1.9 %copy-start.7 = (bf16[288,1792]{1,0:T(8,128)(2,1)}, bf16[288,1792]{1,0:T(8,128)(2,1)S(1)}, u32[]{:S(2)}) copy-start(bf16[288,1792]{1,0:T(8,128)(2,1)S(1)} %collective-permute-done.4.refs_2_) | copy-start | bytes 3096580
  45.1 1.9 %copy-start.8 = (bf16[288,1792]{1,0:T(8,128)(2,1)}, bf16[288,1792]{1,0:T(8,128)(2,1)S(1)}, u32[]{:S(2)}) copy-start(bf16[288,1792]{1,0:T(8,128)(2,1)S(1)} %collective-permute-done.5.refs_3_) | copy-start | bytes 3096580
  45.1 15.5 %collective-permute-start.7 = (bf16[288,1792]{1,0:T(8,128)(2,1)S(1)}, bf16[288,1792]{1,0:T(8,128)(2,1)}, u32[]{:S(2)}, u32[]{:S(2)}) collective-permute-start(bf16[288,1792]{1,0:T(8,128)(2,1)S(1)} %collective-permute-done.3.refs_1_), channel_id=1, source_target_pairs={{0,4},{4,0},{8,12},{12,8},{16,20},{20,16},{24,28},{28,24},{32,36},... | collective-permute-start | bytes 3096584 | tf_op jit(solution)/shard_map/ppermute | solution.py:64
  45.2 15.5 %collective-permute-start.8 = (bf16[288,1792]{1,0:T(8,128)(2,1)S(1)}, bf16[288,1792]{1,0:T(8,128)(2,1)}, u32[]{:S(2)}, u32[]{:S(2)}) collective-permute-start(bf16[288,1792]{1,0:T(8,128)(2,1)S(1)} %collective-permute-done.4.refs_2_), channel_id=1, source_target_pairs={{0,4},{4,0},{8,12},{12,8},{16,20},{20,16},{24,28},{28,24},{32,36},... | collective-permute-start | bytes 3096584 | tf_op jit(solution)/shard_map/ppermute | solution.py:64
  45.7 15.0 %collective-permute-start.9 = (bf16[288,1792]{1,0:T(8,128)(2,1)S(1)}, bf16[288,1792]{1,0:T(8,128)(2,1)}, u32[]{:S(2)}, u32[]{:S(2)}) collective-permute-start(bf16[288,1792]{1,0:T(8,128)(2,1)S(1)} %collective-permute-done.5.refs_3_), channel_id=1, source_target_pairs={{0,4},{4,0},{8,12},{12,8},{16,20},{20,16},{24,28},{28,24},{32,36},... | collective-permute-start | bytes 3096584 | tf_op jit(solution)/shard_map/ppermute | solution.py:64
  74.7 1.7 %collective-permute-start.10 = (bf16[5,128,112]{2,1,0:T(8,128)(2,1)}, bf16[5,128,112]{2,1,0:T(8,128)(2,1)S(1)}, u32[]{:S(2)}, u32[]{:S(2)}) collective-permute-start(bf16[5,128,112]{2,1,0:T(8,128)(2,1)} %get-tuple-element.30), channel_id=1, source_target_pairs={{0,4},{4,0},{8,12},{12,8},{16,20},{20,16},{24,28},{28,24},{32,36},... | collective-permute-start | bytes 430088 | tf_op jit(solution)/shard_map/ppermute | solution.py:64
  77.3 17.5 %collective-permute-start.11 = (bf16[5,128,112]{2,1,0:T(8,128)(2,1)S(1)}, bf16[5,128,112]{2,1,0:T(8,128)(2,1)S(1)}, u32[]{:S(2)}, u32[]{:S(2)}) collective-permute-start(bf16[5,128,112]{2,1,0:T(8,128)(2,1)S(1)} %fusion.6), channel_id=1, source_target_pairs={{0,8},{4,12},{8,16},{12,20},{16,24},{20,28},{24,0},{28,4},{32,40},... | collective-permute-start | bytes 430088 | tf_op jit(solution)/shard_map/ppermute | solution.py:64
  78.6 16.2 %collective-permute-start.12 = (bf16[5,128,112]{2,1,0:T(8,128)(2,1)S(1)}, bf16[5,128,112]{2,1,0:T(8,128)(2,1)S(1)}, u32[]{:S(2)}, u32[]{:S(2)}) collective-permute-start(bf16[5,128,112]{2,1,0:T(8,128)(2,1)S(1)} %fusion.6), channel_id=1, source_target_pairs={{0,16},{4,20},{8,24},{12,28},{16,0},{20,4},{24,8},{28,12},{32,48},... | collective-permute-start | bytes 430088 | tf_op jit(solution)/shard_map/ppermute | solution.py:64
  80.7 14.1 %collective-permute-start.13 = (bf16[5,128,112]{2,1,0:T(8,128)(2,1)S(1)}, bf16[5,128,112]{2,1,0:T(8,128)(2,1)S(1)}, u32[]{:S(2)}, u32[]{:S(2)}) collective-permute-start(bf16[5,128,112]{2,1,0:T(8,128)(2,1)S(1)} %fusion.6), channel_id=1, source_target_pairs={{0,24},{4,28},{8,0},{12,4},{16,8},{20,12},{24,16},{28,20},{32,56},... | collective-permute-start | bytes 430088 | tf_op jit(solution)/shard_map/ppermute | solution.py:64
  83.0 22.7 %copy-start.1 = (bf16[5,2048,112]{2,1,0:T(8,128)(2,1)S(1)}, bf16[5,2048,112]{2,1,0:T(8,128)(2,1)}, u32[]{:S(2)}) copy-start(bf16[5,2048,112]{2,1,0:T(8,128)(2,1)} %get-tuple-element.37.fk_ref) | copy-start | bytes 6881284
  83.0 22.7 %copy-start.4 = (s32[4]{0:T(128)S(1)}, s32[4]{0:T(128)}, u32[]{:S(2)}) copy-start(s32[4]{0:T(128)} %codes.1) | copy-start | bytes 52
  95.6 20.7 %collective-permute-start.14 = (bf16[5,128,112]{2,1,0:T(8,128)(2,1)}, bf16[5,128,112]{2,1,0:T(8,128)(2,1)S(1)}, u32[]{:S(2)}, u32[]{:S(2)}) collective-permute-start(bf16[5,128,112]{2,1,0:T(8,128)(2,1)} %fusion.7), channel_id=1, source_target_pairs={{0,32},{4,36},{8,40},{12,44},{16,48},{20,52},{24,56},{28,60},{32,6... | collective-permute-start | bytes 430088 | tf_op jit(solution)/shard_map/ppermute | solution.py:64
  99.0 17.2 %collective-permute-start.15 = (bf16[5,128,112]{2,1,0:T(8,128)(2,1)}, bf16[5,128,112]{2,1,0:T(8,128)(2,1)}, u32[]{:S(2)}, u32[]{:S(2)}) collective-permute-start(bf16[5,128,112]{2,1,0:T(8,128)(2,1)} %fusion.7), channel_id=1, source_target_pairs={{0,64},{4,68},{8,72},{12,76},{16,80},{20,84},{24,88},{28,92},{32,9... | collective-permute-start | bytes 430088 | tf_op jit(solution)/shard_map/ppermute | solution.py:64
  103.7 12.5 %collective-permute-start.16 = (bf16[5,128,112]{2,1,0:T(8,128)(2,1)}, bf16[5,128,112]{2,1,0:T(8,128)(2,1)}, u32[]{:S(2)}, u32[]{:S(2)}) collective-permute-start(bf16[5,128,112]{2,1,0:T(8,128)(2,1)} %fusion.7), channel_id=1, source_target_pairs={{0,96},{4,100},{8,104},{12,108},{16,112},{20,116},{24,120},{28,124... | collective-permute-start | bytes 430088 | tf_op jit(solution)/shard_map/ppermute | solution.py:64
  105.7 1.6 %copy-start = (bf16[560,2048]{1,0:T(8,128)(2,1)S(1)}, bf16[560,2048]{1,0:T(8,128)(2,1)}, u32[]{:S(2)}) copy-start(bf16[560,2048]{1,0:T(8,128)(2,1)} %queries.1.fq_ref) | copy-start | bytes 6881284
  107.3 1.7 %copy-start.2 = (bf16[5,128,2048]{2,1,0:T(8,128)(2,1)S(1)}, bf16[5,128,2048]{2,1,0:T(8,128)(2,1)}, u32[]{:S(2)}) copy-start(bf16[5,128,2048]{2,1,0:T(8,128)(2,1)} %get-tuple-element.38.v_ref) | copy-start | bytes 7864324
  109.1 8.4 %copy-start.3 = (f32[4,5,128,112]{3,2,1,0:T(8,128)S(1)}, f32[4,5,128,112]{3,2,1,0:T(8,128)}, u32[]{:S(2)}) copy-start(f32[4,5,128,112]{3,2,1,0:T(8,128)} %get-tuple-element.35.pre_ref) | copy-start | bytes 3440644
  109.1 8.4 %copy-start.5 = (f32[5]{0:T(128)S(1)}, f32[5]{0:T(128)}, u32[]{:S(2)}) copy-start(f32[5]{0:T(128)} %scale.1) | copy-start | bytes 64
  117.5 9.8 %copy-start.12 = (f32[560]{0:T(1024)S(1)}, f32[560]{0:T(1024)}, u32[]{:S(2)}) copy-start(f32[560]{0:T(1024)} %param.9) | copy-start | bytes 6724
  120.7 6.7 %collective-permute-start.17 = (f32[1,2048]{1,0:T(1,128)S(1)}, f32[1,2048]{1,0:T(1,128)S(1)}, u32[]{:S(2)}, u32[]{:S(2)}) collective-permute-start(f32[1,2048]{1,0:T(1,128)S(1)} %get-tuple-element.40), channel_id=1, source_target_pairs={{0,1},{1,2},{2,3},{3,0},{4,5},{5,6},{6,7},{7,4},{8,9},{9,10},{10,1... | collective-permute-start | bytes 24584 | tf_op jit(solution)/shard_map/ppermute | solution.py:503
  122.7 5.3 %collective-permute-start.18 = (f32[1,2048]{1,0:T(1,128)S(1)}, f32[1,2048]{1,0:T(1,128)S(1)}, u32[]{:S(2)}, u32[]{:S(2)}) collective-permute-start(f32[1,2048]{1,0:T(1,128)S(1)} %get-tuple-element.40), channel_id=1, source_target_pairs={{0,2},{1,3},{2,0},{3,1},{4,6},{5,7},{6,4},{7,5},{8,10},{9,11},{10,... | collective-permute-start | bytes 24584 | tf_op jit(solution)/shard_map/ppermute | solution.py:503
  126.3 3.7 %collective-permute-start.19 = (f32[1,2048]{1,0:T(1,128)S(1)}, f32[1,2048]{1,0:T(1,128)S(1)}, u32[]{:S(2)}, u32[]{:S(2)}) collective-permute-start(f32[1,2048]{1,0:T(1,128)S(1)} %get-tuple-element.40), channel_id=1, source_target_pairs={{0,3},{1,0},{2,1},{3,2},{4,7},{5,4},{6,5},{7,6},{8,11},{9,8},{10,9... | collective-permute-start | bytes 24584 | tf_op jit(solution)/shard_map/ppermute | solution.py:503
  (1 other events, 0.7 us)

commit v4 on v3

--- a/solution.py
+++ b/solution.py
@@ -19,7 +19,6 @@
 BF = jnp.bfloat16
 F32 = jnp.float32
 MIB = 1 << 20
-VMEM = 60 * MIB
 QUICK = pl.CostEstimate(flops=1, bytes_accessed=1, transcendentals=0)
 
 
@@ -64,43 +63,33 @@
     return lax.ppermute(a, "tm", moves)
 
 
-def pack_kernel(pos, a0, a1, a2, a3, g_ref, parts, wide, sem):
+def pack_kernel(pos, a0, a1, a2, a3, g_ref, wide):
     coord = jnp.where(pos[2] == 0, pos[1], pos[0])
-    copies = [
-        pltpu.make_async_copy(a, parts.at[(coord + 4 - r) & 3], sem.at[r])
-        for r, a in enumerate((a0, a1, a2, a3))
-    ]
-    for copy in copies:
-        copy.start()
     wide[...] = jnp.zeros_like(wide)
-    for copy in copies:
-        copy.wait()
-    for p in range(4):
-        shard = parts[p].astype(F32)
+    for r, a in enumerate((a0, a1, a2, a3)):
+        at = pl.multiple_of(((coord + 4 - r) & 3) * PAD, 8)
+        shard = a[...].astype(F32)
         for kind, base in ((0, QCOL), (1, 0), (2, HL * DH)):
             for h in range(HL):
-                at = h * 3 * DH + kind * DH
+                col = h * 3 * DH + kind * DH
                 to = base + h * DH
-                wide[p * PAD : p * PAD + SHARD, to : to + DH] = shard[:, at : at + DH]
+                wide[pl.ds(at, SHARD), to : to + DH] = shard[:, col : col + DH]
     g_ref[...] = wide[...].astype(BF)
 
 
 def pack(pos, shards):
+    whole = pl.BlockSpec((SHARD, 3 * HL * DH), lambda g, p: (0, 0))
     return pl.pallas_call(
         pack_kernel,
         grid_spec=pltpu.PrefetchScalarGridSpec(
             num_scalar_prefetch=1,
             grid=(1,),
-            in_specs=[pl.BlockSpec(memory_space=pl.ANY)] * 4,
+            in_specs=[whole] * 4,
             out_specs=pl.BlockSpec((BLK, COLS), lambda g, p: (0, 0)),
-            scratch_shapes=[
-                pltpu.VMEM((4, SHARD, 3 * HL * DH), BF),
-                pltpu.VMEM((BLK, COLS), F32),
-                pltpu.SemaphoreType.DMA((4,)),
-            ],
+            scratch_shapes=[pltpu.VMEM((BLK, COLS), F32)],
         ),
         out_shape=jax.ShapeDtypeStruct((BLK, COLS), BF),
-        compiler_params=pltpu.CompilerParams(vmem_limit_bytes=VMEM),
+        compiler_params=pltpu.CompilerParams(vmem_limit_bytes=10 * MIB),
         cost_estimate=QUICK,
         name="pack",
     )(pos, *shards)
@@ -127,7 +116,7 @@
         in_specs=[pl.BlockSpec((D, blk), lambda g: (0, g))],
         out_specs=pl.BlockSpec((8, BLK, blk), lambda g: (0, 0, g)),
         out_shape=jax.ShapeDtypeStruct((8, BLK, n), BF),
-        compiler_params=pltpu.CompilerParams(vmem_limit_bytes=VMEM),
+        compiler_params=pltpu.CompilerParams(vmem_limit_bytes=8 * MIB),
         cost_estimate=QUICK,
         name="spread",
     )(xt)
@@ -194,7 +183,7 @@
             jax.ShapeDtypeStruct((2 * HL * DH, n), F32),
             jax.ShapeDtypeStruct((HL * DH, n), F32),
         ],
-        compiler_params=pltpu.CompilerParams(vmem_limit_bytes=VMEM),
+        compiler_params=pltpu.CompilerParams(vmem_limit_bytes=24 * MIB),
         cost_estimate=QUICK,
         name="part_first",
     )(blocks, *pieces, *([xp] * count))
@@ -202,19 +191,19 @@
 
 def more_kernel(count, blocks, *refs):
     pieces, x_refs = refs[:count], refs[count : 2 * count]
-    sum_ref, kv_ref, wbuf, sem = refs[2 * count :]
+    sum_ref, q_ref, wbuf, sem = refs[2 * count :]
 
     @pl.when(pl.program_id(0) == 0)
     def _():
-        fetch(pieces, wbuf, sem, 0, QCOL)
+        fetch(pieces, wbuf, sem, QCOL, COLS - QCOL)
 
     x = rows_of(x_refs)
-    kv_ref[...] = product(wbuf[:, : 2 * HL * DH], x) + sum_ref[...]
+    q_ref[...] = product(wbuf[:, : HL * DH], x) + sum_ref[...]
 
 
 def more_call(blocks, pieces, xp, sums):
     count, n = len(pieces), xp.shape[2]
-    spec = pl.BlockSpec((2 * HL * DH, GROUP), lambda g, b: (0, g))
+    spec = pl.BlockSpec((HL * DH, GROUP), lambda g, b: (0, g))
     return pl.pallas_call(
         lambda *refs: more_kernel(count, *refs),
         grid_spec=pltpu.PrefetchScalarGridSpec(
@@ -223,12 +212,12 @@
             in_specs=[pl.BlockSpec(memory_space=pl.ANY)] * count + x_specs(count) + [spec],
             out_specs=spec,
             scratch_shapes=[
-                pltpu.VMEM((count * BLK, QCOL), BF),
+                pltpu.VMEM((count * BLK, COLS - QCOL), BF),
                 pltpu.SemaphoreType.DMA((count,)),
             ],
         ),
-        out_shape=jax.ShapeDtypeStruct((2 * HL * DH, n), F32),
-        compiler_params=pltpu.CompilerParams(vmem_limit_bytes=VMEM),
+        out_shape=jax.ShapeDtypeStruct((HL * DH, n), F32),
+        compiler_params=pltpu.CompilerParams(vmem_limit_bytes=16 * MIB),
         cost_estimate=QUICK,
         name="part_more",
     )(blocks, *pieces, *([xp] * count), sums)
@@ -298,7 +287,7 @@
             jax.ShapeDtypeStruct((groups, HL, VA, DH), F32),
             jax.ShapeDtypeStruct((HL, VA, DH), BF),
         ],
-        compiler_params=pltpu.CompilerParams(vmem_limit_bytes=VMEM),
+        compiler_params=pltpu.CompilerParams(vmem_limit_bytes=24 * MIB),
         cost_estimate=QUICK,
         name="keys_values",
     )(blocks, *pieces, *([xp] * count), sums)
@@ -332,7 +321,7 @@
             ],
         ),
         out_shape=jax.ShapeDtypeStruct((HL * DH, n), BF),
-        compiler_params=pltpu.CompilerParams(vmem_limit_bytes=VMEM),
+        compiler_params=pltpu.CompilerParams(vmem_limit_bytes=16 * MIB),
         cost_estimate=QUICK,
         name="queries",
     )(blocks, *pieces, *([xp] * count), sums)
@@ -383,7 +372,7 @@
             out_specs=pl.BlockSpec((HL, VA, GROUP), lambda g, m: (0, 0, g)),
         ),
         out_shape=jax.ShapeDtypeStruct((HL, VA, n), F32),
-        compiler_params=pltpu.CompilerParams(vmem_limit_bytes=20 * MIB),
+        compiler_params=pltpu.CompilerParams(vmem_limit_bytes=12 * MIB),
         cost_estimate=QUICK,
         name="attend",
     )(codes, fk, v, fq)
@@ -424,7 +413,7 @@
             jax.ShapeDtypeStruct((HL * DH, n), F32),
             jax.ShapeDtypeStruct((1, n), F32),
         ],
-        compiler_params=pltpu.CompilerParams(vmem_limit_bytes=20 * MIB),
+        compiler_params=pltpu.CompilerParams(vmem_limit_bytes=14 * MIB),
         cost_estimate=QUICK,
         name="join",
     )(scale, dev, pre, fq, num)
@@ -447,7 +436,7 @@
         ],
         out_specs=pl.BlockSpec((HL * DH, GROUP), lambda g: (0, g)),
         out_shape=jax.ShapeDtypeStruct((HL * DH, n), BF),
-        compiler_params=pltpu.CompilerParams(vmem_limit_bytes=20 * MIB),
+        compiler_params=pltpu.CompilerParams(vmem_limit_bytes=10 * MIB),
         cost_estimate=QUICK,
         name="norm",
     )(out, squares, gain)
@@ -478,16 +467,17 @@
     mine = [(True, d) for d in (1, 2, 3)]
     last = [(False, d) for d in (1, 2, 3)]
     kv_sum, q_sum = part_call(blocks(first), pieces(first), xp)
-    *own, kv_sum = lax.optimization_barrier((*own, kv_sum))
+    *own, q_sum = lax.optimization_barrier((*own, q_sum))
     sib += [shift(a, SIBLING) for a in own[1:]]
-    kv_sum = more_call(blocks(mine), pieces(mine), xp, kv_sum)
-    fk, v, pre, tot = kv_call(blocks(last), pieces(last), xp, kv_sum)
+    q_sum = more_call(blocks(mine), pieces(mine), xp, q_sum)
+    sib[1], q_sum = lax.optimization_barrier((sib[1], q_sum))
+    fk, v, pre, tot = kv_call(blocks(mine + last), pieces(mine + last), xp, kv_sum)
 
     other = shift(tot, SIBLING).astype(F32)
     before = jnp.where(core == 1, other, 0.0)
     chip = (tot.astype(F32) + other).astype(BF)
     chip, q_sum = lax.optimization_barrier((chip, q_sum))
-    fq = q_call(blocks(mine + last), pieces(mine + last), xp, q_sum)
+    fq = q_call(blocks(last), pieces(last), xp, q_sum)
     row = chip.astype(F32)
     for d in (1, 2, 3):
         got = shift(chip, along_x(d)).astype(F32)

time: 133 us -> 129 us (0.970)
  local copies, waits for them, and re-layouts: 5.6 us -> 23.7 us
  Pallas kernels: 76.4 us -> 59.6 us
  other arithmetic: 5.48 us -> 1.56 us
    unnamed x26 -> x40, local copies, waits for them, and re-layouts: 4.81 us -> 23.5 us
    pallas_call x1, Pallas kernels: 13.6 us -> 4.89 us  [more_call(): pl.pallas_call(lambda *refs: more_kernel(count, *refs), grid_spec=pltpu.P...]
    pallas_call x1, Pallas kernels: 9.74 us -> 3.64 us  [spread(): pl.pallas_call(spread_kernel, grid=(n // blk,), in_specs=[pl.BlockSpec((D...]
    pallas_call x1, Pallas kernels: 11.8 us -> 6.61 us  [q_call(): pl.pallas_call(lambda *refs: q_kernel(count, *refs), grid_spec=pltpu.Pref...]
    pallas_call x1, Pallas kernels: 13.9 us -> 18.5 us  [kv_call(): pl.pallas_call(lambda *refs: kv_kernel(count, *refs), grid_spec=pltpu.Pre...]
    another operation x3, other arithmetic: 1.92 us -> 0.23 us  [blocks(): return jnp.stack([block(mine, d) for mine, d in which])]
  transfers between devices with their start and end apart: 20 -> 20, of which waited for: 6 -> 5; matrix products, arithmetic and copies ran while one was open for 3% -> 0% of each run, Pallas kernels for 40% -> 26%
where the time goes in v4:
time: 129 us; the launch traced here: 128 us
  Pallas kernels  59.6 us (46%)
  starting transfers between devices  33.7 us (26%)
  local copies, waits for them, and re-layouts  23.7 us (18%)
  waiting for transfers between devices  9.34 us (7%)
  other arithmetic  1.56 us (1%)
    ppermute x17, starting transfers between devices, shift(): return lax.ppermute(a, 'tm', moves)  27.1 us
    unnamed x40, local copies, waits for them, and re-layouts  23.5 us
    pallas_call x1, Pallas kernels, kv_call(): pl.pallas_call(lambda *refs: kv_kernel(count, *refs), grid_spec=pltpu.Pre...  18.5 us
    pallas_call x1, Pallas kernels, part_call(): pl.pallas_call(lambda *refs: part_kernel(count, *refs), grid_spec=pltpu.P...  10.9 us
    pallas_call x1, Pallas kernels, attend_call(): pl.pallas_call(attend_kernel, grid_spec=pltpu.PrefetchScalarGridSpec(num_...  7.16 us
    ppermute x17, waiting for transfers between devices, shift(): return lax.ppermute(a, 'tm', moves)  6.83 us
    pallas_call x1, Pallas kernels, q_call(): pl.pallas_call(lambda *refs: q_kernel(count, *refs), grid_spec=pltpu.Pref...  6.61 us
    ppermute x3, starting transfers between devices, body(): lax.ppermute(squares, 'head', [(i, (i + d) % 4) for i in range(4)])  6.58 us
  transfers between devices with their start and end apart: 20, of which 5 were waited for; matrix products, arithmetic and copies ran while one was open for 0% of the time, Pallas kernels for 26%

profile of v4, /device:TPU:0, one launch (start us, length us, event | category | flops | bytes accessed | tf_op | source)
XLA Modules:
  0.0 128.3 jit_solution(273186392381097795)
XLA Ops:
  0.0 1.6 %collective-permute-start = (bf16[70,1680]{1,0:T(8,128)(2,1)}, bf16[70,1680]{1,0:T(8,128)(2,1)S(1)}, u32[]{:S(2)}, u32[]{:S(2)}) collective-permute-start(bf16[70,1680]{1,0:T(8,128)(2,1)} %a0.1), channel_id=1, source_target_pairs={{0,8},{4,36},{8,16},{12,44},{16,24},{20,52},{24,0},{28,60},{32,40}... | collective-permute-start | bytes 705608 | tf_op jit(solution)/shard_map/ppermute | solution.py:63
  1.6 2.7 %collective-permute-start.1 = (bf16[70,1680]{1,0:T(8,128)(2,1)}, bf16[70,1680]{1,0:T(8,128)(2,1)S(1)}, u32[]{:S(2)}, u32[]{:S(2)}) collective-permute-start(bf16[70,1680]{1,0:T(8,128)(2,1)} %a0.1), channel_id=1, source_target_pairs={{0,16},{4,68},{8,24},{12,76},{16,0},{20,84},{24,8},{28,92},{32,48}... | collective-permute-start | bytes 705608 | tf_op jit(solution)/shard_map/ppermute | solution.py:63
  5.8 1.9 %collective-permute-done.a1 = bf16[70,1680]{1,0:T(8,128)(2,1)S(1)} collective-permute-done((bf16[70,1680]{1,0:T(8,128)(2,1)}, bf16[70,1680]{1,0:T(8,128)(2,1)S(1)}, u32[]{:S(2)}, u32[]{:S(2)}) %collective-permute-start) | collective-permute-done | bytes 235232 | tf_op jit(solution)/shard_map/ppermute | solution.py:63
  7.8 3.8 %collective-permute-done.1.a2 = bf16[70,1680]{1,0:T(8,128)(2,1)S(1)} collective-permute-done((bf16[70,1680]{1,0:T(8,128)(2,1)}, bf16[70,1680]{1,0:T(8,128)(2,1)S(1)}, u32[]{:S(2)}, u32[]{:S(2)}) %collective-permute-start.1) | collective-permute-done | bytes 235232 | tf_op jit(solution)/shard_map/ppermute | solution.py:63
  12.5 2.4 %pack.1.refs_1_ = bf16[288,1792]{1,0:T(8,128)(2,1)} custom-call(s32[3]{0:T(128)S(1)} %pad_add_fusion.pos, bf16[70,1680]{1,0:T(8,128)(2,1)S(1)} %copy-done.13, bf16[70,1680]{1,0:T(8,128)(2,1)S(1)} %collective-permute-done.a1, bf16[70,1680]{1,0:T(8,128)(2,1)S(1)} %collective-permute-done.1.a2, bf16[70,1680]{1,0:T(8,128)(2,1)S(1)} %collective-permute-done.2.a3), custom_call_target="tpu_custom_call" | custom-call | flops 1 | bytes 1 | tf_op jit(solution)/shard_map/pack/pallas_call | solution.py:82
  14.9 1.6 %collective-permute-start.3 = (bf16[288,1792]{1,0:T(8,128)(2,1)}, bf16[288,1792]{1,0:T(8,128)(2,1)S(1)}, u32[]{:S(2)}, u32[]{:S(2)}) collective-permute-start(bf16[288,1792]{1,0:T(8,128)(2,1)} %pack.1.refs_1_), channel_id=1, source_target_pairs={{0,32},{4,12},{8,40},{12,20},{16,48},{20,28},{24,56},{28,4},{32,64... | collective-permute-start | bytes 3096584 | tf_op jit(solution)/shard_map/ppermute | solution.py:63
  16.5 2.9 %collective-permute-start.4 = (bf16[288,1792]{1,0:T(8,128)(2,1)}, bf16[288,1792]{1,0:T(8,128)(2,1)S(1)}, u32[]{:S(2)}, u32[]{:S(2)}) collective-permute-start(bf16[288,1792]{1,0:T(8,128)(2,1)} %pack.1.refs_1_), channel_id=1, source_target_pairs={{0,64},{4,20},{8,72},{12,28},{16,80},{20,4},{24,88},{28,12},{32,96... | collective-permute-start | bytes 3096584 | tf_op jit(solution)/shard_map/ppermute | solution.py:63
  20.8 3.6 %copy-done.4 = bf16[2048,2240]{0,1:T(8,128)(2,1)S(1)} copy-done((bf16[2048,2240]{0,1:T(8,128)(2,1)S(1)}, bf16[2048,2240]{0,1:T(8,128)(2,1)}, u32[]{:S(2)}) %copy-start.4) | copy-done | bytes 9175064
  24.4 3.6 %spread.1.refs_3_.refs_4_.refs_5_.refs_6_.refs_7_.refs_8_.refs_9_.refs_10_.refs_11_.refs_12_ = bf16[8,288,2048]{2,1,0:T(8,128)(2,1)S(1)} custom-call(bf16[2240,2048]{1,0:T(8,128)(2,1)S(1)} %bitcast.15), custom_call_target="tpu_custom_call" | custom-call | flops 1 | bytes 1 | tf_op jit(solution)/shard_map/spread/pallas_call | solution.py:113
  28.1 10.9 %part_first.1 = (f32[1120,2048]{1,0:T(8,128)S(1)}, f32[560,2048]{1,0:T(8,128)S(1)}) custom-call(s32[2]{0:T(128)S(1)} %pad_add_fusion.1.refs_0_, bf16[288,1792]{1,0:T(8,128)(2,1)} %pack.1.refs_1_, bf16[288,1792]{1,0:T(8,128)(2,1)} %collective-permute-done.6.refs_2_, ...), custom_call_target="tpu_custom_call" | custom-call | flops 1 | bytes 1 | tf_op jit(solution)/shard_map/part_first/pallas_call | solution.py:167
  39.0 3.5 %copy-done.2 = f32[1120,2048]{1,0:T(8,128)} copy-done((f32[1120,2048]{1,0:T(8,128)}, f32[1120,2048]{1,0:T(8,128)S(1)}, u32[]{:S(2)}) %copy-start.2) | copy-done | bytes 9175064
  42.6 2.2 %copy-done.5 = f32[560,2048]{1,0:T(8,128)} copy-done((f32[560,2048]{1,0:T(8,128)}, f32[560,2048]{1,0:T(8,128)S(1)}, u32[]{:S(2)}) %copy-start.5) | copy-done | bytes 4587544
  45.6 3.7 %copy-done.1 = bf16[8,288,2048]{2,1,0:T(8,128)(2,1)S(1)} copy-done((bf16[8,288,2048]{2,1,0:T(8,128)(2,1)S(1)}, bf16[8,288,2048]{2,1,0:T(8,128)(2,1)}, u32[]{:S(2)}) %copy-start.1) | copy-done | bytes 9437208
  49.3 2.3 %copy-done.6 = f32[560,2048]{1,0:T(8,128)S(1)} copy-done((f32[560,2048]{1,0:T(8,128)S(1)}, f32[560,2048]{1,0:T(8,128)}, u32[]{:S(2)}) %copy-start.6) | copy-done | bytes 4587544
  51.6 4.9 %part_more.1.refs_7_ = f32[560,2048]{1,0:T(8,128)S(1)} custom-call(s32[3]{0:T(128)S(1)} %pad_add_fusion.2.refs_0_, bf16[288,1792]{1,0:T(8,128)(2,1)S(1)} %collective-permute-done.3.refs_1_, bf16[288,1792]{1,0:T(8,128)(2,1)S(1)} %collective-permute-done.4.refs_2_, bf16[288,1792]{1,0:T(8,128)(2,1)S(1)} %collective-permute-done.5.refs_3_, ...), custom_call_target="tpu_custom_call" | custom-call | flops 1 | bytes 1 | tf_op jit(solution)/shard_map/part_more/pallas_call | solution.py:207
  56.5 3.7 %copy-done.3 = f32[1120,2048]{1,0:T(8,128)S(1)} copy-done((f32[1120,2048]{1,0:T(8,128)S(1)}, f32[1120,2048]{1,0:T(8,128)}, u32[]{:S(2)}) %copy-start.3) | copy-done | bytes 9175064
  60.3 18.5 %keys_values.1 = (bf16[5,2048,112]{2,1,0:T(8,128)(2,1)S(1)}, bf16[5,128,2048]{2,1,0:T(8,128)(2,1)S(1)}, f32[4,5,128,112]{3,2,1,0:T(8,128)S(1)}, bf16[5,128,112]{2,1,0:T(8,128)(2,1)S(1)}) custom-call(s32[6]{0:T(128)S(1)} %stack.60.refs_0_, bf16[288,1792]{1,0:T(8,128)(2,1)S(1)} %collective-permute-done.3.refs_1_, ...), custom_call_target="tpu_custom_call" | custom-call | flops 1 | bytes 1 | tf_op jit(solution)/shard_map/keys_values/pallas_call | solution.py:264
  80.3 2.0 %collective-permute-start.11 = (bf16[5,128,112]{2,1,0:T(8,128)(2,1)S(1)}, bf16[5,128,112]{2,1,0:T(8,128)(2,1)S(1)}, u32[]{:S(2)}, u32[]{:S(2)}) collective-permute-start(bf16[5,128,112]{2,1,0:T(8,128)(2,1)S(1)} %fusion.6), channel_id=1, source_target_pairs={{0,8},{4,12},{8,16},{12,20},{16,24},{20,28},{24,0},{28,4},{32,40},... | collective-permute-start | bytes 430088 | tf_op jit(solution)/shard_map/ppermute | solution.py:63
  82.3 2.1 %collective-permute-start.12 = (bf16[5,128,112]{2,1,0:T(8,128)(2,1)S(1)}, bf16[5,128,112]{2,1,0:T(8,128)(2,1)S(1)}, u32[]{:S(2)}, u32[]{:S(2)}) collective-permute-start(bf16[5,128,112]{2,1,0:T(8,128)(2,1)S(1)} %fusion.6), channel_id=1, source_target_pairs={{0,16},{4,20},{8,24},{12,28},{16,0},{20,4},{24,8},{28,12},{32,48},... | collective-permute-start | bytes 430088 | tf_op jit(solution)/shard_map/ppermute | solution.py:63
  84.4 1.6 %collective-permute-start.13 = (bf16[5,128,112]{2,1,0:T(8,128)(2,1)S(1)}, bf16[5,128,112]{2,1,0:T(8,128)(2,1)S(1)}, u32[]{:S(2)}, u32[]{:S(2)}) collective-permute-start(bf16[5,128,112]{2,1,0:T(8,128)(2,1)S(1)} %fusion.6), channel_id=1, source_target_pairs={{0,24},{4,28},{8,0},{12,4},{16,8},{20,12},{24,16},{28,20},{32,56},... | collective-permute-start | bytes 430088 | tf_op jit(solution)/shard_map/ppermute | solution.py:63
  86.1 6.6 %queries.1.fq_ref = bf16[560,2048]{1,0:T(8,128)(2,1)S(1)} custom-call(s32[3]{0:T(128)S(1)} %pad_add_fusion.3.refs_0_, bf16[288,1792]{1,0:T(8,128)(2,1)} %collective-permute-done.7.refs_4_.refs_1_, bf16[288,1792]{1,0:T(8,128)(2,1)} %collective-permute-done.8.refs_5_.refs_2_, bf16[288,1792]{1,0:T(8,128)(2,1)} %collective-permute-done.9.refs_6_.refs_3_, ...), custom_call_target="tpu_custom_call" | custom-call | flops 1 | bytes 1 | tf_op jit(solution)/shard_map/queries/pallas_call | solution.py:311
  92.9 2.6 %collective-permute-start.14 = (bf16[5,128,112]{2,1,0:T(8,128)(2,1)S(1)}, bf16[5,128,112]{2,1,0:T(8,128)(2,1)S(1)}, u32[]{:S(2)}, u32[]{:S(2)}) collective-permute-start(bf16[5,128,112]{2,1,0:T(8,128)(2,1)S(1)} %fusion.7), channel_id=1, source_target_pairs={{0,32},{4,36},{8,40},{12,44},{16,48},{20,52},{24,56},{28,60},{32,6... | collective-permute-start | bytes 430088 | tf_op jit(solution)/shard_map/ppermute | solution.py:63
  95.5 4.2 %collective-permute-start.15 = (bf16[5,128,112]{2,1,0:T(8,128)(2,1)S(1)}, bf16[5,128,112]{2,1,0:T(8,128)(2,1)S(1)}, u32[]{:S(2)}, u32[]{:S(2)}) collective-permute-start(bf16[5,128,112]{2,1,0:T(8,128)(2,1)S(1)} %fusion.7), channel_id=1, source_target_pairs={{0,64},{4,68},{8,72},{12,76},{16,80},{20,84},{24,88},{28,92},{32,9... | collective-permute-start | bytes 430088 | tf_op jit(solution)/shard_map/ppermute | solution.py:63
  99.7 2.0 %collective-permute-start.16 = (bf16[5,128,112]{2,1,0:T(8,128)(2,1)S(1)}, bf16[5,128,112]{2,1,0:T(8,128)(2,1)}, u32[]{:S(2)}, u32[]{:S(2)}) collective-permute-start(bf16[5,128,112]{2,1,0:T(8,128)(2,1)S(1)} %fusion.7), channel_id=1, source_target_pairs={{0,96},{4,100},{8,104},{12,108},{16,112},{20,116},{24,120},{28,124... | collective-permute-start | bytes 430088 | tf_op jit(solution)/shard_map/ppermute | solution.py:63
  101.6 1.7 %copy-done.8 = bf16[5,2048,112]{2,1,0:T(8,128)(2,1)S(1)} copy-done((bf16[5,2048,112]{2,1,0:T(8,128)(2,1)S(1)}, bf16[5,2048,112]{2,1,0:T(8,128)(2,1)}, u32[]{:S(2)}) %copy-start.8) | copy-done | bytes 2293784
  103.4 1.7 %copy-done.10 = bf16[5,128,2048]{2,1,0:T(8,128)(2,1)S(1)} copy-done((bf16[5,128,2048]{2,1,0:T(8,128)(2,1)S(1)}, bf16[5,128,2048]{2,1,0:T(8,128)(2,1)}, u32[]{:S(2)}) %copy-start.10) | copy-done | bytes 2621464
  105.1 7.2 %attend.1.num_ref = f32[5,128,2048]{2,1,0:T(8,128)S(1)} custom-call(s32[4]{0:T(128)S(1)} %copy-done.14, bf16[5,2048,112]{2,1,0:T(8,128)(2,1)S(1)} %copy-done.8, bf16[5,128,2048]{2,1,0:T(8,128)(2,1)S(1)} %copy-done.10, bf16[560,2048]{1,0:T(8,128)(2,1)S(1)} %queries.1.fq_ref), custom_call_target="tpu_custom_call" | custom-call | flops 1 | bytes 1 | tf_op jit(solution)/shard_map/attend/pallas_call | solution.py:362
  113.5 3.2 %join.1 = (f32[560,2048]{1,0:T(8,128)S(1)}, f32[1,2048]{1,0:T(1,128)S(1)}) custom-call(f32[5]{0:T(128)S(1)} %copy-done.15, f32[5,128,112]{2,1,0:T(8,128)S(1)} %fusion.5.dev_ref, f32[4,5,128,112]{3,2,1,0:T(8,128)S(1)} %copy-done.12, bf16[560,2048]{1,0:T(8,128)(2,1)S(1)} %queries.1.fq_ref, f32[5,128,2048]{2,1,0:T(8,128)S(1)} %attend.1.num_ref), custom_call_target="tpu_custom_call" | custom-call | flops 1 | bytes 1 | tf_op jit(solution)/shard_map/join/pallas_call | solution.py:396
  116.7 2.0 %collective-permute-start.17 = (f32[1,2048]{1,0:T(1,128)S(1)}, f32[1,2048]{1,0:T(1,128)S(1)}, u32[]{:S(2)}, u32[]{:S(2)}) collective-permute-start(f32[1,2048]{1,0:T(1,128)S(1)} %get-tuple-element.44), channel_id=1, source_target_pairs={{0,1},{1,2},{2,3},{3,0},{4,5},{5,6},{6,7},{7,4},{8,9},{9,10},{10,1... | collective-permute-start | bytes 24584 | tf_op jit(solution)/shard_map/ppermute | solution.py:493
  118.7 3.6 %collective-permute-start.18 = (f32[1,2048]{1,0:T(1,128)S(1)}, f32[1,2048]{1,0:T(1,128)S(1)}, u32[]{:S(2)}, u32[]{:S(2)}) collective-permute-start(f32[1,2048]{1,0:T(1,128)S(1)} %get-tuple-element.44), channel_id=1, source_target_pairs={{0,2},{1,3},{2,0},{3,1},{4,6},{5,7},{6,4},{7,5},{8,10},{9,11},{10,... | collective-permute-start | bytes 24584 | tf_op jit(solution)/shard_map/ppermute | solution.py:493
  123.9 1.9 %collective-permute-done.19 = f32[1,2048]{1,0:T(1,128)S(1)} collective-permute-done((f32[1,2048]{1,0:T(1,128)S(1)}, f32[1,2048]{1,0:T(1,128)S(1)}, u32[]{:S(2)}, u32[]{:S(2)}) %collective-permute-start.19) | collective-permute-done | bytes 8224 | tf_op jit(solution)/shard_map/ppermute | solution.py:493
  125.9 2.4 %norm.1 = bf16[560,2048]{1,0:T(8,128)(2,1)} custom-call(f32[560,2048]{1,0:T(8,128)S(1)} %get-tuple-element.43.out_ref, f32[1,2048]{1,0:T(1,128)S(1)} %add_add_fusion.sq_ref, f32[560,1]{1,0:T(8,128)S(1)} %reshape.4.gain_ref), custom_call_target="tpu_custom_call" | custom-call | flops 1 | bytes 1 | tf_op jit(solution)/shard_map/norm/pallas_call | solution.py:429
  (68 shorter events, 9.4 us)
Async XLA Ops:
  0.0 7.7 %collective-permute-start = (bf16[70,1680]{1,0:T(8,128)(2,1)}, bf16[70,1680]{1,0:T(8,128)(2,1)S(1)}, u32[]{:S(2)}, u32[]{:S(2)}) collective-permute-start(bf16[70,1680]{1,0:T(8,128)(2,1)} %a0.1), channel_id=1, source_target_pairs={{0,8},{4,36},{8,16},{12,44},{16,24},{20,52},{24,0},{28,60},{32,40}... | collective-permute-start | bytes 705608 | tf_op jit(solution)/shard_map/ppermute | solution.py:63
  1.6 10.0 %collective-permute-start.1 = (bf16[70,1680]{1,0:T(8,128)(2,1)}, bf16[70,1680]{1,0:T(8,128)(2,1)S(1)}, u32[]{:S(2)}, u32[]{:S(2)}) collective-permute-start(bf16[70,1680]{1,0:T(8,128)(2,1)} %a0.1), channel_id=1, source_target_pairs={{0,16},{4,68},{8,24},{12,76},{16,0},{20,84},{24,8},{28,92},{32,48}... | collective-permute-start | bytes 705608 | tf_op jit(solution)/shard_map/ppermute | solution.py:63
  4.3 7.3 %collective-permute-start.2 = (bf16[70,1680]{1,0:T(8,128)(2,1)}, bf16[70,1680]{1,0:T(8,128)(2,1)S(1)}, u32[]{:S(2)}, u32[]{:S(2)}) collective-permute-start(bf16[70,1680]{1,0:T(8,128)(2,1)} %a0.1), channel_id=1, source_target_pairs={{0,24},{4,100},{8,0},{12,108},{16,8},{20,116},{24,16},{28,124},{32... | collective-permute-start | bytes 705608 | tf_op jit(solution)/shard_map/ppermute | solution.py:63
  14.9 13.2 %collective-permute-start.6 = (bf16[288,1792]{1,0:T(8,128)(2,1)}, bf16[288,1792]{1,0:T(8,128)(2,1)}, u32[]{:S(2)}, u32[]{:S(2)}) collective-permute-start(bf16[288,1792]{1,0:T(8,128)(2,1)} %pack.1.refs_1_), channel_id=1, source_target_pairs={{0,4},{4,0},{8,12},{12,8},{16,20},{20,16},{24,28},{28,24},{32,36},... | collective-permute-start | bytes 3096584 | tf_op jit(solution)/shard_map/ppermute | solution.py:63
  14.9 29.8 %collective-permute-start.3 = (bf16[288,1792]{1,0:T(8,128)(2,1)}, bf16[288,1792]{1,0:T(8,128)(2,1)S(1)}, u32[]{:S(2)}, u32[]{:S(2)}) collective-permute-start(bf16[288,1792]{1,0:T(8,128)(2,1)} %pack.1.refs_1_), channel_id=1, source_target_pairs={{0,32},{4,12},{8,40},{12,20},{16,48},{20,28},{24,56},{28,4},{32,64... | collective-permute-start | bytes 3096584 | tf_op jit(solution)/shard_map/ppermute | solution.py:63
  16.5 28.3 %collective-permute-start.4 = (bf16[288,1792]{1,0:T(8,128)(2,1)}, bf16[288,1792]{1,0:T(8,128)(2,1)S(1)}, u32[]{:S(2)}, u32[]{:S(2)}) collective-permute-start(bf16[288,1792]{1,0:T(8,128)(2,1)} %pack.1.refs_1_), channel_id=1, source_target_pairs={{0,64},{4,20},{8,72},{12,28},{16,80},{20,4},{24,88},{28,12},{32,96... | collective-permute-start | bytes 3096584 | tf_op jit(solution)/shard_map/ppermute | solution.py:63
  19.4 25.4 %collective-permute-start.5 = (bf16[288,1792]{1,0:T(8,128)(2,1)}, bf16[288,1792]{1,0:T(8,128)(2,1)S(1)}, u32[]{:S(2)}, u32[]{:S(2)}) collective-permute-start(bf16[288,1792]{1,0:T(8,128)(2,1)} %pack.1.refs_1_), channel_id=1, source_target_pairs={{0,96},{4,28},{8,104},{12,4},{16,112},{20,12},{24,120},{28,20},{32... | collective-permute-start | bytes 3096584 | tf_op jit(solution)/shard_map/ppermute | solution.py:63
  28.0 11.0 %copy-start = (bf16[8,288,2048]{2,1,0:T(8,128)(2,1)}, bf16[8,288,2048]{2,1,0:T(8,128)(2,1)S(1)}, u32[]{:S(2)}) copy-start(bf16[8,288,2048]{2,1,0:T(8,128)(2,1)S(1)} %spread.1.refs_3_.refs_4_.refs_5_.refs_6_.refs_7_.refs_8_.refs_9_.refs_10_.refs_11_.refs_12_) | copy-start | bytes 28311556
  44.7 11.7 %collective-permute-start.7 = (bf16[288,1792]{1,0:T(8,128)(2,1)S(1)}, bf16[288,1792]{1,0:T(8,128)(2,1)}, u32[]{:S(2)}, u32[]{:S(2)}) collective-permute-start(bf16[288,1792]{1,0:T(8,128)(2,1)S(1)} %collective-permute-done.3.refs_1_), channel_id=1, source_target_pairs={{0,4},{4,0},{8,12},{12,8},{16,20},{20,16},{24,28},{28,24},{32,36},... | collective-permute-start | bytes 3096584 | tf_op jit(solution)/shard_map/ppermute | solution.py:63
  44.8 11.6 %collective-permute-start.8 = (bf16[288,1792]{1,0:T(8,128)(2,1)S(1)}, bf16[288,1792]{1,0:T(8,128)(2,1)}, u32[]{:S(2)}, u32[]{:S(2)}) collective-permute-start(bf16[288,1792]{1,0:T(8,128)(2,1)S(1)} %collective-permute-done.4.refs_2_), channel_id=1, source_target_pairs={{0,4},{4,0},{8,12},{12,8},{16,20},{20,16},{24,28},{28,24},{32,36},... | collective-permute-start | bytes 3096584 | tf_op jit(solution)/shard_map/ppermute | solution.py:63
  45.3 11.2 %collective-permute-start.9 = (bf16[288,1792]{1,0:T(8,128)(2,1)S(1)}, bf16[288,1792]{1,0:T(8,128)(2,1)}, u32[]{:S(2)}, u32[]{:S(2)}) collective-permute-start(bf16[288,1792]{1,0:T(8,128)(2,1)S(1)} %collective-permute-done.5.refs_3_), channel_id=1, source_target_pairs={{0,4},{4,0},{8,12},{12,8},{16,20},{20,16},{24,28},{28,24},{32,36},... | collective-permute-start | bytes 3096584 | tf_op jit(solution)/shard_map/ppermute | solution.py:63
  56.5 29.6 %slice-start = ((s8[9437184]{0:T(1024)(128)(4,1)}), s8[4194304]{0:T(1024)(128)(4,1)S(1)}, s32[]{:S(2)}) async-start(s8[9437184]{0:T(1024)(128)(4,1)} %bitcast.13), calls=%async_computation | async-start | bytes 8388608
  56.5 3.8 %copy-start.3 = (f32[1120,2048]{1,0:T(8,128)S(1)}, f32[1120,2048]{1,0:T(8,128)}, u32[]{:S(2)}) copy-start(f32[1120,2048]{1,0:T(8,128)} %copy-done.2) | copy-start | bytes 27525124
  60.3 25.8 %slice-start.1 = ((s8[9437184]{0:T(1024)(128)(4,1)}), s8[4194304]{0:T(1024)(128)(4,1)S(1)}, s32[]{:S(2)}) async-start(s8[9437184]{0:T(1024)(128)(4,1)} %bitcast.13), calls=%async_computation.1 | async-start | bytes 8388608
  60.3 25.8 %slice-start.2 = ((s8[9437184]{0:T(1024)(128)(4,1)}), s8[1048576]{0:T(1024)(128)(4,1)S(1)}, s32[]{:S(2)}) async-start(s8[9437184]{0:T(1024)(128)(4,1)} %bitcast.13), calls=%async_computation.2 | async-start | bytes 2097152
  78.7 14.0 %copy-start.7 = (bf16[5,2048,112]{2,1,0:T(8,128)(2,1)}, bf16[5,2048,112]{2,1,0:T(8,128)(2,1)S(1)}, u32[]{:S(2)}) copy-start(bf16[5,2048,112]{2,1,0:T(8,128)(2,1)S(1)} %get-tuple-element.41.fk_ref) | copy-start | bytes 6881284
  78.8 14.0 %copy-start.9 = (bf16[5,128,2048]{2,1,0:T(8,128)(2,1)}, bf16[5,128,2048]{2,1,0:T(8,128)(2,1)S(1)}, u32[]{:S(2)}) copy-start(bf16[5,128,2048]{2,1,0:T(8,128)(2,1)S(1)} %get-tuple-element.42.v_ref) | copy-start | bytes 7864324
  78.8 14.0 %copy-start.11 = (f32[4,5,128,112]{3,2,1,0:T(8,128)}, f32[4,5,128,112]{3,2,1,0:T(8,128)S(1)}, u32[]{:S(2)}) copy-start(f32[4,5,128,112]{3,2,1,0:T(8,128)S(1)} %get-tuple-element.39.pre_ref) | copy-start | bytes 3440644
  78.8 1.5 %collective-permute-start.10 = (bf16[5,128,112]{2,1,0:T(8,128)(2,1)S(1)}, bf16[5,128,112]{2,1,0:T(8,128)(2,1)S(1)}, u32[]{:S(2)}, u32[]{:S(2)}) collective-permute-start(bf16[5,128,112]{2,1,0:T(8,128)(2,1)S(1)} %get-tuple-element.34), channel_id=1, source_target_pairs={{0,4},{4,0},{8,12},{12,8},{16,20},{20,16},{24,28},{28,24},{32,36},... | collective-permute-start | bytes 430088 | tf_op jit(solution)/shard_map/ppermute | solution.py:63
  80.3 12.4 %collective-permute-start.11 = (bf16[5,128,112]{2,1,0:T(8,128)(2,1)S(1)}, bf16[5,128,112]{2,1,0:T(8,128)(2,1)S(1)}, u32[]{:S(2)}, u32[]{:S(2)}) collective-permute-start(bf16[5,128,112]{2,1,0:T(8,128)(2,1)S(1)} %fusion.6), channel_id=1, source_target_pairs={{0,8},{4,12},{8,16},{12,20},{16,24},{20,28},{24,0},{28,4},{32,40},... | collective-permute-start | bytes 430088 | tf_op jit(solution)/shard_map/ppermute | solution.py:63
  82.3 10.4 %collective-permute-start.12 = (bf16[5,128,112]{2,1,0:T(8,128)(2,1)S(1)}, bf16[5,128,112]{2,1,0:T(8,128)(2,1)S(1)}, u32[]{:S(2)}, u32[]{:S(2)}) collective-permute-start(bf16[5,128,112]{2,1,0:T(8,128)(2,1)S(1)} %fusion.6), channel_id=1, source_target_pairs={{0,16},{4,20},{8,24},{12,28},{16,0},{20,4},{24,8},{28,12},{32,48},... | collective-permute-start | bytes 430088 | tf_op jit(solution)/shard_map/ppermute | solution.py:63
  84.4 8.3 %collective-permute-start.13 = (bf16[5,128,112]{2,1,0:T(8,128)(2,1)S(1)}, bf16[5,128,112]{2,1,0:T(8,128)(2,1)S(1)}, u32[]{:S(2)}, u32[]{:S(2)}) collective-permute-start(bf16[5,128,112]{2,1,0:T(8,128)(2,1)S(1)} %fusion.6), channel_id=1, source_target_pairs={{0,24},{4,28},{8,0},{12,4},{16,8},{20,12},{24,16},{28,20},{32,56},... | collective-permute-start | bytes 430088 | tf_op jit(solution)/shard_map/ppermute | solution.py:63
  86.1 15.6 %copy-start.14 = (s32[4]{0:T(128)S(1)}, s32[4]{0:T(128)}, u32[]{:S(2)}) copy-start(s32[4]{0:T(128)} %codes.1) | copy-start | bytes 52
  92.9 19.4 %collective-permute-start.14 = (bf16[5,128,112]{2,1,0:T(8,128)(2,1)S(1)}, bf16[5,128,112]{2,1,0:T(8,128)(2,1)S(1)}, u32[]{:S(2)}, u32[]{:S(2)}) collective-permute-start(bf16[5,128,112]{2,1,0:T(8,128)(2,1)S(1)} %fusion.7), channel_id=1, source_target_pairs={{0,32},{4,36},{8,40},{12,44},{16,48},{20,52},{24,56},{28,60},{32,6... | collective-permute-start | bytes 430088 | tf_op jit(solution)/shard_map/ppermute | solution.py:63
  95.5 16.8 %collective-permute-start.15 = (bf16[5,128,112]{2,1,0:T(8,128)(2,1)S(1)}, bf16[5,128,112]{2,1,0:T(8,128)(2,1)S(1)}, u32[]{:S(2)}, u32[]{:S(2)}) collective-permute-start(bf16[5,128,112]{2,1,0:T(8,128)(2,1)S(1)} %fusion.7), channel_id=1, source_target_pairs={{0,64},{4,68},{8,72},{12,76},{16,80},{20,84},{24,88},{28,92},{32,9... | collective-permute-start | bytes 430088 | tf_op jit(solution)/shard_map/ppermute | solution.py:63
  99.7 12.6 %collective-permute-start.16 = (bf16[5,128,112]{2,1,0:T(8,128)(2,1)S(1)}, bf16[5,128,112]{2,1,0:T(8,128)(2,1)}, u32[]{:S(2)}, u32[]{:S(2)}) collective-permute-start(bf16[5,128,112]{2,1,0:T(8,128)(2,1)S(1)} %fusion.7), channel_id=1, source_target_pairs={{0,96},{4,100},{8,104},{12,108},{16,112},{20,116},{24,120},{28,124... | collective-permute-start | bytes 430088 | tf_op jit(solution)/shard_map/ppermute | solution.py:63
  105.1 8.3 %copy-start.12 = (f32[4,5,128,112]{3,2,1,0:T(8,128)S(1)}, f32[4,5,128,112]{3,2,1,0:T(8,128)}, u32[]{:S(2)}) copy-start(f32[4,5,128,112]{3,2,1,0:T(8,128)} %copy-done.11) | copy-start | bytes 3440644
  105.1 8.3 %copy-start.15 = (f32[5]{0:T(128)S(1)}, f32[5]{0:T(128)}, u32[]{:S(2)}) copy-start(f32[5]{0:T(128)} %scale.1) | copy-start | bytes 64
  113.4 9.8 %copy-start.16 = (f32[560]{0:T(1024)S(1)}, f32[560]{0:T(1024)}, u32[]{:S(2)}) copy-start(f32[560]{0:T(1024)} %param.9) | copy-start | bytes 6724
  116.7 6.7 %collective-permute-start.17 = (f32[1,2048]{1,0:T(1,128)S(1)}, f32[1,2048]{1,0:T(1,128)S(1)}, u32[]{:S(2)}, u32[]{:S(2)}) collective-permute-start(f32[1,2048]{1,0:T(1,128)S(1)} %get-tuple-element.44), channel_id=1, source_target_pairs={{0,1},{1,2},{2,3},{3,0},{4,5},{5,6},{6,7},{7,4},{8,9},{9,10},{10,1... | collective-permute-start | bytes 24584 | tf_op jit(solution)/shard_map/ppermute | solution.py:493
  118.7 5.3 %collective-permute-start.18 = (f32[1,2048]{1,0:T(1,128)S(1)}, f32[1,2048]{1,0:T(1,128)S(1)}, u32[]{:S(2)}, u32[]{:S(2)}) collective-permute-start(f32[1,2048]{1,0:T(1,128)S(1)} %get-tuple-element.44), channel_id=1, source_target_pairs={{0,2},{1,3},{2,0},{3,1},{4,6},{5,7},{6,4},{7,5},{8,10},{9,11},{10,... | collective-permute-start | bytes 24584 | tf_op jit(solution)/shard_map/ppermute | solution.py:493
  122.2 3.7 %collective-permute-start.19 = (f32[1,2048]{1,0:T(1,128)S(1)}, f32[1,2048]{1,0:T(1,128)S(1)}, u32[]{:S(2)}, u32[]{:S(2)}) collective-permute-start(f32[1,2048]{1,0:T(1,128)S(1)} %get-tuple-element.44), channel_id=1, source_target_pairs={{0,3},{1,0},{2,1},{3,2},{4,7},{5,4},{6,5},{7,6},{8,11},{9,8},{10,9... | collective-permute-start | bytes 24584 | tf_op jit(solution)/shard_map/ppermute | solution.py:493
  (8 other events, 19.7 us)

commit v5 on v0

v5 whole, which is shorter than its diff:
```python
import functools

import jax
import jax.numpy as jnp
from jax import lax
from jax.experimental import pallas as pl
from jax.experimental.pallas import tpu as pltpu
from jax.sharding import PartitionSpec as P

H = 20
DH = 112
GROUP = 512
D = 2240
HL = 5
SHARD = 70
PAD = 72
BLK = 4 * PAD
VA = 128
QCOL = 1152
COLS = 1792
BF = jnp.bfloat16
F32 = jnp.float32
MIB = 1 << 20
QUICK = pl.CostEstimate(flops=1, bytes_accessed=1, transcendentals=0)


def place(y, x, c):
    return (y % 4) * 8 + (x % 4) * 2 + c


def perm(move):
    return [
        (place(y, x, c), place(*move(y, x, c)))
        for y in range(4)
        for x in range(4)
        for c in range(2)
    ]


SIBLING = perm(lambda y, x, c: (y, x, 1 - c))


def first_leg(d):
    return perm(lambda y, x, c: (y, x + d, c) if c == 0 else (y + d, x, c))


def second_leg(d):
    return perm(lambda y, x, c: (y + d, x, c) if c == 0 else (y, x + d, c))


def along_x(d):
    return perm(lambda y, x, c: (y, x + d, c))


def later_y(d):
    return [
        (place(y, x, c), place(y + d, x, c))
        for y in range(4 - d)
        for x in range(4)
        for c in range(2)
    ]


def shift(a, moves):
    return lax.ppermute(a, "tm", moves)


def pack_kernel(pos, a0, a1, a2, a3, g_ref, wide):
    coord = jnp.where(pos[2] == 0, pos[1], pos[0])
    wide[...] = jnp.zeros_like(wide)
    for r, a in enumerate((a0, a1, a2, a3)):
        at = pl.multiple_of(((coord + 4 - r) & 3) * PAD, 8)
        shard = a[...].astype(F32)
        for kind, base in ((0, QCOL), (1, 0), (2, HL * DH)):
            for h in range(HL):
                col = h * 3 * DH + kind * DH
                to = base + h * DH
                wide[pl.ds(at, SHARD), to : to + DH] = shard[:, col : col + DH]
    g_ref[...] = wide[...].astype(BF)


def pack(pos, shards):
    whole = pl.BlockSpec((SHARD, 3 * HL * DH), lambda g, p: (0, 0))
    return pl.pallas_call(
        pack_kernel,
        grid_spec=pltpu.PrefetchScalarGridSpec(
            num_scalar_prefetch=1,
            grid=(1,),
            in_specs=[whole] * 4,
            out_specs=pl.BlockSpec((BLK, COLS), lambda g, p: (0, 0)),
            scratch_shapes=[pltpu.VMEM((BLK, COLS), F32)],
        ),
        out_shape=jax.ShapeDtypeStruct((BLK, COLS), BF),
        compiler_params=pltpu.CompilerParams(vmem_limit_bytes=10 * MIB),
        cost_estimate=QUICK,
        name="pack",
    )(pos, *shards)


def spread_kernel(x_ref, o_ref):
    gap = jnp.zeros((PAD - SHARD, x_ref.shape[1]), BF)
    for y in range(4):
        for x in range(4):
            for c in range(2):
                block, slot = (y, x) if c == 0 else (4 + x, y)
                dev = place(y, x, c)
                at = slot * PAD
                o_ref[block, at : at + SHARD, :] = x_ref[dev * SHARD : (dev + 1) * SHARD, :]
                o_ref[block, at + SHARD : at + PAD, :] = gap


def spread(xt):
    n = xt.shape[1]
    blk = 256
    return pl.pallas_call(
        spread_kernel,
        grid=(n // blk,),
        in_specs=[pl.BlockSpec((D, blk), lambda g: (0, g))],
        out_specs=pl.BlockSpec((8, BLK, blk), lambda g: (0, 0, g)),
        out_shape=jax.ShapeDtypeStruct((8, BLK, n), BF),
        compiler_params=pltpu.CompilerParams(vmem_limit_bytes=8 * MIB),
        cost_estimate=QUICK,
        name="spread",
    )(xt)


def product(w, x):
    return lax.dot_general(w, x, (((0,), (0,)), ((), ())), preferred_element_type=F32)


def fast(a):
    return pltpu.with_memory_space_constraint(a, pltpu.VMEM)


def lay(pieces, wbuf, first, cols):
    for i, piece in enumerate(pieces):
        wbuf[i * BLK : (i + 1) * BLK, :] = piece[:, first : first + cols]


def block(pos, mine, d):
    which = pos[2] if mine else 1 - pos[2]
    return which * 4 + ((jnp.where(which == 0, pos[0], pos[1]) + 4 - d) & 3)


def rows_of(pos, steps, x_ref, at):
    return jnp.concatenate([x_ref[block(pos, *step), :, at] for step in steps], axis=0)


def each_group(n, step):
    def run(g, carry):
        step(g, pl.ds(pl.multiple_of(g * GROUP, GROUP), GROUP))
        return carry

    lax.fori_loop(0, n // GROUP, run, 0)


def resident(kernel, small, large, outs, scratch, limit, name, alias=None):
    return pl.pallas_call(
        kernel,
        in_specs=[pl.BlockSpec(memory_space=pltpu.SMEM)] * len(small)
        + [pl.BlockSpec(memory_space=pltpu.VMEM)] * len(large),
        out_specs=[pl.BlockSpec(memory_space=pltpu.VMEM)] * len(outs),
        out_shape=[pltpu.VMEM(shape, kind) for shape, kind in outs],
        scratch_shapes=scratch,
        input_output_aliases=alias or {},
        compiler_params=pltpu.CompilerParams(vmem_limit_bytes=limit * MIB),
        cost_estimate=QUICK,
        name=name,
    )(*small, *(fast(a) for a in large))


def part_kernel(steps, pos, *refs):
    count = len(refs) - 4
    pieces, (x_ref, kv_ref, q_ref, wbuf) = refs[:count], refs[count:]
    lay(pieces, wbuf, 0, COLS)

    def step(g, at):
        x = rows_of(pos, steps, x_ref, at)
        kv_ref[:, at] = product(wbuf[:, : 2 * HL * DH], x)
        q_ref[:, at] = product(wbuf[:, QCOL : QCOL + HL * DH], x)

    each_group(x_ref.shape[2], step)


def part_call(steps, pos, pieces, xp):
    n = xp.shape[2]
    return resident(
        functools.partial(part_kernel, steps),
        [pos],
        [*pieces, xp],
        [((2 * HL * DH, n), F32), ((HL * DH, n), F32)],
        [pltpu.VMEM((len(pieces) * BLK, COLS), BF)],
        16,
        "part_first",
    )


def more_kernel(steps, pos, *refs):
    count = len(refs) - 4
    pieces, (x_ref, sum_ref, q_ref, wbuf) = refs[:count], refs[count:]
    lay(pieces, wbuf, QCOL, COLS - QCOL)

    def step(g, at):
        x = rows_of(pos, steps, x_ref, at)
        q_ref[:, at] = product(wbuf[:, : HL * DH], x) + sum_ref[:, at]

    each_group(x_ref.shape[2], step)


def more_call(steps, pos, pieces, xp, sums):
    (out,) = resident(
        functools.partial(more_kernel, steps),
        [pos],
        [*pieces, xp, sums],
        [(sums.shape, F32)],
        [pltpu.VMEM((len(pieces) * BLK, COLS - QCOL), BF)],
        12,
        "part_more",
        {len(pieces) + 2: 0},
    )
    return out


def feature(raw):
    a = raw.astype(BF).astype(F32)
    return jnp.where(a > 0, a + 1.0, jnp.exp(jnp.minimum(a, 0.0))).astype(BF)


def kv_kernel(steps, pos, *refs):
    count = len(refs) - 8
    pieces = refs[:count]
    x_ref, sum_ref, fk_ref, v_ref, pre_ref, tot_ref, wbuf, run = refs[count:]
    lay(pieces, wbuf, 0, QCOL)
    run[...] = jnp.zeros_like(run)
    half = HL * DH

    def step(g, at):
        x = rows_of(pos, steps, x_ref, at)
        raw = product(wbuf[:, : 2 * half], x) + sum_ref[:, at]
        fk = feature(raw[:half, :])
        tail = (lax.broadcasted_iota(jnp.int32, (VA - DH, GROUP), 0) == 0).astype(F32).astype(BF)
        for h in range(HL):
            kn = fk[h * DH : (h + 1) * DH, :].T
            fk_ref[h, at, :] = kn
            val = raw[half + h * DH : half + (h + 1) * DH, :].astype(BF)
            va = jnp.concatenate([val, tail], axis=0)
            v_ref[h, :, at] = va
            state = jnp.dot(va, kn, preferred_element_type=F32)
            before = run[h]
            pre_ref[g, h] = before
            run[h] = before + state

    each_group(x_ref.shape[2], step)
    tot_ref[...] = run[...].astype(BF)


def kv_call(steps, pos, pieces, xp, sums):
    n = xp.shape[2]
    return resident(
        functools.partial(kv_kernel, steps),
        [pos],
        [*pieces, xp, sums],
        [
            ((HL, n, DH), BF),
            ((HL, VA, n), BF),
            ((n // GROUP, HL, VA, DH), F32),
            ((HL, VA, DH), BF),
        ],
        [pltpu.VMEM((len(pieces) * BLK, QCOL), BF), pltpu.VMEM((HL, VA, DH), F32)],
        20,
        "keys_values",
    )


def q_kernel(steps, pos, *refs):
    count = len(refs) - 4
    pieces, (x_ref, sum_ref, fq_ref, wbuf) = refs[:count], refs[count:]
    lay(pieces, wbuf, QCOL, COLS - QCOL)

    def step(g, at):
        x = rows_of(pos, steps, x_ref, at)
        fq_ref[:, at] = feature(product(wbuf[:, : HL * DH], x) + sum_ref[:, at])

    each_group(x_ref.shape[2], step)


def q_call(steps, pos, pieces, xp, sums):
    (out,) = resident(
        functools.partial(q_kernel, steps),
        [pos],
        [*pieces, xp, sums],
        [(sums.shape, BF)],
        [pltpu.VMEM((len(pieces) * BLK, COLS - QCOL), BF)],
        12,
        "queries",
    )
    return out


def mask_rows(code, j0, rows, t0, cols):
    parts = []
    for j in range(j0, j0 + rows // 64):
        t = lax.broadcasted_iota(jnp.int32, (64, cols), 1) + t0
        s = lax.broadcasted_iota(jnp.int32, (64, cols), 0)
        i = t >> 6
        bit = (jnp.full((64, cols), code, jnp.int32) >> (((i * (i - 1)) >> 1) + j)) & 1
        same = jnp.where(s <= (t & 63), 1, 0)
        keep = jnp.where(i > j, bit, jnp.where(i == j, same, 0))
        parts.append(keep.astype(F32).astype(BF))
    return jnp.concatenate(parts, axis=0)


def attend_kernel(codes, fk_ref, v_ref, fq_ref, num_ref):
    half = GROUP // 2

    def step(g, at):
        code = codes[g]
        start = pl.multiple_of(g * GROUP, GROUP)
        one, two = pl.ds(start, half), pl.ds(start + half, half)
        upper = mask_rows(code, 0, half, 0, GROUP)
        lower = mask_rows(code, 4, half, half, half)
        for h in range(HL):
            fq = fq_ref[h * DH : (h + 1) * DH, at]
            top = jnp.dot(fk_ref[h, one, :], fq, preferred_element_type=F32)
            top = top.astype(BF) * upper
            low = jnp.dot(fk_ref[h, two, :], fq[:, half:], preferred_element_type=F32)
            low = low.astype(BF) * lower
            num = jnp.dot(v_ref[h, :, one], top, preferred_element_type=F32)
            more = jnp.dot(v_ref[h, :, two], low, preferred_element_type=F32)
            num_ref[h, :, one] = num[:, :half]
            num_ref[h, :, two] = num[:, half:] + more

    each_group(fq_ref.shape[1], step)


def attend_call(codes, fk, v, fq):
    (out,) = resident(
        attend_kernel,
        [codes],
        [fk, v, fq],
        [((HL, VA, fq.shape[1]), F32)],
        [],
        12,
        "attend",
    )
    return out


def chip_kernel(tot_ref, other_ref, chip_ref):
    chip_ref[...] = (tot_ref[...].astype(F32) + other_ref[...].astype(F32)).astype(BF)


def row_kernel(a, b, c, d, row_ref):
    total = a[...].astype(F32) + b[...].astype(F32) + c[...].astype(F32) + d[...].astype(F32)
    row_ref[...] = total.astype(BF)


def small(kernel, args, name):
    (out,) = resident(kernel, [], args, [(args[0].shape, BF)], [], 4, name)
    return out


def join_kernel(pos, scale, *refs):
    other, near, far = refs[0], refs[1:4], refs[4:7]
    pre_ref, fq_ref, num_ref, out_ref, sq_ref, dev = refs[7:]
    total = far[0][...].astype(F32) + far[1][...].astype(F32) + far[2][...].astype(F32)
    total = total + jnp.where(pos[2] == 1, other[...].astype(F32), 0.0)
    for d, got in enumerate(near):
        total = total + jnp.where(pos[1] >= d + 1, got[...].astype(F32), 0.0)
    dev[...] = total

    def step(g, at):
        squares = jnp.zeros((1, GROUP), F32)
        for h in range(HL):
            prefix = (dev[h] + pre_ref[g, h]).astype(BF)
            fq = fq_ref[h * DH : (h + 1) * DH, at]
            num = num_ref[h, :, at] + jnp.dot(prefix, fq, preferred_element_type=F32)
            out = num[:DH, :] * (scale[h] / num[DH : DH + 1, :])
            out_ref[h * DH : (h + 1) * DH, at] = out
            squares = squares + jnp.sum(out * out, axis=0, keepdims=True)
        sq_ref[:, at] = squares

    each_group(fq_ref.shape[1], step)


def join_call(pos, scale, states, pre, fq, num):
    n = fq.shape[1]
    return resident(
        join_kernel,
        [pos, scale],
        [*states, pre, fq, num],
        [((HL * DH, n), F32), ((1, n), F32)],
        [pltpu.VMEM((HL, VA, DH), F32)],
        12,
        "join",
    )


def norm_kernel(out_ref, s0, s1, s2, s3, gain_ref, o_ref, buf, sem):
    eye = lax.broadcasted_iota(jnp.int32, (DH, DH), 0) == lax.broadcasted_iota(
        jnp.int32, (DH, DH), 1
    )
    gains = [
        jnp.sum(jnp.where(eye, gain_ref[h : h + 1, :], 0.0), axis=1, keepdims=True)
        for h in range(HL)
    ]
    copies = []
    for g in range(out_ref.shape[1] // GROUP):
        at = slice(g * GROUP, (g + 1) * GROUP)
        squares = s0[:, at] + s1[:, at] + s2[:, at] + s3[:, at]
        inv = lax.rsqrt(squares * (1.0 / (H * DH)) + 1e-06)
        for h in range(HL):
            rows = slice(h * DH, (h + 1) * DH)
            buf[rows, at] = (out_ref[rows, at] * inv * gains[h]).astype(BF)
        here = pl.ds(g * GROUP, GROUP)
        copies.append(pltpu.make_async_copy(buf.at[:, here], o_ref.at[:, here], sem.at[g]))
        copies[-1].start()
    for copy in copies:
        copy.wait()


def norm_call(out, squares, gain):
    n = out.shape[1]
    return pl.pallas_call(
        norm_kernel,
        in_specs=[pl.BlockSpec(memory_space=pltpu.VMEM)] * 6,
        out_specs=pl.BlockSpec(memory_space=pl.ANY),
        out_shape=jax.ShapeDtypeStruct((HL * DH, n), BF),
        scratch_shapes=[
            pltpu.VMEM((HL * DH, n), BF),
            pltpu.SemaphoreType.DMA((n // GROUP,)),
        ],
        compiler_params=pltpu.CompilerParams(vmem_limit_bytes=8 * MIB),
        cost_estimate=QUICK,
        name="norm",
    )(fast(out), *(fast(a) for a in squares), fast(gain))


def body(tokens, qkv_weight, block_mask, head_scale, norm_gain):
    me = lax.axis_index("tm").astype(jnp.int32)
    y, x, core = me // 8, (me // 2) % 4, me % 2
    pos = jnp.stack([y, x, core])
    pos, gain = lax.optimization_barrier((pos, norm_gain.reshape(HL, DH)))
    shards = [qkv_weight] + [shift(qkv_weight, first_leg(d)) for d in (1, 2, 3)]
    near = pack(pos, shards)
    near, xt = lax.optimization_barrier((near, tokens.T))
    own = [near] + [shift(near, second_leg(d)) for d in (1, 2, 3)]
    sib = [shift(near, SIBLING)]
    xp = spread(pltpu.with_memory_space_constraint(xt, pltpu.HBM))

    def pieces(steps):
        return [(own if mine else sib)[d] for mine, d in steps]

    first = [(True, 0), (False, 0)]
    mine = [(True, d) for d in (1, 2, 3)]
    last = [(False, d) for d in (1, 2, 3)]
    kv_sum, q_sum = part_call(first, pos, pieces(first), xp)
    *own, q_sum = lax.optimization_barrier((*own, q_sum))
    sib += [shift(a, SIBLING) for a in own[1:]]
    q_sum = more_call(mine, pos, pieces(mine), xp, q_sum)
    sib[1], q_sum = lax.optimization_barrier((sib[1], q_sum))
    fk, v, pre, tot = kv_call(mine + last, pos, pieces(mine + last), xp, kv_sum)

    other = shift(tot, SIBLING)
    chip = small(chip_kernel, [tot, other], "chip")
    chip, q_sum = lax.optimization_barrier((chip, q_sum))
    fq = q_call(last, pos, pieces(last), xp, q_sum)
    in_row = [shift(chip, along_x(d)) for d in (1, 2, 3)]
    row = small(row_kernel, [chip, *in_row], "row")
    row, fq = lax.optimization_barrier((row, fq))
    num = attend_call(block_mask, fk, v, fq)
    above = [shift(row, later_y(d)) for d in (1, 2, 3)]

    out, squares = join_call(pos, head_scale, [other, *in_row, *above], pre, fq, num)
    squares = [squares] + [
        lax.ppermute(squares, "head", [(i, (i + d) % 4) for i in range(4)]) for d in (1, 2, 3)
    ]
    return norm_call(out, squares, gain).T


def solution(mesh):
    in_specs = (P("tm", None), P("tm", "head"), P("tm"), P("head"), P("head"))
    out_specs = P("tm", "head")
    return jax.shard_map(body, mesh=mesh, in_specs=in_specs, out_specs=out_specs, check_vma=False)
```

time: 238 us -> 105 us (0.44)
  the two profiles are of different devices: /device:TPU:30 before, /device:TPU:0 now
where the time goes in v5:
time: 105 us
  Pallas kernels  47.4 us (45%)
  starting transfers between devices  28.1 us (27%)
  waiting for transfers between devices  27.2 us (26%)
  local copies, waits for them, and re-layouts  1.72 us (2%)
    pallas_call x8, Pallas kernels, resident(): pl.pallas_call(kernel, in_specs=[pl.BlockSpec(memory_space=pltpu.SMEM)] *...  37.4 us
    ppermute x17, waiting for transfers between devices, shift(): return lax.ppermute(a, 'tm', moves)  23.3 us
    ppermute x17, starting transfers between devices, shift(): return lax.ppermute(a, 'tm', moves)  22.8 us
    pallas_call x1, Pallas kernels, spread(): pl.pallas_call(spread_kernel, grid=(n // blk,), in_specs=[pl.BlockSpec((D...  6.8 us
    ppermute x3, starting transfers between devices, body(): lax.ppermute(squares, 'head', [(i, (i + d) % 4) for i in range(4)])  5.36 us
    ppermute x3, waiting for transfers between devices, body(): lax.ppermute(squares, 'head', [(i, (i + d) % 4) for i in range(4)])  3.9 us
  transfers between devices with their start and end apart: 20, of which 12 were waited for; matrix products, arithmetic and copies ran while one was open for 1% of the time, Pallas kernels for 27%

profile of v5, /device:TPU:0, one launch (start us, length us, event | category | flops | bytes accessed | tf_op | source)
XLA Modules:
  0.0 104.9 jit_solution(17560796290677718551)
XLA Ops:
  0.0 3.1 %collective-permute-start.1 = (bf16[70,1680]{1,0:T(8,128)(2,1)}, bf16[70,1680]{1,0:T(8,128)(2,1)S(1)}, u32[]{:S(2)}, u32[]{:S(2)}) collective-permute-start(bf16[70,1680]{1,0:T(8,128)(2,1)} %a0.1), channel_id=1, source_target_pairs={{0,16},{4,68},{8,24},{12,76},{16,0},{20,84},{24,8},{28,92},{32,48}... | collective-permute-start | bytes 705608 | tf_op jit(solution)/shard_map/ppermute | solution.py:65
  3.7 2.6 %collective-permute-start.2 = (bf16[70,1680]{1,0:T(8,128)(2,1)}, bf16[70,1680]{1,0:T(8,128)(2,1)S(1)}, u32[]{:S(2)}, u32[]{:S(2)}) collective-permute-start(bf16[70,1680]{1,0:T(8,128)(2,1)} %a0.1), channel_id=1, source_target_pairs={{0,24},{4,100},{8,0},{12,108},{16,8},{20,116},{24,16},{28,124},{32... | collective-permute-start | bytes 705608 | tf_op jit(solution)/shard_map/ppermute | solution.py:65
  6.3 0.8 reshape.3.gain_ref
  7.2 0.9 collective-permute-done.1.a2
  8.0 2.8 %collective-permute-done.a1 = bf16[70,1680]{1,0:T(8,128)(2,1)S(1)} collective-permute-done((bf16[70,1680]{1,0:T(8,128)(2,1)}, bf16[70,1680]{1,0:T(8,128)(2,1)S(1)}, u32[]{:S(2)}, u32[]{:S(2)}) %collective-permute-start) | collective-permute-done | bytes 235232 | tf_op jit(solution)/shard_map/ppermute | solution.py:65
  11.0 0.9 copy-done
  11.9 1.4 %pack.1.refs_0_ = bf16[288,1792]{1,0:T(8,128)(2,1)S(1)} custom-call(s32[3]{0:T(128)S(1)} %pad_add_fusion.pos, bf16[70,1680]{1,0:T(8,128)(2,1)S(1)} %copy-done, bf16[70,1680]{1,0:T(8,128)(2,1)S(1)} %collective-permute-done.a1, bf16[70,1680]{1,0:T(8,128)(2,1)S(1)} %collective-permute-done.1.a2, bf16[70,1680]{1,0:T(8,128)(2,1)S(1)} %collective-permute-done.2.a3), custom_call_target="tpu_custom_call" | custom-call | flops 1 | bytes 1 | tf_op jit(solution)/shard_map/pack/pallas_call | solution.py:84
  13.4 3.1 %collective-permute-start.5 = (bf16[288,1792]{1,0:T(8,128)(2,1)S(1)}, bf16[288,1792]{1,0:T(8,128)(2,1)S(1)}, u32[]{:S(2)}, u32[]{:S(2)}) collective-permute-start(bf16[288,1792]{1,0:T(8,128)(2,1)S(1)} %pack.1.refs_0_), channel_id=1, source_target_pairs={{0,96},{4,28},{8,104},{12,4},{16,112},{20,12},{24,120},{28,20},{32... | collective-permute-start | bytes 3096584 | tf_op jit(solution)/shard_map/ppermute | solution.py:65
  16.5 0.6 collective-permute-start.4
  17.1 1.0 collective-permute-start.3
  18.1 6.8 %spread.1.refs_2_.refs_3_.refs_6_ = bf16[8,288,2048]{2,1,0:T(8,128)(2,1)S(1)} custom-call(bf16[2240,2048]{1,0:T(8,128)(2,1)} %bitcast.5), custom_call_target="tpu_custom_call" | custom-call | flops 1 | bytes 1 | tf_op jit(solution)/shard_map/spread/pallas_call | solution.py:115
  24.9 6.8 %part_first.1 = (f32[1120,2048]{1,0:T(8,128)S(1)}, f32[560,2048]{1,0:T(8,128)S(1)}) custom-call(s32[3]{0:T(128)S(1)} %pad_add_fusion.pos, bf16[288,1792]{1,0:T(8,128)(2,1)S(1)} %pack.1.refs_0_, bf16[288,1792]{1,0:T(8,128)(2,1)S(1)} %collective-permute-done.6.refs_1_, bf16[8,288,2048]{2,1,0:T(8,128)(2,1)S(1)} %spread.1.refs_2_.refs_3_.refs_6_), custom_call_target="tpu_custom_call" | custom-call | flops 1 | bytes 1 | tf_op jit(solution)/shard_map/part_first/pallas_call | solution.py:158
  31.8 7.9 %collective-permute-done.5.refs_2_ = bf16[288,1792]{1,0:T(8,128)(2,1)S(1)} collective-permute-done((bf16[288,1792]{1,0:T(8,128)(2,1)S(1)}, bf16[288,1792]{1,0:T(8,128)(2,1)S(1)}, u32[]{:S(2)}, u32[]{:S(2)}) %collective-permute-start.5) | collective-permute-done | bytes 1032224 | tf_op jit(solution)/shard_map/ppermute | solution.py:65
  39.7 4.0 %collective-permute-done.3.refs_0_ = bf16[288,1792]{1,0:T(8,128)(2,1)S(1)} collective-permute-done((bf16[288,1792]{1,0:T(8,128)(2,1)S(1)}, bf16[288,1792]{1,0:T(8,128)(2,1)S(1)}, u32[]{:S(2)}, u32[]{:S(2)}) %collective-permute-start.3) | collective-permute-done | bytes 1032224 | tf_op jit(solution)/shard_map/ppermute | solution.py:65
  44.2 4.0 %part_more.1.refs_4_ = f32[560,2048]{1,0:T(8,128)S(1)} custom-call(s32[3]{0:T(128)S(1)} %pad_add_fusion.pos, bf16[288,1792]{1,0:T(8,128)(2,1)S(1)} %collective-permute-done.3.refs_0_, bf16[288,1792]{1,0:T(8,128)(2,1)S(1)} %collective-permute-done.4.refs_1_, bf16[288,1792]{1,0:T(8,128)(2,1)S(1)} %collective-permute-done.5.refs_2_, ...), custom_call_target="tpu_custom_call", output_to_operand_aliasing={{}: (5, {})} | custom-call | flops 1 | bytes 1 | tf_op jit(solution)/shard_map/part_more/pallas_call | solution.py:158
  48.2 1.1 %collective-permute-done.9.refs_5_.refs_2_ = bf16[288,1792]{1,0:T(8,128)(2,1)S(1)} collective-permute-done((bf16[288,1792]{1,0:T(8,128)(2,1)S(1)}, bf16[288,1792]{1,0:T(8,128)(2,1)S(1)}, u32[]{:S(2)}, u32[]{:S(2)}) %collective-permute-start.9) | collective-permute-done | bytes 1032224 | tf_op jit(solution)/shard_map/ppermute | solution.py:65
  49.3 12.7 %keys_values.1 = (bf16[5,2048,112]{2,1,0:T(8,128)(2,1)S(1)}, bf16[5,128,2048]{2,1,0:T(8,128)(2,1)S(1)}, f32[4,5,128,112]{3,2,1,0:T(8,128)S(1)}, bf16[5,128,112]{2,1,0:T(8,128)(2,1)S(1)}) custom-call(s32[3]{0:T(128)S(1)} %pad_add_fusion.pos, bf16[288,1792]{1,0:T(8,128)(2,1)S(1)} %collective-permute-done.3.refs_0_, ...), custom_call_target="tpu_custom_call" | custom-call | flops 1 | bytes 1 | tf_op jit(solution)/shard_map/keys_values/pallas_call | solution.py:158
  62.2 1.3 %collective-permute-done.10.other_ref.refs_0_ = bf16[5,128,112]{2,1,0:T(8,128)(2,1)S(1)} collective-permute-done((bf16[5,128,112]{2,1,0:T(8,128)(2,1)S(1)}, bf16[5,128,112]{2,1,0:T(8,128)(2,1)S(1)}, u32[]{:S(2)}, u32[]{:S(2)}) %collective-permute-start.10) | collective-permute-done | bytes 143392 | tf_op jit(solution)/shard_map/ppermute | solution.py:65
  63.5 3.2 %collective-permute-start.13 = (bf16[5,128,112]{2,1,0:T(8,128)(2,1)S(1)}, bf16[5,128,112]{2,1,0:T(8,128)(2,1)S(1)}, u32[]{:S(2)}, u32[]{:S(2)}) collective-permute-start(bf16[5,128,112]{2,1,0:T(8,128)(2,1)S(1)} %chip.1.a), channel_id=1, source_target_pairs={{0,24},{4,28},{8,0},{12,4},{16,8},{20,12},{24,16},{28,20},{32,56},... | collective-permute-start | bytes 430088 | tf_op jit(solution)/shard_map/ppermute | solution.py:65
  67.7 4.6 %queries.1.fq_ref.refs_8_ = bf16[560,2048]{1,0:T(8,128)(2,1)S(1)} custom-call(s32[3]{0:T(128)S(1)} %pad_add_fusion.pos, bf16[288,1792]{1,0:T(8,128)(2,1)S(1)} %collective-permute-done.7.refs_3_.refs_0_, bf16[288,1792]{1,0:T(8,128)(2,1)S(1)} %collective-permute-done.8.refs_4_.refs_1_, bf16[288,1792]{1,0:T(8,128)(2,1)S(1)} %collective-permute-done.9.refs_5_.refs_2_, ...), custom_call_target="tpu_custom_call" | custom-call | flops 1 | bytes 1 | tf_op jit(solution)/shard_map/queries/pallas_call | solution.py:158
  72.3 1.7 %collective-permute-done.13.d.refs_3_ = bf16[5,128,112]{2,1,0:T(8,128)(2,1)S(1)} collective-permute-done((bf16[5,128,112]{2,1,0:T(8,128)(2,1)S(1)}, bf16[5,128,112]{2,1,0:T(8,128)(2,1)S(1)}, u32[]{:S(2)}, u32[]{:S(2)}) %collective-permute-start.13) | collective-permute-done | bytes 143392 | tf_op jit(solution)/shard_map/ppermute | solution.py:65
  74.0 1.3 %collective-permute-done.12.c.refs_2_ = bf16[5,128,112]{2,1,0:T(8,128)(2,1)S(1)} collective-permute-done((bf16[5,128,112]{2,1,0:T(8,128)(2,1)S(1)}, bf16[5,128,112]{2,1,0:T(8,128)(2,1)S(1)}, u32[]{:S(2)}, u32[]{:S(2)}) %collective-permute-start.12) | collective-permute-done | bytes 143392 | tf_op jit(solution)/shard_map/ppermute | solution.py:65
  75.3 2.3 %collective-permute-done.11.b.refs_1_ = bf16[5,128,112]{2,1,0:T(8,128)(2,1)S(1)} collective-permute-done((bf16[5,128,112]{2,1,0:T(8,128)(2,1)S(1)}, bf16[5,128,112]{2,1,0:T(8,128)(2,1)S(1)}, u32[]{:S(2)}, u32[]{:S(2)}) %collective-permute-start.11) | collective-permute-done | bytes 143392 | tf_op jit(solution)/shard_map/ppermute | solution.py:65
  77.7 2.5 %collective-permute-start.16 = (bf16[5,128,112]{2,1,0:T(8,128)(2,1)S(1)}, bf16[5,128,112]{2,1,0:T(8,128)(2,1)S(1)}, u32[]{:S(2)}, u32[]{:S(2)}) collective-permute-start(bf16[5,128,112]{2,1,0:T(8,128)(2,1)S(1)} %row.1), channel_id=1, source_target_pairs={{0,96},{4,100},{8,104},{12,108},{16,112},{20,116},{24,120},{28,124... | collective-permute-start | bytes 430088 | tf_op jit(solution)/shard_map/ppermute | solution.py:65
  80.2 1.3 %collective-permute-start.15 = (bf16[5,128,112]{2,1,0:T(8,128)(2,1)S(1)}, bf16[5,128,112]{2,1,0:T(8,128)(2,1)S(1)}, u32[]{:S(2)}, u32[]{:S(2)}) collective-permute-start(bf16[5,128,112]{2,1,0:T(8,128)(2,1)S(1)} %row.1), channel_id=1, source_target_pairs={{0,64},{4,68},{8,72},{12,76},{16,80},{20,84},{24,88},{28,92},{32,9... | collective-permute-start | bytes 430088 | tf_op jit(solution)/shard_map/ppermute | solution.py:65
  81.5 2.9 %collective-permute-start.14 = (bf16[5,128,112]{2,1,0:T(8,128)(2,1)S(1)}, bf16[5,128,112]{2,1,0:T(8,128)(2,1)S(1)}, u32[]{:S(2)}, u32[]{:S(2)}) collective-permute-start(bf16[5,128,112]{2,1,0:T(8,128)(2,1)S(1)} %row.1), channel_id=1, source_target_pairs={{0,32},{4,36},{8,40},{12,44},{16,48},{20,52},{24,56},{28,60},{32,6... | collective-permute-start | bytes 430088 | tf_op jit(solution)/shard_map/ppermute | solution.py:65
  84.5 6.5 %attend.1.refs_9_ = f32[5,128,2048]{2,1,0:T(8,128)S(1)} custom-call(s32[4]{0:T(128)S(1)} %copy-done.1, bf16[5,2048,112]{2,1,0:T(8,128)(2,1)S(1)} %get-tuple-element.44.fk_ref, bf16[5,128,2048]{2,1,0:T(8,128)(2,1)S(1)} %get-tuple-element.45.v_ref, bf16[560,2048]{1,0:T(8,128)(2,1)S(1)} %queries.1.fq_ref.refs_8_), custom_call_target="tpu_custom_call" | custom-call | flops 1 | bytes 1 | tf_op jit(solution)/shard_map/attend/pallas_call | solution.py:158
  91.0 2.6 %join.1 = (f32[560,2048]{1,0:T(8,128)S(1)}, f32[1,2048]{1,0:T(1,128)S(1)}) custom-call(s32[3]{0:T(128)S(1)} %pad_add_fusion.pos, f32[5]{0:T(128)S(1)} %copy-done.2, bf16[5,128,112]{2,1,0:T(8,128)(2,1)S(1)} %collective-permute-done.10.other_ref.refs_0_, bf16[5,128,112]{2,1,0:T(8,128)(2,1)S(1)} %collective-permute-done.11.b.refs_1_, ...), custom_call_target="tpu_custom_call" | custom-call | flops 1 | bytes 1 | tf_op jit(solution)/shard_map/join/pallas_call | solution.py:158
  93.6 4.1 %collective-permute-start.19 = (f32[1,2048]{1,0:T(1,128)S(1)}, f32[1,2048]{1,0:T(1,128)S(1)}, u32[]{:S(2)}, u32[]{:S(2)}) collective-permute-start(f32[1,2048]{1,0:T(1,128)S(1)} %get-tuple-element.47.s0), channel_id=1, source_target_pairs={{0,3},{1,0},{2,1},{3,2},{4,7},{5,4},{6,5},{7,6},{8,11},{9,8},{10,9... | collective-permute-start | bytes 24584 | tf_op jit(solution)/shard_map/ppermute | solution.py:476
  97.7 1.3 %collective-permute-start.17 = (f32[1,2048]{1,0:T(1,128)S(1)}, f32[1,2048]{1,0:T(1,128)S(1)}, u32[]{:S(2)}, u32[]{:S(2)}) collective-permute-start(f32[1,2048]{1,0:T(1,128)S(1)} %get-tuple-element.47.s0), channel_id=1, source_target_pairs={{0,1},{1,2},{2,3},{3,0},{4,5},{5,6},{6,7},{7,4},{8,9},{9,10},{10,1... | collective-permute-start | bytes 24584 | tf_op jit(solution)/shard_map/ppermute | solution.py:476
  99.1 3.8 %collective-permute-done.18.s2 = f32[1,2048]{1,0:T(1,128)S(1)} collective-permute-done((f32[1,2048]{1,0:T(1,128)S(1)}, f32[1,2048]{1,0:T(1,128)S(1)}, u32[]{:S(2)}, u32[]{:S(2)}) %collective-permute-start.18) | collective-permute-done | bytes 8224 | tf_op jit(solution)/shard_map/ppermute | solution.py:476
  102.9 1.9 %norm.1 = bf16[560,2048]{1,0:T(8,128)(2,1)} custom-call(f32[560,2048]{1,0:T(8,128)S(1)} %get-tuple-element.46.out_ref, f32[1,2048]{1,0:T(1,128)S(1)} %get-tuple-element.47.s0, f32[1,2048]{1,0:T(1,128)S(1)} %collective-permute-done.17.s1, f32[1,2048]{1,0:T(1,128)S(1)} %collective-permute-done.18.s2, f32[1,2048]{1,0:T(1,128)S(1)} %collective-permute-done.19.s3, ...), custom_call_target="tpu_custom_call" | custom-call | flops 1 | bytes 1 | tf_op jit(solution)/shard_map/norm/pallas_call | solution.py:424
  (27 shorter events, 2.8 us)
Async XLA Ops:
  0.0 8.0 %collective-permute-start.1 = (bf16[70,1680]{1,0:T(8,128)(2,1)}, bf16[70,1680]{1,0:T(8,128)(2,1)S(1)}, u32[]{:S(2)}, u32[]{:S(2)}) collective-permute-start(bf16[70,1680]{1,0:T(8,128)(2,1)} %a0.1), channel_id=1, source_target_pairs={{0,16},{4,68},{8,24},{12,76},{16,0},{20,84},{24,8},{28,92},{32,48}... | collective-permute-start | bytes 705608 | tf_op jit(solution)/shard_map/ppermute | solution.py:65
  3.1 7.7 %collective-permute-start = (bf16[70,1680]{1,0:T(8,128)(2,1)}, bf16[70,1680]{1,0:T(8,128)(2,1)S(1)}, u32[]{:S(2)}, u32[]{:S(2)}) collective-permute-start(bf16[70,1680]{1,0:T(8,128)(2,1)} %a0.1), channel_id=1, source_target_pairs={{0,8},{4,36},{8,16},{12,44},{16,24},{20,52},{24,0},{28,60},{32,40}... | collective-permute-start | bytes 705608 | tf_op jit(solution)/shard_map/ppermute | solution.py:65
  3.7 7.3 %collective-permute-start.2 = (bf16[70,1680]{1,0:T(8,128)(2,1)}, bf16[70,1680]{1,0:T(8,128)(2,1)S(1)}, u32[]{:S(2)}, u32[]{:S(2)}) collective-permute-start(bf16[70,1680]{1,0:T(8,128)(2,1)} %a0.1), channel_id=1, source_target_pairs={{0,24},{4,100},{8,0},{12,108},{16,8},{20,116},{24,16},{28,124},{32... | collective-permute-start | bytes 705608 | tf_op jit(solution)/shard_map/ppermute | solution.py:65
  11.0 0.9 copy-start
  13.3 11.6 %collective-permute-start.6 = (bf16[288,1792]{1,0:T(8,128)(2,1)S(1)}, bf16[288,1792]{1,0:T(8,128)(2,1)S(1)}, u32[]{:S(2)}, u32[]{:S(2)}) collective-permute-start(bf16[288,1792]{1,0:T(8,128)(2,1)S(1)} %pack.1.refs_0_), channel_id=1, source_target_pairs={{0,4},{4,0},{8,12},{12,8},{16,20},{20,16},{24,28},{28,24},{32,36},... | collective-permute-start | bytes 3096584 | tf_op jit(solution)/shard_map/ppermute | solution.py:65
  13.4 26.3 %collective-permute-start.5 = (bf16[288,1792]{1,0:T(8,128)(2,1)S(1)}, bf16[288,1792]{1,0:T(8,128)(2,1)S(1)}, u32[]{:S(2)}, u32[]{:S(2)}) collective-permute-start(bf16[288,1792]{1,0:T(8,128)(2,1)S(1)} %pack.1.refs_0_), channel_id=1, source_target_pairs={{0,96},{4,28},{8,104},{12,4},{16,112},{20,12},{24,120},{28,20},{32... | collective-permute-start | bytes 3096584 | tf_op jit(solution)/shard_map/ppermute | solution.py:65
  16.5 23.2 %collective-permute-start.4 = (bf16[288,1792]{1,0:T(8,128)(2,1)S(1)}, bf16[288,1792]{1,0:T(8,128)(2,1)S(1)}, u32[]{:S(2)}, u32[]{:S(2)}) collective-permute-start(bf16[288,1792]{1,0:T(8,128)(2,1)S(1)} %pack.1.refs_0_), channel_id=1, source_target_pairs={{0,64},{4,20},{8,72},{12,28},{16,80},{20,4},{24,88},{28,12},{32,96... | collective-permute-start | bytes 3096584 | tf_op jit(solution)/shard_map/ppermute | solution.py:65
  17.1 26.6 %collective-permute-start.3 = (bf16[288,1792]{1,0:T(8,128)(2,1)S(1)}, bf16[288,1792]{1,0:T(8,128)(2,1)S(1)}, u32[]{:S(2)}, u32[]{:S(2)}) collective-permute-start(bf16[288,1792]{1,0:T(8,128)(2,1)S(1)} %pack.1.refs_0_), channel_id=1, source_target_pairs={{0,32},{4,12},{8,40},{12,20},{16,48},{20,28},{24,56},{28,4},{32,64... | collective-permute-start | bytes 3096584 | tf_op jit(solution)/shard_map/ppermute | solution.py:65
  43.7 4.5 %collective-permute-start.7 = (bf16[288,1792]{1,0:T(8,128)(2,1)S(1)}, bf16[288,1792]{1,0:T(8,128)(2,1)S(1)}, u32[]{:S(2)}, u32[]{:S(2)}) collective-permute-start(bf16[288,1792]{1,0:T(8,128)(2,1)S(1)} %collective-permute-done.3.refs_0_), channel_id=1, source_target_pairs={{0,4},{4,0},{8,12},{12,8},{16,20},{20,16},{24,28},{28,24},{32,36},... | collective-permute-start | bytes 3096584 | tf_op jit(solution)/shard_map/ppermute | solution.py:65
  43.7 4.5 %collective-permute-start.8 = (bf16[288,1792]{1,0:T(8,128)(2,1)S(1)}, bf16[288,1792]{1,0:T(8,128)(2,1)S(1)}, u32[]{:S(2)}, u32[]{:S(2)}) collective-permute-start(bf16[288,1792]{1,0:T(8,128)(2,1)S(1)} %collective-permute-done.4.refs_1_), channel_id=1, source_target_pairs={{0,4},{4,0},{8,12},{12,8},{16,20},{20,16},{24,28},{28,24},{32,36},... | collective-permute-start | bytes 3096584 | tf_op jit(solution)/shard_map/ppermute | solution.py:65
  44.2 5.1 %collective-permute-start.9 = (bf16[288,1792]{1,0:T(8,128)(2,1)S(1)}, bf16[288,1792]{1,0:T(8,128)(2,1)S(1)}, u32[]{:S(2)}, u32[]{:S(2)}) collective-permute-start(bf16[288,1792]{1,0:T(8,128)(2,1)S(1)} %collective-permute-done.5.refs_2_), channel_id=1, source_target_pairs={{0,4},{4,0},{8,12},{12,8},{16,20},{20,16},{24,28},{28,24},{32,36},... | collective-permute-start | bytes 3096584 | tf_op jit(solution)/shard_map/ppermute | solution.py:65
  62.0 1.5 %collective-permute-start.10 = (bf16[5,128,112]{2,1,0:T(8,128)(2,1)S(1)}, bf16[5,128,112]{2,1,0:T(8,128)(2,1)S(1)}, u32[]{:S(2)}, u32[]{:S(2)}) collective-permute-start(bf16[5,128,112]{2,1,0:T(8,128)(2,1)S(1)} %get-tuple-element.37.tot_ref), channel_id=1, source_target_pairs={{0,4},{4,0},{8,12},{12,8},{16,20},{20,16},{24,28},{28,24},{32,36},... | collective-permute-start | bytes 430088 | tf_op jit(solution)/shard_map/ppermute | solution.py:65
  63.5 20.9 %copy-start.1 = (s32[4]{0:T(128)S(1)}, s32[4]{0:T(128)}, u32[]{:S(2)}) copy-start(s32[4]{0:T(128)} %codes.1) | copy-start | bytes 52
  63.5 10.5 %collective-permute-start.13 = (bf16[5,128,112]{2,1,0:T(8,128)(2,1)S(1)}, bf16[5,128,112]{2,1,0:T(8,128)(2,1)S(1)}, u32[]{:S(2)}, u32[]{:S(2)}) collective-permute-start(bf16[5,128,112]{2,1,0:T(8,128)(2,1)S(1)} %chip.1.a), channel_id=1, source_target_pairs={{0,24},{4,28},{8,0},{12,4},{16,8},{20,12},{24,16},{28,20},{32,56},... | collective-permute-start | bytes 430088 | tf_op jit(solution)/shard_map/ppermute | solution.py:65
  66.7 8.6 %collective-permute-start.12 = (bf16[5,128,112]{2,1,0:T(8,128)(2,1)S(1)}, bf16[5,128,112]{2,1,0:T(8,128)(2,1)S(1)}, u32[]{:S(2)}, u32[]{:S(2)}) collective-permute-start(bf16[5,128,112]{2,1,0:T(8,128)(2,1)S(1)} %chip.1.a), channel_id=1, source_target_pairs={{0,16},{4,20},{8,24},{12,28},{16,0},{20,4},{24,8},{28,12},{32,48},... | collective-permute-start | bytes 430088 | tf_op jit(solution)/shard_map/ppermute | solution.py:65
  67.2 10.4 %collective-permute-start.11 = (bf16[5,128,112]{2,1,0:T(8,128)(2,1)S(1)}, bf16[5,128,112]{2,1,0:T(8,128)(2,1)S(1)}, u32[]{:S(2)}, u32[]{:S(2)}) collective-permute-start(bf16[5,128,112]{2,1,0:T(8,128)(2,1)S(1)} %chip.1.a), channel_id=1, source_target_pairs={{0,8},{4,12},{8,16},{12,20},{16,24},{20,28},{24,0},{28,4},{32,40},... | collective-permute-start | bytes 430088 | tf_op jit(solution)/shard_map/ppermute | solution.py:65
  77.7 13.3 %collective-permute-start.16 = (bf16[5,128,112]{2,1,0:T(8,128)(2,1)S(1)}, bf16[5,128,112]{2,1,0:T(8,128)(2,1)S(1)}, u32[]{:S(2)}, u32[]{:S(2)}) collective-permute-start(bf16[5,128,112]{2,1,0:T(8,128)(2,1)S(1)} %row.1), channel_id=1, source_target_pairs={{0,96},{4,100},{8,104},{12,108},{16,112},{20,116},{24,120},{28,124... | collective-permute-start | bytes 430088 | tf_op jit(solution)/shard_map/ppermute | solution.py:65
  80.2 10.8 %collective-permute-start.15 = (bf16[5,128,112]{2,1,0:T(8,128)(2,1)S(1)}, bf16[5,128,112]{2,1,0:T(8,128)(2,1)S(1)}, u32[]{:S(2)}, u32[]{:S(2)}) collective-permute-start(bf16[5,128,112]{2,1,0:T(8,128)(2,1)S(1)} %row.1), channel_id=1, source_target_pairs={{0,64},{4,68},{8,72},{12,76},{16,80},{20,84},{24,88},{28,92},{32,9... | collective-permute-start | bytes 430088 | tf_op jit(solution)/shard_map/ppermute | solution.py:65
  81.5 9.5 %collective-permute-start.14 = (bf16[5,128,112]{2,1,0:T(8,128)(2,1)S(1)}, bf16[5,128,112]{2,1,0:T(8,128)(2,1)S(1)}, u32[]{:S(2)}, u32[]{:S(2)}) collective-permute-start(bf16[5,128,112]{2,1,0:T(8,128)(2,1)S(1)} %row.1), channel_id=1, source_target_pairs={{0,32},{4,36},{8,40},{12,44},{16,48},{20,52},{24,56},{28,60},{32,6... | collective-permute-start | bytes 430088 | tf_op jit(solution)/shard_map/ppermute | solution.py:65
  84.5 6.5 %copy-start.2 = (f32[5]{0:T(128)S(1)}, f32[5]{0:T(128)}, u32[]{:S(2)}) copy-start(f32[5]{0:T(128)} %scale.1) | copy-start | bytes 64
  93.6 5.5 %collective-permute-start.19 = (f32[1,2048]{1,0:T(1,128)S(1)}, f32[1,2048]{1,0:T(1,128)S(1)}, u32[]{:S(2)}, u32[]{:S(2)}) collective-permute-start(f32[1,2048]{1,0:T(1,128)S(1)} %get-tuple-element.47.s0), channel_id=1, source_target_pairs={{0,3},{1,0},{2,1},{3,2},{4,7},{5,4},{6,5},{7,6},{8,11},{9,8},{10,9... | collective-permute-start | bytes 24584 | tf_op jit(solution)/shard_map/ppermute | solution.py:476
  97.7 5.2 %collective-permute-start.18 = (f32[1,2048]{1,0:T(1,128)S(1)}, f32[1,2048]{1,0:T(1,128)S(1)}, u32[]{:S(2)}, u32[]{:S(2)}) collective-permute-start(f32[1,2048]{1,0:T(1,128)S(1)} %get-tuple-element.47.s0), channel_id=1, source_target_pairs={{0,2},{1,3},{2,0},{3,1},{4,6},{5,7},{6,4},{7,5},{8,10},{9,11},{10,... | collective-permute-start | bytes 24584 | tf_op jit(solution)/shard_map/ppermute | solution.py:476
  97.7 5.2 %collective-permute-start.17 = (f32[1,2048]{1,0:T(1,128)S(1)}, f32[1,2048]{1,0:T(1,128)S(1)}, u32[]{:S(2)}, u32[]{:S(2)}) collective-permute-start(f32[1,2048]{1,0:T(1,128)S(1)} %get-tuple-element.47.s0), channel_id=1, source_target_pairs={{0,1},{1,2},{2,3},{3,0},{4,5},{5,6},{6,7},{7,4},{8,9},{9,10},{10,1... | collective-permute-start | bytes 24584 | tf_op jit(solution)/shard_map/ppermute | solution.py:476

commit v6 on v5

--- a/solution.py
+++ b/solution.py
@@ -65,7 +65,7 @@
     return lax.ppermute(a, "tm", moves)
 
 
-def pack_kernel(pos, a0, a1, a2, a3, g_ref, wide):
+def pack_kernel(pos, a0, a1, a2, a3, kv_ref, q_ref, wide):
     coord = jnp.where(pos[2] == 0, pos[1], pos[0])
     wide[...] = jnp.zeros_like(wide)
     for r, a in enumerate((a0, a1, a2, a3)):
@@ -76,25 +76,20 @@
                 col = h * 3 * DH + kind * DH
                 to = base + h * DH
                 wide[pl.ds(at, SHARD), to : to + DH] = shard[:, col : col + DH]
-    g_ref[...] = wide[...].astype(BF)
+    kv_ref[...] = wide[:, :QCOL].astype(BF)
+    q_ref[...] = wide[:, QCOL:].astype(BF)
 
 
 def pack(pos, shards):
-    whole = pl.BlockSpec((SHARD, 3 * HL * DH), lambda g, p: (0, 0))
-    return pl.pallas_call(
+    return resident(
         pack_kernel,
-        grid_spec=pltpu.PrefetchScalarGridSpec(
-            num_scalar_prefetch=1,
-            grid=(1,),
-            in_specs=[whole] * 4,
-            out_specs=pl.BlockSpec((BLK, COLS), lambda g, p: (0, 0)),
-            scratch_shapes=[pltpu.VMEM((BLK, COLS), F32)],
-        ),
-        out_shape=jax.ShapeDtypeStruct((BLK, COLS), BF),
-        compiler_params=pltpu.CompilerParams(vmem_limit_bytes=10 * MIB),
-        cost_estimate=QUICK,
-        name="pack",
-    )(pos, *shards)
+        [pos],
+        shards,
+        [((BLK, QCOL), BF), ((BLK, COLS - QCOL), BF)],
+        [pltpu.VMEM((BLK, COLS), F32)],
+        10,
+        "pack",
+    )
 
 
 def spread_kernel(x_ref, o_ref):
@@ -132,9 +127,9 @@
     return pltpu.with_memory_space_constraint(a, pltpu.VMEM)
 
 
-def lay(pieces, wbuf, first, cols):
+def lay(pieces, wbuf):
     for i, piece in enumerate(pieces):
-        wbuf[i * BLK : (i + 1) * BLK, :] = piece[:, first : first + cols]
+        wbuf[i * BLK : (i + 1) * BLK, :] = piece[...]
 
 
 def block(pos, mine, d):
@@ -170,55 +165,34 @@
 
 
 def part_kernel(steps, pos, *refs):
-    count = len(refs) - 4
-    pieces, (x_ref, kv_ref, q_ref, wbuf) = refs[:count], refs[count:]
-    lay(pieces, wbuf, 0, COLS)
+    count = len(steps)
+    kv_pieces, q_pieces = refs[:count], refs[count : 2 * count]
+    x_ref, kv_ref, q_ref, kv_buf, q_buf = refs[2 * count :]
+    lay(kv_pieces, kv_buf)
+    lay(q_pieces, q_buf)
 
     def step(g, at):
         x = rows_of(pos, steps, x_ref, at)
-        kv_ref[:, at] = product(wbuf[:, : 2 * HL * DH], x)
-        q_ref[:, at] = product(wbuf[:, QCOL : QCOL + HL * DH], x)
+        kv_ref[:, at] = product(kv_buf[:, : 2 * HL * DH], x)
+        q_ref[:, at] = product(q_buf[:, : HL * DH], x)
 
     each_group(x_ref.shape[2], step)
 
 
-def part_call(steps, pos, pieces, xp):
+def part_call(steps, pos, kv_pieces, q_pieces, xp):
     n = xp.shape[2]
     return resident(
         functools.partial(part_kernel, steps),
         [pos],
-        [*pieces, xp],
+        [*kv_pieces, *q_pieces, xp],
         [((2 * HL * DH, n), F32), ((HL * DH, n), F32)],
-        [pltpu.VMEM((len(pieces) * BLK, COLS), BF)],
+        [
+            pltpu.VMEM((len(steps) * BLK, QCOL), BF),
+            pltpu.VMEM((len(steps) * BLK, COLS - QCOL), BF),
+        ],
         16,
         "part_first",
     )
-
-
-def more_kernel(steps, pos, *refs):
-    count = len(refs) - 4
-    pieces, (x_ref, sum_ref, q_ref, wbuf) = refs[:count], refs[count:]
-    lay(pieces, wbuf, QCOL, COLS - QCOL)
-
-    def step(g, at):
-        x = rows_of(pos, steps, x_ref, at)
-        q_ref[:, at] = product(wbuf[:, : HL * DH], x) + sum_ref[:, at]
-
-    each_group(x_ref.shape[2], step)
-
-
-def more_call(steps, pos, pieces, xp, sums):
-    (out,) = resident(
-        functools.partial(more_kernel, steps),
-        [pos],
-        [*pieces, xp, sums],
-        [(sums.shape, F32)],
-        [pltpu.VMEM((len(pieces) * BLK, COLS - QCOL), BF)],
-        12,
-        "part_more",
-        {len(pieces) + 2: 0},
-    )
-    return out
 
 
 def feature(raw):
@@ -230,7 +204,7 @@
     count = len(refs) - 8
     pieces = refs[:count]
     x_ref, sum_ref, fk_ref, v_ref, pre_ref, tot_ref, wbuf, run = refs[count:]
-    lay(pieces, wbuf, 0, QCOL)
+    lay(pieces, wbuf)
     run[...] = jnp.zeros_like(run)
     half = HL * DH
 
@@ -275,7 +249,7 @@
 def q_kernel(steps, pos, *refs):
     count = len(refs) - 4
     pieces, (x_ref, sum_ref, fq_ref, wbuf) = refs[:count], refs[count:]
-    lay(pieces, wbuf, QCOL, COLS - QCOL)
+    lay(pieces, wbuf)
 
     def step(g, at):
         x = rows_of(pos, steps, x_ref, at)
@@ -442,30 +416,30 @@
     pos = jnp.stack([y, x, core])
     pos, gain = lax.optimization_barrier((pos, norm_gain.reshape(HL, DH)))
     shards = [qkv_weight] + [shift(qkv_weight, first_leg(d)) for d in (1, 2, 3)]
-    near = pack(pos, shards)
-    near, xt = lax.optimization_barrier((near, tokens.T))
-    own = [near] + [shift(near, second_leg(d)) for d in (1, 2, 3)]
-    sib = [shift(near, SIBLING)]
+    near_kv, near_q = pack(pos, shards)
+    near_kv, xt = lax.optimization_barrier((near_kv, tokens.T))
+    own_kv = [near_kv] + [shift(near_kv, second_leg(d)) for d in (1, 2, 3)]
+    sib_kv, first_q = [shift(near_kv, SIBLING)], [near_q, shift(near_q, SIBLING)]
     xp = spread(pltpu.with_memory_space_constraint(xt, pltpu.HBM))
 
-    def pieces(steps):
-        return [(own if mine else sib)[d] for mine, d in steps]
-
-    first = [(True, 0), (False, 0)]
-    mine = [(True, d) for d in (1, 2, 3)]
-    last = [(False, d) for d in (1, 2, 3)]
-    kv_sum, q_sum = part_call(first, pos, pieces(first), xp)
-    *own, q_sum = lax.optimization_barrier((*own, q_sum))
-    sib += [shift(a, SIBLING) for a in own[1:]]
-    q_sum = more_call(mine, pos, pieces(mine), xp, q_sum)
-    sib[1], q_sum = lax.optimization_barrier((sib[1], q_sum))
-    fk, v, pre, tot = kv_call(mine + last, pos, pieces(mine + last), xp, kv_sum)
+    both = ((True, 0), (False, 0))
+    mine = tuple((True, d) for d in (1, 2, 3))
+    last = tuple((False, d) for d in (1, 2, 3))
+    kv_sum, q_sum = part_call(both, pos, [near_kv, sib_kv[0]], first_q, xp)
+    near_q, kv_sum, q_sum = lax.optimization_barrier((near_q, kv_sum, q_sum))
+    own_q = [shift(near_q, second_leg(d)) for d in (1, 2, 3)]
+    *own_kv, kv_sum = lax.optimization_barrier((*own_kv, kv_sum))
+    sib_kv = [shift(a, SIBLING) for a in own_kv[1:]]
+    fk, v, pre, tot = kv_call(mine + last, pos, [*own_kv[1:], *sib_kv], xp, kv_sum)
 
     other = shift(tot, SIBLING)
+    *own_q, other = lax.optimization_barrier((*own_q, other))
+    sib_q = [shift(a, SIBLING) for a in own_q]
     chip = small(chip_kernel, [tot, other], "chip")
     chip, q_sum = lax.optimization_barrier((chip, q_sum))
-    fq = q_call(last, pos, pieces(last), xp, q_sum)
+    fq = q_call(mine + last, pos, [*own_q, *sib_q], xp, q_sum)
     in_row = [shift(chip, along_x(d)) for d in (1, 2, 3)]
+    *in_row, fq = lax.optimization_barrier((*in_row, fq))
     row = small(row_kernel, [chip, *in_row], "row")
     row, fq = lax.optimization_barrier((row, fq))
     num = attend_call(block_mask, fk, v, fq)

time: 105 us -> 96 us (0.914)
  waiting for transfers between devices: 27.2 us -> 12.9 us
  starting transfers between devices: 28.1 us -> 35.2 us
  Pallas kernels: 47.4 us -> 45.4 us
    ppermute x17 -> x24, waiting for transfers between devices: 23.3 us -> 10.3 us  [shift(): return lax.ppermute(a, 'tm', moves)]
    ppermute x17 -> x24, starting transfers between devices: 22.8 us -> 28.6 us  [shift(): return lax.ppermute(a, 'tm', moves)]
    pallas_call x1 -> x0, Pallas kernels: 1.39 us -> none  [pack(): pl.pallas_call(pack_kernel, grid_spec=pltpu.PrefetchScalarGridSpec(num_sc...]
    ppermute x3, waiting for transfers between devices: 3.9 us -> 2.63 us  [body(): lax.ppermute(squares, 'head', [(i, (i + d) % 4) for i in range(4)])]
    ppermute x3, starting transfers between devices: 5.36 us -> 6.57 us  [body(): lax.ppermute(squares, 'head', [(i, (i + d) % 4) for i in range(4)])]
  transfers between devices with their start and end apart: 20 -> 27, of which waited for: 12 -> 8; matrix products, arithmetic and copies ran while one was open for 1% -> 1% of each run, Pallas kernels for 27% -> 41%
where the time goes in v6:
time: 96 us; the launch traced here: 95.6 us
  Pallas kernels  45.4 us (47%)
  starting transfers between devices  35.2 us (37%)
  waiting for transfers between devices  12.9 us (13%)
  local copies, waits for them, and re-layouts  1.72 us (2%)
    pallas_call x8, Pallas kernels, resident(): pl.pallas_call(kernel, in_specs=[pl.BlockSpec(memory_space=pltpu.SMEM)] *...  36.7 us
    ppermute x24, starting transfers between devices, shift(): return lax.ppermute(a, 'tm', moves)  28.6 us
    ppermute x24, waiting for transfers between devices, shift(): return lax.ppermute(a, 'tm', moves)  10.3 us
    pallas_call x1, Pallas kernels, spread(): pl.pallas_call(spread_kernel, grid=(n // blk,), in_specs=[pl.BlockSpec((D...  6.8 us
    ppermute x3, starting transfers between devices, body(): lax.ppermute(squares, 'head', [(i, (i + d) % 4) for i in range(4)])  6.57 us
    ppermute x3, waiting for transfers between devices, body(): lax.ppermute(squares, 'head', [(i, (i + d) % 4) for i in range(4)])  2.63 us
  transfers between devices with their start and end apart: 27, of which 8 were waited for; matrix products, arithmetic and copies ran while one was open for 1% of the time, Pallas kernels for 41%

profile of v6, /device:TPU:0, one launch (start us, length us, event | category | flops | bytes accessed | tf_op | source)
XLA Modules:
  0.0 95.6 jit_solution(6021972088812747151)
XLA Ops:
  0.0 1.6 %collective-permute-start = (bf16[70,1680]{1,0:T(8,128)(2,1)}, bf16[70,1680]{1,0:T(8,128)(2,1)S(1)}, u32[]{:S(2)}, u32[]{:S(2)}) collective-permute-start(bf16[70,1680]{1,0:T(8,128)(2,1)} %a0.1), channel_id=1, source_target_pairs={{0,8},{4,36},{8,16},{12,44},{16,24},{20,52},{24,0},{28,60},{32,40}... | collective-permute-start | bytes 705608 | tf_op jit(solution)/shard_map/ppermute | solution.py:65
  1.6 2.7 %collective-permute-start.1 = (bf16[70,1680]{1,0:T(8,128)(2,1)}, bf16[70,1680]{1,0:T(8,128)(2,1)S(1)}, u32[]{:S(2)}, u32[]{:S(2)}) collective-permute-start(bf16[70,1680]{1,0:T(8,128)(2,1)} %a0.1), channel_id=1, source_target_pairs={{0,16},{4,68},{8,24},{12,76},{16,0},{20,84},{24,8},{28,92},{32,48}... | collective-permute-start | bytes 705608 | tf_op jit(solution)/shard_map/ppermute | solution.py:65
  4.3 1.4 %collective-permute-start.2 = (bf16[70,1680]{1,0:T(8,128)(2,1)}, bf16[70,1680]{1,0:T(8,128)(2,1)S(1)}, u32[]{:S(2)}, u32[]{:S(2)}) collective-permute-start(bf16[70,1680]{1,0:T(8,128)(2,1)} %a0.1), channel_id=1, source_target_pairs={{0,24},{4,100},{8,0},{12,108},{16,8},{20,116},{24,16},{28,124},{32... | collective-permute-start | bytes 705608 | tf_op jit(solution)/shard_map/ppermute | solution.py:65
  5.7 0.8 reshape.3.gain_ref
  6.6 1.2 %collective-permute-done.a1 = bf16[70,1680]{1,0:T(8,128)(2,1)S(1)} collective-permute-done((bf16[70,1680]{1,0:T(8,128)(2,1)}, bf16[70,1680]{1,0:T(8,128)(2,1)S(1)}, u32[]{:S(2)}, u32[]{:S(2)}) %collective-permute-start) | collective-permute-done | bytes 235232 | tf_op jit(solution)/shard_map/ppermute | solution.py:65
  7.8 3.8 %collective-permute-done.1.a2 = bf16[70,1680]{1,0:T(8,128)(2,1)S(1)} collective-permute-done((bf16[70,1680]{1,0:T(8,128)(2,1)}, bf16[70,1680]{1,0:T(8,128)(2,1)S(1)}, u32[]{:S(2)}, u32[]{:S(2)}) %collective-permute-start.1) | collective-permute-done | bytes 235232 | tf_op jit(solution)/shard_map/ppermute | solution.py:65
  11.6 0.9 copy-done
  12.5 1.4 %pack.1 = (bf16[288,1152]{1,0:T(8,128)(2,1)S(1)}, bf16[288,640]{1,0:T(8,128)(2,1)S(1)}) custom-call(s32[3]{0:T(128)S(1)} %pad_add_fusion.pos, bf16[70,1680]{1,0:T(8,128)(2,1)S(1)} %copy-done, bf16[70,1680]{1,0:T(8,128)(2,1)S(1)} %collective-permute-done.a1, bf16[70,1680]{1,0:T(8,128)(2,1)S(1)} %collective-permute-done.1.a2, ...), custom_call_target="tpu_custom_call" | custom-call | flops 1 | bytes 1 | tf_op jit(solution)/shard_map/pack/pallas_call | solution.py:153
  14.1 3.1 %collective-permute-start.10 = (bf16[288,1152]{1,0:T(8,128)(2,1)S(1)}, bf16[288,1152]{1,0:T(8,128)(2,1)S(1)}, u32[]{:S(2)}, u32[]{:S(2)}) collective-permute-start(bf16[288,1152]{1,0:T(8,128)(2,1)S(1)} %get-tuple-element.41.refs_0_), channel_id=1, source_target_pairs={{0,96},{4,28},{8,104},{12,4},{16,112},{20,12},{24,120},{28,20},{32... | collective-permute-start | bytes 1990664 | tf_op jit(solution)/shard_map/ppermute | solution.py:65
  17.2 2.2 %collective-permute-start.9 = (bf16[288,1152]{1,0:T(8,128)(2,1)S(1)}, bf16[288,1152]{1,0:T(8,128)(2,1)S(1)}, u32[]{:S(2)}, u32[]{:S(2)}) collective-permute-start(bf16[288,1152]{1,0:T(8,128)(2,1)S(1)} %get-tuple-element.41.refs_0_), channel_id=1, source_target_pairs={{0,64},{4,20},{8,72},{12,28},{16,80},{20,4},{24,88},{28,12},{32,96... | collective-permute-start | bytes 1990664 | tf_op jit(solution)/shard_map/ppermute | solution.py:65
  19.4 6.8 %spread.1.refs_4_.refs_6_ = bf16[8,288,2048]{2,1,0:T(8,128)(2,1)S(1)} custom-call(bf16[2240,2048]{1,0:T(8,128)(2,1)} %bitcast.5), custom_call_target="tpu_custom_call" | custom-call | flops 1 | bytes 1 | tf_op jit(solution)/shard_map/spread/pallas_call | solution.py:110
  26.2 6.8 %part_first.1 = (f32[1120,2048]{1,0:T(8,128)S(1)}, f32[560,2048]{1,0:T(8,128)S(1)}) custom-call(s32[3]{0:T(128)S(1)} %pad_add_fusion.pos, bf16[288,1152]{1,0:T(8,128)(2,1)S(1)} %get-tuple-element.41.refs_0_, bf16[288,1152]{1,0:T(8,128)(2,1)S(1)} %collective-permute-done.3.refs_1_, bf16[288,640]{1,0:T(8,128)(2,1)S(1)} %get-tuple-element.45.refs_2_, ...), custom_call_target="tpu_custom_call" | custom-call | flops 1 | bytes 1 | tf_op jit(solution)/shard_map/part_first/pallas_call | solution.py:153
  33.0 3.1 %collective-permute-done.8.refs_0_ = bf16[288,1152]{1,0:T(8,128)(2,1)S(1)} collective-permute-done((bf16[288,1152]{1,0:T(8,128)(2,1)S(1)}, bf16[288,1152]{1,0:T(8,128)(2,1)S(1)}, u32[]{:S(2)}, u32[]{:S(2)}) %collective-permute-start.8) | collective-permute-done | bytes 663584 | tf_op jit(solution)/shard_map/ppermute | solution.py:65
  36.8 2.9 %collective-permute-start.6 = (bf16[288,640]{1,0:T(8,128)(2,1)S(1)}, bf16[288,640]{1,0:T(8,128)(2,1)S(1)}, u32[]{:S(2)}, u32[]{:S(2)}) collective-permute-start(bf16[288,640]{1,0:T(8,128)(2,1)S(1)} %get-tuple-element.45.refs_2_), channel_id=1, source_target_pairs={{0,64},{4,20},{8,72},{12,28},{16,80},{20,4},{24,88},{28,12},{32,96... | collective-permute-start | bytes 1105928 | tf_op jit(solution)/shard_map/ppermute | solution.py:65
  39.7 1.3 %collective-permute-start.7 = (bf16[288,640]{1,0:T(8,128)(2,1)S(1)}, bf16[288,640]{1,0:T(8,128)(2,1)S(1)}, u32[]{:S(2)}, u32[]{:S(2)}) collective-permute-start(bf16[288,640]{1,0:T(8,128)(2,1)S(1)} %get-tuple-element.45.refs_2_), channel_id=1, source_target_pairs={{0,96},{4,28},{8,104},{12,4},{16,112},{20,12},{24,120},{28,20},{32... | collective-permute-start | bytes 1105928 | tf_op jit(solution)/shard_map/ppermute | solution.py:65
  41.0 12.7 %keys_values.1 = (bf16[5,2048,112]{2,1,0:T(8,128)(2,1)S(1)}, bf16[5,128,2048]{2,1,0:T(8,128)(2,1)S(1)}, f32[4,5,128,112]{3,2,1,0:T(8,128)S(1)}, bf16[5,128,112]{2,1,0:T(8,128)(2,1)S(1)}) custom-call(s32[3]{0:T(128)S(1)} %pad_add_fusion.pos, bf16[288,1152]{1,0:T(8,128)(2,1)S(1)} %collective-permute-done.8.refs_0_, ...), custom_call_target="tpu_custom_call" | custom-call | flops 1 | bytes 1 | tf_op jit(solution)/shard_map/keys_values/pallas_call | solution.py:153
  53.8 1.0 %collective-permute-start.14 = (bf16[5,128,112]{2,1,0:T(8,128)(2,1)S(1)}, bf16[5,128,112]{2,1,0:T(8,128)(2,1)S(1)}, u32[]{:S(2)}, u32[]{:S(2)}) collective-permute-start(bf16[5,128,112]{2,1,0:T(8,128)(2,1)S(1)} %get-tuple-element.51.tot_ref), channel_id=1, source_target_pairs={{0,4},{4,0},{8,12},{12,8},{16,20},{20,16},{24,28},{28,24},{32,36},... | collective-permute-start | bytes 430088 | tf_op jit(solution)/shard_map/ppermute | solution.py:65
  54.7 1.0 %collective-permute-done.14.other_ref.refs_0_ = bf16[5,128,112]{2,1,0:T(8,128)(2,1)S(1)} collective-permute-done((bf16[5,128,112]{2,1,0:T(8,128)(2,1)S(1)}, bf16[5,128,112]{2,1,0:T(8,128)(2,1)S(1)}, u32[]{:S(2)}, u32[]{:S(2)}) %collective-permute-start.14) | collective-permute-done | bytes 143392 | tf_op jit(solution)/shard_map/ppermute | solution.py:65
  57.2 1.9 %collective-permute-start.16 = (bf16[5,128,112]{2,1,0:T(8,128)(2,1)S(1)}, bf16[5,128,112]{2,1,0:T(8,128)(2,1)S(1)}, u32[]{:S(2)}, u32[]{:S(2)}) collective-permute-start(bf16[5,128,112]{2,1,0:T(8,128)(2,1)S(1)} %chip.1.a), channel_id=1, source_target_pairs={{0,16},{4,20},{8,24},{12,28},{16,0},{20,4},{24,8},{28,12},{32,48},... | collective-permute-start | bytes 430088 | tf_op jit(solution)/shard_map/ppermute | solution.py:65
  59.2 1.6 %collective-permute-start.17 = (bf16[5,128,112]{2,1,0:T(8,128)(2,1)S(1)}, bf16[5,128,112]{2,1,0:T(8,128)(2,1)S(1)}, u32[]{:S(2)}, u32[]{:S(2)}) collective-permute-start(bf16[5,128,112]{2,1,0:T(8,128)(2,1)S(1)} %chip.1.a), channel_id=1, source_target_pairs={{0,24},{4,28},{8,0},{12,4},{16,8},{20,12},{24,16},{28,20},{32,56},... | collective-permute-start | bytes 430088 | tf_op jit(solution)/shard_map/ppermute | solution.py:65
  60.7 6.5 %queries.1.fq_ref.refs_8_ = bf16[560,2048]{1,0:T(8,128)(2,1)S(1)} custom-call(s32[3]{0:T(128)S(1)} %pad_add_fusion.pos, bf16[288,640]{1,0:T(8,128)(2,1)S(1)} %collective-permute-done.5.refs_0_, bf16[288,640]{1,0:T(8,128)(2,1)S(1)} %collective-permute-done.6.refs_1_, bf16[288,640]{1,0:T(8,128)(2,1)S(1)} %collective-permute-done.7.refs_2_, ...), custom_call_target="tpu_custom_call" | custom-call | flops 1 | bytes 1 | tf_op jit(solution)/shard_map/queries/pallas_call | solution.py:153
  68.5 2.1 %collective-permute-start.21 = (bf16[5,128,112]{2,1,0:T(8,128)(2,1)S(1)}, bf16[5,128,112]{2,1,0:T(8,128)(2,1)S(1)}, u32[]{:S(2)}, u32[]{:S(2)}) collective-permute-start(bf16[5,128,112]{2,1,0:T(8,128)(2,1)S(1)} %row.1), channel_id=1, source_target_pairs={{0,32},{4,36},{8,40},{12,44},{16,48},{20,52},{24,56},{28,60},{32,6... | collective-permute-start | bytes 430088 | tf_op jit(solution)/shard_map/ppermute | solution.py:65
  70.5 3.4 %collective-permute-start.22 = (bf16[5,128,112]{2,1,0:T(8,128)(2,1)S(1)}, bf16[5,128,112]{2,1,0:T(8,128)(2,1)S(1)}, u32[]{:S(2)}, u32[]{:S(2)}) collective-permute-start(bf16[5,128,112]{2,1,0:T(8,128)(2,1)S(1)} %row.1), channel_id=1, source_target_pairs={{0,64},{4,68},{8,72},{12,76},{16,80},{20,84},{24,88},{28,92},{32,9... | collective-permute-start | bytes 430088 | tf_op jit(solution)/shard_map/ppermute | solution.py:65
  73.9 1.3 %collective-permute-start.23 = (bf16[5,128,112]{2,1,0:T(8,128)(2,1)S(1)}, bf16[5,128,112]{2,1,0:T(8,128)(2,1)S(1)}, u32[]{:S(2)}, u32[]{:S(2)}) collective-permute-start(bf16[5,128,112]{2,1,0:T(8,128)(2,1)S(1)} %row.1), channel_id=1, source_target_pairs={{0,96},{4,100},{8,104},{12,108},{16,112},{20,116},{24,120},{28,124... | collective-permute-start | bytes 430088 | tf_op jit(solution)/shard_map/ppermute | solution.py:65
  75.3 6.5 %attend.1.refs_9_ = f32[5,128,2048]{2,1,0:T(8,128)S(1)} custom-call(s32[4]{0:T(128)S(1)} %copy-done.1, bf16[5,2048,112]{2,1,0:T(8,128)(2,1)S(1)} %get-tuple-element.66.fk_ref, bf16[5,128,2048]{2,1,0:T(8,128)(2,1)S(1)} %get-tuple-element.67.v_ref, bf16[560,2048]{1,0:T(8,128)(2,1)S(1)} %queries.1.fq_ref.refs_8_), custom_call_target="tpu_custom_call" | custom-call | flops 1 | bytes 1 | tf_op jit(solution)/shard_map/attend/pallas_call | solution.py:153
  81.8 2.6 %join.1 = (f32[560,2048]{1,0:T(8,128)S(1)}, f32[1,2048]{1,0:T(1,128)S(1)}) custom-call(s32[3]{0:T(128)S(1)} %pad_add_fusion.pos, f32[5]{0:T(128)S(1)} %copy-done.2, bf16[5,128,112]{2,1,0:T(8,128)(2,1)S(1)} %collective-permute-done.14.other_ref.refs_0_, bf16[5,128,112]{2,1,0:T(8,128)(2,1)S(1)} %collective-permute-done.15.b.refs_1_, ...), custom_call_target="tpu_custom_call" | custom-call | flops 1 | bytes 1 | tf_op jit(solution)/shard_map/join/pallas_call | solution.py:153
  84.4 2.0 %collective-permute-start.24 = (f32[1,2048]{1,0:T(1,128)S(1)}, f32[1,2048]{1,0:T(1,128)S(1)}, u32[]{:S(2)}, u32[]{:S(2)}) collective-permute-start(f32[1,2048]{1,0:T(1,128)S(1)} %get-tuple-element.69.s0), channel_id=1, source_target_pairs={{0,1},{1,2},{2,3},{3,0},{4,5},{5,6},{6,7},{7,4},{8,9},{9,10},{10,1... | collective-permute-start | bytes 24584 | tf_op jit(solution)/shard_map/ppermute | solution.py:450
  86.4 3.6 %collective-permute-start.25 = (f32[1,2048]{1,0:T(1,128)S(1)}, f32[1,2048]{1,0:T(1,128)S(1)}, u32[]{:S(2)}, u32[]{:S(2)}) collective-permute-start(f32[1,2048]{1,0:T(1,128)S(1)} %get-tuple-element.69.s0), channel_id=1, source_target_pairs={{0,2},{1,3},{2,0},{3,1},{4,6},{5,7},{6,4},{7,5},{8,10},{9,11},{10,... | collective-permute-start | bytes 24584 | tf_op jit(solution)/shard_map/ppermute | solution.py:450
  90.0 1.0 %collective-permute-start.26 = (f32[1,2048]{1,0:T(1,128)S(1)}, f32[1,2048]{1,0:T(1,128)S(1)}, u32[]{:S(2)}, u32[]{:S(2)}) collective-permute-start(f32[1,2048]{1,0:T(1,128)S(1)} %get-tuple-element.69.s0), channel_id=1, source_target_pairs={{0,3},{1,0},{2,1},{3,2},{4,7},{5,4},{6,5},{7,6},{8,11},{9,8},{10,9... | collective-permute-start | bytes 24584 | tf_op jit(solution)/shard_map/ppermute | solution.py:450
  91.0 0.7 collective-permute-done.25.s2
  91.7 1.9 %collective-permute-done.26.s3 = f32[1,2048]{1,0:T(1,128)S(1)} collective-permute-done((f32[1,2048]{1,0:T(1,128)S(1)}, f32[1,2048]{1,0:T(1,128)S(1)}, u32[]{:S(2)}, u32[]{:S(2)}) %collective-permute-start.26) | collective-permute-done | bytes 8224 | tf_op jit(solution)/shard_map/ppermute | solution.py:450
  93.6 1.9 %norm.1 = bf16[560,2048]{1,0:T(8,128)(2,1)} custom-call(f32[560,2048]{1,0:T(8,128)S(1)} %get-tuple-element.68.out_ref, f32[1,2048]{1,0:T(1,128)S(1)} %get-tuple-element.69.s0, f32[1,2048]{1,0:T(1,128)S(1)} %collective-permute-done.24.s1, f32[1,2048]{1,0:T(1,128)S(1)} %collective-permute-done.25.s2, f32[1,2048]{1,0:T(1,128)S(1)} %collective-permute-done.26.s3, ...), custom_call_target="tpu_custom_call" | custom-call | flops 1 | bytes 1 | tf_op jit(solution)/shard_map/norm/pallas_call | solution.py:398
  (40 shorter events, 3.5 us)
Async XLA Ops:
  0.0 7.7 %collective-permute-start = (bf16[70,1680]{1,0:T(8,128)(2,1)}, bf16[70,1680]{1,0:T(8,128)(2,1)S(1)}, u32[]{:S(2)}, u32[]{:S(2)}) collective-permute-start(bf16[70,1680]{1,0:T(8,128)(2,1)} %a0.1), channel_id=1, source_target_pairs={{0,8},{4,36},{8,16},{12,44},{16,24},{20,52},{24,0},{28,60},{32,40}... | collective-permute-start | bytes 705608 | tf_op jit(solution)/shard_map/ppermute | solution.py:65
  1.6 10.0 %collective-permute-start.1 = (bf16[70,1680]{1,0:T(8,128)(2,1)}, bf16[70,1680]{1,0:T(8,128)(2,1)S(1)}, u32[]{:S(2)}, u32[]{:S(2)}) collective-permute-start(bf16[70,1680]{1,0:T(8,128)(2,1)} %a0.1), channel_id=1, source_target_pairs={{0,16},{4,68},{8,24},{12,76},{16,0},{20,84},{24,8},{28,92},{32,48}... | collective-permute-start | bytes 705608 | tf_op jit(solution)/shard_map/ppermute | solution.py:65
  4.3 7.3 %collective-permute-start.2 = (bf16[70,1680]{1,0:T(8,128)(2,1)}, bf16[70,1680]{1,0:T(8,128)(2,1)S(1)}, u32[]{:S(2)}, u32[]{:S(2)}) collective-permute-start(bf16[70,1680]{1,0:T(8,128)(2,1)} %a0.1), channel_id=1, source_target_pairs={{0,24},{4,100},{8,0},{12,108},{16,8},{20,116},{24,16},{28,124},{32... | collective-permute-start | bytes 705608 | tf_op jit(solution)/shard_map/ppermute | solution.py:65
  11.6 0.9 copy-start
  14.0 12.2 %collective-permute-start.3 = (bf16[288,1152]{1,0:T(8,128)(2,1)S(1)}, bf16[288,1152]{1,0:T(8,128)(2,1)S(1)}, u32[]{:S(2)}, u32[]{:S(2)}) collective-permute-start(bf16[288,1152]{1,0:T(8,128)(2,1)S(1)} %get-tuple-element.41.refs_0_), channel_id=1, source_target_pairs={{0,4},{4,0},{8,12},{12,8},{16,20},{20,16},{24,28},{28,24},{32,36},... | collective-permute-start | bytes 1990664 | tf_op jit(solution)/shard_map/ppermute | solution.py:65
  14.1 18.9 %collective-permute-start.10 = (bf16[288,1152]{1,0:T(8,128)(2,1)S(1)}, bf16[288,1152]{1,0:T(8,128)(2,1)S(1)}, u32[]{:S(2)}, u32[]{:S(2)}) collective-permute-start(bf16[288,1152]{1,0:T(8,128)(2,1)S(1)} %get-tuple-element.41.refs_0_), channel_id=1, source_target_pairs={{0,96},{4,28},{8,104},{12,4},{16,112},{20,12},{24,120},{28,20},{32... | collective-permute-start | bytes 1990664 | tf_op jit(solution)/shard_map/ppermute | solution.py:65
  17.2 19.0 %collective-permute-start.8 = (bf16[288,1152]{1,0:T(8,128)(2,1)S(1)}, bf16[288,1152]{1,0:T(8,128)(2,1)S(1)}, u32[]{:S(2)}, u32[]{:S(2)}) collective-permute-start(bf16[288,1152]{1,0:T(8,128)(2,1)S(1)} %get-tuple-element.41.refs_0_), channel_id=1, source_target_pairs={{0,32},{4,12},{8,40},{12,20},{16,48},{20,28},{24,56},{28,4},{32,64... | collective-permute-start | bytes 1990664 | tf_op jit(solution)/shard_map/ppermute | solution.py:65
  17.2 19.0 %collective-permute-start.9 = (bf16[288,1152]{1,0:T(8,128)(2,1)S(1)}, bf16[288,1152]{1,0:T(8,128)(2,1)S(1)}, u32[]{:S(2)}, u32[]{:S(2)}) collective-permute-start(bf16[288,1152]{1,0:T(8,128)(2,1)S(1)} %get-tuple-element.41.refs_0_), channel_id=1, source_target_pairs={{0,64},{4,20},{8,72},{12,28},{16,80},{20,4},{24,88},{28,12},{32,96... | collective-permute-start | bytes 1990664 | tf_op jit(solution)/shard_map/ppermute | solution.py:65
  19.4 6.8 %collective-permute-start.4 = (bf16[288,640]{1,0:T(8,128)(2,1)S(1)}, bf16[288,640]{1,0:T(8,128)(2,1)S(1)}, u32[]{:S(2)}, u32[]{:S(2)}) collective-permute-start(bf16[288,640]{1,0:T(8,128)(2,1)S(1)} %get-tuple-element.45.refs_2_), channel_id=1, source_target_pairs={{0,4},{4,0},{8,12},{12,8},{16,20},{20,16},{24,28},{28,24},{32,36},... | collective-permute-start | bytes 1105928 | tf_op jit(solution)/shard_map/ppermute | solution.py:65
  36.2 3.5 %collective-permute-start.11 = (bf16[288,1152]{1,0:T(8,128)(2,1)S(1)}, bf16[288,1152]{1,0:T(8,128)(2,1)S(1)}, u32[]{:S(2)}, u32[]{:S(2)}) collective-permute-start(bf16[288,1152]{1,0:T(8,128)(2,1)S(1)} %collective-permute-done.8.refs_0_), channel_id=1, source_target_pairs={{0,4},{4,0},{8,12},{12,8},{16,20},{20,16},{24,28},{28,24},{32,36},... | collective-permute-start | bytes 1990664 | tf_op jit(solution)/shard_map/ppermute | solution.py:65
  36.2 4.9 %collective-permute-start.12 = (bf16[288,1152]{1,0:T(8,128)(2,1)S(1)}, bf16[288,1152]{1,0:T(8,128)(2,1)S(1)}, u32[]{:S(2)}, u32[]{:S(2)}) collective-permute-start(bf16[288,1152]{1,0:T(8,128)(2,1)S(1)} %collective-permute-done.9.refs_1_), channel_id=1, source_target_pairs={{0,4},{4,0},{8,12},{12,8},{16,20},{20,16},{24,28},{28,24},{32,36},... | collective-permute-start | bytes 1990664 | tf_op jit(solution)/shard_map/ppermute | solution.py:65
  36.7 4.4 %collective-permute-start.13 = (bf16[288,1152]{1,0:T(8,128)(2,1)S(1)}, bf16[288,1152]{1,0:T(8,128)(2,1)S(1)}, u32[]{:S(2)}, u32[]{:S(2)}) collective-permute-start(bf16[288,1152]{1,0:T(8,128)(2,1)S(1)} %collective-permute-done.10.refs_2_), channel_id=1, source_target_pairs={{0,4},{4,0},{8,12},{12,8},{16,20},{20,16},{24,28},{28,24},{32,36},... | collective-permute-start | bytes 1990664 | tf_op jit(solution)/shard_map/ppermute | solution.py:65
  36.7 18.1 %collective-permute-start.5 = (bf16[288,640]{1,0:T(8,128)(2,1)S(1)}, bf16[288,640]{1,0:T(8,128)(2,1)S(1)}, u32[]{:S(2)}, u32[]{:S(2)}) collective-permute-start(bf16[288,640]{1,0:T(8,128)(2,1)S(1)} %get-tuple-element.45.refs_2_), channel_id=1, source_target_pairs={{0,32},{4,12},{8,40},{12,20},{16,48},{20,28},{24,56},{28,4},{32,64... | collective-permute-start | bytes 1105928 | tf_op jit(solution)/shard_map/ppermute | solution.py:65
  36.8 18.0 %collective-permute-start.6 = (bf16[288,640]{1,0:T(8,128)(2,1)S(1)}, bf16[288,640]{1,0:T(8,128)(2,1)S(1)}, u32[]{:S(2)}, u32[]{:S(2)}) collective-permute-start(bf16[288,640]{1,0:T(8,128)(2,1)S(1)} %get-tuple-element.45.refs_2_), channel_id=1, source_target_pairs={{0,64},{4,20},{8,72},{12,28},{16,80},{20,4},{24,88},{28,12},{32,96... | collective-permute-start | bytes 1105928 | tf_op jit(solution)/shard_map/ppermute | solution.py:65
  39.7 15.1 %collective-permute-start.7 = (bf16[288,640]{1,0:T(8,128)(2,1)S(1)}, bf16[288,640]{1,0:T(8,128)(2,1)S(1)}, u32[]{:S(2)}, u32[]{:S(2)}) collective-permute-start(bf16[288,640]{1,0:T(8,128)(2,1)S(1)} %get-tuple-element.45.refs_2_), channel_id=1, source_target_pairs={{0,96},{4,28},{8,104},{12,4},{16,112},{20,12},{24,120},{28,20},{32... | collective-permute-start | bytes 1105928 | tf_op jit(solution)/shard_map/ppermute | solution.py:65
  53.8 2.0 %collective-permute-start.14 = (bf16[5,128,112]{2,1,0:T(8,128)(2,1)S(1)}, bf16[5,128,112]{2,1,0:T(8,128)(2,1)S(1)}, u32[]{:S(2)}, u32[]{:S(2)}) collective-permute-start(bf16[5,128,112]{2,1,0:T(8,128)(2,1)S(1)} %get-tuple-element.51.tot_ref), channel_id=1, source_target_pairs={{0,4},{4,0},{8,12},{12,8},{16,20},{20,16},{24,28},{28,24},{32,36},... | collective-permute-start | bytes 430088 | tf_op jit(solution)/shard_map/ppermute | solution.py:65
  55.8 3.4 %collective-permute-start.18 = (bf16[288,640]{1,0:T(8,128)(2,1)S(1)}, bf16[288,640]{1,0:T(8,128)(2,1)S(1)}, u32[]{:S(2)}, u32[]{:S(2)}) collective-permute-start(bf16[288,640]{1,0:T(8,128)(2,1)S(1)} %collective-permute-done.5.refs_0_), channel_id=1, source_target_pairs={{0,4},{4,0},{8,12},{12,8},{16,20},{20,16},{24,28},{28,24},{32,36},... | collective-permute-start | bytes 1105928 | tf_op jit(solution)/shard_map/ppermute | solution.py:65
  56.1 4.6 %collective-permute-start.19 = (bf16[288,640]{1,0:T(8,128)(2,1)S(1)}, bf16[288,640]{1,0:T(8,128)(2,1)S(1)}, u32[]{:S(2)}, u32[]{:S(2)}) collective-permute-start(bf16[288,640]{1,0:T(8,128)(2,1)S(1)} %collective-permute-done.6.refs_1_), channel_id=1, source_target_pairs={{0,4},{4,0},{8,12},{12,8},{16,20},{20,16},{24,28},{28,24},{32,36},... | collective-permute-start | bytes 1105928 | tf_op jit(solution)/shard_map/ppermute | solution.py:65
  56.3 4.5 %collective-permute-start.20 = (bf16[288,640]{1,0:T(8,128)(2,1)S(1)}, bf16[288,640]{1,0:T(8,128)(2,1)S(1)}, u32[]{:S(2)}, u32[]{:S(2)}) collective-permute-start(bf16[288,640]{1,0:T(8,128)(2,1)S(1)} %collective-permute-done.7.refs_2_), channel_id=1, source_target_pairs={{0,4},{4,0},{8,12},{12,8},{16,20},{20,16},{24,28},{28,24},{32,36},... | collective-permute-start | bytes 1105928 | tf_op jit(solution)/shard_map/ppermute | solution.py:65
  56.7 18.6 %copy-start.1 = (s32[4]{0:T(128)S(1)}, s32[4]{0:T(128)}, u32[]{:S(2)}) copy-start(s32[4]{0:T(128)} %codes.1) | copy-start | bytes 52
  56.7 11.0 %collective-permute-start.15 = (bf16[5,128,112]{2,1,0:T(8,128)(2,1)S(1)}, bf16[5,128,112]{2,1,0:T(8,128)(2,1)S(1)}, u32[]{:S(2)}, u32[]{:S(2)}) collective-permute-start(bf16[5,128,112]{2,1,0:T(8,128)(2,1)S(1)} %chip.1.a), channel_id=1, source_target_pairs={{0,8},{4,12},{8,16},{12,20},{16,24},{20,28},{24,0},{28,4},{32,40},... | collective-permute-start | bytes 430088 | tf_op jit(solution)/shard_map/ppermute | solution.py:65
  57.2 10.5 %collective-permute-start.16 = (bf16[5,128,112]{2,1,0:T(8,128)(2,1)S(1)}, bf16[5,128,112]{2,1,0:T(8,128)(2,1)S(1)}, u32[]{:S(2)}, u32[]{:S(2)}) collective-permute-start(bf16[5,128,112]{2,1,0:T(8,128)(2,1)S(1)} %chip.1.a), channel_id=1, source_target_pairs={{0,16},{4,20},{8,24},{12,28},{16,0},{20,4},{24,8},{28,12},{32,48},... | collective-permute-start | bytes 430088 | tf_op jit(solution)/shard_map/ppermute | solution.py:65
  59.2 9.2 %collective-permute-start.17 = (bf16[5,128,112]{2,1,0:T(8,128)(2,1)S(1)}, bf16[5,128,112]{2,1,0:T(8,128)(2,1)S(1)}, u32[]{:S(2)}, u32[]{:S(2)}) collective-permute-start(bf16[5,128,112]{2,1,0:T(8,128)(2,1)S(1)} %chip.1.a), channel_id=1, source_target_pairs={{0,24},{4,28},{8,0},{12,4},{16,8},{20,12},{24,16},{28,20},{32,56},... | collective-permute-start | bytes 430088 | tf_op jit(solution)/shard_map/ppermute | solution.py:65
  68.5 13.3 %collective-permute-start.21 = (bf16[5,128,112]{2,1,0:T(8,128)(2,1)S(1)}, bf16[5,128,112]{2,1,0:T(8,128)(2,1)S(1)}, u32[]{:S(2)}, u32[]{:S(2)}) collective-permute-start(bf16[5,128,112]{2,1,0:T(8,128)(2,1)S(1)} %row.1), channel_id=1, source_target_pairs={{0,32},{4,36},{8,40},{12,44},{16,48},{20,52},{24,56},{28,60},{32,6... | collective-permute-start | bytes 430088 | tf_op jit(solution)/shard_map/ppermute | solution.py:65
  70.5 11.3 %collective-permute-start.22 = (bf16[5,128,112]{2,1,0:T(8,128)(2,1)S(1)}, bf16[5,128,112]{2,1,0:T(8,128)(2,1)S(1)}, u32[]{:S(2)}, u32[]{:S(2)}) collective-permute-start(bf16[5,128,112]{2,1,0:T(8,128)(2,1)S(1)} %row.1), channel_id=1, source_target_pairs={{0,64},{4,68},{8,72},{12,76},{16,80},{20,84},{24,88},{28,92},{32,9... | collective-permute-start | bytes 430088 | tf_op jit(solution)/shard_map/ppermute | solution.py:65
  73.9 7.8 %collective-permute-start.23 = (bf16[5,128,112]{2,1,0:T(8,128)(2,1)S(1)}, bf16[5,128,112]{2,1,0:T(8,128)(2,1)S(1)}, u32[]{:S(2)}, u32[]{:S(2)}) collective-permute-start(bf16[5,128,112]{2,1,0:T(8,128)(2,1)S(1)} %row.1), channel_id=1, source_target_pairs={{0,96},{4,100},{8,104},{12,108},{16,112},{20,116},{24,120},{28,124... | collective-permute-start | bytes 430088 | tf_op jit(solution)/shard_map/ppermute | solution.py:65
  75.3 6.5 %copy-start.2 = (f32[5]{0:T(128)S(1)}, f32[5]{0:T(128)}, u32[]{:S(2)}) copy-start(f32[5]{0:T(128)} %scale.1) | copy-start | bytes 64
  84.4 6.6 %collective-permute-start.24 = (f32[1,2048]{1,0:T(1,128)S(1)}, f32[1,2048]{1,0:T(1,128)S(1)}, u32[]{:S(2)}, u32[]{:S(2)}) collective-permute-start(f32[1,2048]{1,0:T(1,128)S(1)} %get-tuple-element.69.s0), channel_id=1, source_target_pairs={{0,1},{1,2},{2,3},{3,0},{4,5},{5,6},{6,7},{7,4},{8,9},{9,10},{10,1... | collective-permute-start | bytes 24584 | tf_op jit(solution)/shard_map/ppermute | solution.py:450
  86.4 5.3 %collective-permute-start.25 = (f32[1,2048]{1,0:T(1,128)S(1)}, f32[1,2048]{1,0:T(1,128)S(1)}, u32[]{:S(2)}, u32[]{:S(2)}) collective-permute-start(f32[1,2048]{1,0:T(1,128)S(1)} %get-tuple-element.69.s0), channel_id=1, source_target_pairs={{0,2},{1,3},{2,0},{3,1},{4,6},{5,7},{6,4},{7,5},{8,10},{9,11},{10,... | collective-permute-start | bytes 24584 | tf_op jit(solution)/shard_map/ppermute | solution.py:450
  90.0 3.7 %collective-permute-start.26 = (f32[1,2048]{1,0:T(1,128)S(1)}, f32[1,2048]{1,0:T(1,128)S(1)}, u32[]{:S(2)}, u32[]{:S(2)}) collective-permute-start(f32[1,2048]{1,0:T(1,128)S(1)} %get-tuple-element.69.s0), channel_id=1, source_target_pairs={{0,3},{1,0},{2,1},{3,2},{4,7},{5,4},{6,5},{7,6},{8,11},{9,8},{10,9... | collective-permute-start | bytes 24584 | tf_op jit(solution)/shard_map/ppermute | solution.py:450

commit v7 on v6

--- a/solution.py
+++ b/solution.py
@@ -23,6 +23,8 @@
 MIB = 1 << 20
 QUICK = pl.CostEstimate(flops=1, bytes_accessed=1, transcendentals=0)
 
+LONG = pl.CostEstimate(flops=11500000000, bytes_accessed=1, transcendentals=0)
+
 
 def place(y, x, c):
     return (y % 4) * 8 + (x % 4) * 2 + c
@@ -92,7 +94,7 @@
     )
 
 
-def spread_kernel(x_ref, o_ref):
+def spread_kernel(x_ref, w_ref, o_ref, w_out):
     gap = jnp.zeros((PAD - SHARD, x_ref.shape[1]), BF)
     for y in range(4):
         for x in range(4):
@@ -103,20 +105,31 @@
                 o_ref[block, at : at + SHARD, :] = x_ref[dev * SHARD : (dev + 1) * SHARD, :]
                 o_ref[block, at + SHARD : at + PAD, :] = gap
 
-
-def spread(xt):
+    @pl.when(pl.program_id(0) == 0)
+    def _():
+        w_out[...] = w_ref[...]
+
+
+def spread(xt, w):
     n = xt.shape[1]
     blk = 256
+    slow = pltpu.with_memory_space_constraint
     return pl.pallas_call(
         spread_kernel,
         grid=(n // blk,),
-        in_specs=[pl.BlockSpec((D, blk), lambda g: (0, g))],
-        out_specs=pl.BlockSpec((8, BLK, blk), lambda g: (0, 0, g)),
-        out_shape=jax.ShapeDtypeStruct((8, BLK, n), BF),
+        in_specs=[
+            pl.BlockSpec((D, blk), lambda g: (0, g)),
+            pl.BlockSpec(w.shape, lambda g: (0, 0)),
+        ],
+        out_specs=[
+            pl.BlockSpec((8, BLK, blk), lambda g: (0, 0, g)),
+            pl.BlockSpec(w.shape, lambda g: (0, 0)),
+        ],
+        out_shape=[pltpu.VMEM((8, BLK, n), BF), pltpu.VMEM(w.shape, BF)],
         compiler_params=pltpu.CompilerParams(vmem_limit_bytes=8 * MIB),
         cost_estimate=QUICK,
         name="spread",
-    )(xt)
+    )(slow(xt, pltpu.HBM), slow(w, pltpu.HBM))
 
 
 def product(w, x):
@@ -149,7 +162,7 @@
     lax.fori_loop(0, n // GROUP, run, 0)
 
 
-def resident(kernel, small, large, outs, scratch, limit, name, alias=None):
+def resident(kernel, small, large, outs, scratch, limit, name, alias=None, cost=QUICK):
     return pl.pallas_call(
         kernel,
         in_specs=[pl.BlockSpec(memory_space=pltpu.SMEM)] * len(small)
@@ -159,40 +172,38 @@
         scratch_shapes=scratch,
         input_output_aliases=alias or {},
         compiler_params=pltpu.CompilerParams(vmem_limit_bytes=limit * MIB),
-        cost_estimate=QUICK,
+        cost_estimate=cost,
         name=name,
     )(*small, *(fast(a) for a in large))
 
 
 def part_kernel(steps, pos, *refs):
     count = len(steps)
-    kv_pieces, q_pieces = refs[:count], refs[count : 2 * count]
-    x_ref, kv_ref, q_ref, kv_buf, q_buf = refs[2 * count :]
-    lay(kv_pieces, kv_buf)
-    lay(q_pieces, q_buf)
+    pieces, x_ref, sum_ref, wbuf = refs[:count], refs[count], refs[-2], refs[-1]
+    lay(pieces, wbuf)
+    rows = sum_ref.shape[0]
 
     def step(g, at):
-        x = rows_of(pos, steps, x_ref, at)
-        kv_ref[:, at] = product(kv_buf[:, : 2 * HL * DH], x)
-        q_ref[:, at] = product(q_buf[:, : HL * DH], x)
+        new = product(wbuf[:, :rows], rows_of(pos, steps, x_ref, at))
+        sum_ref[:, at] = new + refs[count + 1][:, at] if len(refs) == count + 4 else new
 
     each_group(x_ref.shape[2], step)
 
 
-def part_call(steps, pos, kv_pieces, q_pieces, xp):
-    n = xp.shape[2]
-    return resident(
+def part_call(steps, pos, pieces, xp, rows, sums=None, name="part", cost=QUICK):
+    earlier = [] if sums is None else [sums]
+    (out,) = resident(
         functools.partial(part_kernel, steps),
         [pos],
-        [*kv_pieces, *q_pieces, xp],
-        [((2 * HL * DH, n), F32), ((HL * DH, n), F32)],
-        [
-            pltpu.VMEM((len(steps) * BLK, QCOL), BF),
-            pltpu.VMEM((len(steps) * BLK, COLS - QCOL), BF),
-        ],
+        [*pieces, xp, *earlier],
+        [((rows, xp.shape[2]), F32)],
+        [pltpu.VMEM((len(steps) * BLK, pieces[0].shape[1]), BF)],
         16,
-        "part_first",
-    )
+        name,
+        {len(pieces) + 2: 0} if earlier else None,
+        cost,
+    )
+    return out
 
 
 def feature(raw):
@@ -414,30 +425,46 @@
     me = lax.axis_index("tm").astype(jnp.int32)
     y, x, core = me // 8, (me // 2) % 4, me % 2
     pos = jnp.stack([y, x, core])
-    pos, gain = lax.optimization_barrier((pos, norm_gain.reshape(HL, DH)))
-    shards = [qkv_weight] + [shift(qkv_weight, first_leg(d)) for d in (1, 2, 3)]
-    near_kv, near_q = pack(pos, shards)
-    near_kv, xt = lax.optimization_barrier((near_kv, tokens.T))
+    pos, gain, xt = lax.optimization_barrier((pos, norm_gain.reshape(HL, DH), tokens.T))
+    shards = [shift(qkv_weight, first_leg(d)) for d in (1, 2, 3)]
+    xp, staged = spread(xt, qkv_weight)
+    near_kv, near_q = pack(pos, [staged, *shards])
     own_kv = [near_kv] + [shift(near_kv, second_leg(d)) for d in (1, 2, 3)]
-    sib_kv, first_q = [shift(near_kv, SIBLING)], [near_q, shift(near_q, SIBLING)]
-    xp = spread(pltpu.with_memory_space_constraint(xt, pltpu.HBM))
+    sib_kv = [shift(near_kv, SIBLING)] + [None] * 3
+    first_q = [near_q, shift(near_q, SIBLING)]
 
     both = ((True, 0), (False, 0))
-    mine = tuple((True, d) for d in (1, 2, 3))
-    last = tuple((False, d) for d in (1, 2, 3))
-    kv_sum, q_sum = part_call(both, pos, [near_kv, sib_kv[0]], first_q, xp)
-    near_q, kv_sum, q_sum = lax.optimization_barrier((near_q, kv_sum, q_sum))
+    beside = ((True, 1), (False, 1), (True, 3), (False, 3))
+    across = ((True, 2), (False, 2))
+    rest = tuple((mine, d) for mine in (True, False) for d in (1, 2, 3))
+    half = HL * DH
+    kv_sum = part_call(both, pos, [near_kv, sib_kv[0]], xp, 2 * half, name="part_kv")
+    own_kv[1], own_kv[3], kv_sum, *first_q = lax.optimization_barrier(
+        (own_kv[1], own_kv[3], kv_sum, *first_q)
+    )
+    sib_kv[1], sib_kv[3] = shift(own_kv[1], SIBLING), shift(own_kv[3], SIBLING)
+    q_sum = part_call(both, pos, first_q, xp, half, name="part_q", cost=LONG)
+    kv_sum, q_sum = lax.optimization_barrier((kv_sum, q_sum))
+    kv_sum = part_call(
+        beside,
+        pos,
+        [(own_kv if mine else sib_kv)[d] for mine, d in beside],
+        xp,
+        2 * half,
+        kv_sum,
+        name="part_more",
+    )
+    near_q, own_kv[2], kv_sum = lax.optimization_barrier((first_q[0], own_kv[2], kv_sum))
+    sib_kv[2] = shift(own_kv[2], SIBLING)
     own_q = [shift(near_q, second_leg(d)) for d in (1, 2, 3)]
-    *own_kv, kv_sum = lax.optimization_barrier((*own_kv, kv_sum))
-    sib_kv = [shift(a, SIBLING) for a in own_kv[1:]]
-    fk, v, pre, tot = kv_call(mine + last, pos, [*own_kv[1:], *sib_kv], xp, kv_sum)
+    fk, v, pre, tot = kv_call(across, pos, [own_kv[2], sib_kv[2]], xp, kv_sum)
 
     other = shift(tot, SIBLING)
     *own_q, other = lax.optimization_barrier((*own_q, other))
     sib_q = [shift(a, SIBLING) for a in own_q]
     chip = small(chip_kernel, [tot, other], "chip")
     chip, q_sum = lax.optimization_barrier((chip, q_sum))
-    fq = q_call(mine + last, pos, [*own_q, *sib_q], xp, q_sum)
+    fq = q_call(rest, pos, [*own_q, *sib_q], xp, q_sum)
     in_row = [shift(chip, along_x(d)) for d in (1, 2, 3)]
     *in_row, fq = lax.optimization_barrier((*in_row, fq))
     row = small(row_kernel, [chip, *in_row], "row")

time: 96 us -> 102 us (1.062)
  waiting for transfers between devices: 12.9 us -> 21.4 us
  starting transfers between devices: 35.2 us -> 30.2 us
  Pallas kernels: 45.4 us -> 48.9 us
    ppermute x24, waiting for transfers between devices: 10.3 us -> 17.5 us  [shift(): return lax.ppermute(a, 'tm', moves)]
    ppermute x24, starting transfers between devices: 28.6 us -> 24.9 us  [shift(): return lax.ppermute(a, 'tm', moves)]
    pallas_call x8 -> x10, Pallas kernels: 36.7 us -> 40.2 us  [resident(): pl.pallas_call(kernel, in_specs=[pl.BlockSpec(memory_space=pltpu.SMEM)] *...]
    ppermute x3, waiting for transfers between devices: 2.63 us -> 3.88 us  [body(): lax.ppermute(squares, 'head', [(i, (i + d) % 4) for i in range(4)])]
    ppermute x3, starting transfers between devices: 6.57 us -> 5.38 us  [body(): lax.ppermute(squares, 'head', [(i, (i + d) % 4) for i in range(4)])]
  transfers between devices with their start and end apart: 27 -> 27, of which waited for: 8 -> 6; matrix products, arithmetic and copies ran while one was open for 1% -> 1% of each run, Pallas kernels for 41% -> 42%
where the time goes in v7:
time: 102 us
  Pallas kernels  48.9 us (48%)
  starting transfers between devices  30.2 us (30%)
  waiting for transfers between devices  21.4 us (21%)
    pallas_call x10, Pallas kernels, resident(): pl.pallas_call(kernel, in_specs=[pl.BlockSpec(memory_space=pltpu.SMEM)] *...  40.2 us
    ppermute x24, starting transfers between devices, shift(): return lax.ppermute(a, 'tm', moves)  24.9 us
    ppermute x24, waiting for transfers between devices, shift(): return lax.ppermute(a, 'tm', moves)  17.5 us
    pallas_call x1, Pallas kernels, spread(): pl.pallas_call(spread_kernel, grid=(n // blk,), in_specs=[pl.BlockSpec((D...  6.91 us
    ppermute x3, starting transfers between devices, body(): lax.ppermute(squares, 'head', [(i, (i + d) % 4) for i in range(4)])  5.38 us
    ppermute x3, waiting for transfers between devices, body(): lax.ppermute(squares, 'head', [(i, (i + d) % 4) for i in range(4)])  3.88 us
  transfers between devices with their start and end apart: 27, of which 6 were waited for; matrix products, arithmetic and copies ran while one was open for 1% of the time, Pallas kernels for 42%

profile of v7, /device:TPU:0, one launch (start us, length us, event | category | flops | bytes accessed | tf_op | source)
XLA Modules:
  0.0 101.8 jit_solution(6561003504445363629)
XLA Ops:
  0.0 1.6 %collective-permute-start = (bf16[70,1680]{1,0:T(8,128)(2,1)}, bf16[70,1680]{1,0:T(8,128)(2,1)S(1)}, u32[]{:S(2)}, u32[]{:S(2)}) collective-permute-start(bf16[70,1680]{1,0:T(8,128)(2,1)} %w_ref.1), channel_id=1, source_target_pairs={{0,8},{4,36},{8,16},{12,44},{16,24},{20,52},{24,0},{28,60},{32,40}... | collective-permute-start | bytes 705608 | tf_op jit(solution)/shard_map/ppermute | solution.py:67
  1.6 1.7 %collective-permute-start.2 = (bf16[70,1680]{1,0:T(8,128)(2,1)}, bf16[70,1680]{1,0:T(8,128)(2,1)S(1)}, u32[]{:S(2)}, u32[]{:S(2)}) collective-permute-start(bf16[70,1680]{1,0:T(8,128)(2,1)} %w_ref.1), channel_id=1, source_target_pairs={{0,24},{4,100},{8,0},{12,108},{16,8},{20,116},{24,16},{28,124},{32... | collective-permute-start | bytes 705608 | tf_op jit(solution)/shard_map/ppermute | solution.py:67
  3.2 1.9 %collective-permute-start.1 = (bf16[70,1680]{1,0:T(8,128)(2,1)}, bf16[70,1680]{1,0:T(8,128)(2,1)S(1)}, u32[]{:S(2)}, u32[]{:S(2)}) collective-permute-start(bf16[70,1680]{1,0:T(8,128)(2,1)} %w_ref.1), channel_id=1, source_target_pairs={{0,16},{4,68},{8,24},{12,76},{16,0},{20,84},{24,8},{28,92},{32,48}... | collective-permute-start | bytes 705608 | tf_op jit(solution)/shard_map/ppermute | solution.py:67
  5.1 0.8 reshape.3.gain_ref
  6.0 6.9 %spread.1 = (bf16[8,288,2048]{2,1,0:T(8,128)(2,1)S(1)}, bf16[70,1680]{1,0:T(8,128)(2,1)S(1)}) custom-call(bf16[2240,2048]{1,0:T(8,128)(2,1)} %bitcast.5, bf16[70,1680]{1,0:T(8,128)(2,1)} %w_ref.1), custom_call_target="tpu_custom_call" | custom-call | flops 1 | bytes 1 | tf_op jit(solution)/shard_map/spread/pallas_call | solution.py:117
  12.9 1.4 %pack.1 = (bf16[288,1152]{1,0:T(8,128)(2,1)S(1)}, bf16[288,640]{1,0:T(8,128)(2,1)S(1)}) custom-call(s32[3]{0:T(128)S(1)} %pad_add_fusion.pos, bf16[70,1680]{1,0:T(8,128)(2,1)S(1)} %get-tuple-element.42.a0, bf16[70,1680]{1,0:T(8,128)(2,1)S(1)} %collective-permute-done.a1, bf16[70,1680]{1,0:T(8,128)(2,1)S(1)} %collective-permute-done.1.a2, ...), custom_call_target="tpu_custom_call" | custom-call | flops 1 | bytes 1 | tf_op jit(solution)/shard_map/pack/pallas_call | solution.py:166
  14.5 3.1 %collective-permute-start.4 = (bf16[288,1152]{1,0:T(8,128)(2,1)S(1)}, bf16[288,1152]{1,0:T(8,128)(2,1)S(1)}, u32[]{:S(2)}, u32[]{:S(2)}) collective-permute-start(bf16[288,1152]{1,0:T(8,128)(2,1)S(1)} %get-tuple-element.43.refs_0_), channel_id=1, source_target_pairs={{0,96},{4,28},{8,104},{12,4},{16,112},{20,12},{24,120},{28,20},{32... | collective-permute-start | bytes 1990664 | tf_op jit(solution)/shard_map/ppermute | solution.py:67
  17.6 2.2 %collective-permute-start.7 = (bf16[288,1152]{1,0:T(8,128)(2,1)S(1)}, bf16[288,1152]{1,0:T(8,128)(2,1)S(1)}, u32[]{:S(2)}, u32[]{:S(2)}) collective-permute-start(bf16[288,1152]{1,0:T(8,128)(2,1)S(1)} %get-tuple-element.43.refs_0_), channel_id=1, source_target_pairs={{0,64},{4,20},{8,72},{12,28},{16,80},{20,4},{24,88},{28,12},{32,96... | collective-permute-start | bytes 1990664 | tf_op jit(solution)/shard_map/ppermute | solution.py:67
  19.8 5.0 %part_kv.1.refs_5_ = f32[1120,2048]{1,0:T(8,128)S(1)} custom-call(s32[3]{0:T(128)S(1)} %pad_add_fusion.pos, bf16[288,1152]{1,0:T(8,128)(2,1)S(1)} %get-tuple-element.43.refs_0_, bf16[288,1152]{1,0:T(8,128)(2,1)S(1)} %collective-permute-done.5.refs_1_, bf16[8,288,2048]{2,1,0:T(8,128)(2,1)S(1)} %get-tuple-element.44.refs_2_.refs_4_.refs_6_), custom_call_target="tpu_custom_call" | custom-call | flops 1 | bytes 1 | tf_op jit(solution)/shard_map/part_kv/pallas_call | solution.py:166
  24.8 8.1 %collective-permute-done.4.refs_2_ = bf16[288,1152]{1,0:T(8,128)(2,1)S(1)} collective-permute-done((bf16[288,1152]{1,0:T(8,128)(2,1)S(1)}, bf16[288,1152]{1,0:T(8,128)(2,1)S(1)}, u32[]{:S(2)}, u32[]{:S(2)}) %collective-permute-start.4) | collective-permute-done | bytes 663584 | tf_op jit(solution)/shard_map/ppermute | solution.py:67
  32.9 3.7 %collective-permute-done.3.refs_0_ = bf16[288,1152]{1,0:T(8,128)(2,1)S(1)} collective-permute-done((bf16[288,1152]{1,0:T(8,128)(2,1)S(1)}, bf16[288,1152]{1,0:T(8,128)(2,1)S(1)}, u32[]{:S(2)}, u32[]{:S(2)}) %collective-permute-start.3) | collective-permute-done | bytes 663584 | tf_op jit(solution)/shard_map/ppermute | solution.py:67
  37.1 3.2 %part_q.1.refs_7_ = f32[560,2048]{1,0:T(8,128)S(1)} custom-call(s32[3]{0:T(128)S(1)} %pad_add_fusion.pos, bf16[288,640]{1,0:T(8,128)(2,1)S(1)} %get-tuple-element.52.refs_0_, bf16[288,640]{1,0:T(8,128)(2,1)S(1)} %collective-permute-done.6.refs_1_, bf16[8,288,2048]{2,1,0:T(8,128)(2,1)S(1)} %get-tuple-element.44.refs_2_.refs_4_.refs_6_), custom_call_target="tpu_custom_call" | custom-call | flops 11500000256 | bytes 1 | tf_op jit(solution)/shard_map/part_q/pallas_call | solution.py:166
  40.3 7.5 %part_more.1.refs_3_ = f32[1120,2048]{1,0:T(8,128)S(1)} custom-call(s32[3]{0:T(128)S(1)} %pad_add_fusion.pos, bf16[288,1152]{1,0:T(8,128)(2,1)S(1)} %collective-permute-done.3.refs_0_, bf16[288,1152]{1,0:T(8,128)(2,1)S(1)} %collective-permute-done.8.refs_1_, bf16[288,1152]{1,0:T(8,128)(2,1)S(1)} %collective-permute-done.4.refs_2_, ...), custom_call_target="tpu_custom_call", output_to_operand_aliasing={{}: (6, {})} | custom-call | flops 1 | bytes 1 | tf_op jit(solution)/shard_map/part_more/pallas_call | solution.py:166
  48.0 0.6 collective-permute-start.11
  48.7 1.3 %collective-permute-start.10 = (bf16[288,640]{1,0:T(8,128)(2,1)S(1)}, bf16[288,640]{1,0:T(8,128)(2,1)S(1)}, u32[]{:S(2)}, u32[]{:S(2)}) collective-permute-start(bf16[288,640]{1,0:T(8,128)(2,1)S(1)} %get-tuple-element.52.refs_0_), channel_id=1, source_target_pairs={{0,32},{4,12},{8,40},{12,20},{16,48},{20,28},{24,56},{28,4},{32,64... | collective-permute-start | bytes 1105928 | tf_op jit(solution)/shard_map/ppermute | solution.py:67
  50.0 7.2 %keys_values.1 = (bf16[5,2048,112]{2,1,0:T(8,128)(2,1)S(1)}, bf16[5,128,2048]{2,1,0:T(8,128)(2,1)S(1)}, f32[4,5,128,112]{3,2,1,0:T(8,128)S(1)}, bf16[5,128,112]{2,1,0:T(8,128)(2,1)S(1)}) custom-call(s32[3]{0:T(128)S(1)} %pad_add_fusion.pos, bf16[288,1152]{1,0:T(8,128)(2,1)S(1)} %collective-permute-done.7.refs_0_, ...), custom_call_target="tpu_custom_call" | custom-call | flops 1 | bytes 1 | tf_op jit(solution)/shard_map/keys_values/pallas_call | solution.py:166
  57.3 0.8 collective-permute-start.14
  58.0 3.0 %collective-permute-done.10.refs_0_ = bf16[288,640]{1,0:T(8,128)(2,1)S(1)} collective-permute-done((bf16[288,640]{1,0:T(8,128)(2,1)S(1)}, bf16[288,640]{1,0:T(8,128)(2,1)S(1)}, u32[]{:S(2)}, u32[]{:S(2)}) %collective-permute-start.10) | collective-permute-done | bytes 368672 | tf_op jit(solution)/shard_map/ppermute | solution.py:67
  61.7 1.1 %collective-permute-start.17 = (bf16[5,128,112]{2,1,0:T(8,128)(2,1)S(1)}, bf16[5,128,112]{2,1,0:T(8,128)(2,1)S(1)}, u32[]{:S(2)}, u32[]{:S(2)}) collective-permute-start(bf16[5,128,112]{2,1,0:T(8,128)(2,1)S(1)} %chip.1.a), channel_id=1, source_target_pairs={{0,24},{4,28},{8,0},{12,4},{16,8},{20,12},{24,16},{28,20},{32,56},... | collective-permute-start | bytes 430088 | tf_op jit(solution)/shard_map/ppermute | solution.py:67
  62.8 1.5 %collective-permute-start.16 = (bf16[5,128,112]{2,1,0:T(8,128)(2,1)S(1)}, bf16[5,128,112]{2,1,0:T(8,128)(2,1)S(1)}, u32[]{:S(2)}, u32[]{:S(2)}) collective-permute-start(bf16[5,128,112]{2,1,0:T(8,128)(2,1)S(1)} %chip.1.a), channel_id=1, source_target_pairs={{0,16},{4,20},{8,24},{12,28},{16,0},{20,4},{24,8},{28,12},{32,48},... | collective-permute-start | bytes 430088 | tf_op jit(solution)/shard_map/ppermute | solution.py:67
  64.4 0.6 collective-permute-start.15
  65.0 6.5 %queries.1.fq_ref.refs_8_ = bf16[560,2048]{1,0:T(8,128)(2,1)S(1)} custom-call(s32[3]{0:T(128)S(1)} %pad_add_fusion.pos, bf16[288,640]{1,0:T(8,128)(2,1)S(1)} %collective-permute-done.10.refs_0_, bf16[288,640]{1,0:T(8,128)(2,1)S(1)} %collective-permute-done.11.refs_1_, bf16[288,640]{1,0:T(8,128)(2,1)S(1)} %collective-permute-done.12.refs_2_, ...), custom_call_target="tpu_custom_call" | custom-call | flops 1 | bytes 1 | tf_op jit(solution)/shard_map/queries/pallas_call | solution.py:166
  71.5 2.7 %collective-permute-done.15.b.refs_1_ = bf16[5,128,112]{2,1,0:T(8,128)(2,1)S(1)} collective-permute-done((bf16[5,128,112]{2,1,0:T(8,128)(2,1)S(1)}, bf16[5,128,112]{2,1,0:T(8,128)(2,1)S(1)}, u32[]{:S(2)}, u32[]{:S(2)}) %collective-permute-start.15) | collective-permute-done | bytes 143392 | tf_op jit(solution)/shard_map/ppermute | solution.py:67
  74.3 3.0 %collective-permute-start.23 = (bf16[5,128,112]{2,1,0:T(8,128)(2,1)S(1)}, bf16[5,128,112]{2,1,0:T(8,128)(2,1)S(1)}, u32[]{:S(2)}, u32[]{:S(2)}) collective-permute-start(bf16[5,128,112]{2,1,0:T(8,128)(2,1)S(1)} %row.1), channel_id=1, source_target_pairs={{0,96},{4,100},{8,104},{12,108},{16,112},{20,116},{24,120},{28,124... | collective-permute-start | bytes 430088 | tf_op jit(solution)/shard_map/ppermute | solution.py:67
  77.3 1.4 %collective-permute-start.22 = (bf16[5,128,112]{2,1,0:T(8,128)(2,1)S(1)}, bf16[5,128,112]{2,1,0:T(8,128)(2,1)S(1)}, u32[]{:S(2)}, u32[]{:S(2)}) collective-permute-start(bf16[5,128,112]{2,1,0:T(8,128)(2,1)S(1)} %row.1), channel_id=1, source_target_pairs={{0,64},{4,68},{8,72},{12,76},{16,80},{20,84},{24,88},{28,92},{32,9... | collective-permute-start | bytes 430088 | tf_op jit(solution)/shard_map/ppermute | solution.py:67
  78.7 2.7 %collective-permute-start.21 = (bf16[5,128,112]{2,1,0:T(8,128)(2,1)S(1)}, bf16[5,128,112]{2,1,0:T(8,128)(2,1)S(1)}, u32[]{:S(2)}, u32[]{:S(2)}) collective-permute-start(bf16[5,128,112]{2,1,0:T(8,128)(2,1)S(1)} %row.1), channel_id=1, source_target_pairs={{0,32},{4,36},{8,40},{12,44},{16,48},{20,52},{24,56},{28,60},{32,6... | collective-permute-start | bytes 430088 | tf_op jit(solution)/shard_map/ppermute | solution.py:67
  81.4 6.5 %attend.1.refs_9_ = f32[5,128,2048]{2,1,0:T(8,128)S(1)} custom-call(s32[4]{0:T(128)S(1)} %copy-done, bf16[5,2048,112]{2,1,0:T(8,128)(2,1)S(1)} %get-tuple-element.70.fk_ref, bf16[5,128,2048]{2,1,0:T(8,128)(2,1)S(1)} %get-tuple-element.71.v_ref, bf16[560,2048]{1,0:T(8,128)(2,1)S(1)} %queries.1.fq_ref.refs_8_), custom_call_target="tpu_custom_call" | custom-call | flops 1 | bytes 1 | tf_op jit(solution)/shard_map/attend/pallas_call | solution.py:166
  87.9 2.6 %join.1 = (f32[560,2048]{1,0:T(8,128)S(1)}, f32[1,2048]{1,0:T(1,128)S(1)}) custom-call(s32[3]{0:T(128)S(1)} %pad_add_fusion.pos, f32[5]{0:T(128)S(1)} %copy-done.1, bf16[5,128,112]{2,1,0:T(8,128)(2,1)S(1)} %collective-permute-done.14.other_ref.refs_0_, bf16[5,128,112]{2,1,0:T(8,128)(2,1)S(1)} %collective-permute-done.15.b.refs_1_, ...), custom_call_target="tpu_custom_call" | custom-call | flops 1 | bytes 1 | tf_op jit(solution)/shard_map/join/pallas_call | solution.py:166
  90.5 4.1 %collective-permute-start.26 = (f32[1,2048]{1,0:T(1,128)S(1)}, f32[1,2048]{1,0:T(1,128)S(1)}, u32[]{:S(2)}, u32[]{:S(2)}) collective-permute-start(f32[1,2048]{1,0:T(1,128)S(1)} %get-tuple-element.73.s0), channel_id=1, source_target_pairs={{0,3},{1,0},{2,1},{3,2},{4,7},{5,4},{6,5},{7,6},{8,11},{9,8},{10,9... | collective-permute-start | bytes 24584 | tf_op jit(solution)/shard_map/ppermute | solution.py:477
  94.6 1.3 %collective-permute-start.24 = (f32[1,2048]{1,0:T(1,128)S(1)}, f32[1,2048]{1,0:T(1,128)S(1)}, u32[]{:S(2)}, u32[]{:S(2)}) collective-permute-start(f32[1,2048]{1,0:T(1,128)S(1)} %get-tuple-element.73.s0), channel_id=1, source_target_pairs={{0,1},{1,2},{2,3},{3,0},{4,5},{5,6},{6,7},{7,4},{8,9},{9,10},{10,1... | collective-permute-start | bytes 24584 | tf_op jit(solution)/shard_map/ppermute | solution.py:477
  96.0 3.8 %collective-permute-done.25.s2 = f32[1,2048]{1,0:T(1,128)S(1)} collective-permute-done((f32[1,2048]{1,0:T(1,128)S(1)}, f32[1,2048]{1,0:T(1,128)S(1)}, u32[]{:S(2)}, u32[]{:S(2)}) %collective-permute-start.25) | collective-permute-done | bytes 8224 | tf_op jit(solution)/shard_map/ppermute | solution.py:477
  99.8 1.9 %norm.1 = bf16[560,2048]{1,0:T(8,128)(2,1)} custom-call(f32[560,2048]{1,0:T(8,128)S(1)} %get-tuple-element.72.out_ref, f32[1,2048]{1,0:T(1,128)S(1)} %get-tuple-element.73.s0, f32[1,2048]{1,0:T(1,128)S(1)} %collective-permute-done.24.s1, f32[1,2048]{1,0:T(1,128)S(1)} %collective-permute-done.25.s2, f32[1,2048]{1,0:T(1,128)S(1)} %collective-permute-done.26.s3, ...), custom_call_target="tpu_custom_call" | custom-call | flops 1 | bytes 1 | tf_op jit(solution)/shard_map/norm/pallas_call | solution.py:409
  (40 shorter events, 1.8 us)
Async XLA Ops:
  0.0 12.9 %collective-permute-start = (bf16[70,1680]{1,0:T(8,128)(2,1)}, bf16[70,1680]{1,0:T(8,128)(2,1)S(1)}, u32[]{:S(2)}, u32[]{:S(2)}) collective-permute-start(bf16[70,1680]{1,0:T(8,128)(2,1)} %w_ref.1), channel_id=1, source_target_pairs={{0,8},{4,36},{8,16},{12,44},{16,24},{20,52},{24,0},{28,60},{32,40}... | collective-permute-start | bytes 705608 | tf_op jit(solution)/shard_map/ppermute | solution.py:67
  1.6 11.3 %collective-permute-start.2 = (bf16[70,1680]{1,0:T(8,128)(2,1)}, bf16[70,1680]{1,0:T(8,128)(2,1)S(1)}, u32[]{:S(2)}, u32[]{:S(2)}) collective-permute-start(bf16[70,1680]{1,0:T(8,128)(2,1)} %w_ref.1), channel_id=1, source_target_pairs={{0,24},{4,100},{8,0},{12,108},{16,8},{20,116},{24,16},{28,124},{32... | collective-permute-start | bytes 705608 | tf_op jit(solution)/shard_map/ppermute | solution.py:67
  3.2 9.7 %collective-permute-start.1 = (bf16[70,1680]{1,0:T(8,128)(2,1)}, bf16[70,1680]{1,0:T(8,128)(2,1)S(1)}, u32[]{:S(2)}, u32[]{:S(2)}) collective-permute-start(bf16[70,1680]{1,0:T(8,128)(2,1)} %w_ref.1), channel_id=1, source_target_pairs={{0,16},{4,68},{8,24},{12,76},{16,0},{20,84},{24,8},{28,92},{32,48}... | collective-permute-start | bytes 705608 | tf_op jit(solution)/shard_map/ppermute | solution.py:67
  14.4 5.4 %collective-permute-start.5 = (bf16[288,1152]{1,0:T(8,128)(2,1)S(1)}, bf16[288,1152]{1,0:T(8,128)(2,1)S(1)}, u32[]{:S(2)}, u32[]{:S(2)}) collective-permute-start(bf16[288,1152]{1,0:T(8,128)(2,1)S(1)} %get-tuple-element.43.refs_0_), channel_id=1, source_target_pairs={{0,4},{4,0},{8,12},{12,8},{16,20},{20,16},{24,28},{28,24},{32,36},... | collective-permute-start | bytes 1990664 | tf_op jit(solution)/shard_map/ppermute | solution.py:67
  14.5 18.4 %collective-permute-start.4 = (bf16[288,1152]{1,0:T(8,128)(2,1)S(1)}, bf16[288,1152]{1,0:T(8,128)(2,1)S(1)}, u32[]{:S(2)}, u32[]{:S(2)}) collective-permute-start(bf16[288,1152]{1,0:T(8,128)(2,1)S(1)} %get-tuple-element.43.refs_0_), channel_id=1, source_target_pairs={{0,96},{4,28},{8,104},{12,4},{16,112},{20,12},{24,120},{28,20},{32... | collective-permute-start | bytes 1990664 | tf_op jit(solution)/shard_map/ppermute | solution.py:67
  17.6 19.0 %collective-permute-start.3 = (bf16[288,1152]{1,0:T(8,128)(2,1)S(1)}, bf16[288,1152]{1,0:T(8,128)(2,1)S(1)}, u32[]{:S(2)}, u32[]{:S(2)}) collective-permute-start(bf16[288,1152]{1,0:T(8,128)(2,1)S(1)} %get-tuple-element.43.refs_0_), channel_id=1, source_target_pairs={{0,32},{4,12},{8,40},{12,20},{16,48},{20,28},{24,56},{28,4},{32,64... | collective-permute-start | bytes 1990664 | tf_op jit(solution)/shard_map/ppermute | solution.py:67
  17.6 7.2 %collective-permute-start.6 = (bf16[288,640]{1,0:T(8,128)(2,1)S(1)}, bf16[288,640]{1,0:T(8,128)(2,1)S(1)}, u32[]{:S(2)}, u32[]{:S(2)}) collective-permute-start(bf16[288,640]{1,0:T(8,128)(2,1)S(1)} %get-tuple-element.52.refs_0_), channel_id=1, source_target_pairs={{0,4},{4,0},{8,12},{12,8},{16,20},{20,16},{24,28},{28,24},{32,36},... | collective-permute-start | bytes 1105928 | tf_op jit(solution)/shard_map/ppermute | solution.py:67
  17.6 30.3 %collective-permute-start.7 = (bf16[288,1152]{1,0:T(8,128)(2,1)S(1)}, bf16[288,1152]{1,0:T(8,128)(2,1)S(1)}, u32[]{:S(2)}, u32[]{:S(2)}) collective-permute-start(bf16[288,1152]{1,0:T(8,128)(2,1)S(1)} %get-tuple-element.43.refs_0_), channel_id=1, source_target_pairs={{0,64},{4,20},{8,72},{12,28},{16,80},{20,4},{24,88},{28,12},{32,96... | collective-permute-start | bytes 1990664 | tf_op jit(solution)/shard_map/ppermute | solution.py:67
  36.5 3.7 %collective-permute-start.8 = (bf16[288,1152]{1,0:T(8,128)(2,1)S(1)}, bf16[288,1152]{1,0:T(8,128)(2,1)S(1)}, u32[]{:S(2)}, u32[]{:S(2)}) collective-permute-start(bf16[288,1152]{1,0:T(8,128)(2,1)S(1)} %collective-permute-done.3.refs_0_), channel_id=1, source_target_pairs={{0,4},{4,0},{8,12},{12,8},{16,20},{20,16},{24,28},{28,24},{32,36},... | collective-permute-start | bytes 1990664 | tf_op jit(solution)/shard_map/ppermute | solution.py:67
  36.6 3.7 %collective-permute-start.9 = (bf16[288,1152]{1,0:T(8,128)(2,1)S(1)}, bf16[288,1152]{1,0:T(8,128)(2,1)S(1)}, u32[]{:S(2)}, u32[]{:S(2)}) collective-permute-start(bf16[288,1152]{1,0:T(8,128)(2,1)S(1)} %collective-permute-done.4.refs_2_), channel_id=1, source_target_pairs={{0,4},{4,0},{8,12},{12,8},{16,20},{20,16},{24,28},{28,24},{32,36},... | collective-permute-start | bytes 1990664 | tf_op jit(solution)/shard_map/ppermute | solution.py:67
  47.8 2.2 %collective-permute-start.13 = (bf16[288,1152]{1,0:T(8,128)(2,1)S(1)}, bf16[288,1152]{1,0:T(8,128)(2,1)S(1)}, u32[]{:S(2)}, u32[]{:S(2)}) collective-permute-start(bf16[288,1152]{1,0:T(8,128)(2,1)S(1)} %collective-permute-done.7.refs_0_), channel_id=1, source_target_pairs={{0,4},{4,0},{8,12},{12,8},{16,20},{20,16},{24,28},{28,24},{32,36},... | collective-permute-start | bytes 1990664 | tf_op jit(solution)/shard_map/ppermute | solution.py:67
  47.9 10.1 %collective-permute-start.12 = (bf16[288,640]{1,0:T(8,128)(2,1)S(1)}, bf16[288,640]{1,0:T(8,128)(2,1)S(1)}, u32[]{:S(2)}, u32[]{:S(2)}) collective-permute-start(bf16[288,640]{1,0:T(8,128)(2,1)S(1)} %get-tuple-element.52.refs_0_), channel_id=1, source_target_pairs={{0,96},{4,28},{8,104},{12,4},{16,112},{20,12},{24,120},{28,20},{32... | collective-permute-start | bytes 1105928 | tf_op jit(solution)/shard_map/ppermute | solution.py:67
  48.0 10.0 %collective-permute-start.11 = (bf16[288,640]{1,0:T(8,128)(2,1)S(1)}, bf16[288,640]{1,0:T(8,128)(2,1)S(1)}, u32[]{:S(2)}, u32[]{:S(2)}) collective-permute-start(bf16[288,640]{1,0:T(8,128)(2,1)S(1)} %get-tuple-element.52.refs_0_), channel_id=1, source_target_pairs={{0,64},{4,20},{8,72},{12,28},{16,80},{20,4},{24,88},{28,12},{32,96... | collective-permute-start | bytes 1105928 | tf_op jit(solution)/shard_map/ppermute | solution.py:67
  48.7 12.4 %collective-permute-start.10 = (bf16[288,640]{1,0:T(8,128)(2,1)S(1)}, bf16[288,640]{1,0:T(8,128)(2,1)S(1)}, u32[]{:S(2)}, u32[]{:S(2)}) collective-permute-start(bf16[288,640]{1,0:T(8,128)(2,1)S(1)} %get-tuple-element.52.refs_0_), channel_id=1, source_target_pairs={{0,32},{4,12},{8,40},{12,20},{16,48},{20,28},{24,56},{28,4},{32,64... | collective-permute-start | bytes 1105928 | tf_op jit(solution)/shard_map/ppermute | solution.py:67
  57.3 3.8 %collective-permute-start.14 = (bf16[5,128,112]{2,1,0:T(8,128)(2,1)S(1)}, bf16[5,128,112]{2,1,0:T(8,128)(2,1)S(1)}, u32[]{:S(2)}, u32[]{:S(2)}) collective-permute-start(bf16[5,128,112]{2,1,0:T(8,128)(2,1)S(1)} %get-tuple-element.55.tot_ref), channel_id=1, source_target_pairs={{0,4},{4,0},{8,12},{12,8},{16,20},{20,16},{24,28},{28,24},{32,36},... | collective-permute-start | bytes 430088 | tf_op jit(solution)/shard_map/ppermute | solution.py:67
  61.0 3.3 %collective-permute-start.18 = (bf16[288,640]{1,0:T(8,128)(2,1)S(1)}, bf16[288,640]{1,0:T(8,128)(2,1)S(1)}, u32[]{:S(2)}, u32[]{:S(2)}) collective-permute-start(bf16[288,640]{1,0:T(8,128)(2,1)S(1)} %collective-permute-done.10.refs_0_), channel_id=1, source_target_pairs={{0,4},{4,0},{8,12},{12,8},{16,20},{20,16},{24,28},{28,24},{32,36},... | collective-permute-start | bytes 1105928 | tf_op jit(solution)/shard_map/ppermute | solution.py:67
  61.2 3.8 %collective-permute-start.19 = (bf16[288,640]{1,0:T(8,128)(2,1)S(1)}, bf16[288,640]{1,0:T(8,128)(2,1)S(1)}, u32[]{:S(2)}, u32[]{:S(2)}) collective-permute-start(bf16[288,640]{1,0:T(8,128)(2,1)S(1)} %collective-permute-done.11.refs_1_), channel_id=1, source_target_pairs={{0,4},{4,0},{8,12},{12,8},{16,20},{20,16},{24,28},{28,24},{32,36},... | collective-permute-start | bytes 1105928 | tf_op jit(solution)/shard_map/ppermute | solution.py:67
  61.6 3.4 %collective-permute-start.20 = (bf16[288,640]{1,0:T(8,128)(2,1)S(1)}, bf16[288,640]{1,0:T(8,128)(2,1)S(1)}, u32[]{:S(2)}, u32[]{:S(2)}) collective-permute-start(bf16[288,640]{1,0:T(8,128)(2,1)S(1)} %collective-permute-done.12.refs_2_), channel_id=1, source_target_pairs={{0,4},{4,0},{8,12},{12,8},{16,20},{20,16},{24,28},{28,24},{32,36},... | collective-permute-start | bytes 1105928 | tf_op jit(solution)/shard_map/ppermute | solution.py:67
  61.7 19.6 %copy-start = (s32[4]{0:T(128)S(1)}, s32[4]{0:T(128)}, u32[]{:S(2)}) copy-start(s32[4]{0:T(128)} %codes.1) | copy-start | bytes 52
  61.7 9.7 %collective-permute-start.17 = (bf16[5,128,112]{2,1,0:T(8,128)(2,1)S(1)}, bf16[5,128,112]{2,1,0:T(8,128)(2,1)S(1)}, u32[]{:S(2)}, u32[]{:S(2)}) collective-permute-start(bf16[5,128,112]{2,1,0:T(8,128)(2,1)S(1)} %chip.1.a), channel_id=1, source_target_pairs={{0,24},{4,28},{8,0},{12,4},{16,8},{20,12},{24,16},{28,20},{32,56},... | collective-permute-start | bytes 430088 | tf_op jit(solution)/shard_map/ppermute | solution.py:67
  62.8 8.6 %collective-permute-start.16 = (bf16[5,128,112]{2,1,0:T(8,128)(2,1)S(1)}, bf16[5,128,112]{2,1,0:T(8,128)(2,1)S(1)}, u32[]{:S(2)}, u32[]{:S(2)}) collective-permute-start(bf16[5,128,112]{2,1,0:T(8,128)(2,1)S(1)} %chip.1.a), channel_id=1, source_target_pairs={{0,16},{4,20},{8,24},{12,28},{16,0},{20,4},{24,8},{28,12},{32,48},... | collective-permute-start | bytes 430088 | tf_op jit(solution)/shard_map/ppermute | solution.py:67
  64.4 9.8 %collective-permute-start.15 = (bf16[5,128,112]{2,1,0:T(8,128)(2,1)S(1)}, bf16[5,128,112]{2,1,0:T(8,128)(2,1)S(1)}, u32[]{:S(2)}, u32[]{:S(2)}) collective-permute-start(bf16[5,128,112]{2,1,0:T(8,128)(2,1)S(1)} %chip.1.a), channel_id=1, source_target_pairs={{0,8},{4,12},{8,16},{12,20},{16,24},{20,28},{24,0},{28,4},{32,40},... | collective-permute-start | bytes 430088 | tf_op jit(solution)/shard_map/ppermute | solution.py:67
  74.3 13.6 %collective-permute-start.23 = (bf16[5,128,112]{2,1,0:T(8,128)(2,1)S(1)}, bf16[5,128,112]{2,1,0:T(8,128)(2,1)S(1)}, u32[]{:S(2)}, u32[]{:S(2)}) collective-permute-start(bf16[5,128,112]{2,1,0:T(8,128)(2,1)S(1)} %row.1), channel_id=1, source_target_pairs={{0,96},{4,100},{8,104},{12,108},{16,112},{20,116},{24,120},{28,124... | collective-permute-start | bytes 430088 | tf_op jit(solution)/shard_map/ppermute | solution.py:67
  77.3 10.6 %collective-permute-start.22 = (bf16[5,128,112]{2,1,0:T(8,128)(2,1)S(1)}, bf16[5,128,112]{2,1,0:T(8,128)(2,1)S(1)}, u32[]{:S(2)}, u32[]{:S(2)}) collective-permute-start(bf16[5,128,112]{2,1,0:T(8,128)(2,1)S(1)} %row.1), channel_id=1, source_target_pairs={{0,64},{4,68},{8,72},{12,76},{16,80},{20,84},{24,88},{28,92},{32,9... | collective-permute-start | bytes 430088 | tf_op jit(solution)/shard_map/ppermute | solution.py:67
  78.7 9.2 %collective-permute-start.21 = (bf16[5,128,112]{2,1,0:T(8,128)(2,1)S(1)}, bf16[5,128,112]{2,1,0:T(8,128)(2,1)S(1)}, u32[]{:S(2)}, u32[]{:S(2)}) collective-permute-start(bf16[5,128,112]{2,1,0:T(8,128)(2,1)S(1)} %row.1), channel_id=1, source_target_pairs={{0,32},{4,36},{8,40},{12,44},{16,48},{20,52},{24,56},{28,60},{32,6... | collective-permute-start | bytes 430088 | tf_op jit(solution)/shard_map/ppermute | solution.py:67
  81.4 6.5 %copy-start.1 = (f32[5]{0:T(128)S(1)}, f32[5]{0:T(128)}, u32[]{:S(2)}) copy-start(f32[5]{0:T(128)} %scale.1) | copy-start | bytes 64
  90.5 5.5 %collective-permute-start.26 = (f32[1,2048]{1,0:T(1,128)S(1)}, f32[1,2048]{1,0:T(1,128)S(1)}, u32[]{:S(2)}, u32[]{:S(2)}) collective-permute-start(f32[1,2048]{1,0:T(1,128)S(1)} %get-tuple-element.73.s0), channel_id=1, source_target_pairs={{0,3},{1,0},{2,1},{3,2},{4,7},{5,4},{6,5},{7,6},{8,11},{9,8},{10,9... | collective-permute-start | bytes 24584 | tf_op jit(solution)/shard_map/ppermute | solution.py:477
  94.6 5.2 %collective-permute-start.25 = (f32[1,2048]{1,0:T(1,128)S(1)}, f32[1,2048]{1,0:T(1,128)S(1)}, u32[]{:S(2)}, u32[]{:S(2)}) collective-permute-start(f32[1,2048]{1,0:T(1,128)S(1)} %get-tuple-element.73.s0), channel_id=1, source_target_pairs={{0,2},{1,3},{2,0},{3,1},{4,6},{5,7},{6,4},{7,5},{8,10},{9,11},{10,... | collective-permute-start | bytes 24584 | tf_op jit(solution)/shard_map/ppermute | solution.py:477
  94.6 5.2 %collective-permute-start.24 = (f32[1,2048]{1,0:T(1,128)S(1)}, f32[1,2048]{1,0:T(1,128)S(1)}, u32[]{:S(2)}, u32[]{:S(2)}) collective-permute-start(f32[1,2048]{1,0:T(1,128)S(1)} %get-tuple-element.73.s0), channel_id=1, source_target_pairs={{0,1},{1,2},{2,3},{3,0},{4,5},{5,6},{6,7},{7,4},{8,9},{9,10},{10,1... | collective-permute-start | bytes 24584 | tf_op jit(solution)/shard_map/ppermute | solution.py:477

commit v8 on v7

--- a/solution.py
+++ b/solution.py
@@ -22,8 +22,6 @@
 F32 = jnp.float32
 MIB = 1 << 20
 QUICK = pl.CostEstimate(flops=1, bytes_accessed=1, transcendentals=0)
-
-LONG = pl.CostEstimate(flops=11500000000, bytes_accessed=1, transcendentals=0)
 
 
 def place(y, x, c):
@@ -443,7 +441,7 @@
         (own_kv[1], own_kv[3], kv_sum, *first_q)
     )
     sib_kv[1], sib_kv[3] = shift(own_kv[1], SIBLING), shift(own_kv[3], SIBLING)
-    q_sum = part_call(both, pos, first_q, xp, half, name="part_q", cost=LONG)
+    q_sum = part_call(both, pos, first_q, xp, half, name="part_q")
     kv_sum, q_sum = lax.optimization_barrier((kv_sum, q_sum))
     kv_sum = part_call(
         beside,

time: 102 us -> 96.8 us (0.949)
  waiting for transfers between devices: 21.4 us -> 17.3 us
  starting transfers between devices: 30.2 us -> 29 us
    ppermute x24, waiting for transfers between devices: 17.5 us -> 13.4 us  [shift(): return lax.ppermute(a, 'tm', moves)]
    ppermute x24, starting transfers between devices: 24.9 us -> 23.6 us  [shift(): return lax.ppermute(a, 'tm', moves)]
  transfers between devices with their start and end apart: 27 -> 27, of which waited for: 6 -> 8; matrix products, arithmetic and copies ran while one was open for 1% -> 1% of each run, Pallas kernels for 42% -> 45%
where the time goes in v8:
time: 96.8 us; the launch traced here: 96.5 us
  Pallas kernels  48.9 us (51%)
  starting transfers between devices  29 us (30%)
  waiting for transfers between devices  17.3 us (18%)
    pallas_call x10, Pallas kernels, resident(): pl.pallas_call(kernel, in_specs=[pl.BlockSpec(memory_space=pltpu.SMEM)] *...  40.2 us
    ppermute x24, starting transfers between devices, shift(): return lax.ppermute(a, 'tm', moves)  23.6 us
    ppermute x24, waiting for transfers between devices, shift(): return lax.ppermute(a, 'tm', moves)  13.4 us
    pallas_call x1, Pallas kernels, spread(): pl.pallas_call(spread_kernel, grid=(n // blk,), in_specs=[pl.BlockSpec((D...  6.91 us
    ppermute x3, starting transfers between devices, body(): lax.ppermute(squares, 'head', [(i, (i + d) % 4) for i in range(4)])  5.37 us
    ppermute x3, waiting for transfers between devices, body(): lax.ppermute(squares, 'head', [(i, (i + d) % 4) for i in range(4)])  3.9 us
  transfers between devices with their start and end apart: 27, of which 8 were waited for; matrix products, arithmetic and copies ran while one was open for 1% of the time, Pallas kernels for 45%

profile of v8, /device:TPU:0, one launch (start us, length us, event | category | flops | bytes accessed | tf_op | source)
XLA Modules:
  0.0 96.5 jit_solution(791162900882444554)
XLA Ops:
  0.0 1.6 %collective-permute-start = (bf16[70,1680]{1,0:T(8,128)(2,1)}, bf16[70,1680]{1,0:T(8,128)(2,1)S(1)}, u32[]{:S(2)}, u32[]{:S(2)}) collective-permute-start(bf16[70,1680]{1,0:T(8,128)(2,1)} %w_ref.1), channel_id=1, source_target_pairs={{0,8},{4,36},{8,16},{12,44},{16,24},{20,52},{24,0},{28,60},{32,40}... | collective-permute-start | bytes 705608 | tf_op jit(solution)/shard_map/ppermute | solution.py:65
  1.6 1.7 %collective-permute-start.2 = (bf16[70,1680]{1,0:T(8,128)(2,1)}, bf16[70,1680]{1,0:T(8,128)(2,1)S(1)}, u32[]{:S(2)}, u32[]{:S(2)}) collective-permute-start(bf16[70,1680]{1,0:T(8,128)(2,1)} %w_ref.1), channel_id=1, source_target_pairs={{0,24},{4,100},{8,0},{12,108},{16,8},{20,116},{24,16},{28,124},{32... | collective-permute-start | bytes 705608 | tf_op jit(solution)/shard_map/ppermute | solution.py:65
  3.2 1.9 %collective-permute-start.1 = (bf16[70,1680]{1,0:T(8,128)(2,1)}, bf16[70,1680]{1,0:T(8,128)(2,1)S(1)}, u32[]{:S(2)}, u32[]{:S(2)}) collective-permute-start(bf16[70,1680]{1,0:T(8,128)(2,1)} %w_ref.1), channel_id=1, source_target_pairs={{0,16},{4,68},{8,24},{12,76},{16,0},{20,84},{24,8},{28,92},{32,48}... | collective-permute-start | bytes 705608 | tf_op jit(solution)/shard_map/ppermute | solution.py:65
  5.1 0.8 reshape.3.gain_ref
  6.0 6.9 %spread.1 = (bf16[8,288,2048]{2,1,0:T(8,128)(2,1)S(1)}, bf16[70,1680]{1,0:T(8,128)(2,1)S(1)}) custom-call(bf16[2240,2048]{1,0:T(8,128)(2,1)} %bitcast.5, bf16[70,1680]{1,0:T(8,128)(2,1)} %w_ref.1), custom_call_target="tpu_custom_call" | custom-call | flops 1 | bytes 1 | tf_op jit(solution)/shard_map/spread/pallas_call | solution.py:115
  12.9 1.4 %pack.1 = (bf16[288,1152]{1,0:T(8,128)(2,1)S(1)}, bf16[288,640]{1,0:T(8,128)(2,1)S(1)}) custom-call(s32[3]{0:T(128)S(1)} %pad_add_fusion.pos, bf16[70,1680]{1,0:T(8,128)(2,1)S(1)} %get-tuple-element.42.a0, bf16[70,1680]{1,0:T(8,128)(2,1)S(1)} %collective-permute-done.a1, bf16[70,1680]{1,0:T(8,128)(2,1)S(1)} %collective-permute-done.1.a2, ...), custom_call_target="tpu_custom_call" | custom-call | flops 1 | bytes 1 | tf_op jit(solution)/shard_map/pack/pallas_call | solution.py:164
  14.5 3.1 %collective-permute-start.4 = (bf16[288,1152]{1,0:T(8,128)(2,1)S(1)}, bf16[288,1152]{1,0:T(8,128)(2,1)S(1)}, u32[]{:S(2)}, u32[]{:S(2)}) collective-permute-start(bf16[288,1152]{1,0:T(8,128)(2,1)S(1)} %get-tuple-element.43.refs_0_), channel_id=1, source_target_pairs={{0,96},{4,28},{8,104},{12,4},{16,112},{20,12},{24,120},{28,20},{32... | collective-permute-start | bytes 1990664 | tf_op jit(solution)/shard_map/ppermute | solution.py:65
  17.6 5.0 %part_kv.1.refs_5_ = f32[1120,2048]{1,0:T(8,128)S(1)} custom-call(s32[3]{0:T(128)S(1)} %pad_add_fusion.pos, bf16[288,1152]{1,0:T(8,128)(2,1)S(1)} %get-tuple-element.43.refs_0_, bf16[288,1152]{1,0:T(8,128)(2,1)S(1)} %collective-permute-done.5.refs_1_, bf16[8,288,2048]{2,1,0:T(8,128)(2,1)S(1)} %get-tuple-element.44.refs_2_.refs_4_.refs_6_), custom_call_target="tpu_custom_call" | custom-call | flops 1 | bytes 1 | tf_op jit(solution)/shard_map/part_kv/pallas_call | solution.py:164
  22.6 3.1 %collective-permute-done.4.refs_2_ = bf16[288,1152]{1,0:T(8,128)(2,1)S(1)} collective-permute-done((bf16[288,1152]{1,0:T(8,128)(2,1)S(1)}, bf16[288,1152]{1,0:T(8,128)(2,1)S(1)}, u32[]{:S(2)}, u32[]{:S(2)}) %collective-permute-start.4) | collective-permute-done | bytes 663584 | tf_op jit(solution)/shard_map/ppermute | solution.py:65
  25.7 3.7 %collective-permute-done.3.refs_0_ = bf16[288,1152]{1,0:T(8,128)(2,1)S(1)} collective-permute-done((bf16[288,1152]{1,0:T(8,128)(2,1)S(1)}, bf16[288,1152]{1,0:T(8,128)(2,1)S(1)}, u32[]{:S(2)}, u32[]{:S(2)}) %collective-permute-start.3) | collective-permute-done | bytes 663584 | tf_op jit(solution)/shard_map/ppermute | solution.py:65
  29.4 0.5 collective-permute-start.9
  30.0 3.2 %part_q.1.refs_7_ = f32[560,2048]{1,0:T(8,128)S(1)} custom-call(s32[3]{0:T(128)S(1)} %pad_add_fusion.pos, bf16[288,640]{1,0:T(8,128)(2,1)S(1)} %get-tuple-element.52.refs_0_, bf16[288,640]{1,0:T(8,128)(2,1)S(1)} %collective-permute-done.6.refs_1_, bf16[8,288,2048]{2,1,0:T(8,128)(2,1)S(1)} %get-tuple-element.44.refs_2_.refs_4_.refs_6_), custom_call_target="tpu_custom_call" | custom-call | flops 1 | bytes 1 | tf_op jit(solution)/shard_map/part_q/pallas_call | solution.py:164
  33.2 7.5 %part_more.1.refs_3_ = f32[1120,2048]{1,0:T(8,128)S(1)} custom-call(s32[3]{0:T(128)S(1)} %pad_add_fusion.pos, bf16[288,1152]{1,0:T(8,128)(2,1)S(1)} %collective-permute-done.3.refs_0_, bf16[288,1152]{1,0:T(8,128)(2,1)S(1)} %collective-permute-done.8.refs_1_, bf16[288,1152]{1,0:T(8,128)(2,1)S(1)} %collective-permute-done.4.refs_2_, ...), custom_call_target="tpu_custom_call", output_to_operand_aliasing={{}: (6, {})} | custom-call | flops 1 | bytes 1 | tf_op jit(solution)/shard_map/part_more/pallas_call | solution.py:164
  40.7 1.4 %collective-permute-done.7.refs_0_ = bf16[288,1152]{1,0:T(8,128)(2,1)S(1)} collective-permute-done((bf16[288,1152]{1,0:T(8,128)(2,1)S(1)}, bf16[288,1152]{1,0:T(8,128)(2,1)S(1)}, u32[]{:S(2)}, u32[]{:S(2)}) %collective-permute-start.7) | collective-permute-done | bytes 663584 | tf_op jit(solution)/shard_map/ppermute | solution.py:65
  42.3 2.2 %collective-permute-start.11 = (bf16[288,640]{1,0:T(8,128)(2,1)S(1)}, bf16[288,640]{1,0:T(8,128)(2,1)S(1)}, u32[]{:S(2)}, u32[]{:S(2)}) collective-permute-start(bf16[288,640]{1,0:T(8,128)(2,1)S(1)} %get-tuple-element.52.refs_0_), channel_id=1, source_target_pairs={{0,64},{4,20},{8,72},{12,28},{16,80},{20,4},{24,88},{28,12},{32,96... | collective-permute-start | bytes 1105928 | tf_op jit(solution)/shard_map/ppermute | solution.py:65
  44.5 1.3 %collective-permute-start.10 = (bf16[288,640]{1,0:T(8,128)(2,1)S(1)}, bf16[288,640]{1,0:T(8,128)(2,1)S(1)}, u32[]{:S(2)}, u32[]{:S(2)}) collective-permute-start(bf16[288,640]{1,0:T(8,128)(2,1)S(1)} %get-tuple-element.52.refs_0_), channel_id=1, source_target_pairs={{0,32},{4,12},{8,40},{12,20},{16,48},{20,28},{24,56},{28,4},{32,64... | collective-permute-start | bytes 1105928 | tf_op jit(solution)/shard_map/ppermute | solution.py:65
  45.8 7.2 %keys_values.1 = (bf16[5,2048,112]{2,1,0:T(8,128)(2,1)S(1)}, bf16[5,128,2048]{2,1,0:T(8,128)(2,1)S(1)}, f32[4,5,128,112]{3,2,1,0:T(8,128)S(1)}, bf16[5,128,112]{2,1,0:T(8,128)(2,1)S(1)}) custom-call(s32[3]{0:T(128)S(1)} %pad_add_fusion.pos, bf16[288,1152]{1,0:T(8,128)(2,1)S(1)} %collective-permute-done.7.refs_0_, ...), custom_call_target="tpu_custom_call" | custom-call | flops 1 | bytes 1 | tf_op jit(solution)/shard_map/keys_values/pallas_call | solution.py:164
  53.2 2.1 %collective-permute-done.10.refs_0_ = bf16[288,640]{1,0:T(8,128)(2,1)S(1)} collective-permute-done((bf16[288,640]{1,0:T(8,128)(2,1)S(1)}, bf16[288,640]{1,0:T(8,128)(2,1)S(1)}, u32[]{:S(2)}, u32[]{:S(2)}) %collective-permute-start.10) | collective-permute-done | bytes 368672 | tf_op jit(solution)/shard_map/ppermute | solution.py:65
  56.0 1.4 %collective-permute-start.17 = (bf16[5,128,112]{2,1,0:T(8,128)(2,1)S(1)}, bf16[5,128,112]{2,1,0:T(8,128)(2,1)S(1)}, u32[]{:S(2)}, u32[]{:S(2)}) collective-permute-start(bf16[5,128,112]{2,1,0:T(8,128)(2,1)S(1)} %chip.1.a), channel_id=1, source_target_pairs={{0,24},{4,28},{8,0},{12,4},{16,8},{20,12},{24,16},{28,20},{32,56},... | collective-permute-start | bytes 430088 | tf_op jit(solution)/shard_map/ppermute | solution.py:65
  57.4 1.2 %collective-permute-start.16 = (bf16[5,128,112]{2,1,0:T(8,128)(2,1)S(1)}, bf16[5,128,112]{2,1,0:T(8,128)(2,1)S(1)}, u32[]{:S(2)}, u32[]{:S(2)}) collective-permute-start(bf16[5,128,112]{2,1,0:T(8,128)(2,1)S(1)} %chip.1.a), channel_id=1, source_target_pairs={{0,16},{4,20},{8,24},{12,28},{16,0},{20,4},{24,8},{28,12},{32,48},... | collective-permute-start | bytes 430088 | tf_op jit(solution)/shard_map/ppermute | solution.py:65
  58.6 0.6 collective-permute-start.15
  59.2 6.5 %queries.1.fq_ref.refs_8_ = bf16[560,2048]{1,0:T(8,128)(2,1)S(1)} custom-call(s32[3]{0:T(128)S(1)} %pad_add_fusion.pos, bf16[288,640]{1,0:T(8,128)(2,1)S(1)} %collective-permute-done.10.refs_0_, bf16[288,640]{1,0:T(8,128)(2,1)S(1)} %collective-permute-done.11.refs_1_, bf16[288,640]{1,0:T(8,128)(2,1)S(1)} %collective-permute-done.12.refs_2_, ...), custom_call_target="tpu_custom_call" | custom-call | flops 1 | bytes 1 | tf_op jit(solution)/shard_map/queries/pallas_call | solution.py:164
  66.0 2.8 %collective-permute-done.15.b.refs_1_ = bf16[5,128,112]{2,1,0:T(8,128)(2,1)S(1)} collective-permute-done((bf16[5,128,112]{2,1,0:T(8,128)(2,1)S(1)}, bf16[5,128,112]{2,1,0:T(8,128)(2,1)S(1)}, u32[]{:S(2)}, u32[]{:S(2)}) %collective-permute-start.15) | collective-permute-done | bytes 143392 | tf_op jit(solution)/shard_map/ppermute | solution.py:65
  68.8 3.1 %collective-permute-start.23 = (bf16[5,128,112]{2,1,0:T(8,128)(2,1)S(1)}, bf16[5,128,112]{2,1,0:T(8,128)(2,1)S(1)}, u32[]{:S(2)}, u32[]{:S(2)}) collective-permute-start(bf16[5,128,112]{2,1,0:T(8,128)(2,1)S(1)} %row.1), channel_id=1, source_target_pairs={{0,96},{4,100},{8,104},{12,108},{16,112},{20,116},{24,120},{28,124... | collective-permute-start | bytes 430088 | tf_op jit(solution)/shard_map/ppermute | solution.py:65
  71.9 1.4 %collective-permute-start.22 = (bf16[5,128,112]{2,1,0:T(8,128)(2,1)S(1)}, bf16[5,128,112]{2,1,0:T(8,128)(2,1)S(1)}, u32[]{:S(2)}, u32[]{:S(2)}) collective-permute-start(bf16[5,128,112]{2,1,0:T(8,128)(2,1)S(1)} %row.1), channel_id=1, source_target_pairs={{0,64},{4,68},{8,72},{12,76},{16,80},{20,84},{24,88},{28,92},{32,9... | collective-permute-start | bytes 430088 | tf_op jit(solution)/shard_map/ppermute | solution.py:65
  73.4 2.7 %collective-permute-start.21 = (bf16[5,128,112]{2,1,0:T(8,128)(2,1)S(1)}, bf16[5,128,112]{2,1,0:T(8,128)(2,1)S(1)}, u32[]{:S(2)}, u32[]{:S(2)}) collective-permute-start(bf16[5,128,112]{2,1,0:T(8,128)(2,1)S(1)} %row.1), channel_id=1, source_target_pairs={{0,32},{4,36},{8,40},{12,44},{16,48},{20,52},{24,56},{28,60},{32,6... | collective-permute-start | bytes 430088 | tf_op jit(solution)/shard_map/ppermute | solution.py:65
  76.0 6.5 %attend.1.refs_9_ = f32[5,128,2048]{2,1,0:T(8,128)S(1)} custom-call(s32[4]{0:T(128)S(1)} %copy-done, bf16[5,2048,112]{2,1,0:T(8,128)(2,1)S(1)} %get-tuple-element.70.fk_ref, bf16[5,128,2048]{2,1,0:T(8,128)(2,1)S(1)} %get-tuple-element.71.v_ref, bf16[560,2048]{1,0:T(8,128)(2,1)S(1)} %queries.1.fq_ref.refs_8_), custom_call_target="tpu_custom_call" | custom-call | flops 1 | bytes 1 | tf_op jit(solution)/shard_map/attend/pallas_call | solution.py:164
  82.6 2.6 %join.1 = (f32[560,2048]{1,0:T(8,128)S(1)}, f32[1,2048]{1,0:T(1,128)S(1)}) custom-call(s32[3]{0:T(128)S(1)} %pad_add_fusion.pos, f32[5]{0:T(128)S(1)} %copy-done.1, bf16[5,128,112]{2,1,0:T(8,128)(2,1)S(1)} %collective-permute-done.14.other_ref.refs_0_, bf16[5,128,112]{2,1,0:T(8,128)(2,1)S(1)} %collective-permute-done.15.b.refs_1_, ...), custom_call_target="tpu_custom_call" | custom-call | flops 1 | bytes 1 | tf_op jit(solution)/shard_map/join/pallas_call | solution.py:164
  85.2 4.1 %collective-permute-start.26 = (f32[1,2048]{1,0:T(1,128)S(1)}, f32[1,2048]{1,0:T(1,128)S(1)}, u32[]{:S(2)}, u32[]{:S(2)}) collective-permute-start(f32[1,2048]{1,0:T(1,128)S(1)} %get-tuple-element.73.s0), channel_id=1, source_target_pairs={{0,3},{1,0},{2,1},{3,2},{4,7},{5,4},{6,5},{7,6},{8,11},{9,8},{10,9... | collective-permute-start | bytes 24584 | tf_op jit(solution)/shard_map/ppermute | solution.py:475
  89.3 1.3 %collective-permute-start.24 = (f32[1,2048]{1,0:T(1,128)S(1)}, f32[1,2048]{1,0:T(1,128)S(1)}, u32[]{:S(2)}, u32[]{:S(2)}) collective-permute-start(f32[1,2048]{1,0:T(1,128)S(1)} %get-tuple-element.73.s0), channel_id=1, source_target_pairs={{0,1},{1,2},{2,3},{3,0},{4,5},{5,6},{6,7},{7,4},{8,9},{9,10},{10,1... | collective-permute-start | bytes 24584 | tf_op jit(solution)/shard_map/ppermute | solution.py:475
  90.7 3.8 %collective-permute-done.25.s2 = f32[1,2048]{1,0:T(1,128)S(1)} collective-permute-done((f32[1,2048]{1,0:T(1,128)S(1)}, f32[1,2048]{1,0:T(1,128)S(1)}, u32[]{:S(2)}, u32[]{:S(2)}) %collective-permute-start.25) | collective-permute-done | bytes 8224 | tf_op jit(solution)/shard_map/ppermute | solution.py:475
  94.5 1.9 %norm.1 = bf16[560,2048]{1,0:T(8,128)(2,1)} custom-call(f32[560,2048]{1,0:T(8,128)S(1)} %get-tuple-element.72.out_ref, f32[1,2048]{1,0:T(1,128)S(1)} %get-tuple-element.73.s0, f32[1,2048]{1,0:T(1,128)S(1)} %collective-permute-done.24.s1, f32[1,2048]{1,0:T(1,128)S(1)} %collective-permute-done.25.s2, f32[1,2048]{1,0:T(1,128)S(1)} %collective-permute-done.26.s3, ...), custom_call_target="tpu_custom_call" | custom-call | flops 1 | bytes 1 | tf_op jit(solution)/shard_map/norm/pallas_call | solution.py:407
  (40 shorter events, 1.6 us)
Async XLA Ops:
  0.0 12.9 %collective-permute-start = (bf16[70,1680]{1,0:T(8,128)(2,1)}, bf16[70,1680]{1,0:T(8,128)(2,1)S(1)}, u32[]{:S(2)}, u32[]{:S(2)}) collective-permute-start(bf16[70,1680]{1,0:T(8,128)(2,1)} %w_ref.1), channel_id=1, source_target_pairs={{0,8},{4,36},{8,16},{12,44},{16,24},{20,52},{24,0},{28,60},{32,40}... | collective-permute-start | bytes 705608 | tf_op jit(solution)/shard_map/ppermute | solution.py:65
  1.6 11.3 %collective-permute-start.2 = (bf16[70,1680]{1,0:T(8,128)(2,1)}, bf16[70,1680]{1,0:T(8,128)(2,1)S(1)}, u32[]{:S(2)}, u32[]{:S(2)}) collective-permute-start(bf16[70,1680]{1,0:T(8,128)(2,1)} %w_ref.1), channel_id=1, source_target_pairs={{0,24},{4,100},{8,0},{12,108},{16,8},{20,116},{24,16},{28,124},{32... | collective-permute-start | bytes 705608 | tf_op jit(solution)/shard_map/ppermute | solution.py:65
  3.2 9.7 %collective-permute-start.1 = (bf16[70,1680]{1,0:T(8,128)(2,1)}, bf16[70,1680]{1,0:T(8,128)(2,1)S(1)}, u32[]{:S(2)}, u32[]{:S(2)}) collective-permute-start(bf16[70,1680]{1,0:T(8,128)(2,1)} %w_ref.1), channel_id=1, source_target_pairs={{0,16},{4,68},{8,24},{12,76},{16,0},{20,84},{24,8},{28,92},{32,48}... | collective-permute-start | bytes 705608 | tf_op jit(solution)/shard_map/ppermute | solution.py:65
  14.4 3.2 %collective-permute-start.5 = (bf16[288,1152]{1,0:T(8,128)(2,1)S(1)}, bf16[288,1152]{1,0:T(8,128)(2,1)S(1)}, u32[]{:S(2)}, u32[]{:S(2)}) collective-permute-start(bf16[288,1152]{1,0:T(8,128)(2,1)S(1)} %get-tuple-element.43.refs_0_), channel_id=1, source_target_pairs={{0,4},{4,0},{8,12},{12,8},{16,20},{20,16},{24,28},{28,24},{32,36},... | collective-permute-start | bytes 1990664 | tf_op jit(solution)/shard_map/ppermute | solution.py:65
  14.5 11.3 %collective-permute-start.4 = (bf16[288,1152]{1,0:T(8,128)(2,1)S(1)}, bf16[288,1152]{1,0:T(8,128)(2,1)S(1)}, u32[]{:S(2)}, u32[]{:S(2)}) collective-permute-start(bf16[288,1152]{1,0:T(8,128)(2,1)S(1)} %get-tuple-element.43.refs_0_), channel_id=1, source_target_pairs={{0,96},{4,28},{8,104},{12,4},{16,112},{20,12},{24,120},{28,20},{32... | collective-permute-start | bytes 1990664 | tf_op jit(solution)/shard_map/ppermute | solution.py:65
  17.6 11.9 %collective-permute-start.3 = (bf16[288,1152]{1,0:T(8,128)(2,1)S(1)}, bf16[288,1152]{1,0:T(8,128)(2,1)S(1)}, u32[]{:S(2)}, u32[]{:S(2)}) collective-permute-start(bf16[288,1152]{1,0:T(8,128)(2,1)S(1)} %get-tuple-element.43.refs_0_), channel_id=1, source_target_pairs={{0,32},{4,12},{8,40},{12,20},{16,48},{20,28},{24,56},{28,4},{32,64... | collective-permute-start | bytes 1990664 | tf_op jit(solution)/shard_map/ppermute | solution.py:65
  17.6 5.0 %collective-permute-start.6 = (bf16[288,640]{1,0:T(8,128)(2,1)S(1)}, bf16[288,640]{1,0:T(8,128)(2,1)S(1)}, u32[]{:S(2)}, u32[]{:S(2)}) collective-permute-start(bf16[288,640]{1,0:T(8,128)(2,1)S(1)} %get-tuple-element.52.refs_0_), channel_id=1, source_target_pairs={{0,4},{4,0},{8,12},{12,8},{16,20},{20,16},{24,28},{28,24},{32,36},... | collective-permute-start | bytes 1105928 | tf_op jit(solution)/shard_map/ppermute | solution.py:65
  29.4 3.7 %collective-permute-start.8 = (bf16[288,1152]{1,0:T(8,128)(2,1)S(1)}, bf16[288,1152]{1,0:T(8,128)(2,1)S(1)}, u32[]{:S(2)}, u32[]{:S(2)}) collective-permute-start(bf16[288,1152]{1,0:T(8,128)(2,1)S(1)} %collective-permute-done.3.refs_0_), channel_id=1, source_target_pairs={{0,4},{4,0},{8,12},{12,8},{16,20},{20,16},{24,28},{28,24},{32,36},... | collective-permute-start | bytes 1990664 | tf_op jit(solution)/shard_map/ppermute | solution.py:65
  29.4 3.7 %collective-permute-start.9 = (bf16[288,1152]{1,0:T(8,128)(2,1)S(1)}, bf16[288,1152]{1,0:T(8,128)(2,1)S(1)}, u32[]{:S(2)}, u32[]{:S(2)}) collective-permute-start(bf16[288,1152]{1,0:T(8,128)(2,1)S(1)} %collective-permute-done.4.refs_2_), channel_id=1, source_target_pairs={{0,4},{4,0},{8,12},{12,8},{16,20},{20,16},{24,28},{28,24},{32,36},... | collective-permute-start | bytes 1990664 | tf_op jit(solution)/shard_map/ppermute | solution.py:65
  30.0 12.2 %collective-permute-start.7 = (bf16[288,1152]{1,0:T(8,128)(2,1)S(1)}, bf16[288,1152]{1,0:T(8,128)(2,1)S(1)}, u32[]{:S(2)}, u32[]{:S(2)}) collective-permute-start(bf16[288,1152]{1,0:T(8,128)(2,1)S(1)} %get-tuple-element.43.refs_0_), channel_id=1, source_target_pairs={{0,64},{4,20},{8,72},{12,28},{16,80},{20,4},{24,88},{28,12},{32,96... | collective-permute-start | bytes 1990664 | tf_op jit(solution)/shard_map/ppermute | solution.py:65
  42.1 3.7 %collective-permute-start.13 = (bf16[288,1152]{1,0:T(8,128)(2,1)S(1)}, bf16[288,1152]{1,0:T(8,128)(2,1)S(1)}, u32[]{:S(2)}, u32[]{:S(2)}) collective-permute-start(bf16[288,1152]{1,0:T(8,128)(2,1)S(1)} %collective-permute-done.7.refs_0_), channel_id=1, source_target_pairs={{0,4},{4,0},{8,12},{12,8},{16,20},{20,16},{24,28},{28,24},{32,36},... | collective-permute-start | bytes 1990664 | tf_op jit(solution)/shard_map/ppermute | solution.py:65
  42.2 11.0 %collective-permute-start.12 = (bf16[288,640]{1,0:T(8,128)(2,1)S(1)}, bf16[288,640]{1,0:T(8,128)(2,1)S(1)}, u32[]{:S(2)}, u32[]{:S(2)}) collective-permute-start(bf16[288,640]{1,0:T(8,128)(2,1)S(1)} %get-tuple-element.52.refs_0_), channel_id=1, source_target_pairs={{0,96},{4,28},{8,104},{12,4},{16,112},{20,12},{24,120},{28,20},{32... | collective-permute-start | bytes 1105928 | tf_op jit(solution)/shard_map/ppermute | solution.py:65
  42.3 10.9 %collective-permute-start.11 = (bf16[288,640]{1,0:T(8,128)(2,1)S(1)}, bf16[288,640]{1,0:T(8,128)(2,1)S(1)}, u32[]{:S(2)}, u32[]{:S(2)}) collective-permute-start(bf16[288,640]{1,0:T(8,128)(2,1)S(1)} %get-tuple-element.52.refs_0_), channel_id=1, source_target_pairs={{0,64},{4,20},{8,72},{12,28},{16,80},{20,4},{24,88},{28,12},{32,96... | collective-permute-start | bytes 1105928 | tf_op jit(solution)/shard_map/ppermute | solution.py:65
  44.5 10.8 %collective-permute-start.10 = (bf16[288,640]{1,0:T(8,128)(2,1)S(1)}, bf16[288,640]{1,0:T(8,128)(2,1)S(1)}, u32[]{:S(2)}, u32[]{:S(2)}) collective-permute-start(bf16[288,640]{1,0:T(8,128)(2,1)S(1)} %get-tuple-element.52.refs_0_), channel_id=1, source_target_pairs={{0,32},{4,12},{8,40},{12,20},{16,48},{20,28},{24,56},{28,4},{32,64... | collective-permute-start | bytes 1105928 | tf_op jit(solution)/shard_map/ppermute | solution.py:65
  53.1 2.2 %collective-permute-start.14 = (bf16[5,128,112]{2,1,0:T(8,128)(2,1)S(1)}, bf16[5,128,112]{2,1,0:T(8,128)(2,1)S(1)}, u32[]{:S(2)}, u32[]{:S(2)}) collective-permute-start(bf16[5,128,112]{2,1,0:T(8,128)(2,1)S(1)} %get-tuple-element.55.tot_ref), channel_id=1, source_target_pairs={{0,4},{4,0},{8,12},{12,8},{16,20},{20,16},{24,28},{28,24},{32,36},... | collective-permute-start | bytes 430088 | tf_op jit(solution)/shard_map/ppermute | solution.py:65
  55.3 3.3 %collective-permute-start.18 = (bf16[288,640]{1,0:T(8,128)(2,1)S(1)}, bf16[288,640]{1,0:T(8,128)(2,1)S(1)}, u32[]{:S(2)}, u32[]{:S(2)}) collective-permute-start(bf16[288,640]{1,0:T(8,128)(2,1)S(1)} %collective-permute-done.10.refs_0_), channel_id=1, source_target_pairs={{0,4},{4,0},{8,12},{12,8},{16,20},{20,16},{24,28},{28,24},{32,36},... | collective-permute-start | bytes 1105928 | tf_op jit(solution)/shard_map/ppermute | solution.py:65
  55.4 3.8 %collective-permute-start.19 = (bf16[288,640]{1,0:T(8,128)(2,1)S(1)}, bf16[288,640]{1,0:T(8,128)(2,1)S(1)}, u32[]{:S(2)}, u32[]{:S(2)}) collective-permute-start(bf16[288,640]{1,0:T(8,128)(2,1)S(1)} %collective-permute-done.11.refs_1_), channel_id=1, source_target_pairs={{0,4},{4,0},{8,12},{12,8},{16,20},{20,16},{24,28},{28,24},{32,36},... | collective-permute-start | bytes 1105928 | tf_op jit(solution)/shard_map/ppermute | solution.py:65
  55.8 3.4 %collective-permute-start.20 = (bf16[288,640]{1,0:T(8,128)(2,1)S(1)}, bf16[288,640]{1,0:T(8,128)(2,1)S(1)}, u32[]{:S(2)}, u32[]{:S(2)}) collective-permute-start(bf16[288,640]{1,0:T(8,128)(2,1)S(1)} %collective-permute-done.12.refs_2_), channel_id=1, source_target_pairs={{0,4},{4,0},{8,12},{12,8},{16,20},{20,16},{24,28},{28,24},{32,36},... | collective-permute-start | bytes 1105928 | tf_op jit(solution)/shard_map/ppermute | solution.py:65
  56.0 20.0 %copy-start = (s32[4]{0:T(128)S(1)}, s32[4]{0:T(128)}, u32[]{:S(2)}) copy-start(s32[4]{0:T(128)} %codes.1) | copy-start | bytes 52
  56.0 9.7 %collective-permute-start.17 = (bf16[5,128,112]{2,1,0:T(8,128)(2,1)S(1)}, bf16[5,128,112]{2,1,0:T(8,128)(2,1)S(1)}, u32[]{:S(2)}, u32[]{:S(2)}) collective-permute-start(bf16[5,128,112]{2,1,0:T(8,128)(2,1)S(1)} %chip.1.a), channel_id=1, source_target_pairs={{0,24},{4,28},{8,0},{12,4},{16,8},{20,12},{24,16},{28,20},{32,56},... | collective-permute-start | bytes 430088 | tf_op jit(solution)/shard_map/ppermute | solution.py:65
  57.4 8.6 %collective-permute-start.16 = (bf16[5,128,112]{2,1,0:T(8,128)(2,1)S(1)}, bf16[5,128,112]{2,1,0:T(8,128)(2,1)S(1)}, u32[]{:S(2)}, u32[]{:S(2)}) collective-permute-start(bf16[5,128,112]{2,1,0:T(8,128)(2,1)S(1)} %chip.1.a), channel_id=1, source_target_pairs={{0,16},{4,20},{8,24},{12,28},{16,0},{20,4},{24,8},{28,12},{32,48},... | collective-permute-start | bytes 430088 | tf_op jit(solution)/shard_map/ppermute | solution.py:65
  58.6 10.1 %collective-permute-start.15 = (bf16[5,128,112]{2,1,0:T(8,128)(2,1)S(1)}, bf16[5,128,112]{2,1,0:T(8,128)(2,1)S(1)}, u32[]{:S(2)}, u32[]{:S(2)}) collective-permute-start(bf16[5,128,112]{2,1,0:T(8,128)(2,1)S(1)} %chip.1.a), channel_id=1, source_target_pairs={{0,8},{4,12},{8,16},{12,20},{16,24},{20,28},{24,0},{28,4},{32,40},... | collective-permute-start | bytes 430088 | tf_op jit(solution)/shard_map/ppermute | solution.py:65
  68.8 13.7 %collective-permute-start.23 = (bf16[5,128,112]{2,1,0:T(8,128)(2,1)S(1)}, bf16[5,128,112]{2,1,0:T(8,128)(2,1)S(1)}, u32[]{:S(2)}, u32[]{:S(2)}) collective-permute-start(bf16[5,128,112]{2,1,0:T(8,128)(2,1)S(1)} %row.1), channel_id=1, source_target_pairs={{0,96},{4,100},{8,104},{12,108},{16,112},{20,116},{24,120},{28,124... | collective-permute-start | bytes 430088 | tf_op jit(solution)/shard_map/ppermute | solution.py:65
  71.9 10.6 %collective-permute-start.22 = (bf16[5,128,112]{2,1,0:T(8,128)(2,1)S(1)}, bf16[5,128,112]{2,1,0:T(8,128)(2,1)S(1)}, u32[]{:S(2)}, u32[]{:S(2)}) collective-permute-start(bf16[5,128,112]{2,1,0:T(8,128)(2,1)S(1)} %row.1), channel_id=1, source_target_pairs={{0,64},{4,68},{8,72},{12,76},{16,80},{20,84},{24,88},{28,92},{32,9... | collective-permute-start | bytes 430088 | tf_op jit(solution)/shard_map/ppermute | solution.py:65
  73.4 9.2 %collective-permute-start.21 = (bf16[5,128,112]{2,1,0:T(8,128)(2,1)S(1)}, bf16[5,128,112]{2,1,0:T(8,128)(2,1)S(1)}, u32[]{:S(2)}, u32[]{:S(2)}) collective-permute-start(bf16[5,128,112]{2,1,0:T(8,128)(2,1)S(1)} %row.1), channel_id=1, source_target_pairs={{0,32},{4,36},{8,40},{12,44},{16,48},{20,52},{24,56},{28,60},{32,6... | collective-permute-start | bytes 430088 | tf_op jit(solution)/shard_map/ppermute | solution.py:65
  76.0 6.5 %copy-start.1 = (f32[5]{0:T(128)S(1)}, f32[5]{0:T(128)}, u32[]{:S(2)}) copy-start(f32[5]{0:T(128)} %scale.1) | copy-start | bytes 64
  85.2 5.5 %collective-permute-start.26 = (f32[1,2048]{1,0:T(1,128)S(1)}, f32[1,2048]{1,0:T(1,128)S(1)}, u32[]{:S(2)}, u32[]{:S(2)}) collective-permute-start(f32[1,2048]{1,0:T(1,128)S(1)} %get-tuple-element.73.s0), channel_id=1, source_target_pairs={{0,3},{1,0},{2,1},{3,2},{4,7},{5,4},{6,5},{7,6},{8,11},{9,8},{10,9... | collective-permute-start | bytes 24584 | tf_op jit(solution)/shard_map/ppermute | solution.py:475
  89.3 5.2 %collective-permute-start.25 = (f32[1,2048]{1,0:T(1,128)S(1)}, f32[1,2048]{1,0:T(1,128)S(1)}, u32[]{:S(2)}, u32[]{:S(2)}) collective-permute-start(f32[1,2048]{1,0:T(1,128)S(1)} %get-tuple-element.73.s0), channel_id=1, source_target_pairs={{0,2},{1,3},{2,0},{3,1},{4,6},{5,7},{6,4},{7,5},{8,10},{9,11},{10,... | collective-permute-start | bytes 24584 | tf_op jit(solution)/shard_map/ppermute | solution.py:475
  89.3 5.2 %collective-permute-start.24 = (f32[1,2048]{1,0:T(1,128)S(1)}, f32[1,2048]{1,0:T(1,128)S(1)}, u32[]{:S(2)}, u32[]{:S(2)}) collective-permute-start(f32[1,2048]{1,0:T(1,128)S(1)} %get-tuple-element.73.s0), channel_id=1, source_target_pairs={{0,1},{1,2},{2,3},{3,0},{4,5},{5,6},{6,7},{7,4},{8,9},{9,10},{10,1... | collective-permute-start | bytes 24584 | tf_op jit(solution)/shard_map/ppermute | solution.py:475

commit v9 on v8

--- a/solution.py
+++ b/solution.py
@@ -138,9 +138,15 @@
     return pltpu.with_memory_space_constraint(a, pltpu.VMEM)
 
 
-def lay(pieces, wbuf):
-    for i, piece in enumerate(pieces):
-        wbuf[i * BLK : (i + 1) * BLK, :] = piece[...]
+def rows_in(steps):
+    return sum(hi - lo for _, _, lo, hi in steps)
+
+
+def lay(steps, pieces, wbuf):
+    at = 0
+    for (_, _, lo, hi), piece in zip(steps, pieces):
+        wbuf[at : at + hi - lo, :] = piece[lo:hi, :]
+        at += hi - lo
 
 
 def block(pos, mine, d):
@@ -149,7 +155,9 @@
 
 
 def rows_of(pos, steps, x_ref, at):
-    return jnp.concatenate([x_ref[block(pos, *step), :, at] for step in steps], axis=0)
+    return jnp.concatenate(
+        [x_ref[block(pos, mine, d), lo:hi, at] for mine, d, lo, hi in steps], axis=0
+    )
 
 
 def each_group(n, step):
@@ -178,7 +186,7 @@
 def part_kernel(steps, pos, *refs):
     count = len(steps)
     pieces, x_ref, sum_ref, wbuf = refs[:count], refs[count], refs[-2], refs[-1]
-    lay(pieces, wbuf)
+    lay(steps, pieces, wbuf)
     rows = sum_ref.shape[0]
 
     def step(g, at):
@@ -195,7 +203,7 @@
         [pos],
         [*pieces, xp, *earlier],
         [((rows, xp.shape[2]), F32)],
-        [pltpu.VMEM((len(steps) * BLK, pieces[0].shape[1]), BF)],
+        [pltpu.VMEM((rows_in(steps), pieces[0].shape[1]), BF)],
         16,
         name,
         {len(pieces) + 2: 0} if earlier else None,
@@ -213,7 +221,7 @@
     count = len(refs) - 8
     pieces = refs[:count]
     x_ref, sum_ref, fk_ref, v_ref, pre_ref, tot_ref, wbuf, run = refs[count:]
-    lay(pieces, wbuf)
+    lay(steps, pieces, wbuf)
     run[...] = jnp.zeros_like(run)
     half = HL * DH
 
@@ -249,7 +257,7 @@
             ((n // GROUP, HL, VA, DH), F32),
             ((HL, VA, DH), BF),
         ],
-        [pltpu.VMEM((len(pieces) * BLK, QCOL), BF), pltpu.VMEM((HL, VA, DH), F32)],
+        [pltpu.VMEM((rows_in(steps), QCOL), BF), pltpu.VMEM((HL, VA, DH), F32)],
         20,
         "keys_values",
     )
@@ -258,7 +266,7 @@
 def q_kernel(steps, pos, *refs):
     count = len(refs) - 4
     pieces, (x_ref, sum_ref, fq_ref, wbuf) = refs[:count], refs[count:]
-    lay(pieces, wbuf)
+    lay(steps, pieces, wbuf)
 
     def step(g, at):
         x = rows_of(pos, steps, x_ref, at)
@@ -273,7 +281,7 @@
         [pos],
         [*pieces, xp, sums],
         [(sums.shape, BF)],
-        [pltpu.VMEM((len(pieces) * BLK, COLS - QCOL), BF)],
+        [pltpu.VMEM((rows_in(steps), COLS - QCOL), BF)],
         12,
         "queries",
     )
@@ -431,31 +439,34 @@
     sib_kv = [shift(near_kv, SIBLING)] + [None] * 3
     first_q = [near_q, shift(near_q, SIBLING)]
 
-    both = ((True, 0), (False, 0))
-    beside = ((True, 1), (False, 1), (True, 3), (False, 3))
-    across = ((True, 2), (False, 2))
-    rest = tuple((mine, d) for mine in (True, False) for d in (1, 2, 3))
+    def whole(mine, d):
+        return (mine, d, 0, BLK)
+
+    cut = 4 * 256 - 3 * BLK
+    both = (whole(True, 0), whole(False, 0))
+    beside = (whole(True, 1), whole(False, 1), whole(True, 3), (False, 3, 0, cut))
+    across = (whole(True, 2), whole(False, 2), (False, 3, cut, BLK))
+    rest = tuple(whole(mine, d) for mine in (True, False) for d in (1, 2, 3))
     half = HL * DH
     kv_sum = part_call(both, pos, [near_kv, sib_kv[0]], xp, 2 * half, name="part_kv")
-    own_kv[1], own_kv[3], kv_sum, *first_q = lax.optimization_barrier(
-        (own_kv[1], own_kv[3], kv_sum, *first_q)
+    q_sum = part_call(both, pos, first_q, xp, half, name="part_q")
+    own_kv[1], own_kv[3], kv_sum, q_sum = lax.optimization_barrier(
+        (own_kv[1], own_kv[3], kv_sum, q_sum)
     )
     sib_kv[1], sib_kv[3] = shift(own_kv[1], SIBLING), shift(own_kv[3], SIBLING)
-    q_sum = part_call(both, pos, first_q, xp, half, name="part_q")
-    kv_sum, q_sum = lax.optimization_barrier((kv_sum, q_sum))
     kv_sum = part_call(
         beside,
         pos,
-        [(own_kv if mine else sib_kv)[d] for mine, d in beside],
+        [(own_kv if mine else sib_kv)[d] for mine, d, _, _ in beside],
         xp,
         2 * half,
         kv_sum,
         name="part_more",
     )
-    near_q, own_kv[2], kv_sum = lax.optimization_barrier((first_q[0], own_kv[2], kv_sum))
+    near_q, own_kv[2], kv_sum = lax.optimization_barrier((near_q, own_kv[2], kv_sum))
     sib_kv[2] = shift(own_kv[2], SIBLING)
     own_q = [shift(near_q, second_leg(d)) for d in (1, 2, 3)]
-    fk, v, pre, tot = kv_call(across, pos, [own_kv[2], sib_kv[2]], xp, kv_sum)
+    fk, v, pre, tot = kv_call(across, pos, [own_kv[2], sib_kv[2], sib_kv[3]], xp, kv_sum)
 
     other = shift(tot, SIBLING)
     *own_q, other = lax.optimization_barrier((*own_q, other))

time: 96.8 us -> 97.1 us (level)
  waiting for transfers between devices: 17.3 us -> 19.5 us
  starting transfers between devices: 29 us -> 27.9 us
    ppermute x24, waiting for transfers between devices: 13.4 us -> 15.6 us  [shift(): return lax.ppermute(a, 'tm', moves)]
    ppermute x24, starting transfers between devices: 23.6 us -> 22.5 us  [shift(): return lax.ppermute(a, 'tm', moves)]
  transfers between devices with their start and end apart: 27 -> 27, of which waited for: 8 -> 11; matrix products, arithmetic and copies ran while one was open for 1% -> 1% of each run, Pallas kernels for 45% -> 44%
where the time goes in v9:
time: 97.1 us; the launch traced here: 96.8 us
  Pallas kernels  48.2 us (50%)
  starting transfers between devices  27.9 us (29%)
  waiting for transfers between devices  19.5 us (20%)
    pallas_call x10, Pallas kernels, resident(): pl.pallas_call(kernel, in_specs=[pl.BlockSpec(memory_space=pltpu.SMEM)] *...  39.5 us
    ppermute x24, starting transfers between devices, shift(): return lax.ppermute(a, 'tm', moves)  22.5 us
    ppermute x24, waiting for transfers between devices, shift(): return lax.ppermute(a, 'tm', moves)  15.6 us
    pallas_call x1, Pallas kernels, spread(): pl.pallas_call(spread_kernel, grid=(n // blk,), in_specs=[pl.BlockSpec((D...  6.91 us
    ppermute x3, starting transfers between devices, body(): lax.ppermute(squares, 'head', [(i, (i + d) % 4) for i in range(4)])  5.38 us
    ppermute x3, waiting for transfers between devices, body(): lax.ppermute(squares, 'head', [(i, (i + d) % 4) for i in range(4)])  3.88 us
  transfers between devices with their start and end apart: 27, of which 11 were waited for; matrix products, arithmetic and copies ran while one was open for 1% of the time, Pallas kernels for 44%

profile of v9, /device:TPU:0, one launch (start us, length us, event | category | flops | bytes accessed | tf_op | source)
XLA Modules:
  0.0 96.8 jit_solution(5336161987256521305)
XLA Ops:
  0.0 1.6 %collective-permute-start = (bf16[70,1680]{1,0:T(8,128)(2,1)}, bf16[70,1680]{1,0:T(8,128)(2,1)S(1)}, u32[]{:S(2)}, u32[]{:S(2)}) collective-permute-start(bf16[70,1680]{1,0:T(8,128)(2,1)} %w_ref.1), channel_id=1, source_target_pairs={{0,8},{4,36},{8,16},{12,44},{16,24},{20,52},{24,0},{28,60},{32,40}... | collective-permute-start | bytes 705608 | tf_op jit(solution)/shard_map/ppermute | solution.py:65
  1.6 1.7 %collective-permute-start.2 = (bf16[70,1680]{1,0:T(8,128)(2,1)}, bf16[70,1680]{1,0:T(8,128)(2,1)S(1)}, u32[]{:S(2)}, u32[]{:S(2)}) collective-permute-start(bf16[70,1680]{1,0:T(8,128)(2,1)} %w_ref.1), channel_id=1, source_target_pairs={{0,24},{4,100},{8,0},{12,108},{16,8},{20,116},{24,16},{28,124},{32... | collective-permute-start | bytes 705608 | tf_op jit(solution)/shard_map/ppermute | solution.py:65
  3.2 1.9 %collective-permute-start.1 = (bf16[70,1680]{1,0:T(8,128)(2,1)}, bf16[70,1680]{1,0:T(8,128)(2,1)S(1)}, u32[]{:S(2)}, u32[]{:S(2)}) collective-permute-start(bf16[70,1680]{1,0:T(8,128)(2,1)} %w_ref.1), channel_id=1, source_target_pairs={{0,16},{4,68},{8,24},{12,76},{16,0},{20,84},{24,8},{28,92},{32,48}... | collective-permute-start | bytes 705608 | tf_op jit(solution)/shard_map/ppermute | solution.py:65
  5.1 0.8 reshape.3.gain_ref
  6.0 6.9 %spread.1 = (bf16[8,288,2048]{2,1,0:T(8,128)(2,1)S(1)}, bf16[70,1680]{1,0:T(8,128)(2,1)S(1)}) custom-call(bf16[2240,2048]{1,0:T(8,128)(2,1)} %bitcast.5, bf16[70,1680]{1,0:T(8,128)(2,1)} %w_ref.1), custom_call_target="tpu_custom_call" | custom-call | flops 1 | bytes 1 | tf_op jit(solution)/shard_map/spread/pallas_call | solution.py:115
  12.9 1.4 %pack.1 = (bf16[288,1152]{1,0:T(8,128)(2,1)S(1)}, bf16[288,640]{1,0:T(8,128)(2,1)S(1)}) custom-call(s32[3]{0:T(128)S(1)} %pad_add_fusion.pos, bf16[70,1680]{1,0:T(8,128)(2,1)S(1)} %get-tuple-element.39.a0, bf16[70,1680]{1,0:T(8,128)(2,1)S(1)} %collective-permute-done.a1, bf16[70,1680]{1,0:T(8,128)(2,1)S(1)} %collective-permute-done.1.a2, ...), custom_call_target="tpu_custom_call" | custom-call | flops 1 | bytes 1 | tf_op jit(solution)/shard_map/pack/pallas_call | solution.py:172
  14.5 3.1 %collective-permute-start.5 = (bf16[288,1152]{1,0:T(8,128)(2,1)S(1)}, bf16[288,1152]{1,0:T(8,128)(2,1)S(1)}, u32[]{:S(2)}, u32[]{:S(2)}) collective-permute-start(bf16[288,1152]{1,0:T(8,128)(2,1)S(1)} %get-tuple-element.41.refs_0_), channel_id=1, source_target_pairs={{0,96},{4,28},{8,104},{12,4},{16,112},{20,12},{24,120},{28,20},{32... | collective-permute-start | bytes 1990664 | tf_op jit(solution)/shard_map/ppermute | solution.py:65
  17.6 1.7 %collective-permute-done.7.refs_1_ = bf16[288,640]{1,0:T(8,128)(2,1)S(1)} collective-permute-done((bf16[288,640]{1,0:T(8,128)(2,1)S(1)}, bf16[288,640]{1,0:T(8,128)(2,1)S(1)}, u32[]{:S(2)}, u32[]{:S(2)}) %collective-permute-start.7) | collective-permute-done | bytes 368672 | tf_op jit(solution)/shard_map/ppermute | solution.py:65
  19.2 3.2 %part_q.1.refs_7_ = f32[560,2048]{1,0:T(8,128)S(1)} custom-call(s32[3]{0:T(128)S(1)} %pad_add_fusion.pos, bf16[288,640]{1,0:T(8,128)(2,1)S(1)} %get-tuple-element.46.refs_0_, bf16[288,640]{1,0:T(8,128)(2,1)S(1)} %collective-permute-done.7.refs_1_, bf16[8,288,2048]{2,1,0:T(8,128)(2,1)S(1)} %get-tuple-element.42.refs_2_.refs_4_.refs_3_.refs_6_), custom_call_target="tpu_custom_call" | custom-call | flops 1 | bytes 1 | tf_op jit(solution)/shard_map/part_q/pallas_call | solution.py:172
  22.4 5.0 %part_kv.1.refs_5_ = f32[1120,2048]{1,0:T(8,128)S(1)} custom-call(s32[3]{0:T(128)S(1)} %pad_add_fusion.pos, bf16[288,1152]{1,0:T(8,128)(2,1)S(1)} %get-tuple-element.41.refs_0_, bf16[288,1152]{1,0:T(8,128)(2,1)S(1)} %collective-permute-done.6.refs_1_, bf16[8,288,2048]{2,1,0:T(8,128)(2,1)S(1)} %get-tuple-element.42.refs_2_.refs_4_.refs_3_.refs_6_), custom_call_target="tpu_custom_call" | custom-call | flops 1 | bytes 1 | tf_op jit(solution)/shard_map/part_kv/pallas_call | solution.py:172
  27.5 2.0 %collective-permute-done.4.refs_0_ = bf16[288,1152]{1,0:T(8,128)(2,1)S(1)} collective-permute-done((bf16[288,1152]{1,0:T(8,128)(2,1)S(1)}, bf16[288,1152]{1,0:T(8,128)(2,1)S(1)}, u32[]{:S(2)}, u32[]{:S(2)}) %collective-permute-start.4) | collective-permute-done | bytes 663584 | tf_op jit(solution)/shard_map/ppermute | solution.py:65
  30.3 1.3 %collective-permute-done.8.refs_1_ = bf16[288,1152]{1,0:T(8,128)(2,1)S(1)} collective-permute-done((bf16[288,1152]{1,0:T(8,128)(2,1)S(1)}, bf16[288,1152]{1,0:T(8,128)(2,1)S(1)}, u32[]{:S(2)}, u32[]{:S(2)}) %collective-permute-start.8) | collective-permute-done | bytes 663584 | tf_op jit(solution)/shard_map/ppermute | solution.py:65
  31.6 0.9 collective-permute-done.9.refs_3_.refs_2_
  32.5 6.5 %part_more.1.refs_4_ = f32[1120,2048]{1,0:T(8,128)S(1)} custom-call(s32[3]{0:T(128)S(1)} %pad_add_fusion.pos, bf16[288,1152]{1,0:T(8,128)(2,1)S(1)} %collective-permute-done.4.refs_0_, bf16[288,1152]{1,0:T(8,128)(2,1)S(1)} %collective-permute-done.8.refs_1_, bf16[288,1152]{1,0:T(8,128)(2,1)S(1)} %collective-permute-done.5.refs_2_, ...), custom_call_target="tpu_custom_call", output_to_operand_aliasing={{}: (6, {})} | custom-call | flops 1 | bytes 1 | tf_op jit(solution)/shard_map/part_more/pallas_call | solution.py:172
  39.1 3.1 %collective-permute-done.3.refs_0_ = bf16[288,1152]{1,0:T(8,128)(2,1)S(1)} collective-permute-done((bf16[288,1152]{1,0:T(8,128)(2,1)S(1)}, bf16[288,1152]{1,0:T(8,128)(2,1)S(1)}, u32[]{:S(2)}, u32[]{:S(2)}) %collective-permute-start.3) | collective-permute-done | bytes 663584 | tf_op jit(solution)/shard_map/ppermute | solution.py:65
  42.1 1.4 %collective-permute-start.12 = (bf16[288,640]{1,0:T(8,128)(2,1)S(1)}, bf16[288,640]{1,0:T(8,128)(2,1)S(1)}, u32[]{:S(2)}, u32[]{:S(2)}) collective-permute-start(bf16[288,640]{1,0:T(8,128)(2,1)S(1)} %get-tuple-element.46.refs_0_), channel_id=1, source_target_pairs={{0,96},{4,28},{8,104},{12,4},{16,112},{20,12},{24,120},{28,20},{32... | collective-permute-start | bytes 1105928 | tf_op jit(solution)/shard_map/ppermute | solution.py:65
  43.5 0.9 collective-permute-start.10
  44.3 7.5 %keys_values.1 = (bf16[5,2048,112]{2,1,0:T(8,128)(2,1)S(1)}, bf16[5,128,2048]{2,1,0:T(8,128)(2,1)S(1)}, f32[4,5,128,112]{3,2,1,0:T(8,128)S(1)}, bf16[5,128,112]{2,1,0:T(8,128)(2,1)S(1)}) custom-call(s32[3]{0:T(128)S(1)} %pad_add_fusion.pos, bf16[288,1152]{1,0:T(8,128)(2,1)S(1)} %collective-permute-done.3.refs_0_, ...), custom_call_target="tpu_custom_call" | custom-call | flops 1 | bytes 1 | tf_op jit(solution)/shard_map/keys_values/pallas_call | solution.py:172
  52.6 3.7 %collective-permute-done.10.refs_0_ = bf16[288,640]{1,0:T(8,128)(2,1)S(1)} collective-permute-done((bf16[288,640]{1,0:T(8,128)(2,1)S(1)}, bf16[288,640]{1,0:T(8,128)(2,1)S(1)}, u32[]{:S(2)}, u32[]{:S(2)}) %collective-permute-start.10) | collective-permute-done | bytes 368672 | tf_op jit(solution)/shard_map/ppermute | solution.py:65
  56.9 1.2 %collective-permute-start.17 = (bf16[5,128,112]{2,1,0:T(8,128)(2,1)S(1)}, bf16[5,128,112]{2,1,0:T(8,128)(2,1)S(1)}, u32[]{:S(2)}, u32[]{:S(2)}) collective-permute-start(bf16[5,128,112]{2,1,0:T(8,128)(2,1)S(1)} %chip.1.a), channel_id=1, source_target_pairs={{0,24},{4,28},{8,0},{12,4},{16,8},{20,12},{24,16},{28,20},{32,56},... | collective-permute-start | bytes 430088 | tf_op jit(solution)/shard_map/ppermute | solution.py:65
  58.1 1.5 %collective-permute-start.16 = (bf16[5,128,112]{2,1,0:T(8,128)(2,1)S(1)}, bf16[5,128,112]{2,1,0:T(8,128)(2,1)S(1)}, u32[]{:S(2)}, u32[]{:S(2)}) collective-permute-start(bf16[5,128,112]{2,1,0:T(8,128)(2,1)S(1)} %chip.1.a), channel_id=1, source_target_pairs={{0,16},{4,20},{8,24},{12,28},{16,0},{20,4},{24,8},{28,12},{32,48},... | collective-permute-start | bytes 430088 | tf_op jit(solution)/shard_map/ppermute | solution.py:65
  60.1 6.5 %queries.1.fq_ref.refs_8_ = bf16[560,2048]{1,0:T(8,128)(2,1)S(1)} custom-call(s32[3]{0:T(128)S(1)} %pad_add_fusion.pos, bf16[288,640]{1,0:T(8,128)(2,1)S(1)} %collective-permute-done.10.refs_0_, bf16[288,640]{1,0:T(8,128)(2,1)S(1)} %collective-permute-done.11.refs_1_, bf16[288,640]{1,0:T(8,128)(2,1)S(1)} %collective-permute-done.12.refs_2_, ...), custom_call_target="tpu_custom_call" | custom-call | flops 1 | bytes 1 | tf_op jit(solution)/shard_map/queries/pallas_call | solution.py:172
  66.7 2.8 %collective-permute-done.15.b.refs_1_ = bf16[5,128,112]{2,1,0:T(8,128)(2,1)S(1)} collective-permute-done((bf16[5,128,112]{2,1,0:T(8,128)(2,1)S(1)}, bf16[5,128,112]{2,1,0:T(8,128)(2,1)S(1)}, u32[]{:S(2)}, u32[]{:S(2)}) %collective-permute-start.15) | collective-permute-done | bytes 143392 | tf_op jit(solution)/shard_map/ppermute | solution.py:65
  69.5 2.7 %collective-permute-start.23 = (bf16[5,128,112]{2,1,0:T(8,128)(2,1)S(1)}, bf16[5,128,112]{2,1,0:T(8,128)(2,1)S(1)}, u32[]{:S(2)}, u32[]{:S(2)}) collective-permute-start(bf16[5,128,112]{2,1,0:T(8,128)(2,1)S(1)} %row.1), channel_id=1, source_target_pairs={{0,96},{4,100},{8,104},{12,108},{16,112},{20,116},{24,120},{28,124... | collective-permute-start | bytes 430088 | tf_op jit(solution)/shard_map/ppermute | solution.py:65
  72.2 1.3 %collective-permute-start.22 = (bf16[5,128,112]{2,1,0:T(8,128)(2,1)S(1)}, bf16[5,128,112]{2,1,0:T(8,128)(2,1)S(1)}, u32[]{:S(2)}, u32[]{:S(2)}) collective-permute-start(bf16[5,128,112]{2,1,0:T(8,128)(2,1)S(1)} %row.1), channel_id=1, source_target_pairs={{0,64},{4,68},{8,72},{12,76},{16,80},{20,84},{24,88},{28,92},{32,9... | collective-permute-start | bytes 430088 | tf_op jit(solution)/shard_map/ppermute | solution.py:65
  73.5 2.8 %collective-permute-start.21 = (bf16[5,128,112]{2,1,0:T(8,128)(2,1)S(1)}, bf16[5,128,112]{2,1,0:T(8,128)(2,1)S(1)}, u32[]{:S(2)}, u32[]{:S(2)}) collective-permute-start(bf16[5,128,112]{2,1,0:T(8,128)(2,1)S(1)} %row.1), channel_id=1, source_target_pairs={{0,32},{4,36},{8,40},{12,44},{16,48},{20,52},{24,56},{28,60},{32,6... | collective-permute-start | bytes 430088 | tf_op jit(solution)/shard_map/ppermute | solution.py:65
  76.3 6.5 %attend.1.refs_9_ = f32[5,128,2048]{2,1,0:T(8,128)S(1)} custom-call(s32[4]{0:T(128)S(1)} %copy-done, bf16[5,2048,112]{2,1,0:T(8,128)(2,1)S(1)} %get-tuple-element.64.fk_ref, bf16[5,128,2048]{2,1,0:T(8,128)(2,1)S(1)} %get-tuple-element.65.v_ref, bf16[560,2048]{1,0:T(8,128)(2,1)S(1)} %queries.1.fq_ref.refs_8_), custom_call_target="tpu_custom_call" | custom-call | flops 1 | bytes 1 | tf_op jit(solution)/shard_map/attend/pallas_call | solution.py:172
  82.9 2.6 %join.1 = (f32[560,2048]{1,0:T(8,128)S(1)}, f32[1,2048]{1,0:T(1,128)S(1)}) custom-call(s32[3]{0:T(128)S(1)} %pad_add_fusion.pos, f32[5]{0:T(128)S(1)} %copy-done.1, bf16[5,128,112]{2,1,0:T(8,128)(2,1)S(1)} %collective-permute-done.14.other_ref.refs_0_, bf16[5,128,112]{2,1,0:T(8,128)(2,1)S(1)} %collective-permute-done.15.b.refs_1_, ...), custom_call_target="tpu_custom_call" | custom-call | flops 1 | bytes 1 | tf_op jit(solution)/shard_map/join/pallas_call | solution.py:172
  85.5 4.1 %collective-permute-start.26 = (f32[1,2048]{1,0:T(1,128)S(1)}, f32[1,2048]{1,0:T(1,128)S(1)}, u32[]{:S(2)}, u32[]{:S(2)}) collective-permute-start(f32[1,2048]{1,0:T(1,128)S(1)} %get-tuple-element.67.s0), channel_id=1, source_target_pairs={{0,3},{1,0},{2,1},{3,2},{4,7},{5,4},{6,5},{7,6},{8,11},{9,8},{10,9... | collective-permute-start | bytes 24584 | tf_op jit(solution)/shard_map/ppermute | solution.py:486
  89.6 1.3 %collective-permute-start.24 = (f32[1,2048]{1,0:T(1,128)S(1)}, f32[1,2048]{1,0:T(1,128)S(1)}, u32[]{:S(2)}, u32[]{:S(2)}) collective-permute-start(f32[1,2048]{1,0:T(1,128)S(1)} %get-tuple-element.67.s0), channel_id=1, source_target_pairs={{0,1},{1,2},{2,3},{3,0},{4,5},{5,6},{6,7},{7,4},{8,9},{9,10},{10,1... | collective-permute-start | bytes 24584 | tf_op jit(solution)/shard_map/ppermute | solution.py:486
  90.9 3.8 %collective-permute-done.25.s2 = f32[1,2048]{1,0:T(1,128)S(1)} collective-permute-done((f32[1,2048]{1,0:T(1,128)S(1)}, f32[1,2048]{1,0:T(1,128)S(1)}, u32[]{:S(2)}, u32[]{:S(2)}) %collective-permute-start.25) | collective-permute-done | bytes 8224 | tf_op jit(solution)/shard_map/ppermute | solution.py:486
  94.7 1.9 %norm.1 = bf16[560,2048]{1,0:T(8,128)(2,1)} custom-call(f32[560,2048]{1,0:T(8,128)S(1)} %get-tuple-element.66.out_ref, f32[1,2048]{1,0:T(1,128)S(1)} %get-tuple-element.67.s0, f32[1,2048]{1,0:T(1,128)S(1)} %collective-permute-done.24.s1, f32[1,2048]{1,0:T(1,128)S(1)} %collective-permute-done.25.s2, f32[1,2048]{1,0:T(1,128)S(1)} %collective-permute-done.26.s3, ...), custom_call_target="tpu_custom_call" | custom-call | flops 1 | bytes 1 | tf_op jit(solution)/shard_map/norm/pallas_call | solution.py:415
  (40 shorter events, 3.1 us)
Async XLA Ops:
  0.0 12.9 %collective-permute-start = (bf16[70,1680]{1,0:T(8,128)(2,1)}, bf16[70,1680]{1,0:T(8,128)(2,1)S(1)}, u32[]{:S(2)}, u32[]{:S(2)}) collective-permute-start(bf16[70,1680]{1,0:T(8,128)(2,1)} %w_ref.1), channel_id=1, source_target_pairs={{0,8},{4,36},{8,16},{12,44},{16,24},{20,52},{24,0},{28,60},{32,40}... | collective-permute-start | bytes 705608 | tf_op jit(solution)/shard_map/ppermute | solution.py:65
  1.6 11.3 %collective-permute-start.2 = (bf16[70,1680]{1,0:T(8,128)(2,1)}, bf16[70,1680]{1,0:T(8,128)(2,1)S(1)}, u32[]{:S(2)}, u32[]{:S(2)}) collective-permute-start(bf16[70,1680]{1,0:T(8,128)(2,1)} %w_ref.1), channel_id=1, source_target_pairs={{0,24},{4,100},{8,0},{12,108},{16,8},{20,116},{24,16},{28,124},{32... | collective-permute-start | bytes 705608 | tf_op jit(solution)/shard_map/ppermute | solution.py:65
  3.2 9.7 %collective-permute-start.1 = (bf16[70,1680]{1,0:T(8,128)(2,1)}, bf16[70,1680]{1,0:T(8,128)(2,1)S(1)}, u32[]{:S(2)}, u32[]{:S(2)}) collective-permute-start(bf16[70,1680]{1,0:T(8,128)(2,1)} %w_ref.1), channel_id=1, source_target_pairs={{0,16},{4,68},{8,24},{12,76},{16,0},{20,84},{24,8},{28,92},{32,48}... | collective-permute-start | bytes 705608 | tf_op jit(solution)/shard_map/ppermute | solution.py:65
  14.4 8.1 %collective-permute-start.6 = (bf16[288,1152]{1,0:T(8,128)(2,1)S(1)}, bf16[288,1152]{1,0:T(8,128)(2,1)S(1)}, u32[]{:S(2)}, u32[]{:S(2)}) collective-permute-start(bf16[288,1152]{1,0:T(8,128)(2,1)S(1)} %get-tuple-element.41.refs_0_), channel_id=1, source_target_pairs={{0,4},{4,0},{8,12},{12,8},{16,20},{20,16},{24,28},{28,24},{32,36},... | collective-permute-start | bytes 1990664 | tf_op jit(solution)/shard_map/ppermute | solution.py:65
  14.5 13.0 %collective-permute-start.5 = (bf16[288,1152]{1,0:T(8,128)(2,1)S(1)}, bf16[288,1152]{1,0:T(8,128)(2,1)S(1)}, u32[]{:S(2)}, u32[]{:S(2)}) collective-permute-start(bf16[288,1152]{1,0:T(8,128)(2,1)S(1)} %get-tuple-element.41.refs_0_), channel_id=1, source_target_pairs={{0,96},{4,28},{8,104},{12,4},{16,112},{20,12},{24,120},{28,20},{32... | collective-permute-start | bytes 1990664 | tf_op jit(solution)/shard_map/ppermute | solution.py:65
  17.6 11.9 %collective-permute-start.4 = (bf16[288,1152]{1,0:T(8,128)(2,1)S(1)}, bf16[288,1152]{1,0:T(8,128)(2,1)S(1)}, u32[]{:S(2)}, u32[]{:S(2)}) collective-permute-start(bf16[288,1152]{1,0:T(8,128)(2,1)S(1)} %get-tuple-element.41.refs_0_), channel_id=1, source_target_pairs={{0,32},{4,12},{8,40},{12,20},{16,48},{20,28},{24,56},{28,4},{32,64... | collective-permute-start | bytes 1990664 | tf_op jit(solution)/shard_map/ppermute | solution.py:65
  17.6 1.7 %collective-permute-start.7 = (bf16[288,640]{1,0:T(8,128)(2,1)S(1)}, bf16[288,640]{1,0:T(8,128)(2,1)S(1)}, u32[]{:S(2)}, u32[]{:S(2)}) collective-permute-start(bf16[288,640]{1,0:T(8,128)(2,1)S(1)} %get-tuple-element.46.refs_0_), channel_id=1, source_target_pairs={{0,4},{4,0},{8,12},{12,8},{16,20},{20,16},{24,28},{28,24},{32,36},... | collective-permute-start | bytes 1105928 | tf_op jit(solution)/shard_map/ppermute | solution.py:65
  29.4 2.1 %collective-permute-start.8 = (bf16[288,1152]{1,0:T(8,128)(2,1)S(1)}, bf16[288,1152]{1,0:T(8,128)(2,1)S(1)}, u32[]{:S(2)}, u32[]{:S(2)}) collective-permute-start(bf16[288,1152]{1,0:T(8,128)(2,1)S(1)} %collective-permute-done.4.refs_0_), channel_id=1, source_target_pairs={{0,4},{4,0},{8,12},{12,8},{16,20},{20,16},{24,28},{28,24},{32,36},... | collective-permute-start | bytes 1990664 | tf_op jit(solution)/shard_map/ppermute | solution.py:65
  29.4 3.1 %collective-permute-start.9 = (bf16[288,1152]{1,0:T(8,128)(2,1)S(1)}, bf16[288,1152]{1,0:T(8,128)(2,1)S(1)}, u32[]{:S(2)}, u32[]{:S(2)}) collective-permute-start(bf16[288,1152]{1,0:T(8,128)(2,1)S(1)} %collective-permute-done.5.refs_2_), channel_id=1, source_target_pairs={{0,4},{4,0},{8,12},{12,8},{16,20},{20,16},{24,28},{28,24},{32,36},... | collective-permute-start | bytes 1990664 | tf_op jit(solution)/shard_map/ppermute | solution.py:65
  30.0 12.2 %collective-permute-start.3 = (bf16[288,1152]{1,0:T(8,128)(2,1)S(1)}, bf16[288,1152]{1,0:T(8,128)(2,1)S(1)}, u32[]{:S(2)}, u32[]{:S(2)}) collective-permute-start(bf16[288,1152]{1,0:T(8,128)(2,1)S(1)} %get-tuple-element.41.refs_0_), channel_id=1, source_target_pairs={{0,64},{4,20},{8,72},{12,28},{16,80},{20,4},{24,88},{28,12},{32,96... | collective-permute-start | bytes 1990664 | tf_op jit(solution)/shard_map/ppermute | solution.py:65
  42.1 2.2 %collective-permute-start.13 = (bf16[288,1152]{1,0:T(8,128)(2,1)S(1)}, bf16[288,1152]{1,0:T(8,128)(2,1)S(1)}, u32[]{:S(2)}, u32[]{:S(2)}) collective-permute-start(bf16[288,1152]{1,0:T(8,128)(2,1)S(1)} %collective-permute-done.3.refs_0_), channel_id=1, source_target_pairs={{0,4},{4,0},{8,12},{12,8},{16,20},{20,16},{24,28},{28,24},{32,36},... | collective-permute-start | bytes 1990664 | tf_op jit(solution)/shard_map/ppermute | solution.py:65
  42.1 10.4 %collective-permute-start.12 = (bf16[288,640]{1,0:T(8,128)(2,1)S(1)}, bf16[288,640]{1,0:T(8,128)(2,1)S(1)}, u32[]{:S(2)}, u32[]{:S(2)}) collective-permute-start(bf16[288,640]{1,0:T(8,128)(2,1)S(1)} %get-tuple-element.46.refs_0_), channel_id=1, source_target_pairs={{0,96},{4,28},{8,104},{12,4},{16,112},{20,12},{24,120},{28,20},{32... | collective-permute-start | bytes 1105928 | tf_op jit(solution)/shard_map/ppermute | solution.py:65
  43.5 9.1 %collective-permute-start.11 = (bf16[288,640]{1,0:T(8,128)(2,1)S(1)}, bf16[288,640]{1,0:T(8,128)(2,1)S(1)}, u32[]{:S(2)}, u32[]{:S(2)}) collective-permute-start(bf16[288,640]{1,0:T(8,128)(2,1)S(1)} %get-tuple-element.46.refs_0_), channel_id=1, source_target_pairs={{0,64},{4,20},{8,72},{12,28},{16,80},{20,4},{24,88},{28,12},{32,96... | collective-permute-start | bytes 1105928 | tf_op jit(solution)/shard_map/ppermute | solution.py:65
  43.5 12.8 %collective-permute-start.10 = (bf16[288,640]{1,0:T(8,128)(2,1)S(1)}, bf16[288,640]{1,0:T(8,128)(2,1)S(1)}, u32[]{:S(2)}, u32[]{:S(2)}) collective-permute-start(bf16[288,640]{1,0:T(8,128)(2,1)S(1)} %get-tuple-element.46.refs_0_), channel_id=1, source_target_pairs={{0,32},{4,12},{8,40},{12,20},{16,48},{20,28},{24,56},{28,4},{32,64... | collective-permute-start | bytes 1105928 | tf_op jit(solution)/shard_map/ppermute | solution.py:65
  51.9 4.4 %collective-permute-start.14 = (bf16[5,128,112]{2,1,0:T(8,128)(2,1)S(1)}, bf16[5,128,112]{2,1,0:T(8,128)(2,1)S(1)}, u32[]{:S(2)}, u32[]{:S(2)}) collective-permute-start(bf16[5,128,112]{2,1,0:T(8,128)(2,1)S(1)} %get-tuple-element.49.tot_ref), channel_id=1, source_target_pairs={{0,4},{4,0},{8,12},{12,8},{16,20},{20,16},{24,28},{28,24},{32,36},... | collective-permute-start | bytes 430088 | tf_op jit(solution)/shard_map/ppermute | solution.py:65
  56.3 3.3 %collective-permute-start.18 = (bf16[288,640]{1,0:T(8,128)(2,1)S(1)}, bf16[288,640]{1,0:T(8,128)(2,1)S(1)}, u32[]{:S(2)}, u32[]{:S(2)}) collective-permute-start(bf16[288,640]{1,0:T(8,128)(2,1)S(1)} %collective-permute-done.10.refs_0_), channel_id=1, source_target_pairs={{0,4},{4,0},{8,12},{12,8},{16,20},{20,16},{24,28},{28,24},{32,36},... | collective-permute-start | bytes 1105928 | tf_op jit(solution)/shard_map/ppermute | solution.py:65
  56.3 3.8 %collective-permute-start.19 = (bf16[288,640]{1,0:T(8,128)(2,1)S(1)}, bf16[288,640]{1,0:T(8,128)(2,1)S(1)}, u32[]{:S(2)}, u32[]{:S(2)}) collective-permute-start(bf16[288,640]{1,0:T(8,128)(2,1)S(1)} %collective-permute-done.11.refs_1_), channel_id=1, source_target_pairs={{0,4},{4,0},{8,12},{12,8},{16,20},{20,16},{24,28},{28,24},{32,36},... | collective-permute-start | bytes 1105928 | tf_op jit(solution)/shard_map/ppermute | solution.py:65
  56.8 3.3 %collective-permute-start.20 = (bf16[288,640]{1,0:T(8,128)(2,1)S(1)}, bf16[288,640]{1,0:T(8,128)(2,1)S(1)}, u32[]{:S(2)}, u32[]{:S(2)}) collective-permute-start(bf16[288,640]{1,0:T(8,128)(2,1)S(1)} %collective-permute-done.12.refs_2_), channel_id=1, source_target_pairs={{0,4},{4,0},{8,12},{12,8},{16,20},{20,16},{24,28},{28,24},{32,36},... | collective-permute-start | bytes 1105928 | tf_op jit(solution)/shard_map/ppermute | solution.py:65
  56.8 19.5 %copy-start = (s32[4]{0:T(128)S(1)}, s32[4]{0:T(128)}, u32[]{:S(2)}) copy-start(s32[4]{0:T(128)} %codes.1) | copy-start | bytes 52
  56.9 9.7 %collective-permute-start.17 = (bf16[5,128,112]{2,1,0:T(8,128)(2,1)S(1)}, bf16[5,128,112]{2,1,0:T(8,128)(2,1)S(1)}, u32[]{:S(2)}, u32[]{:S(2)}) collective-permute-start(bf16[5,128,112]{2,1,0:T(8,128)(2,1)S(1)} %chip.1.a), channel_id=1, source_target_pairs={{0,24},{4,28},{8,0},{12,4},{16,8},{20,12},{24,16},{28,20},{32,56},... | collective-permute-start | bytes 430088 | tf_op jit(solution)/shard_map/ppermute | solution.py:65
  58.1 8.6 %collective-permute-start.16 = (bf16[5,128,112]{2,1,0:T(8,128)(2,1)S(1)}, bf16[5,128,112]{2,1,0:T(8,128)(2,1)S(1)}, u32[]{:S(2)}, u32[]{:S(2)}) collective-permute-start(bf16[5,128,112]{2,1,0:T(8,128)(2,1)S(1)} %chip.1.a), channel_id=1, source_target_pairs={{0,16},{4,20},{8,24},{12,28},{16,0},{20,4},{24,8},{28,12},{32,48},... | collective-permute-start | bytes 430088 | tf_op jit(solution)/shard_map/ppermute | solution.py:65
  59.6 9.8 %collective-permute-start.15 = (bf16[5,128,112]{2,1,0:T(8,128)(2,1)S(1)}, bf16[5,128,112]{2,1,0:T(8,128)(2,1)S(1)}, u32[]{:S(2)}, u32[]{:S(2)}) collective-permute-start(bf16[5,128,112]{2,1,0:T(8,128)(2,1)S(1)} %chip.1.a), channel_id=1, source_target_pairs={{0,8},{4,12},{8,16},{12,20},{16,24},{20,28},{24,0},{28,4},{32,40},... | collective-permute-start | bytes 430088 | tf_op jit(solution)/shard_map/ppermute | solution.py:65
  69.5 13.3 %collective-permute-start.23 = (bf16[5,128,112]{2,1,0:T(8,128)(2,1)S(1)}, bf16[5,128,112]{2,1,0:T(8,128)(2,1)S(1)}, u32[]{:S(2)}, u32[]{:S(2)}) collective-permute-start(bf16[5,128,112]{2,1,0:T(8,128)(2,1)S(1)} %row.1), channel_id=1, source_target_pairs={{0,96},{4,100},{8,104},{12,108},{16,112},{20,116},{24,120},{28,124... | collective-permute-start | bytes 430088 | tf_op jit(solution)/shard_map/ppermute | solution.py:65
  72.2 10.6 %collective-permute-start.22 = (bf16[5,128,112]{2,1,0:T(8,128)(2,1)S(1)}, bf16[5,128,112]{2,1,0:T(8,128)(2,1)S(1)}, u32[]{:S(2)}, u32[]{:S(2)}) collective-permute-start(bf16[5,128,112]{2,1,0:T(8,128)(2,1)S(1)} %row.1), channel_id=1, source_target_pairs={{0,64},{4,68},{8,72},{12,76},{16,80},{20,84},{24,88},{28,92},{32,9... | collective-permute-start | bytes 430088 | tf_op jit(solution)/shard_map/ppermute | solution.py:65
  73.5 9.3 %collective-permute-start.21 = (bf16[5,128,112]{2,1,0:T(8,128)(2,1)S(1)}, bf16[5,128,112]{2,1,0:T(8,128)(2,1)S(1)}, u32[]{:S(2)}, u32[]{:S(2)}) collective-permute-start(bf16[5,128,112]{2,1,0:T(8,128)(2,1)S(1)} %row.1), channel_id=1, source_target_pairs={{0,32},{4,36},{8,40},{12,44},{16,48},{20,52},{24,56},{28,60},{32,6... | collective-permute-start | bytes 430088 | tf_op jit(solution)/shard_map/ppermute | solution.py:65
  76.3 6.6 %copy-start.1 = (f32[5]{0:T(128)S(1)}, f32[5]{0:T(128)}, u32[]{:S(2)}) copy-start(f32[5]{0:T(128)} %scale.1) | copy-start | bytes 64
  85.5 5.5 %collective-permute-start.26 = (f32[1,2048]{1,0:T(1,128)S(1)}, f32[1,2048]{1,0:T(1,128)S(1)}, u32[]{:S(2)}, u32[]{:S(2)}) collective-permute-start(f32[1,2048]{1,0:T(1,128)S(1)} %get-tuple-element.67.s0), channel_id=1, source_target_pairs={{0,3},{1,0},{2,1},{3,2},{4,7},{5,4},{6,5},{7,6},{8,11},{9,8},{10,9... | collective-permute-start | bytes 24584 | tf_op jit(solution)/shard_map/ppermute | solution.py:486
  89.6 5.2 %collective-permute-start.25 = (f32[1,2048]{1,0:T(1,128)S(1)}, f32[1,2048]{1,0:T(1,128)S(1)}, u32[]{:S(2)}, u32[]{:S(2)}) collective-permute-start(f32[1,2048]{1,0:T(1,128)S(1)} %get-tuple-element.67.s0), channel_id=1, source_target_pairs={{0,2},{1,3},{2,0},{3,1},{4,6},{5,7},{6,4},{7,5},{8,10},{9,11},{10,... | collective-permute-start | bytes 24584 | tf_op jit(solution)/shard_map/ppermute | solution.py:486
  89.6 5.2 %collective-permute-start.24 = (f32[1,2048]{1,0:T(1,128)S(1)}, f32[1,2048]{1,0:T(1,128)S(1)}, u32[]{:S(2)}, u32[]{:S(2)}) collective-permute-start(f32[1,2048]{1,0:T(1,128)S(1)} %get-tuple-element.67.s0), channel_id=1, source_target_pairs={{0,1},{1,2},{2,3},{3,0},{4,5},{5,6},{6,7},{7,4},{8,9},{9,10},{10,1... | collective-permute-start | bytes 24584 | tf_op jit(solution)/shard_map/ppermute | solution.py:486

commit v10 on v6

--- a/solution.py
+++ b/solution.py
@@ -142,11 +142,8 @@
 
 
 def each_group(n, step):
-    def run(g, carry):
-        step(g, pl.ds(pl.multiple_of(g * GROUP, GROUP), GROUP))
-        return carry
-
-    lax.fori_loop(0, n // GROUP, run, 0)
+    for g in range(n // GROUP):
+        step(g, pl.ds(g * GROUP, GROUP))
 
 
 def resident(kernel, small, large, outs, scratch, limit, name, alias=None):
@@ -289,7 +286,7 @@
 
     def step(g, at):
         code = codes[g]
-        start = pl.multiple_of(g * GROUP, GROUP)
+        start = g * GROUP
         one, two = pl.ds(start, half), pl.ds(start + half, half)
         upper = mask_rows(code, 0, half, 0, GROUP)
         lower = mask_rows(code, 4, half, half, half)

time: 96 us -> 94.3 us (0.982)
  Pallas kernels: 45.4 us -> 42.6 us
  waiting for transfers between devices: 12.9 us -> 14.2 us
    pallas_call x8, Pallas kernels: 36.7 us -> 33.9 us  [resident(): pl.pallas_call(kernel, in_specs=[pl.BlockSpec(memory_space=pltpu.SMEM)] *...]
    ppermute x24, waiting for transfers between devices: 10.3 us -> 11.6 us  [shift(): return lax.ppermute(a, 'tm', moves)]
  transfers between devices with their start and end apart: 27 -> 27, of which waited for: 8 -> 9; matrix products, arithmetic and copies ran while one was open for 1% -> 1% of each run, Pallas kernels for 41% -> 39%
where the time goes in v10:
time: 94.3 us; the launch traced here: 94 us
  Pallas kernels  42.6 us (45%)
  starting transfers between devices  35 us (37%)
  waiting for transfers between devices  14.2 us (15%)
  local copies, waits for them, and re-layouts  1.72 us (2%)
    pallas_call x8, Pallas kernels, resident(): pl.pallas_call(kernel, in_specs=[pl.BlockSpec(memory_space=pltpu.SMEM)] *...  33.9 us
    ppermute x24, starting transfers between devices, shift(): return lax.ppermute(a, 'tm', moves)  28.4 us
    ppermute x24, waiting for transfers between devices, shift(): return lax.ppermute(a, 'tm', moves)  11.6 us
    pallas_call x1, Pallas kernels, spread(): pl.pallas_call(spread_kernel, grid=(n // blk,), in_specs=[pl.BlockSpec((D...  6.8 us
    ppermute x3, starting transfers between devices, body(): lax.ppermute(squares, 'head', [(i, (i + d) % 4) for i in range(4)])  6.58 us
    ppermute x3, waiting for transfers between devices, body(): lax.ppermute(squares, 'head', [(i, (i + d) % 4) for i in range(4)])  2.65 us
  transfers between devices with their start and end apart: 27, of which 9 were waited for; matrix products, arithmetic and copies ran while one was open for 1% of the time, Pallas kernels for 39%

profile of v10, /device:TPU:0, one launch (start us, length us, event | category | flops | bytes accessed | tf_op | source)
XLA Modules:
  0.0 94.0 jit_solution(8057900781977018457)
XLA Ops:
  0.0 1.6 %collective-permute-start = (bf16[70,1680]{1,0:T(8,128)(2,1)}, bf16[70,1680]{1,0:T(8,128)(2,1)S(1)}, u32[]{:S(2)}, u32[]{:S(2)}) collective-permute-start(bf16[70,1680]{1,0:T(8,128)(2,1)} %a0.1), channel_id=1, source_target_pairs={{0,8},{4,36},{8,16},{12,44},{16,24},{20,52},{24,0},{28,60},{32,40}... | collective-permute-start | bytes 705608 | tf_op jit(solution)/shard_map/ppermute | solution.py:65
  1.6 2.7 %collective-permute-start.1 = (bf16[70,1680]{1,0:T(8,128)(2,1)}, bf16[70,1680]{1,0:T(8,128)(2,1)S(1)}, u32[]{:S(2)}, u32[]{:S(2)}) collective-permute-start(bf16[70,1680]{1,0:T(8,128)(2,1)} %a0.1), channel_id=1, source_target_pairs={{0,16},{4,68},{8,24},{12,76},{16,0},{20,84},{24,8},{28,92},{32,48}... | collective-permute-start | bytes 705608 | tf_op jit(solution)/shard_map/ppermute | solution.py:65
  4.3 1.4 %collective-permute-start.2 = (bf16[70,1680]{1,0:T(8,128)(2,1)}, bf16[70,1680]{1,0:T(8,128)(2,1)S(1)}, u32[]{:S(2)}, u32[]{:S(2)}) collective-permute-start(bf16[70,1680]{1,0:T(8,128)(2,1)} %a0.1), channel_id=1, source_target_pairs={{0,24},{4,100},{8,0},{12,108},{16,8},{20,116},{24,16},{28,124},{32... | collective-permute-start | bytes 705608 | tf_op jit(solution)/shard_map/ppermute | solution.py:65
  5.7 0.8 reshape.3.gain_ref
  6.6 1.2 %collective-permute-done.a1 = bf16[70,1680]{1,0:T(8,128)(2,1)S(1)} collective-permute-done((bf16[70,1680]{1,0:T(8,128)(2,1)}, bf16[70,1680]{1,0:T(8,128)(2,1)S(1)}, u32[]{:S(2)}, u32[]{:S(2)}) %collective-permute-start) | collective-permute-done | bytes 235232 | tf_op jit(solution)/shard_map/ppermute | solution.py:65
  7.8 3.8 %collective-permute-done.1.a2 = bf16[70,1680]{1,0:T(8,128)(2,1)S(1)} collective-permute-done((bf16[70,1680]{1,0:T(8,128)(2,1)}, bf16[70,1680]{1,0:T(8,128)(2,1)S(1)}, u32[]{:S(2)}, u32[]{:S(2)}) %collective-permute-start.1) | collective-permute-done | bytes 235232 | tf_op jit(solution)/shard_map/ppermute | solution.py:65
  11.6 0.9 %copy-done = bf16[70,1680]{1,0:T(8,128)(2,1)S(1)} copy-done((bf16[70,1680]{1,0:T(8,128)(2,1)S(1)}, bf16[70,1680]{1,0:T(8,128)(2,1)}, u32[]{:S(2)}) %copy-start) | copy-done | bytes 235224
  12.5 1.4 %pack.1 = (bf16[288,1152]{1,0:T(8,128)(2,1)S(1)}, bf16[288,640]{1,0:T(8,128)(2,1)S(1)}) custom-call(s32[3]{0:T(128)S(1)} %pad_add_fusion.pos, bf16[70,1680]{1,0:T(8,128)(2,1)S(1)} %copy-done, bf16[70,1680]{1,0:T(8,128)(2,1)S(1)} %collective-permute-done.a1, bf16[70,1680]{1,0:T(8,128)(2,1)S(1)} %collective-permute-done.1.a2, ...), custom_call_target="tpu_custom_call" | custom-call | flops 1 | bytes 1 | tf_op jit(solution)/shard_map/pack/pallas_call | solution.py:150
  14.1 3.1 %collective-permute-start.10 = (bf16[288,1152]{1,0:T(8,128)(2,1)S(1)}, bf16[288,1152]{1,0:T(8,128)(2,1)S(1)}, u32[]{:S(2)}, u32[]{:S(2)}) collective-permute-start(bf16[288,1152]{1,0:T(8,128)(2,1)S(1)} %get-tuple-element.41.refs_0_), channel_id=1, source_target_pairs={{0,96},{4,28},{8,104},{12,4},{16,112},{20,12},{24,120},{28,20},{32... | collective-permute-start | bytes 1990664 | tf_op jit(solution)/shard_map/ppermute | solution.py:65
  17.2 2.2 %collective-permute-start.9 = (bf16[288,1152]{1,0:T(8,128)(2,1)S(1)}, bf16[288,1152]{1,0:T(8,128)(2,1)S(1)}, u32[]{:S(2)}, u32[]{:S(2)}) collective-permute-start(bf16[288,1152]{1,0:T(8,128)(2,1)S(1)} %get-tuple-element.41.refs_0_), channel_id=1, source_target_pairs={{0,64},{4,20},{8,72},{12,28},{16,80},{20,4},{24,88},{28,12},{32,96... | collective-permute-start | bytes 1990664 | tf_op jit(solution)/shard_map/ppermute | solution.py:65
  19.4 6.8 %spread.1.refs_4_.refs_6_ = bf16[8,288,2048]{2,1,0:T(8,128)(2,1)S(1)} custom-call(bf16[2240,2048]{1,0:T(8,128)(2,1)} %bitcast.5), custom_call_target="tpu_custom_call" | custom-call | flops 1 | bytes 1 | tf_op jit(solution)/shard_map/spread/pallas_call | solution.py:110
  26.2 6.1 %part_first.1 = (f32[1120,2048]{1,0:T(8,128)S(1)}, f32[560,2048]{1,0:T(8,128)S(1)}) custom-call(s32[3]{0:T(128)S(1)} %pad_add_fusion.pos, bf16[288,1152]{1,0:T(8,128)(2,1)S(1)} %get-tuple-element.41.refs_0_, bf16[288,1152]{1,0:T(8,128)(2,1)S(1)} %collective-permute-done.3.refs_1_, bf16[288,640]{1,0:T(8,128)(2,1)S(1)} %get-tuple-element.45.refs_2_, ...), custom_call_target="tpu_custom_call" | custom-call | flops 1 | bytes 1 | tf_op jit(solution)/shard_map/part_first/pallas_call | solution.py:150
  32.5 3.7 %collective-permute-done.8.refs_0_ = bf16[288,1152]{1,0:T(8,128)(2,1)S(1)} collective-permute-done((bf16[288,1152]{1,0:T(8,128)(2,1)S(1)}, bf16[288,1152]{1,0:T(8,128)(2,1)S(1)}, u32[]{:S(2)}, u32[]{:S(2)}) %collective-permute-start.8) | collective-permute-done | bytes 663584 | tf_op jit(solution)/shard_map/ppermute | solution.py:65
  36.8 2.9 %collective-permute-start.6 = (bf16[288,640]{1,0:T(8,128)(2,1)S(1)}, bf16[288,640]{1,0:T(8,128)(2,1)S(1)}, u32[]{:S(2)}, u32[]{:S(2)}) collective-permute-start(bf16[288,640]{1,0:T(8,128)(2,1)S(1)} %get-tuple-element.45.refs_2_), channel_id=1, source_target_pairs={{0,64},{4,20},{8,72},{12,28},{16,80},{20,4},{24,88},{28,12},{32,96... | collective-permute-start | bytes 1105928 | tf_op jit(solution)/shard_map/ppermute | solution.py:65
  39.7 1.3 %collective-permute-start.7 = (bf16[288,640]{1,0:T(8,128)(2,1)S(1)}, bf16[288,640]{1,0:T(8,128)(2,1)S(1)}, u32[]{:S(2)}, u32[]{:S(2)}) collective-permute-start(bf16[288,640]{1,0:T(8,128)(2,1)S(1)} %get-tuple-element.45.refs_2_), channel_id=1, source_target_pairs={{0,96},{4,28},{8,104},{12,4},{16,112},{20,12},{24,120},{28,20},{32... | collective-permute-start | bytes 1105928 | tf_op jit(solution)/shard_map/ppermute | solution.py:65
  41.0 12.1 %keys_values.1 = (bf16[5,2048,112]{2,1,0:T(8,128)(2,1)S(1)}, bf16[5,128,2048]{2,1,0:T(8,128)(2,1)S(1)}, f32[4,5,128,112]{3,2,1,0:T(8,128)S(1)}, bf16[5,128,112]{2,1,0:T(8,128)(2,1)S(1)}) custom-call(s32[3]{0:T(128)S(1)} %pad_add_fusion.pos, bf16[288,1152]{1,0:T(8,128)(2,1)S(1)} %collective-permute-done.8.refs_0_, ...), custom_call_target="tpu_custom_call" | custom-call | flops 1 | bytes 1 | tf_op jit(solution)/shard_map/keys_values/pallas_call | solution.py:150
  53.1 0.9 %collective-permute-start.14 = (bf16[5,128,112]{2,1,0:T(8,128)(2,1)S(1)}, bf16[5,128,112]{2,1,0:T(8,128)(2,1)S(1)}, u32[]{:S(2)}, u32[]{:S(2)}) collective-permute-start(bf16[5,128,112]{2,1,0:T(8,128)(2,1)S(1)} %get-tuple-element.51.tot_ref), channel_id=1, source_target_pairs={{0,4},{4,0},{8,12},{12,8},{16,20},{20,16},{24,28},{28,24},{32,36},... | collective-permute-start | bytes 430088 | tf_op jit(solution)/shard_map/ppermute | solution.py:65
  54.1 1.0 %collective-permute-done.14.other_ref.refs_0_ = bf16[5,128,112]{2,1,0:T(8,128)(2,1)S(1)} collective-permute-done((bf16[5,128,112]{2,1,0:T(8,128)(2,1)S(1)}, bf16[5,128,112]{2,1,0:T(8,128)(2,1)S(1)}, u32[]{:S(2)}, u32[]{:S(2)}) %collective-permute-start.14) | collective-permute-done | bytes 143392 | tf_op jit(solution)/shard_map/ppermute | solution.py:65
  56.6 2.0 %collective-permute-start.16 = (bf16[5,128,112]{2,1,0:T(8,128)(2,1)S(1)}, bf16[5,128,112]{2,1,0:T(8,128)(2,1)S(1)}, u32[]{:S(2)}, u32[]{:S(2)}) collective-permute-start(bf16[5,128,112]{2,1,0:T(8,128)(2,1)S(1)} %chip.1.a), channel_id=1, source_target_pairs={{0,16},{4,20},{8,24},{12,28},{16,0},{20,4},{24,8},{28,12},{32,48},... | collective-permute-start | bytes 430088 | tf_op jit(solution)/shard_map/ppermute | solution.py:65
  58.6 1.5 %collective-permute-start.17 = (bf16[5,128,112]{2,1,0:T(8,128)(2,1)S(1)}, bf16[5,128,112]{2,1,0:T(8,128)(2,1)S(1)}, u32[]{:S(2)}, u32[]{:S(2)}) collective-permute-start(bf16[5,128,112]{2,1,0:T(8,128)(2,1)S(1)} %chip.1.a), channel_id=1, source_target_pairs={{0,24},{4,28},{8,0},{12,4},{16,8},{20,12},{24,16},{28,20},{32,56},... | collective-permute-start | bytes 430088 | tf_op jit(solution)/shard_map/ppermute | solution.py:65
  60.1 5.9 %queries.1.fq_ref.refs_8_ = bf16[560,2048]{1,0:T(8,128)(2,1)S(1)} custom-call(s32[3]{0:T(128)S(1)} %pad_add_fusion.pos, bf16[288,640]{1,0:T(8,128)(2,1)S(1)} %collective-permute-done.5.refs_0_, bf16[288,640]{1,0:T(8,128)(2,1)S(1)} %collective-permute-done.6.refs_1_, bf16[288,640]{1,0:T(8,128)(2,1)S(1)} %collective-permute-done.7.refs_2_, ...), custom_call_target="tpu_custom_call" | custom-call | flops 1 | bytes 1 | tf_op jit(solution)/shard_map/queries/pallas_call | solution.py:150
  66.0 1.1 %collective-permute-done.15.b.refs_1_ = bf16[5,128,112]{2,1,0:T(8,128)(2,1)S(1)} collective-permute-done((bf16[5,128,112]{2,1,0:T(8,128)(2,1)S(1)}, bf16[5,128,112]{2,1,0:T(8,128)(2,1)S(1)}, u32[]{:S(2)}, u32[]{:S(2)}) %collective-permute-start.15) | collective-permute-done | bytes 143392 | tf_op jit(solution)/shard_map/ppermute | solution.py:65
  67.8 2.1 %collective-permute-start.21 = (bf16[5,128,112]{2,1,0:T(8,128)(2,1)S(1)}, bf16[5,128,112]{2,1,0:T(8,128)(2,1)S(1)}, u32[]{:S(2)}, u32[]{:S(2)}) collective-permute-start(bf16[5,128,112]{2,1,0:T(8,128)(2,1)S(1)} %row.1), channel_id=1, source_target_pairs={{0,32},{4,36},{8,40},{12,44},{16,48},{20,52},{24,56},{28,60},{32,6... | collective-permute-start | bytes 430088 | tf_op jit(solution)/shard_map/ppermute | solution.py:65
  69.9 3.2 %collective-permute-start.22 = (bf16[5,128,112]{2,1,0:T(8,128)(2,1)S(1)}, bf16[5,128,112]{2,1,0:T(8,128)(2,1)S(1)}, u32[]{:S(2)}, u32[]{:S(2)}) collective-permute-start(bf16[5,128,112]{2,1,0:T(8,128)(2,1)S(1)} %row.1), channel_id=1, source_target_pairs={{0,64},{4,68},{8,72},{12,76},{16,80},{20,84},{24,88},{28,92},{32,9... | collective-permute-start | bytes 430088 | tf_op jit(solution)/shard_map/ppermute | solution.py:65
  73.1 1.3 %collective-permute-start.23 = (bf16[5,128,112]{2,1,0:T(8,128)(2,1)S(1)}, bf16[5,128,112]{2,1,0:T(8,128)(2,1)S(1)}, u32[]{:S(2)}, u32[]{:S(2)}) collective-permute-start(bf16[5,128,112]{2,1,0:T(8,128)(2,1)S(1)} %row.1), channel_id=1, source_target_pairs={{0,96},{4,100},{8,104},{12,108},{16,112},{20,116},{24,120},{28,124... | collective-permute-start | bytes 430088 | tf_op jit(solution)/shard_map/ppermute | solution.py:65
  74.4 5.9 %attend.1.refs_9_ = f32[5,128,2048]{2,1,0:T(8,128)S(1)} custom-call(s32[4]{0:T(128)S(1)} %copy-done.1, bf16[5,2048,112]{2,1,0:T(8,128)(2,1)S(1)} %get-tuple-element.66.fk_ref, bf16[5,128,2048]{2,1,0:T(8,128)(2,1)S(1)} %get-tuple-element.67.v_ref, bf16[560,2048]{1,0:T(8,128)(2,1)S(1)} %queries.1.fq_ref.refs_8_), custom_call_target="tpu_custom_call" | custom-call | flops 1 | bytes 1 | tf_op jit(solution)/shard_map/attend/pallas_call | solution.py:150
  80.4 2.3 %join.1 = (f32[560,2048]{1,0:T(8,128)S(1)}, f32[1,2048]{1,0:T(1,128)S(1)}) custom-call(s32[3]{0:T(128)S(1)} %pad_add_fusion.pos, f32[5]{0:T(128)S(1)} %copy-done.2, bf16[5,128,112]{2,1,0:T(8,128)(2,1)S(1)} %collective-permute-done.14.other_ref.refs_0_, bf16[5,128,112]{2,1,0:T(8,128)(2,1)S(1)} %collective-permute-done.15.b.refs_1_, ...), custom_call_target="tpu_custom_call" | custom-call | flops 1 | bytes 1 | tf_op jit(solution)/shard_map/join/pallas_call | solution.py:150
  82.7 2.0 %collective-permute-start.24 = (f32[1,2048]{1,0:T(1,128)S(1)}, f32[1,2048]{1,0:T(1,128)S(1)}, u32[]{:S(2)}, u32[]{:S(2)}) collective-permute-start(f32[1,2048]{1,0:T(1,128)S(1)} %get-tuple-element.69.s0), channel_id=1, source_target_pairs={{0,1},{1,2},{2,3},{3,0},{4,5},{5,6},{6,7},{7,4},{8,9},{9,10},{10,1... | collective-permute-start | bytes 24584 | tf_op jit(solution)/shard_map/ppermute | solution.py:447
  84.7 3.6 %collective-permute-start.25 = (f32[1,2048]{1,0:T(1,128)S(1)}, f32[1,2048]{1,0:T(1,128)S(1)}, u32[]{:S(2)}, u32[]{:S(2)}) collective-permute-start(f32[1,2048]{1,0:T(1,128)S(1)} %get-tuple-element.69.s0), channel_id=1, source_target_pairs={{0,2},{1,3},{2,0},{3,1},{4,6},{5,7},{6,4},{7,5},{8,10},{9,11},{10,... | collective-permute-start | bytes 24584 | tf_op jit(solution)/shard_map/ppermute | solution.py:447
  88.3 1.0 %collective-permute-start.26 = (f32[1,2048]{1,0:T(1,128)S(1)}, f32[1,2048]{1,0:T(1,128)S(1)}, u32[]{:S(2)}, u32[]{:S(2)}) collective-permute-start(f32[1,2048]{1,0:T(1,128)S(1)} %get-tuple-element.69.s0), channel_id=1, source_target_pairs={{0,3},{1,0},{2,1},{3,2},{4,7},{5,4},{6,5},{7,6},{8,11},{9,8},{10,9... | collective-permute-start | bytes 24584 | tf_op jit(solution)/shard_map/ppermute | solution.py:447
  90.0 1.9 %collective-permute-done.26.s3 = f32[1,2048]{1,0:T(1,128)S(1)} collective-permute-done((f32[1,2048]{1,0:T(1,128)S(1)}, f32[1,2048]{1,0:T(1,128)S(1)}, u32[]{:S(2)}, u32[]{:S(2)}) %collective-permute-start.26) | collective-permute-done | bytes 8224 | tf_op jit(solution)/shard_map/ppermute | solution.py:447
  91.9 1.9 %norm.1 = bf16[560,2048]{1,0:T(8,128)(2,1)} custom-call(f32[560,2048]{1,0:T(8,128)S(1)} %get-tuple-element.68.out_ref, f32[1,2048]{1,0:T(1,128)S(1)} %get-tuple-element.69.s0, f32[1,2048]{1,0:T(1,128)S(1)} %collective-permute-done.24.s1, f32[1,2048]{1,0:T(1,128)S(1)} %collective-permute-done.25.s2, f32[1,2048]{1,0:T(1,128)S(1)} %collective-permute-done.26.s3, ...), custom_call_target="tpu_custom_call" | custom-call | flops 1 | bytes 1 | tf_op jit(solution)/shard_map/norm/pallas_call | solution.py:395
  (40 shorter events, 3.8 us)
Async XLA Ops:
  0.0 7.7 %collective-permute-start = (bf16[70,1680]{1,0:T(8,128)(2,1)}, bf16[70,1680]{1,0:T(8,128)(2,1)S(1)}, u32[]{:S(2)}, u32[]{:S(2)}) collective-permute-start(bf16[70,1680]{1,0:T(8,128)(2,1)} %a0.1), channel_id=1, source_target_pairs={{0,8},{4,36},{8,16},{12,44},{16,24},{20,52},{24,0},{28,60},{32,40}... | collective-permute-start | bytes 705608 | tf_op jit(solution)/shard_map/ppermute | solution.py:65
  1.6 10.0 %collective-permute-start.1 = (bf16[70,1680]{1,0:T(8,128)(2,1)}, bf16[70,1680]{1,0:T(8,128)(2,1)S(1)}, u32[]{:S(2)}, u32[]{:S(2)}) collective-permute-start(bf16[70,1680]{1,0:T(8,128)(2,1)} %a0.1), channel_id=1, source_target_pairs={{0,16},{4,68},{8,24},{12,76},{16,0},{20,84},{24,8},{28,92},{32,48}... | collective-permute-start | bytes 705608 | tf_op jit(solution)/shard_map/ppermute | solution.py:65
  4.3 7.3 %collective-permute-start.2 = (bf16[70,1680]{1,0:T(8,128)(2,1)}, bf16[70,1680]{1,0:T(8,128)(2,1)S(1)}, u32[]{:S(2)}, u32[]{:S(2)}) collective-permute-start(bf16[70,1680]{1,0:T(8,128)(2,1)} %a0.1), channel_id=1, source_target_pairs={{0,24},{4,100},{8,0},{12,108},{16,8},{20,116},{24,16},{28,124},{32... | collective-permute-start | bytes 705608 | tf_op jit(solution)/shard_map/ppermute | solution.py:65
  11.6 0.9 %copy-start = (bf16[70,1680]{1,0:T(8,128)(2,1)S(1)}, bf16[70,1680]{1,0:T(8,128)(2,1)}, u32[]{:S(2)}) copy-start(bf16[70,1680]{1,0:T(8,128)(2,1)} %a0.1) | copy-start | bytes 705604
  14.0 12.2 %collective-permute-start.3 = (bf16[288,1152]{1,0:T(8,128)(2,1)S(1)}, bf16[288,1152]{1,0:T(8,128)(2,1)S(1)}, u32[]{:S(2)}, u32[]{:S(2)}) collective-permute-start(bf16[288,1152]{1,0:T(8,128)(2,1)S(1)} %get-tuple-element.41.refs_0_), channel_id=1, source_target_pairs={{0,4},{4,0},{8,12},{12,8},{16,20},{20,16},{24,28},{28,24},{32,36},... | collective-permute-start | bytes 1990664 | tf_op jit(solution)/shard_map/ppermute | solution.py:65
  14.1 18.4 %collective-permute-start.10 = (bf16[288,1152]{1,0:T(8,128)(2,1)S(1)}, bf16[288,1152]{1,0:T(8,128)(2,1)S(1)}, u32[]{:S(2)}, u32[]{:S(2)}) collective-permute-start(bf16[288,1152]{1,0:T(8,128)(2,1)S(1)} %get-tuple-element.41.refs_0_), channel_id=1, source_target_pairs={{0,96},{4,28},{8,104},{12,4},{16,112},{20,12},{24,120},{28,20},{32... | collective-permute-start | bytes 1990664 | tf_op jit(solution)/shard_map/ppermute | solution.py:65
  17.2 19.0 %collective-permute-start.8 = (bf16[288,1152]{1,0:T(8,128)(2,1)S(1)}, bf16[288,1152]{1,0:T(8,128)(2,1)S(1)}, u32[]{:S(2)}, u32[]{:S(2)}) collective-permute-start(bf16[288,1152]{1,0:T(8,128)(2,1)S(1)} %get-tuple-element.41.refs_0_), channel_id=1, source_target_pairs={{0,32},{4,12},{8,40},{12,20},{16,48},{20,28},{24,56},{28,4},{32,64... | collective-permute-start | bytes 1990664 | tf_op jit(solution)/shard_map/ppermute | solution.py:65
  17.2 19.0 %collective-permute-start.9 = (bf16[288,1152]{1,0:T(8,128)(2,1)S(1)}, bf16[288,1152]{1,0:T(8,128)(2,1)S(1)}, u32[]{:S(2)}, u32[]{:S(2)}) collective-permute-start(bf16[288,1152]{1,0:T(8,128)(2,1)S(1)} %get-tuple-element.41.refs_0_), channel_id=1, source_target_pairs={{0,64},{4,20},{8,72},{12,28},{16,80},{20,4},{24,88},{28,12},{32,96... | collective-permute-start | bytes 1990664 | tf_op jit(solution)/shard_map/ppermute | solution.py:65
  19.4 6.8 %collective-permute-start.4 = (bf16[288,640]{1,0:T(8,128)(2,1)S(1)}, bf16[288,640]{1,0:T(8,128)(2,1)S(1)}, u32[]{:S(2)}, u32[]{:S(2)}) collective-permute-start(bf16[288,640]{1,0:T(8,128)(2,1)S(1)} %get-tuple-element.45.refs_2_), channel_id=1, source_target_pairs={{0,4},{4,0},{8,12},{12,8},{16,20},{20,16},{24,28},{28,24},{32,36},... | collective-permute-start | bytes 1105928 | tf_op jit(solution)/shard_map/ppermute | solution.py:65
  36.2 3.5 %collective-permute-start.11 = (bf16[288,1152]{1,0:T(8,128)(2,1)S(1)}, bf16[288,1152]{1,0:T(8,128)(2,1)S(1)}, u32[]{:S(2)}, u32[]{:S(2)}) collective-permute-start(bf16[288,1152]{1,0:T(8,128)(2,1)S(1)} %collective-permute-done.8.refs_0_), channel_id=1, source_target_pairs={{0,4},{4,0},{8,12},{12,8},{16,20},{20,16},{24,28},{28,24},{32,36},... | collective-permute-start | bytes 1990664 | tf_op jit(solution)/shard_map/ppermute | solution.py:65
  36.2 4.9 %collective-permute-start.12 = (bf16[288,1152]{1,0:T(8,128)(2,1)S(1)}, bf16[288,1152]{1,0:T(8,128)(2,1)S(1)}, u32[]{:S(2)}, u32[]{:S(2)}) collective-permute-start(bf16[288,1152]{1,0:T(8,128)(2,1)S(1)} %collective-permute-done.9.refs_1_), channel_id=1, source_target_pairs={{0,4},{4,0},{8,12},{12,8},{16,20},{20,16},{24,28},{28,24},{32,36},... | collective-permute-start | bytes 1990664 | tf_op jit(solution)/shard_map/ppermute | solution.py:65
  36.7 4.4 %collective-permute-start.13 = (bf16[288,1152]{1,0:T(8,128)(2,1)S(1)}, bf16[288,1152]{1,0:T(8,128)(2,1)S(1)}, u32[]{:S(2)}, u32[]{:S(2)}) collective-permute-start(bf16[288,1152]{1,0:T(8,128)(2,1)S(1)} %collective-permute-done.10.refs_2_), channel_id=1, source_target_pairs={{0,4},{4,0},{8,12},{12,8},{16,20},{20,16},{24,28},{28,24},{32,36},... | collective-permute-start | bytes 1990664 | tf_op jit(solution)/shard_map/ppermute | solution.py:65
  36.7 17.4 %collective-permute-start.5 = (bf16[288,640]{1,0:T(8,128)(2,1)S(1)}, bf16[288,640]{1,0:T(8,128)(2,1)S(1)}, u32[]{:S(2)}, u32[]{:S(2)}) collective-permute-start(bf16[288,640]{1,0:T(8,128)(2,1)S(1)} %get-tuple-element.45.refs_2_), channel_id=1, source_target_pairs={{0,32},{4,12},{8,40},{12,20},{16,48},{20,28},{24,56},{28,4},{32,64... | collective-permute-start | bytes 1105928 | tf_op jit(solution)/shard_map/ppermute | solution.py:65
  36.8 17.3 %collective-permute-start.6 = (bf16[288,640]{1,0:T(8,128)(2,1)S(1)}, bf16[288,640]{1,0:T(8,128)(2,1)S(1)}, u32[]{:S(2)}, u32[]{:S(2)}) collective-permute-start(bf16[288,640]{1,0:T(8,128)(2,1)S(1)} %get-tuple-element.45.refs_2_), channel_id=1, source_target_pairs={{0,64},{4,20},{8,72},{12,28},{16,80},{20,4},{24,88},{28,12},{32,96... | collective-permute-start | bytes 1105928 | tf_op jit(solution)/shard_map/ppermute | solution.py:65
  39.7 14.4 %collective-permute-start.7 = (bf16[288,640]{1,0:T(8,128)(2,1)S(1)}, bf16[288,640]{1,0:T(8,128)(2,1)S(1)}, u32[]{:S(2)}, u32[]{:S(2)}) collective-permute-start(bf16[288,640]{1,0:T(8,128)(2,1)S(1)} %get-tuple-element.45.refs_2_), channel_id=1, source_target_pairs={{0,96},{4,28},{8,104},{12,4},{16,112},{20,12},{24,120},{28,20},{32... | collective-permute-start | bytes 1105928 | tf_op jit(solution)/shard_map/ppermute | solution.py:65
  53.1 2.0 %collective-permute-start.14 = (bf16[5,128,112]{2,1,0:T(8,128)(2,1)S(1)}, bf16[5,128,112]{2,1,0:T(8,128)(2,1)S(1)}, u32[]{:S(2)}, u32[]{:S(2)}) collective-permute-start(bf16[5,128,112]{2,1,0:T(8,128)(2,1)S(1)} %get-tuple-element.51.tot_ref), channel_id=1, source_target_pairs={{0,4},{4,0},{8,12},{12,8},{16,20},{20,16},{24,28},{28,24},{32,36},... | collective-permute-start | bytes 430088 | tf_op jit(solution)/shard_map/ppermute | solution.py:65
  55.1 3.4 %collective-permute-start.18 = (bf16[288,640]{1,0:T(8,128)(2,1)S(1)}, bf16[288,640]{1,0:T(8,128)(2,1)S(1)}, u32[]{:S(2)}, u32[]{:S(2)}) collective-permute-start(bf16[288,640]{1,0:T(8,128)(2,1)S(1)} %collective-permute-done.5.refs_0_), channel_id=1, source_target_pairs={{0,4},{4,0},{8,12},{12,8},{16,20},{20,16},{24,28},{28,24},{32,36},... | collective-permute-start | bytes 1105928 | tf_op jit(solution)/shard_map/ppermute | solution.py:65
  55.5 4.6 %collective-permute-start.19 = (bf16[288,640]{1,0:T(8,128)(2,1)S(1)}, bf16[288,640]{1,0:T(8,128)(2,1)S(1)}, u32[]{:S(2)}, u32[]{:S(2)}) collective-permute-start(bf16[288,640]{1,0:T(8,128)(2,1)S(1)} %collective-permute-done.6.refs_1_), channel_id=1, source_target_pairs={{0,4},{4,0},{8,12},{12,8},{16,20},{20,16},{24,28},{28,24},{32,36},... | collective-permute-start | bytes 1105928 | tf_op jit(solution)/shard_map/ppermute | solution.py:65
  55.6 4.5 %collective-permute-start.20 = (bf16[288,640]{1,0:T(8,128)(2,1)S(1)}, bf16[288,640]{1,0:T(8,128)(2,1)S(1)}, u32[]{:S(2)}, u32[]{:S(2)}) collective-permute-start(bf16[288,640]{1,0:T(8,128)(2,1)S(1)} %collective-permute-done.7.refs_2_), channel_id=1, source_target_pairs={{0,4},{4,0},{8,12},{12,8},{16,20},{20,16},{24,28},{28,24},{32,36},... | collective-permute-start | bytes 1105928 | tf_op jit(solution)/shard_map/ppermute | solution.py:65
  56.0 18.4 %copy-start.1 = (s32[4]{0:T(128)S(1)}, s32[4]{0:T(128)}, u32[]{:S(2)}) copy-start(s32[4]{0:T(128)} %codes.1) | copy-start | bytes 52
  56.1 11.0 %collective-permute-start.15 = (bf16[5,128,112]{2,1,0:T(8,128)(2,1)S(1)}, bf16[5,128,112]{2,1,0:T(8,128)(2,1)S(1)}, u32[]{:S(2)}, u32[]{:S(2)}) collective-permute-start(bf16[5,128,112]{2,1,0:T(8,128)(2,1)S(1)} %chip.1.a), channel_id=1, source_target_pairs={{0,8},{4,12},{8,16},{12,20},{16,24},{20,28},{24,0},{28,4},{32,40},... | collective-permute-start | bytes 430088 | tf_op jit(solution)/shard_map/ppermute | solution.py:65
  56.6 10.5 %collective-permute-start.16 = (bf16[5,128,112]{2,1,0:T(8,128)(2,1)S(1)}, bf16[5,128,112]{2,1,0:T(8,128)(2,1)S(1)}, u32[]{:S(2)}, u32[]{:S(2)}) collective-permute-start(bf16[5,128,112]{2,1,0:T(8,128)(2,1)S(1)} %chip.1.a), channel_id=1, source_target_pairs={{0,16},{4,20},{8,24},{12,28},{16,0},{20,4},{24,8},{28,12},{32,48},... | collective-permute-start | bytes 430088 | tf_op jit(solution)/shard_map/ppermute | solution.py:65
  58.6 9.2 %collective-permute-start.17 = (bf16[5,128,112]{2,1,0:T(8,128)(2,1)S(1)}, bf16[5,128,112]{2,1,0:T(8,128)(2,1)S(1)}, u32[]{:S(2)}, u32[]{:S(2)}) collective-permute-start(bf16[5,128,112]{2,1,0:T(8,128)(2,1)S(1)} %chip.1.a), channel_id=1, source_target_pairs={{0,24},{4,28},{8,0},{12,4},{16,8},{20,12},{24,16},{28,20},{32,56},... | collective-permute-start | bytes 430088 | tf_op jit(solution)/shard_map/ppermute | solution.py:65
  67.8 12.6 %collective-permute-start.21 = (bf16[5,128,112]{2,1,0:T(8,128)(2,1)S(1)}, bf16[5,128,112]{2,1,0:T(8,128)(2,1)S(1)}, u32[]{:S(2)}, u32[]{:S(2)}) collective-permute-start(bf16[5,128,112]{2,1,0:T(8,128)(2,1)S(1)} %row.1), channel_id=1, source_target_pairs={{0,32},{4,36},{8,40},{12,44},{16,48},{20,52},{24,56},{28,60},{32,6... | collective-permute-start | bytes 430088 | tf_op jit(solution)/shard_map/ppermute | solution.py:65
  69.9 10.5 %collective-permute-start.22 = (bf16[5,128,112]{2,1,0:T(8,128)(2,1)S(1)}, bf16[5,128,112]{2,1,0:T(8,128)(2,1)S(1)}, u32[]{:S(2)}, u32[]{:S(2)}) collective-permute-start(bf16[5,128,112]{2,1,0:T(8,128)(2,1)S(1)} %row.1), channel_id=1, source_target_pairs={{0,64},{4,68},{8,72},{12,76},{16,80},{20,84},{24,88},{28,92},{32,9... | collective-permute-start | bytes 430088 | tf_op jit(solution)/shard_map/ppermute | solution.py:65
  73.1 7.3 %collective-permute-start.23 = (bf16[5,128,112]{2,1,0:T(8,128)(2,1)S(1)}, bf16[5,128,112]{2,1,0:T(8,128)(2,1)S(1)}, u32[]{:S(2)}, u32[]{:S(2)}) collective-permute-start(bf16[5,128,112]{2,1,0:T(8,128)(2,1)S(1)} %row.1), channel_id=1, source_target_pairs={{0,96},{4,100},{8,104},{12,108},{16,112},{20,116},{24,120},{28,124... | collective-permute-start | bytes 430088 | tf_op jit(solution)/shard_map/ppermute | solution.py:65
  74.4 6.0 %copy-start.2 = (f32[5]{0:T(128)S(1)}, f32[5]{0:T(128)}, u32[]{:S(2)}) copy-start(f32[5]{0:T(128)} %scale.1) | copy-start | bytes 64
  82.7 6.6 %collective-permute-start.24 = (f32[1,2048]{1,0:T(1,128)S(1)}, f32[1,2048]{1,0:T(1,128)S(1)}, u32[]{:S(2)}, u32[]{:S(2)}) collective-permute-start(f32[1,2048]{1,0:T(1,128)S(1)} %get-tuple-element.69.s0), channel_id=1, source_target_pairs={{0,1},{1,2},{2,3},{3,0},{4,5},{5,6},{6,7},{7,4},{8,9},{9,10},{10,1... | collective-permute-start | bytes 24584 | tf_op jit(solution)/shard_map/ppermute | solution.py:447
  84.7 5.3 %collective-permute-start.25 = (f32[1,2048]{1,0:T(1,128)S(1)}, f32[1,2048]{1,0:T(1,128)S(1)}, u32[]{:S(2)}, u32[]{:S(2)}) collective-permute-start(f32[1,2048]{1,0:T(1,128)S(1)} %get-tuple-element.69.s0), channel_id=1, source_target_pairs={{0,2},{1,3},{2,0},{3,1},{4,6},{5,7},{6,4},{7,5},{8,10},{9,11},{10,... | collective-permute-start | bytes 24584 | tf_op jit(solution)/shard_map/ppermute | solution.py:447
  88.3 3.7 %collective-permute-start.26 = (f32[1,2048]{1,0:T(1,128)S(1)}, f32[1,2048]{1,0:T(1,128)S(1)}, u32[]{:S(2)}, u32[]{:S(2)}) collective-permute-start(f32[1,2048]{1,0:T(1,128)S(1)} %get-tuple-element.69.s0), channel_id=1, source_target_pairs={{0,3},{1,0},{2,1},{3,2},{4,7},{5,4},{6,5},{7,6},{8,11},{9,8},{10,9... | collective-permute-start | bytes 24584 | tf_op jit(solution)/shard_map/ppermute | solution.py:447

commit v11 on v10

--- a/solution.py
+++ b/solution.py
@@ -90,6 +90,25 @@
         10,
         "pack",
     )
+
+
+def stage_kernel(w_ref, o_ref, sem):
+    copy = pltpu.make_async_copy(w_ref, o_ref, sem)
+    copy.start()
+    copy.wait()
+
+
+def stage(w):
+    return pl.pallas_call(
+        stage_kernel,
+        in_specs=[pl.BlockSpec(memory_space=pl.ANY)],
+        out_specs=pl.BlockSpec(memory_space=pltpu.VMEM),
+        out_shape=pltpu.VMEM(w.shape, w.dtype),
+        scratch_shapes=[pltpu.SemaphoreType.DMA],
+        compiler_params=pltpu.CompilerParams(vmem_limit_bytes=4 * MIB),
+        cost_estimate=QUICK,
+        name="stage",
+    )(pltpu.with_memory_space_constraint(w, pltpu.HBM))
 
 
 def spread_kernel(x_ref, o_ref):
@@ -412,7 +431,7 @@
     y, x, core = me // 8, (me // 2) % 4, me % 2
     pos = jnp.stack([y, x, core])
     pos, gain = lax.optimization_barrier((pos, norm_gain.reshape(HL, DH)))
-    shards = [qkv_weight] + [shift(qkv_weight, first_leg(d)) for d in (1, 2, 3)]
+    shards = [stage(qkv_weight)] + [shift(qkv_weight, first_leg(d)) for d in (1, 2, 3)]
     near_kv, near_q = pack(pos, shards)
     near_kv, xt = lax.optimization_barrier((near_kv, tokens.T))
     own_kv = [near_kv] + [shift(near_kv, second_leg(d)) for d in (1, 2, 3)]

time: 94.3 us -> 93.3 us (0.989)
  waiting for transfers between devices: 14.2 us -> 13.2 us
  local copies, waits for them, and re-layouts: 1.72 us -> 0.77 us
    ppermute x24, waiting for transfers between devices: 11.6 us -> 10.6 us  [shift(): return lax.ppermute(a, 'tm', moves)]
    pallas_call x0 -> x1, Pallas kernels: none -> 0.99 us  [stage(): pl.pallas_call(stage_kernel, in_specs=[pl.BlockSpec(memory_space=pl.ANY)]...]
    unnamed x6 -> x4, local copies, waits for them, and re-layouts: 0.96 us -> 0.01 us
  transfers between devices with their start and end apart: 27 -> 27, of which waited for: 9 -> 9; matrix products, arithmetic and copies ran while one was open for 1% -> 1% of each run, Pallas kernels for 39% -> 41%
where the time goes in v11:
time: 93.3 us; the launch traced here: 93 us
  Pallas kernels  43.5 us (47%)
  starting transfers between devices  35 us (38%)
  waiting for transfers between devices  13.2 us (14%)
    pallas_call x8, Pallas kernels, resident(): pl.pallas_call(kernel, in_specs=[pl.BlockSpec(memory_space=pltpu.SMEM)] *...  33.9 us
    ppermute x24, starting transfers between devices, shift(): return lax.ppermute(a, 'tm', moves)  28.4 us
    ppermute x24, waiting for transfers between devices, shift(): return lax.ppermute(a, 'tm', moves)  10.6 us
    pallas_call x1, Pallas kernels, spread(): pl.pallas_call(spread_kernel, grid=(n // blk,), in_specs=[pl.BlockSpec((D...  6.8 us
    ppermute x3, starting transfers between devices, body(): lax.ppermute(squares, 'head', [(i, (i + d) % 4) for i in range(4)])  6.6 us
    ppermute x3, waiting for transfers between devices, body(): lax.ppermute(squares, 'head', [(i, (i + d) % 4) for i in range(4)])  2.63 us
  transfers between devices with their start and end apart: 27, of which 9 were waited for; matrix products, arithmetic and copies ran while one was open for 1% of the time, Pallas kernels for 41%

profile of v11, /device:TPU:0, one launch (start us, length us, event | category | flops | bytes accessed | tf_op | source)
XLA Modules:
  0.0 93.0 jit_solution(3595279022600640071)
XLA Ops:
  0.0 1.6 %collective-permute-start = (bf16[70,1680]{1,0:T(8,128)(2,1)}, bf16[70,1680]{1,0:T(8,128)(2,1)S(1)}, u32[]{:S(2)}, u32[]{:S(2)}) collective-permute-start(bf16[70,1680]{1,0:T(8,128)(2,1)} %w_ref.1), channel_id=1, source_target_pairs={{0,8},{4,36},{8,16},{12,44},{16,24},{20,52},{24,0},{28,60},{32,40}... | collective-permute-start | bytes 705608 | tf_op jit(solution)/shard_map/ppermute | solution.py:65
  1.6 2.7 %collective-permute-start.1 = (bf16[70,1680]{1,0:T(8,128)(2,1)}, bf16[70,1680]{1,0:T(8,128)(2,1)S(1)}, u32[]{:S(2)}, u32[]{:S(2)}) collective-permute-start(bf16[70,1680]{1,0:T(8,128)(2,1)} %w_ref.1), channel_id=1, source_target_pairs={{0,16},{4,68},{8,24},{12,76},{16,0},{20,84},{24,8},{28,92},{32,48}... | collective-permute-start | bytes 705608 | tf_op jit(solution)/shard_map/ppermute | solution.py:65
  4.3 1.4 %collective-permute-start.2 = (bf16[70,1680]{1,0:T(8,128)(2,1)}, bf16[70,1680]{1,0:T(8,128)(2,1)S(1)}, u32[]{:S(2)}, u32[]{:S(2)}) collective-permute-start(bf16[70,1680]{1,0:T(8,128)(2,1)} %w_ref.1), channel_id=1, source_target_pairs={{0,24},{4,100},{8,0},{12,108},{16,8},{20,116},{24,16},{28,124},{32... | collective-permute-start | bytes 705608 | tf_op jit(solution)/shard_map/ppermute | solution.py:65
  5.7 1.0 %stage.1.a0 = bf16[70,1680]{1,0:T(8,128)(2,1)S(1)} custom-call(bf16[70,1680]{1,0:T(8,128)(2,1)} %w_ref.1), custom_call_target="tpu_custom_call" | custom-call | flops 1 | bytes 1 | tf_op jit(solution)/shard_map/stage/pallas_call | solution.py:102
  6.8 0.8 reshape.3.gain_ref
  7.8 3.8 %collective-permute-done.1.a2 = bf16[70,1680]{1,0:T(8,128)(2,1)S(1)} collective-permute-done((bf16[70,1680]{1,0:T(8,128)(2,1)}, bf16[70,1680]{1,0:T(8,128)(2,1)S(1)}, u32[]{:S(2)}, u32[]{:S(2)}) %collective-permute-start.1) | collective-permute-done | bytes 235232 | tf_op jit(solution)/shard_map/ppermute | solution.py:65
  11.6 1.4 %pack.1 = (bf16[288,1152]{1,0:T(8,128)(2,1)S(1)}, bf16[288,640]{1,0:T(8,128)(2,1)S(1)}) custom-call(s32[3]{0:T(128)S(1)} %pad_add_fusion.pos, bf16[70,1680]{1,0:T(8,128)(2,1)S(1)} %stage.1.a0, bf16[70,1680]{1,0:T(8,128)(2,1)S(1)} %collective-permute-done.a1, bf16[70,1680]{1,0:T(8,128)(2,1)S(1)} %collective-permute-done.1.a2, ...), custom_call_target="tpu_custom_call" | custom-call | flops 1 | bytes 1 | tf_op jit(solution)/shard_map/pack/pallas_call | solution.py:169
  13.1 3.1 %collective-permute-start.10 = (bf16[288,1152]{1,0:T(8,128)(2,1)S(1)}, bf16[288,1152]{1,0:T(8,128)(2,1)S(1)}, u32[]{:S(2)}, u32[]{:S(2)}) collective-permute-start(bf16[288,1152]{1,0:T(8,128)(2,1)S(1)} %get-tuple-element.41.refs_0_), channel_id=1, source_target_pairs={{0,96},{4,28},{8,104},{12,4},{16,112},{20,12},{24,120},{28,20},{32... | collective-permute-start | bytes 1990664 | tf_op jit(solution)/shard_map/ppermute | solution.py:65
  16.2 2.2 %collective-permute-start.9 = (bf16[288,1152]{1,0:T(8,128)(2,1)S(1)}, bf16[288,1152]{1,0:T(8,128)(2,1)S(1)}, u32[]{:S(2)}, u32[]{:S(2)}) collective-permute-start(bf16[288,1152]{1,0:T(8,128)(2,1)S(1)} %get-tuple-element.41.refs_0_), channel_id=1, source_target_pairs={{0,64},{4,20},{8,72},{12,28},{16,80},{20,4},{24,88},{28,12},{32,96... | collective-permute-start | bytes 1990664 | tf_op jit(solution)/shard_map/ppermute | solution.py:65
  18.4 6.8 %spread.1.refs_4_.refs_6_ = bf16[8,288,2048]{2,1,0:T(8,128)(2,1)S(1)} custom-call(bf16[2240,2048]{1,0:T(8,128)(2,1)} %bitcast.5), custom_call_target="tpu_custom_call" | custom-call | flops 1 | bytes 1 | tf_op jit(solution)/shard_map/spread/pallas_call | solution.py:129
  25.3 6.1 %part_first.1 = (f32[1120,2048]{1,0:T(8,128)S(1)}, f32[560,2048]{1,0:T(8,128)S(1)}) custom-call(s32[3]{0:T(128)S(1)} %pad_add_fusion.pos, bf16[288,1152]{1,0:T(8,128)(2,1)S(1)} %get-tuple-element.41.refs_0_, bf16[288,1152]{1,0:T(8,128)(2,1)S(1)} %collective-permute-done.3.refs_1_, bf16[288,640]{1,0:T(8,128)(2,1)S(1)} %get-tuple-element.45.refs_2_, ...), custom_call_target="tpu_custom_call" | custom-call | flops 1 | bytes 1 | tf_op jit(solution)/shard_map/part_first/pallas_call | solution.py:169
  31.5 3.7 %collective-permute-done.8.refs_0_ = bf16[288,1152]{1,0:T(8,128)(2,1)S(1)} collective-permute-done((bf16[288,1152]{1,0:T(8,128)(2,1)S(1)}, bf16[288,1152]{1,0:T(8,128)(2,1)S(1)}, u32[]{:S(2)}, u32[]{:S(2)}) %collective-permute-start.8) | collective-permute-done | bytes 663584 | tf_op jit(solution)/shard_map/ppermute | solution.py:65
  35.8 2.9 %collective-permute-start.6 = (bf16[288,640]{1,0:T(8,128)(2,1)S(1)}, bf16[288,640]{1,0:T(8,128)(2,1)S(1)}, u32[]{:S(2)}, u32[]{:S(2)}) collective-permute-start(bf16[288,640]{1,0:T(8,128)(2,1)S(1)} %get-tuple-element.45.refs_2_), channel_id=1, source_target_pairs={{0,64},{4,20},{8,72},{12,28},{16,80},{20,4},{24,88},{28,12},{32,96... | collective-permute-start | bytes 1105928 | tf_op jit(solution)/shard_map/ppermute | solution.py:65
  38.7 1.3 %collective-permute-start.7 = (bf16[288,640]{1,0:T(8,128)(2,1)S(1)}, bf16[288,640]{1,0:T(8,128)(2,1)S(1)}, u32[]{:S(2)}, u32[]{:S(2)}) collective-permute-start(bf16[288,640]{1,0:T(8,128)(2,1)S(1)} %get-tuple-element.45.refs_2_), channel_id=1, source_target_pairs={{0,96},{4,28},{8,104},{12,4},{16,112},{20,12},{24,120},{28,20},{32... | collective-permute-start | bytes 1105928 | tf_op jit(solution)/shard_map/ppermute | solution.py:65
  40.1 12.1 %keys_values.1 = (bf16[5,2048,112]{2,1,0:T(8,128)(2,1)S(1)}, bf16[5,128,2048]{2,1,0:T(8,128)(2,1)S(1)}, f32[4,5,128,112]{3,2,1,0:T(8,128)S(1)}, bf16[5,128,112]{2,1,0:T(8,128)(2,1)S(1)}) custom-call(s32[3]{0:T(128)S(1)} %pad_add_fusion.pos, bf16[288,1152]{1,0:T(8,128)(2,1)S(1)} %collective-permute-done.8.refs_0_, ...), custom_call_target="tpu_custom_call" | custom-call | flops 1 | bytes 1 | tf_op jit(solution)/shard_map/keys_values/pallas_call | solution.py:169
  52.2 1.0 %collective-permute-start.14 = (bf16[5,128,112]{2,1,0:T(8,128)(2,1)S(1)}, bf16[5,128,112]{2,1,0:T(8,128)(2,1)S(1)}, u32[]{:S(2)}, u32[]{:S(2)}) collective-permute-start(bf16[5,128,112]{2,1,0:T(8,128)(2,1)S(1)} %get-tuple-element.51.tot_ref), channel_id=1, source_target_pairs={{0,4},{4,0},{8,12},{12,8},{16,20},{20,16},{24,28},{28,24},{32,36},... | collective-permute-start | bytes 430088 | tf_op jit(solution)/shard_map/ppermute | solution.py:65
  53.1 1.0 %collective-permute-done.14.other_ref.refs_0_ = bf16[5,128,112]{2,1,0:T(8,128)(2,1)S(1)} collective-permute-done((bf16[5,128,112]{2,1,0:T(8,128)(2,1)S(1)}, bf16[5,128,112]{2,1,0:T(8,128)(2,1)S(1)}, u32[]{:S(2)}, u32[]{:S(2)}) %collective-permute-start.14) | collective-permute-done | bytes 143392 | tf_op jit(solution)/shard_map/ppermute | solution.py:65
  55.6 2.0 %collective-permute-start.16 = (bf16[5,128,112]{2,1,0:T(8,128)(2,1)S(1)}, bf16[5,128,112]{2,1,0:T(8,128)(2,1)S(1)}, u32[]{:S(2)}, u32[]{:S(2)}) collective-permute-start(bf16[5,128,112]{2,1,0:T(8,128)(2,1)S(1)} %chip.1.a), channel_id=1, source_target_pairs={{0,16},{4,20},{8,24},{12,28},{16,0},{20,4},{24,8},{28,12},{32,48},... | collective-permute-start | bytes 430088 | tf_op jit(solution)/shard_map/ppermute | solution.py:65
  57.6 1.6 %collective-permute-start.17 = (bf16[5,128,112]{2,1,0:T(8,128)(2,1)S(1)}, bf16[5,128,112]{2,1,0:T(8,128)(2,1)S(1)}, u32[]{:S(2)}, u32[]{:S(2)}) collective-permute-start(bf16[5,128,112]{2,1,0:T(8,128)(2,1)S(1)} %chip.1.a), channel_id=1, source_target_pairs={{0,24},{4,28},{8,0},{12,4},{16,8},{20,12},{24,16},{28,20},{32,56},... | collective-permute-start | bytes 430088 | tf_op jit(solution)/shard_map/ppermute | solution.py:65
  59.2 5.9 %queries.1.fq_ref.refs_8_ = bf16[560,2048]{1,0:T(8,128)(2,1)S(1)} custom-call(s32[3]{0:T(128)S(1)} %pad_add_fusion.pos, bf16[288,640]{1,0:T(8,128)(2,1)S(1)} %collective-permute-done.5.refs_0_, bf16[288,640]{1,0:T(8,128)(2,1)S(1)} %collective-permute-done.6.refs_1_, bf16[288,640]{1,0:T(8,128)(2,1)S(1)} %collective-permute-done.7.refs_2_, ...), custom_call_target="tpu_custom_call" | custom-call | flops 1 | bytes 1 | tf_op jit(solution)/shard_map/queries/pallas_call | solution.py:169
  65.0 1.1 %collective-permute-done.15.b.refs_1_ = bf16[5,128,112]{2,1,0:T(8,128)(2,1)S(1)} collective-permute-done((bf16[5,128,112]{2,1,0:T(8,128)(2,1)S(1)}, bf16[5,128,112]{2,1,0:T(8,128)(2,1)S(1)}, u32[]{:S(2)}, u32[]{:S(2)}) %collective-permute-start.15) | collective-permute-done | bytes 143392 | tf_op jit(solution)/shard_map/ppermute | solution.py:65
  66.9 2.1 %collective-permute-start.21 = (bf16[5,128,112]{2,1,0:T(8,128)(2,1)S(1)}, bf16[5,128,112]{2,1,0:T(8,128)(2,1)S(1)}, u32[]{:S(2)}, u32[]{:S(2)}) collective-permute-start(bf16[5,128,112]{2,1,0:T(8,128)(2,1)S(1)} %row.1), channel_id=1, source_target_pairs={{0,32},{4,36},{8,40},{12,44},{16,48},{20,52},{24,56},{28,60},{32,6... | collective-permute-start | bytes 430088 | tf_op jit(solution)/shard_map/ppermute | solution.py:65
  68.9 3.2 %collective-permute-start.22 = (bf16[5,128,112]{2,1,0:T(8,128)(2,1)S(1)}, bf16[5,128,112]{2,1,0:T(8,128)(2,1)S(1)}, u32[]{:S(2)}, u32[]{:S(2)}) collective-permute-start(bf16[5,128,112]{2,1,0:T(8,128)(2,1)S(1)} %row.1), channel_id=1, source_target_pairs={{0,64},{4,68},{8,72},{12,76},{16,80},{20,84},{24,88},{28,92},{32,9... | collective-permute-start | bytes 430088 | tf_op jit(solution)/shard_map/ppermute | solution.py:65
  72.2 1.3 %collective-permute-start.23 = (bf16[5,128,112]{2,1,0:T(8,128)(2,1)S(1)}, bf16[5,128,112]{2,1,0:T(8,128)(2,1)S(1)}, u32[]{:S(2)}, u32[]{:S(2)}) collective-permute-start(bf16[5,128,112]{2,1,0:T(8,128)(2,1)S(1)} %row.1), channel_id=1, source_target_pairs={{0,96},{4,100},{8,104},{12,108},{16,112},{20,116},{24,120},{28,124... | collective-permute-start | bytes 430088 | tf_op jit(solution)/shard_map/ppermute | solution.py:65
  73.5 5.9 %attend.1.refs_9_ = f32[5,128,2048]{2,1,0:T(8,128)S(1)} custom-call(s32[4]{0:T(128)S(1)} %copy-done, bf16[5,2048,112]{2,1,0:T(8,128)(2,1)S(1)} %get-tuple-element.66.fk_ref, bf16[5,128,2048]{2,1,0:T(8,128)(2,1)S(1)} %get-tuple-element.67.v_ref, bf16[560,2048]{1,0:T(8,128)(2,1)S(1)} %queries.1.fq_ref.refs_8_), custom_call_target="tpu_custom_call" | custom-call | flops 1 | bytes 1 | tf_op jit(solution)/shard_map/attend/pallas_call | solution.py:169
  79.4 2.3 %join.1 = (f32[560,2048]{1,0:T(8,128)S(1)}, f32[1,2048]{1,0:T(1,128)S(1)}) custom-call(s32[3]{0:T(128)S(1)} %pad_add_fusion.pos, f32[5]{0:T(128)S(1)} %copy-done.1, bf16[5,128,112]{2,1,0:T(8,128)(2,1)S(1)} %collective-permute-done.14.other_ref.refs_0_, bf16[5,128,112]{2,1,0:T(8,128)(2,1)S(1)} %collective-permute-done.15.b.refs_1_, ...), custom_call_target="tpu_custom_call" | custom-call | flops 1 | bytes 1 | tf_op jit(solution)/shard_map/join/pallas_call | solution.py:169
  81.7 2.0 %collective-permute-start.24 = (f32[1,2048]{1,0:T(1,128)S(1)}, f32[1,2048]{1,0:T(1,128)S(1)}, u32[]{:S(2)}, u32[]{:S(2)}) collective-permute-start(f32[1,2048]{1,0:T(1,128)S(1)} %get-tuple-element.69.s0), channel_id=1, source_target_pairs={{0,1},{1,2},{2,3},{3,0},{4,5},{5,6},{6,7},{7,4},{8,9},{9,10},{10,1... | collective-permute-start | bytes 24584 | tf_op jit(solution)/shard_map/ppermute | solution.py:466
  83.7 3.6 %collective-permute-start.25 = (f32[1,2048]{1,0:T(1,128)S(1)}, f32[1,2048]{1,0:T(1,128)S(1)}, u32[]{:S(2)}, u32[]{:S(2)}) collective-permute-start(f32[1,2048]{1,0:T(1,128)S(1)} %get-tuple-element.69.s0), channel_id=1, source_target_pairs={{0,2},{1,3},{2,0},{3,1},{4,6},{5,7},{6,4},{7,5},{8,10},{9,11},{10,... | collective-permute-start | bytes 24584 | tf_op jit(solution)/shard_map/ppermute | solution.py:466
  87.3 1.0 %collective-permute-start.26 = (f32[1,2048]{1,0:T(1,128)S(1)}, f32[1,2048]{1,0:T(1,128)S(1)}, u32[]{:S(2)}, u32[]{:S(2)}) collective-permute-start(f32[1,2048]{1,0:T(1,128)S(1)} %get-tuple-element.69.s0), channel_id=1, source_target_pairs={{0,3},{1,0},{2,1},{3,2},{4,7},{5,4},{6,5},{7,6},{8,11},{9,8},{10,9... | collective-permute-start | bytes 24584 | tf_op jit(solution)/shard_map/ppermute | solution.py:466
  88.3 0.7 collective-permute-done.25.s2
  89.0 1.9 %collective-permute-done.26.s3 = f32[1,2048]{1,0:T(1,128)S(1)} collective-permute-done((f32[1,2048]{1,0:T(1,128)S(1)}, f32[1,2048]{1,0:T(1,128)S(1)}, u32[]{:S(2)}, u32[]{:S(2)}) %collective-permute-start.26) | collective-permute-done | bytes 8224 | tf_op jit(solution)/shard_map/ppermute | solution.py:466
  91.0 1.9 %norm.1 = bf16[560,2048]{1,0:T(8,128)(2,1)} custom-call(f32[560,2048]{1,0:T(8,128)S(1)} %get-tuple-element.68.out_ref, f32[1,2048]{1,0:T(1,128)S(1)} %get-tuple-element.69.s0, f32[1,2048]{1,0:T(1,128)S(1)} %collective-permute-done.24.s1, f32[1,2048]{1,0:T(1,128)S(1)} %collective-permute-done.25.s2, f32[1,2048]{1,0:T(1,128)S(1)} %collective-permute-done.26.s3, ...), custom_call_target="tpu_custom_call" | custom-call | flops 1 | bytes 1 | tf_op jit(solution)/shard_map/norm/pallas_call | solution.py:414
  (39 shorter events, 3.2 us)
Async XLA Ops:
  0.0 7.7 %collective-permute-start = (bf16[70,1680]{1,0:T(8,128)(2,1)}, bf16[70,1680]{1,0:T(8,128)(2,1)S(1)}, u32[]{:S(2)}, u32[]{:S(2)}) collective-permute-start(bf16[70,1680]{1,0:T(8,128)(2,1)} %w_ref.1), channel_id=1, source_target_pairs={{0,8},{4,36},{8,16},{12,44},{16,24},{20,52},{24,0},{28,60},{32,40}... | collective-permute-start | bytes 705608 | tf_op jit(solution)/shard_map/ppermute | solution.py:65
  1.6 10.0 %collective-permute-start.1 = (bf16[70,1680]{1,0:T(8,128)(2,1)}, bf16[70,1680]{1,0:T(8,128)(2,1)S(1)}, u32[]{:S(2)}, u32[]{:S(2)}) collective-permute-start(bf16[70,1680]{1,0:T(8,128)(2,1)} %w_ref.1), channel_id=1, source_target_pairs={{0,16},{4,68},{8,24},{12,76},{16,0},{20,84},{24,8},{28,92},{32,48}... | collective-permute-start | bytes 705608 | tf_op jit(solution)/shard_map/ppermute | solution.py:65
  4.3 7.3 %collective-permute-start.2 = (bf16[70,1680]{1,0:T(8,128)(2,1)}, bf16[70,1680]{1,0:T(8,128)(2,1)S(1)}, u32[]{:S(2)}, u32[]{:S(2)}) collective-permute-start(bf16[70,1680]{1,0:T(8,128)(2,1)} %w_ref.1), channel_id=1, source_target_pairs={{0,24},{4,100},{8,0},{12,108},{16,8},{20,116},{24,16},{28,124},{32... | collective-permute-start | bytes 705608 | tf_op jit(solution)/shard_map/ppermute | solution.py:65
  13.0 12.2 %collective-permute-start.3 = (bf16[288,1152]{1,0:T(8,128)(2,1)S(1)}, bf16[288,1152]{1,0:T(8,128)(2,1)S(1)}, u32[]{:S(2)}, u32[]{:S(2)}) collective-permute-start(bf16[288,1152]{1,0:T(8,128)(2,1)S(1)} %get-tuple-element.41.refs_0_), channel_id=1, source_target_pairs={{0,4},{4,0},{8,12},{12,8},{16,20},{20,16},{24,28},{28,24},{32,36},... | collective-permute-start | bytes 1990664 | tf_op jit(solution)/shard_map/ppermute | solution.py:65
  13.1 18.4 %collective-permute-start.10 = (bf16[288,1152]{1,0:T(8,128)(2,1)S(1)}, bf16[288,1152]{1,0:T(8,128)(2,1)S(1)}, u32[]{:S(2)}, u32[]{:S(2)}) collective-permute-start(bf16[288,1152]{1,0:T(8,128)(2,1)S(1)} %get-tuple-element.41.refs_0_), channel_id=1, source_target_pairs={{0,96},{4,28},{8,104},{12,4},{16,112},{20,12},{24,120},{28,20},{32... | collective-permute-start | bytes 1990664 | tf_op jit(solution)/shard_map/ppermute | solution.py:65
  16.2 19.0 %collective-permute-start.8 = (bf16[288,1152]{1,0:T(8,128)(2,1)S(1)}, bf16[288,1152]{1,0:T(8,128)(2,1)S(1)}, u32[]{:S(2)}, u32[]{:S(2)}) collective-permute-start(bf16[288,1152]{1,0:T(8,128)(2,1)S(1)} %get-tuple-element.41.refs_0_), channel_id=1, source_target_pairs={{0,32},{4,12},{8,40},{12,20},{16,48},{20,28},{24,56},{28,4},{32,64... | collective-permute-start | bytes 1990664 | tf_op jit(solution)/shard_map/ppermute | solution.py:65
  16.2 19.0 %collective-permute-start.9 = (bf16[288,1152]{1,0:T(8,128)(2,1)S(1)}, bf16[288,1152]{1,0:T(8,128)(2,1)S(1)}, u32[]{:S(2)}, u32[]{:S(2)}) collective-permute-start(bf16[288,1152]{1,0:T(8,128)(2,1)S(1)} %get-tuple-element.41.refs_0_), channel_id=1, source_target_pairs={{0,64},{4,20},{8,72},{12,28},{16,80},{20,4},{24,88},{28,12},{32,96... | collective-permute-start | bytes 1990664 | tf_op jit(solution)/shard_map/ppermute | solution.py:65
  18.4 6.8 %collective-permute-start.4 = (bf16[288,640]{1,0:T(8,128)(2,1)S(1)}, bf16[288,640]{1,0:T(8,128)(2,1)S(1)}, u32[]{:S(2)}, u32[]{:S(2)}) collective-permute-start(bf16[288,640]{1,0:T(8,128)(2,1)S(1)} %get-tuple-element.45.refs_2_), channel_id=1, source_target_pairs={{0,4},{4,0},{8,12},{12,8},{16,20},{20,16},{24,28},{28,24},{32,36},... | collective-permute-start | bytes 1105928 | tf_op jit(solution)/shard_map/ppermute | solution.py:65
  35.2 3.5 %collective-permute-start.11 = (bf16[288,1152]{1,0:T(8,128)(2,1)S(1)}, bf16[288,1152]{1,0:T(8,128)(2,1)S(1)}, u32[]{:S(2)}, u32[]{:S(2)}) collective-permute-start(bf16[288,1152]{1,0:T(8,128)(2,1)S(1)} %collective-permute-done.8.refs_0_), channel_id=1, source_target_pairs={{0,4},{4,0},{8,12},{12,8},{16,20},{20,16},{24,28},{28,24},{32,36},... | collective-permute-start | bytes 1990664 | tf_op jit(solution)/shard_map/ppermute | solution.py:65
  35.2 4.9 %collective-permute-start.12 = (bf16[288,1152]{1,0:T(8,128)(2,1)S(1)}, bf16[288,1152]{1,0:T(8,128)(2,1)S(1)}, u32[]{:S(2)}, u32[]{:S(2)}) collective-permute-start(bf16[288,1152]{1,0:T(8,128)(2,1)S(1)} %collective-permute-done.9.refs_1_), channel_id=1, source_target_pairs={{0,4},{4,0},{8,12},{12,8},{16,20},{20,16},{24,28},{28,24},{32,36},... | collective-permute-start | bytes 1990664 | tf_op jit(solution)/shard_map/ppermute | solution.py:65
  35.7 4.4 %collective-permute-start.13 = (bf16[288,1152]{1,0:T(8,128)(2,1)S(1)}, bf16[288,1152]{1,0:T(8,128)(2,1)S(1)}, u32[]{:S(2)}, u32[]{:S(2)}) collective-permute-start(bf16[288,1152]{1,0:T(8,128)(2,1)S(1)} %collective-permute-done.10.refs_2_), channel_id=1, source_target_pairs={{0,4},{4,0},{8,12},{12,8},{16,20},{20,16},{24,28},{28,24},{32,36},... | collective-permute-start | bytes 1990664 | tf_op jit(solution)/shard_map/ppermute | solution.py:65
  35.7 17.4 %collective-permute-start.5 = (bf16[288,640]{1,0:T(8,128)(2,1)S(1)}, bf16[288,640]{1,0:T(8,128)(2,1)S(1)}, u32[]{:S(2)}, u32[]{:S(2)}) collective-permute-start(bf16[288,640]{1,0:T(8,128)(2,1)S(1)} %get-tuple-element.45.refs_2_), channel_id=1, source_target_pairs={{0,32},{4,12},{8,40},{12,20},{16,48},{20,28},{24,56},{28,4},{32,64... | collective-permute-start | bytes 1105928 | tf_op jit(solution)/shard_map/ppermute | solution.py:65
  35.8 17.3 %collective-permute-start.6 = (bf16[288,640]{1,0:T(8,128)(2,1)S(1)}, bf16[288,640]{1,0:T(8,128)(2,1)S(1)}, u32[]{:S(2)}, u32[]{:S(2)}) collective-permute-start(bf16[288,640]{1,0:T(8,128)(2,1)S(1)} %get-tuple-element.45.refs_2_), channel_id=1, source_target_pairs={{0,64},{4,20},{8,72},{12,28},{16,80},{20,4},{24,88},{28,12},{32,96... | collective-permute-start | bytes 1105928 | tf_op jit(solution)/shard_map/ppermute | solution.py:65
  38.7 14.4 %collective-permute-start.7 = (bf16[288,640]{1,0:T(8,128)(2,1)S(1)}, bf16[288,640]{1,0:T(8,128)(2,1)S(1)}, u32[]{:S(2)}, u32[]{:S(2)}) collective-permute-start(bf16[288,640]{1,0:T(8,128)(2,1)S(1)} %get-tuple-element.45.refs_2_), channel_id=1, source_target_pairs={{0,96},{4,28},{8,104},{12,4},{16,112},{20,12},{24,120},{28,20},{32... | collective-permute-start | bytes 1105928 | tf_op jit(solution)/shard_map/ppermute | solution.py:65
  52.2 2.0 %collective-permute-start.14 = (bf16[5,128,112]{2,1,0:T(8,128)(2,1)S(1)}, bf16[5,128,112]{2,1,0:T(8,128)(2,1)S(1)}, u32[]{:S(2)}, u32[]{:S(2)}) collective-permute-start(bf16[5,128,112]{2,1,0:T(8,128)(2,1)S(1)} %get-tuple-element.51.tot_ref), channel_id=1, source_target_pairs={{0,4},{4,0},{8,12},{12,8},{16,20},{20,16},{24,28},{28,24},{32,36},... | collective-permute-start | bytes 430088 | tf_op jit(solution)/shard_map/ppermute | solution.py:65
  54.2 3.4 %collective-permute-start.18 = (bf16[288,640]{1,0:T(8,128)(2,1)S(1)}, bf16[288,640]{1,0:T(8,128)(2,1)S(1)}, u32[]{:S(2)}, u32[]{:S(2)}) collective-permute-start(bf16[288,640]{1,0:T(8,128)(2,1)S(1)} %collective-permute-done.5.refs_0_), channel_id=1, source_target_pairs={{0,4},{4,0},{8,12},{12,8},{16,20},{20,16},{24,28},{28,24},{32,36},... | collective-permute-start | bytes 1105928 | tf_op jit(solution)/shard_map/ppermute | solution.py:65
  54.5 4.6 %collective-permute-start.19 = (bf16[288,640]{1,0:T(8,128)(2,1)S(1)}, bf16[288,640]{1,0:T(8,128)(2,1)S(1)}, u32[]{:S(2)}, u32[]{:S(2)}) collective-permute-start(bf16[288,640]{1,0:T(8,128)(2,1)S(1)} %collective-permute-done.6.refs_1_), channel_id=1, source_target_pairs={{0,4},{4,0},{8,12},{12,8},{16,20},{20,16},{24,28},{28,24},{32,36},... | collective-permute-start | bytes 1105928 | tf_op jit(solution)/shard_map/ppermute | solution.py:65
  54.7 4.5 %collective-permute-start.20 = (bf16[288,640]{1,0:T(8,128)(2,1)S(1)}, bf16[288,640]{1,0:T(8,128)(2,1)S(1)}, u32[]{:S(2)}, u32[]{:S(2)}) collective-permute-start(bf16[288,640]{1,0:T(8,128)(2,1)S(1)} %collective-permute-done.7.refs_2_), channel_id=1, source_target_pairs={{0,4},{4,0},{8,12},{12,8},{16,20},{20,16},{24,28},{28,24},{32,36},... | collective-permute-start | bytes 1105928 | tf_op jit(solution)/shard_map/ppermute | solution.py:65
  55.1 18.4 %copy-start = (s32[4]{0:T(128)S(1)}, s32[4]{0:T(128)}, u32[]{:S(2)}) copy-start(s32[4]{0:T(128)} %codes.1) | copy-start | bytes 52
  55.1 11.0 %collective-permute-start.15 = (bf16[5,128,112]{2,1,0:T(8,128)(2,1)S(1)}, bf16[5,128,112]{2,1,0:T(8,128)(2,1)S(1)}, u32[]{:S(2)}, u32[]{:S(2)}) collective-permute-start(bf16[5,128,112]{2,1,0:T(8,128)(2,1)S(1)} %chip.1.a), channel_id=1, source_target_pairs={{0,8},{4,12},{8,16},{12,20},{16,24},{20,28},{24,0},{28,4},{32,40},... | collective-permute-start | bytes 430088 | tf_op jit(solution)/shard_map/ppermute | solution.py:65
  55.6 10.5 %collective-permute-start.16 = (bf16[5,128,112]{2,1,0:T(8,128)(2,1)S(1)}, bf16[5,128,112]{2,1,0:T(8,128)(2,1)S(1)}, u32[]{:S(2)}, u32[]{:S(2)}) collective-permute-start(bf16[5,128,112]{2,1,0:T(8,128)(2,1)S(1)} %chip.1.a), channel_id=1, source_target_pairs={{0,16},{4,20},{8,24},{12,28},{16,0},{20,4},{24,8},{28,12},{32,48},... | collective-permute-start | bytes 430088 | tf_op jit(solution)/shard_map/ppermute | solution.py:65
  57.6 9.2 %collective-permute-start.17 = (bf16[5,128,112]{2,1,0:T(8,128)(2,1)S(1)}, bf16[5,128,112]{2,1,0:T(8,128)(2,1)S(1)}, u32[]{:S(2)}, u32[]{:S(2)}) collective-permute-start(bf16[5,128,112]{2,1,0:T(8,128)(2,1)S(1)} %chip.1.a), channel_id=1, source_target_pairs={{0,24},{4,28},{8,0},{12,4},{16,8},{20,12},{24,16},{28,20},{32,56},... | collective-permute-start | bytes 430088 | tf_op jit(solution)/shard_map/ppermute | solution.py:65
  66.9 12.5 %collective-permute-start.21 = (bf16[5,128,112]{2,1,0:T(8,128)(2,1)S(1)}, bf16[5,128,112]{2,1,0:T(8,128)(2,1)S(1)}, u32[]{:S(2)}, u32[]{:S(2)}) collective-permute-start(bf16[5,128,112]{2,1,0:T(8,128)(2,1)S(1)} %row.1), channel_id=1, source_target_pairs={{0,32},{4,36},{8,40},{12,44},{16,48},{20,52},{24,56},{28,60},{32,6... | collective-permute-start | bytes 430088 | tf_op jit(solution)/shard_map/ppermute | solution.py:65
  68.9 10.5 %collective-permute-start.22 = (bf16[5,128,112]{2,1,0:T(8,128)(2,1)S(1)}, bf16[5,128,112]{2,1,0:T(8,128)(2,1)S(1)}, u32[]{:S(2)}, u32[]{:S(2)}) collective-permute-start(bf16[5,128,112]{2,1,0:T(8,128)(2,1)S(1)} %row.1), channel_id=1, source_target_pairs={{0,64},{4,68},{8,72},{12,76},{16,80},{20,84},{24,88},{28,92},{32,9... | collective-permute-start | bytes 430088 | tf_op jit(solution)/shard_map/ppermute | solution.py:65
  72.2 7.3 %collective-permute-start.23 = (bf16[5,128,112]{2,1,0:T(8,128)(2,1)S(1)}, bf16[5,128,112]{2,1,0:T(8,128)(2,1)S(1)}, u32[]{:S(2)}, u32[]{:S(2)}) collective-permute-start(bf16[5,128,112]{2,1,0:T(8,128)(2,1)S(1)} %row.1), channel_id=1, source_target_pairs={{0,96},{4,100},{8,104},{12,108},{16,112},{20,116},{24,120},{28,124... | collective-permute-start | bytes 430088 | tf_op jit(solution)/shard_map/ppermute | solution.py:65
  73.5 6.0 %copy-start.1 = (f32[5]{0:T(128)S(1)}, f32[5]{0:T(128)}, u32[]{:S(2)}) copy-start(f32[5]{0:T(128)} %scale.1) | copy-start | bytes 64
  81.7 6.6 %collective-permute-start.24 = (f32[1,2048]{1,0:T(1,128)S(1)}, f32[1,2048]{1,0:T(1,128)S(1)}, u32[]{:S(2)}, u32[]{:S(2)}) collective-permute-start(f32[1,2048]{1,0:T(1,128)S(1)} %get-tuple-element.69.s0), channel_id=1, source_target_pairs={{0,1},{1,2},{2,3},{3,0},{4,5},{5,6},{6,7},{7,4},{8,9},{9,10},{10,1... | collective-permute-start | bytes 24584 | tf_op jit(solution)/shard_map/ppermute | solution.py:466
  83.7 5.3 %collective-permute-start.25 = (f32[1,2048]{1,0:T(1,128)S(1)}, f32[1,2048]{1,0:T(1,128)S(1)}, u32[]{:S(2)}, u32[]{:S(2)}) collective-permute-start(f32[1,2048]{1,0:T(1,128)S(1)} %get-tuple-element.69.s0), channel_id=1, source_target_pairs={{0,2},{1,3},{2,0},{3,1},{4,6},{5,7},{6,4},{7,5},{8,10},{9,11},{10,... | collective-permute-start | bytes 24584 | tf_op jit(solution)/shard_map/ppermute | solution.py:466
  87.3 3.7 %collective-permute-start.26 = (f32[1,2048]{1,0:T(1,128)S(1)}, f32[1,2048]{1,0:T(1,128)S(1)}, u32[]{:S(2)}, u32[]{:S(2)}) collective-permute-start(f32[1,2048]{1,0:T(1,128)S(1)} %get-tuple-element.69.s0), channel_id=1, source_target_pairs={{0,3},{1,0},{2,1},{3,2},{4,7},{5,4},{6,5},{7,6},{8,11},{9,8},{10,9... | collective-permute-start | bytes 24584 | tf_op jit(solution)/shard_map/ppermute | solution.py:466

commit v12 on v11

--- a/solution.py
+++ b/solution.py
@@ -300,13 +300,15 @@
     return jnp.concatenate(parts, axis=0)
 
 
-def attend_kernel(codes, fk_ref, v_ref, fq_ref, num_ref):
+def attend_kernel(groups, codes, fk_ref, v_ref, fq_ref, num_ref):
     half = GROUP // 2
 
-    def step(g, at):
+    for i, g in enumerate(groups):
         code = codes[g]
         start = g * GROUP
+        at = pl.ds(start, GROUP)
         one, two = pl.ds(start, half), pl.ds(start + half, half)
+        to = i * GROUP
         upper = mask_rows(code, 0, half, 0, GROUP)
         lower = mask_rows(code, 4, half, half, half)
         for h in range(HL):
@@ -317,18 +319,16 @@
             low = low.astype(BF) * lower
             num = jnp.dot(v_ref[h, :, one], top, preferred_element_type=F32)
             more = jnp.dot(v_ref[h, :, two], low, preferred_element_type=F32)
-            num_ref[h, :, one] = num[:, :half]
-            num_ref[h, :, two] = num[:, half:] + more
-
-    each_group(fq_ref.shape[1], step)
-
-
-def attend_call(codes, fk, v, fq):
+            num_ref[h, :, to : to + half] = num[:, :half]
+            num_ref[h, :, to + half : to + GROUP] = num[:, half:] + more
+
+
+def attend_call(groups, codes, fk, v, fq):
     (out,) = resident(
-        attend_kernel,
+        functools.partial(attend_kernel, groups),
         [codes],
         [fk, v, fq],
-        [((HL, VA, fq.shape[1]), F32)],
+        [((HL, VA, len(groups) * GROUP), F32)],
         [],
         12,
         "attend",
@@ -352,7 +352,7 @@
 
 def join_kernel(pos, scale, *refs):
     other, near, far = refs[0], refs[1:4], refs[4:7]
-    pre_ref, fq_ref, num_ref, out_ref, sq_ref, dev = refs[7:]
+    pre_ref, fq_ref, num_one, num_rest, out_ref, sq_ref, dev = refs[7:]
     total = far[0][...].astype(F32) + far[1][...].astype(F32) + far[2][...].astype(F32)
     total = total + jnp.where(pos[2] == 1, other[...].astype(F32), 0.0)
     for d, got in enumerate(near):
@@ -364,7 +364,8 @@
         for h in range(HL):
             prefix = (dev[h] + pre_ref[g, h]).astype(BF)
             fq = fq_ref[h * DH : (h + 1) * DH, at]
-            num = num_ref[h, :, at] + jnp.dot(prefix, fq, preferred_element_type=F32)
+            from_ref, to = (num_one, 0) if g == 0 else (num_rest, (g - 1) * GROUP)
+            num = from_ref[h, :, to : to + GROUP] + jnp.dot(prefix, fq, preferred_element_type=F32)
             out = num[:DH, :] * (scale[h] / num[DH : DH + 1, :])
             out_ref[h * DH : (h + 1) * DH, at] = out
             squares = squares + jnp.sum(out * out, axis=0, keepdims=True)
@@ -373,12 +374,12 @@
     each_group(fq_ref.shape[1], step)
 
 
-def join_call(pos, scale, states, pre, fq, num):
+def join_call(pos, scale, states, pre, fq, nums):
     n = fq.shape[1]
     return resident(
         join_kernel,
         [pos, scale],
-        [*states, pre, fq, num],
+        [*states, pre, fq, *nums],
         [((HL * DH, n), F32), ((1, n), F32)],
         [pltpu.VMEM((HL, VA, DH), F32)],
         12,
@@ -455,13 +456,14 @@
     chip, q_sum = lax.optimization_barrier((chip, q_sum))
     fq = q_call(mine + last, pos, [*own_q, *sib_q], xp, q_sum)
     in_row = [shift(chip, along_x(d)) for d in (1, 2, 3)]
-    *in_row, fq = lax.optimization_barrier((*in_row, fq))
+    one = attend_call((0,), block_mask, fk, v, fq)
+    *in_row, one = lax.optimization_barrier((*in_row, one))
     row = small(row_kernel, [chip, *in_row], "row")
     row, fq = lax.optimization_barrier((row, fq))
-    num = attend_call(block_mask, fk, v, fq)
+    rest = attend_call((1, 2, 3), block_mask, fk, v, fq)
     above = [shift(row, later_y(d)) for d in (1, 2, 3)]
 
-    out, squares = join_call(pos, head_scale, [other, *in_row, *above], pre, fq, num)
+    out, squares = join_call(pos, head_scale, [other, *in_row, *above], pre, fq, (one, rest))
     squares = [squares] + [
         lax.ppermute(squares, "head", [(i, (i + d) % 4) for i in range(4)]) for d in (1, 2, 3)
     ]

time: 93.3 us -> 93.7 us (level)
  waiting for transfers between devices: 13.2 us -> 11.5 us
  starting transfers between devices: 35 us -> 36.2 us
    ppermute x24, waiting for transfers between devices: 10.6 us -> 8.84 us  [shift(): return lax.ppermute(a, 'tm', moves)]
    ppermute x24, starting transfers between devices: 28.4 us -> 29.7 us  [shift(): return lax.ppermute(a, 'tm', moves)]
    pallas_call x8 -> x9, Pallas kernels: 33.9 us -> 34.7 us  [resident(): pl.pallas_call(kernel, in_specs=[pl.BlockSpec(memory_space=pltpu.SMEM)] *...]
  transfers between devices with their start and end apart: 27 -> 27, of which waited for: 9 -> 7; matrix products, arithmetic and copies ran while one was open for 1% -> 1% of each run, Pallas kernels for 41% -> 41%
where the time goes in v12:
time: 93.7 us; the launch traced here: 93.4 us
  Pallas kernels  44.4 us (47%)
  starting transfers between devices  36.2 us (39%)
  waiting for transfers between devices  11.5 us (12%)
    pallas_call x9, Pallas kernels, resident(): pl.pallas_call(kernel, in_specs=[pl.BlockSpec(memory_space=pltpu.SMEM)] *...  34.7 us
    ppermute x24, starting transfers between devices, shift(): return lax.ppermute(a, 'tm', moves)  29.7 us
    ppermute x24, waiting for transfers between devices, shift(): return lax.ppermute(a, 'tm', moves)  8.84 us
    pallas_call x1, Pallas kernels, spread(): pl.pallas_call(spread_kernel, grid=(n // blk,), in_specs=[pl.BlockSpec((D...  6.8 us
    ppermute x3, starting transfers between devices, body(): lax.ppermute(squares, 'head', [(i, (i + d) % 4) for i in range(4)])  6.55 us
    ppermute x3, waiting for transfers between devices, body(): lax.ppermute(squares, 'head', [(i, (i + d) % 4) for i in range(4)])  2.64 us
  transfers between devices with their start and end apart: 27, of which 7 were waited for; matrix products, arithmetic and copies ran while one was open for 1% of the time, Pallas kernels for 41%

profile of v12, /device:TPU:0, one launch (start us, length us, event | category | flops | bytes accessed | tf_op | source)
XLA Modules:
  0.0 93.4 jit_solution(539538766006649935)
XLA Ops:
  0.0 1.6 %collective-permute-start = (bf16[70,1680]{1,0:T(8,128)(2,1)}, bf16[70,1680]{1,0:T(8,128)(2,1)S(1)}, u32[]{:S(2)}, u32[]{:S(2)}) collective-permute-start(bf16[70,1680]{1,0:T(8,128)(2,1)} %w_ref.1), channel_id=1, source_target_pairs={{0,8},{4,36},{8,16},{12,44},{16,24},{20,52},{24,0},{28,60},{32,40}... | collective-permute-start | bytes 705608 | tf_op jit(solution)/shard_map/ppermute | solution.py:65
  1.6 2.7 %collective-permute-start.1 = (bf16[70,1680]{1,0:T(8,128)(2,1)}, bf16[70,1680]{1,0:T(8,128)(2,1)S(1)}, u32[]{:S(2)}, u32[]{:S(2)}) collective-permute-start(bf16[70,1680]{1,0:T(8,128)(2,1)} %w_ref.1), channel_id=1, source_target_pairs={{0,16},{4,68},{8,24},{12,76},{16,0},{20,84},{24,8},{28,92},{32,48}... | collective-permute-start | bytes 705608 | tf_op jit(solution)/shard_map/ppermute | solution.py:65
  4.3 1.4 %collective-permute-start.2 = (bf16[70,1680]{1,0:T(8,128)(2,1)}, bf16[70,1680]{1,0:T(8,128)(2,1)S(1)}, u32[]{:S(2)}, u32[]{:S(2)}) collective-permute-start(bf16[70,1680]{1,0:T(8,128)(2,1)} %w_ref.1), channel_id=1, source_target_pairs={{0,24},{4,100},{8,0},{12,108},{16,8},{20,116},{24,16},{28,124},{32... | collective-permute-start | bytes 705608 | tf_op jit(solution)/shard_map/ppermute | solution.py:65
  5.7 1.0 %stage.1.a0 = bf16[70,1680]{1,0:T(8,128)(2,1)S(1)} custom-call(bf16[70,1680]{1,0:T(8,128)(2,1)} %w_ref.1), custom_call_target="tpu_custom_call" | custom-call | flops 1 | bytes 1 | tf_op jit(solution)/shard_map/stage/pallas_call | solution.py:102
  6.8 0.8 reshape.3.gain_ref
  7.8 3.8 %collective-permute-done.1.a2 = bf16[70,1680]{1,0:T(8,128)(2,1)S(1)} collective-permute-done((bf16[70,1680]{1,0:T(8,128)(2,1)}, bf16[70,1680]{1,0:T(8,128)(2,1)S(1)}, u32[]{:S(2)}, u32[]{:S(2)}) %collective-permute-start.1) | collective-permute-done | bytes 235232 | tf_op jit(solution)/shard_map/ppermute | solution.py:65
  11.6 1.4 %pack.1 = (bf16[288,1152]{1,0:T(8,128)(2,1)S(1)}, bf16[288,640]{1,0:T(8,128)(2,1)S(1)}) custom-call(s32[3]{0:T(128)S(1)} %pad_add_fusion.pos, bf16[70,1680]{1,0:T(8,128)(2,1)S(1)} %stage.1.a0, bf16[70,1680]{1,0:T(8,128)(2,1)S(1)} %collective-permute-done.a1, bf16[70,1680]{1,0:T(8,128)(2,1)S(1)} %collective-permute-done.1.a2, ...), custom_call_target="tpu_custom_call" | custom-call | flops 1 | bytes 1 | tf_op jit(solution)/shard_map/pack/pallas_call | solution.py:169
  13.1 3.1 %collective-permute-start.10 = (bf16[288,1152]{1,0:T(8,128)(2,1)S(1)}, bf16[288,1152]{1,0:T(8,128)(2,1)S(1)}, u32[]{:S(2)}, u32[]{:S(2)}) collective-permute-start(bf16[288,1152]{1,0:T(8,128)(2,1)S(1)} %get-tuple-element.41.refs_0_), channel_id=1, source_target_pairs={{0,96},{4,28},{8,104},{12,4},{16,112},{20,12},{24,120},{28,20},{32... | collective-permute-start | bytes 1990664 | tf_op jit(solution)/shard_map/ppermute | solution.py:65
  16.2 2.2 %collective-permute-start.9 = (bf16[288,1152]{1,0:T(8,128)(2,1)S(1)}, bf16[288,1152]{1,0:T(8,128)(2,1)S(1)}, u32[]{:S(2)}, u32[]{:S(2)}) collective-permute-start(bf16[288,1152]{1,0:T(8,128)(2,1)S(1)} %get-tuple-element.41.refs_0_), channel_id=1, source_target_pairs={{0,64},{4,20},{8,72},{12,28},{16,80},{20,4},{24,88},{28,12},{32,96... | collective-permute-start | bytes 1990664 | tf_op jit(solution)/shard_map/ppermute | solution.py:65
  18.4 6.8 %spread.1.refs_4_.refs_6_ = bf16[8,288,2048]{2,1,0:T(8,128)(2,1)S(1)} custom-call(bf16[2240,2048]{1,0:T(8,128)(2,1)} %bitcast.5), custom_call_target="tpu_custom_call" | custom-call | flops 1 | bytes 1 | tf_op jit(solution)/shard_map/spread/pallas_call | solution.py:129
  25.3 6.1 %part_first.1 = (f32[1120,2048]{1,0:T(8,128)S(1)}, f32[560,2048]{1,0:T(8,128)S(1)}) custom-call(s32[3]{0:T(128)S(1)} %pad_add_fusion.pos, bf16[288,1152]{1,0:T(8,128)(2,1)S(1)} %get-tuple-element.41.refs_0_, bf16[288,1152]{1,0:T(8,128)(2,1)S(1)} %collective-permute-done.3.refs_1_, bf16[288,640]{1,0:T(8,128)(2,1)S(1)} %get-tuple-element.45.refs_2_, ...), custom_call_target="tpu_custom_call" | custom-call | flops 1 | bytes 1 | tf_op jit(solution)/shard_map/part_first/pallas_call | solution.py:169
  31.5 3.7 %collective-permute-done.8.refs_0_ = bf16[288,1152]{1,0:T(8,128)(2,1)S(1)} collective-permute-done((bf16[288,1152]{1,0:T(8,128)(2,1)S(1)}, bf16[288,1152]{1,0:T(8,128)(2,1)S(1)}, u32[]{:S(2)}, u32[]{:S(2)}) %collective-permute-start.8) | collective-permute-done | bytes 663584 | tf_op jit(solution)/shard_map/ppermute | solution.py:65
  35.8 2.9 %collective-permute-start.6 = (bf16[288,640]{1,0:T(8,128)(2,1)S(1)}, bf16[288,640]{1,0:T(8,128)(2,1)S(1)}, u32[]{:S(2)}, u32[]{:S(2)}) collective-permute-start(bf16[288,640]{1,0:T(8,128)(2,1)S(1)} %get-tuple-element.45.refs_2_), channel_id=1, source_target_pairs={{0,64},{4,20},{8,72},{12,28},{16,80},{20,4},{24,88},{28,12},{32,96... | collective-permute-start | bytes 1105928 | tf_op jit(solution)/shard_map/ppermute | solution.py:65
  38.7 1.3 %collective-permute-start.7 = (bf16[288,640]{1,0:T(8,128)(2,1)S(1)}, bf16[288,640]{1,0:T(8,128)(2,1)S(1)}, u32[]{:S(2)}, u32[]{:S(2)}) collective-permute-start(bf16[288,640]{1,0:T(8,128)(2,1)S(1)} %get-tuple-element.45.refs_2_), channel_id=1, source_target_pairs={{0,96},{4,28},{8,104},{12,4},{16,112},{20,12},{24,120},{28,20},{32... | collective-permute-start | bytes 1105928 | tf_op jit(solution)/shard_map/ppermute | solution.py:65
  40.1 12.1 %keys_values.1 = (bf16[5,2048,112]{2,1,0:T(8,128)(2,1)S(1)}, bf16[5,128,2048]{2,1,0:T(8,128)(2,1)S(1)}, f32[4,5,128,112]{3,2,1,0:T(8,128)S(1)}, bf16[5,128,112]{2,1,0:T(8,128)(2,1)S(1)}) custom-call(s32[3]{0:T(128)S(1)} %pad_add_fusion.pos, bf16[288,1152]{1,0:T(8,128)(2,1)S(1)} %collective-permute-done.8.refs_0_, ...), custom_call_target="tpu_custom_call" | custom-call | flops 1 | bytes 1 | tf_op jit(solution)/shard_map/keys_values/pallas_call | solution.py:169
  52.2 1.0 %collective-permute-start.14 = (bf16[5,128,112]{2,1,0:T(8,128)(2,1)S(1)}, bf16[5,128,112]{2,1,0:T(8,128)(2,1)S(1)}, u32[]{:S(2)}, u32[]{:S(2)}) collective-permute-start(bf16[5,128,112]{2,1,0:T(8,128)(2,1)S(1)} %get-tuple-element.51.tot_ref), channel_id=1, source_target_pairs={{0,4},{4,0},{8,12},{12,8},{16,20},{20,16},{24,28},{28,24},{32,36},... | collective-permute-start | bytes 430088 | tf_op jit(solution)/shard_map/ppermute | solution.py:65
  53.1 1.0 %collective-permute-done.14.other_ref.refs_0_ = bf16[5,128,112]{2,1,0:T(8,128)(2,1)S(1)} collective-permute-done((bf16[5,128,112]{2,1,0:T(8,128)(2,1)S(1)}, bf16[5,128,112]{2,1,0:T(8,128)(2,1)S(1)}, u32[]{:S(2)}, u32[]{:S(2)}) %collective-permute-start.14) | collective-permute-done | bytes 143392 | tf_op jit(solution)/shard_map/ppermute | solution.py:65
  55.6 2.0 %collective-permute-start.16 = (bf16[5,128,112]{2,1,0:T(8,128)(2,1)S(1)}, bf16[5,128,112]{2,1,0:T(8,128)(2,1)S(1)}, u32[]{:S(2)}, u32[]{:S(2)}) collective-permute-start(bf16[5,128,112]{2,1,0:T(8,128)(2,1)S(1)} %chip.1.a), channel_id=1, source_target_pairs={{0,16},{4,20},{8,24},{12,28},{16,0},{20,4},{24,8},{28,12},{32,48},... | collective-permute-start | bytes 430088 | tf_op jit(solution)/shard_map/ppermute | solution.py:65
  57.6 1.6 %collective-permute-start.17 = (bf16[5,128,112]{2,1,0:T(8,128)(2,1)S(1)}, bf16[5,128,112]{2,1,0:T(8,128)(2,1)S(1)}, u32[]{:S(2)}, u32[]{:S(2)}) collective-permute-start(bf16[5,128,112]{2,1,0:T(8,128)(2,1)S(1)} %chip.1.a), channel_id=1, source_target_pairs={{0,24},{4,28},{8,0},{12,4},{16,8},{20,12},{24,16},{28,20},{32,56},... | collective-permute-start | bytes 430088 | tf_op jit(solution)/shard_map/ppermute | solution.py:65
  59.2 5.9 %queries.1.fq_ref.refs_8_ = bf16[560,2048]{1,0:T(8,128)(2,1)S(1)} custom-call(s32[3]{0:T(128)S(1)} %pad_add_fusion.pos, bf16[288,640]{1,0:T(8,128)(2,1)S(1)} %collective-permute-done.5.refs_0_, bf16[288,640]{1,0:T(8,128)(2,1)S(1)} %collective-permute-done.6.refs_1_, bf16[288,640]{1,0:T(8,128)(2,1)S(1)} %collective-permute-done.7.refs_2_, ...), custom_call_target="tpu_custom_call" | custom-call | flops 1 | bytes 1 | tf_op jit(solution)/shard_map/queries/pallas_call | solution.py:169
  65.0 2.0 %attend.2.refs_9_ = f32[5,128,512]{2,1,0:T(8,128)S(1)} custom-call(s32[4]{0:T(128)S(1)} %copy-done, bf16[5,2048,112]{2,1,0:T(8,128)(2,1)S(1)} %get-tuple-element.55.fk_ref, bf16[5,128,2048]{2,1,0:T(8,128)(2,1)S(1)} %get-tuple-element.56.v_ref, bf16[560,2048]{1,0:T(8,128)(2,1)S(1)} %queries.1.fq_ref.refs_8_), custom_call_target="tpu_custom_call" | custom-call | flops 1 | bytes 1 | tf_op jit(solution)/shard_map/attend/pallas_call | solution.py:169
  67.2 2.5 %collective-permute-start.21 = (bf16[5,128,112]{2,1,0:T(8,128)(2,1)S(1)}, bf16[5,128,112]{2,1,0:T(8,128)(2,1)S(1)}, u32[]{:S(2)}, u32[]{:S(2)}) collective-permute-start(bf16[5,128,112]{2,1,0:T(8,128)(2,1)S(1)} %row.1), channel_id=1, source_target_pairs={{0,32},{4,36},{8,40},{12,44},{16,48},{20,52},{24,56},{28,60},{32,6... | collective-permute-start | bytes 430088 | tf_op jit(solution)/shard_map/ppermute | solution.py:65
  69.8 4.0 %collective-permute-start.22 = (bf16[5,128,112]{2,1,0:T(8,128)(2,1)S(1)}, bf16[5,128,112]{2,1,0:T(8,128)(2,1)S(1)}, u32[]{:S(2)}, u32[]{:S(2)}) collective-permute-start(bf16[5,128,112]{2,1,0:T(8,128)(2,1)S(1)} %row.1), channel_id=1, source_target_pairs={{0,64},{4,68},{8,72},{12,76},{16,80},{20,84},{24,88},{28,92},{32,9... | collective-permute-start | bytes 430088 | tf_op jit(solution)/shard_map/ppermute | solution.py:65
  73.8 1.3 %collective-permute-start.23 = (bf16[5,128,112]{2,1,0:T(8,128)(2,1)S(1)}, bf16[5,128,112]{2,1,0:T(8,128)(2,1)S(1)}, u32[]{:S(2)}, u32[]{:S(2)}) collective-permute-start(bf16[5,128,112]{2,1,0:T(8,128)(2,1)S(1)} %row.1), channel_id=1, source_target_pairs={{0,96},{4,100},{8,104},{12,108},{16,112},{20,116},{24,120},{28,124... | collective-permute-start | bytes 430088 | tf_op jit(solution)/shard_map/ppermute | solution.py:65
  75.1 4.7 %attend.3.refs_10_ = f32[5,128,1536]{2,1,0:T(8,128)S(1)} custom-call(s32[4]{0:T(128)S(1)} %copy-done, bf16[5,2048,112]{2,1,0:T(8,128)(2,1)S(1)} %get-tuple-element.55.fk_ref, bf16[5,128,2048]{2,1,0:T(8,128)(2,1)S(1)} %get-tuple-element.56.v_ref, bf16[560,2048]{1,0:T(8,128)(2,1)S(1)} %queries.1.fq_ref.refs_8_), custom_call_target="tpu_custom_call" | custom-call | flops 1 | bytes 1 | tf_op jit(solution)/shard_map/attend/pallas_call | solution.py:169
  79.8 2.4 %join.1 = (f32[560,2048]{1,0:T(8,128)S(1)}, f32[1,2048]{1,0:T(1,128)S(1)}) custom-call(s32[3]{0:T(128)S(1)} %pad_add_fusion.pos, f32[5]{0:T(128)S(1)} %copy-done.1, bf16[5,128,112]{2,1,0:T(8,128)(2,1)S(1)} %collective-permute-done.14.other_ref.refs_0_, bf16[5,128,112]{2,1,0:T(8,128)(2,1)S(1)} %collective-permute-done.15.b.refs_1_, ...), custom_call_target="tpu_custom_call" | custom-call | flops 1 | bytes 1 | tf_op jit(solution)/shard_map/join/pallas_call | solution.py:169
  82.1 2.0 %collective-permute-start.24 = (f32[1,2048]{1,0:T(1,128)S(1)}, f32[1,2048]{1,0:T(1,128)S(1)}, u32[]{:S(2)}, u32[]{:S(2)}) collective-permute-start(f32[1,2048]{1,0:T(1,128)S(1)} %get-tuple-element.69.s0), channel_id=1, source_target_pairs={{0,1},{1,2},{2,3},{3,0},{4,5},{5,6},{6,7},{7,4},{8,9},{9,10},{10,1... | collective-permute-start | bytes 24584 | tf_op jit(solution)/shard_map/ppermute | solution.py:468
  84.1 3.6 %collective-permute-start.25 = (f32[1,2048]{1,0:T(1,128)S(1)}, f32[1,2048]{1,0:T(1,128)S(1)}, u32[]{:S(2)}, u32[]{:S(2)}) collective-permute-start(f32[1,2048]{1,0:T(1,128)S(1)} %get-tuple-element.69.s0), channel_id=1, source_target_pairs={{0,2},{1,3},{2,0},{3,1},{4,6},{5,7},{6,4},{7,5},{8,10},{9,11},{10,... | collective-permute-start | bytes 24584 | tf_op jit(solution)/shard_map/ppermute | solution.py:468
  87.7 1.0 %collective-permute-start.26 = (f32[1,2048]{1,0:T(1,128)S(1)}, f32[1,2048]{1,0:T(1,128)S(1)}, u32[]{:S(2)}, u32[]{:S(2)}) collective-permute-start(f32[1,2048]{1,0:T(1,128)S(1)} %get-tuple-element.69.s0), channel_id=1, source_target_pairs={{0,3},{1,0},{2,1},{3,2},{4,7},{5,4},{6,5},{7,6},{8,11},{9,8},{10,9... | collective-permute-start | bytes 24584 | tf_op jit(solution)/shard_map/ppermute | solution.py:468
  88.7 0.7 collective-permute-done.25.s2
  89.4 1.9 %collective-permute-done.26.s3 = f32[1,2048]{1,0:T(1,128)S(1)} collective-permute-done((f32[1,2048]{1,0:T(1,128)S(1)}, f32[1,2048]{1,0:T(1,128)S(1)}, u32[]{:S(2)}, u32[]{:S(2)}) %collective-permute-start.26) | collective-permute-done | bytes 8224 | tf_op jit(solution)/shard_map/ppermute | solution.py:468
  91.3 1.9 %norm.1 = bf16[560,2048]{1,0:T(8,128)(2,1)} custom-call(f32[560,2048]{1,0:T(8,128)S(1)} %get-tuple-element.68.out_ref, f32[1,2048]{1,0:T(1,128)S(1)} %get-tuple-element.69.s0, f32[1,2048]{1,0:T(1,128)S(1)} %collective-permute-done.24.s1, f32[1,2048]{1,0:T(1,128)S(1)} %collective-permute-done.25.s2, f32[1,2048]{1,0:T(1,128)S(1)} %collective-permute-done.26.s3, ...), custom_call_target="tpu_custom_call" | custom-call | flops 1 | bytes 1 | tf_op jit(solution)/shard_map/norm/pallas_call | solution.py:415
  (40 shorter events, 2.6 us)
Async XLA Ops:
  0.0 7.7 %collective-permute-start = (bf16[70,1680]{1,0:T(8,128)(2,1)}, bf16[70,1680]{1,0:T(8,128)(2,1)S(1)}, u32[]{:S(2)}, u32[]{:S(2)}) collective-permute-start(bf16[70,1680]{1,0:T(8,128)(2,1)} %w_ref.1), channel_id=1, source_target_pairs={{0,8},{4,36},{8,16},{12,44},{16,24},{20,52},{24,0},{28,60},{32,40}... | collective-permute-start | bytes 705608 | tf_op jit(solution)/shard_map/ppermute | solution.py:65
  1.6 10.0 %collective-permute-start.1 = (bf16[70,1680]{1,0:T(8,128)(2,1)}, bf16[70,1680]{1,0:T(8,128)(2,1)S(1)}, u32[]{:S(2)}, u32[]{:S(2)}) collective-permute-start(bf16[70,1680]{1,0:T(8,128)(2,1)} %w_ref.1), channel_id=1, source_target_pairs={{0,16},{4,68},{8,24},{12,76},{16,0},{20,84},{24,8},{28,92},{32,48}... | collective-permute-start | bytes 705608 | tf_op jit(solution)/shard_map/ppermute | solution.py:65
  4.3 7.3 %collective-permute-start.2 = (bf16[70,1680]{1,0:T(8,128)(2,1)}, bf16[70,1680]{1,0:T(8,128)(2,1)S(1)}, u32[]{:S(2)}, u32[]{:S(2)}) collective-permute-start(bf16[70,1680]{1,0:T(8,128)(2,1)} %w_ref.1), channel_id=1, source_target_pairs={{0,24},{4,100},{8,0},{12,108},{16,8},{20,116},{24,16},{28,124},{32... | collective-permute-start | bytes 705608 | tf_op jit(solution)/shard_map/ppermute | solution.py:65
  13.0 12.2 %collective-permute-start.3 = (bf16[288,1152]{1,0:T(8,128)(2,1)S(1)}, bf16[288,1152]{1,0:T(8,128)(2,1)S(1)}, u32[]{:S(2)}, u32[]{:S(2)}) collective-permute-start(bf16[288,1152]{1,0:T(8,128)(2,1)S(1)} %get-tuple-element.41.refs_0_), channel_id=1, source_target_pairs={{0,4},{4,0},{8,12},{12,8},{16,20},{20,16},{24,28},{28,24},{32,36},... | collective-permute-start | bytes 1990664 | tf_op jit(solution)/shard_map/ppermute | solution.py:65
  13.1 18.4 %collective-permute-start.10 = (bf16[288,1152]{1,0:T(8,128)(2,1)S(1)}, bf16[288,1152]{1,0:T(8,128)(2,1)S(1)}, u32[]{:S(2)}, u32[]{:S(2)}) collective-permute-start(bf16[288,1152]{1,0:T(8,128)(2,1)S(1)} %get-tuple-element.41.refs_0_), channel_id=1, source_target_pairs={{0,96},{4,28},{8,104},{12,4},{16,112},{20,12},{24,120},{28,20},{32... | collective-permute-start | bytes 1990664 | tf_op jit(solution)/shard_map/ppermute | solution.py:65
  16.2 19.0 %collective-permute-start.8 = (bf16[288,1152]{1,0:T(8,128)(2,1)S(1)}, bf16[288,1152]{1,0:T(8,128)(2,1)S(1)}, u32[]{:S(2)}, u32[]{:S(2)}) collective-permute-start(bf16[288,1152]{1,0:T(8,128)(2,1)S(1)} %get-tuple-element.41.refs_0_), channel_id=1, source_target_pairs={{0,32},{4,12},{8,40},{12,20},{16,48},{20,28},{24,56},{28,4},{32,64... | collective-permute-start | bytes 1990664 | tf_op jit(solution)/shard_map/ppermute | solution.py:65
  16.2 19.0 %collective-permute-start.9 = (bf16[288,1152]{1,0:T(8,128)(2,1)S(1)}, bf16[288,1152]{1,0:T(8,128)(2,1)S(1)}, u32[]{:S(2)}, u32[]{:S(2)}) collective-permute-start(bf16[288,1152]{1,0:T(8,128)(2,1)S(1)} %get-tuple-element.41.refs_0_), channel_id=1, source_target_pairs={{0,64},{4,20},{8,72},{12,28},{16,80},{20,4},{24,88},{28,12},{32,96... | collective-permute-start | bytes 1990664 | tf_op jit(solution)/shard_map/ppermute | solution.py:65
  18.4 6.8 %collective-permute-start.4 = (bf16[288,640]{1,0:T(8,128)(2,1)S(1)}, bf16[288,640]{1,0:T(8,128)(2,1)S(1)}, u32[]{:S(2)}, u32[]{:S(2)}) collective-permute-start(bf16[288,640]{1,0:T(8,128)(2,1)S(1)} %get-tuple-element.45.refs_2_), channel_id=1, source_target_pairs={{0,4},{4,0},{8,12},{12,8},{16,20},{20,16},{24,28},{28,24},{32,36},... | collective-permute-start | bytes 1105928 | tf_op jit(solution)/shard_map/ppermute | solution.py:65
  35.2 3.5 %collective-permute-start.11 = (bf16[288,1152]{1,0:T(8,128)(2,1)S(1)}, bf16[288,1152]{1,0:T(8,128)(2,1)S(1)}, u32[]{:S(2)}, u32[]{:S(2)}) collective-permute-start(bf16[288,1152]{1,0:T(8,128)(2,1)S(1)} %collective-permute-done.8.refs_0_), channel_id=1, source_target_pairs={{0,4},{4,0},{8,12},{12,8},{16,20},{20,16},{24,28},{28,24},{32,36},... | collective-permute-start | bytes 1990664 | tf_op jit(solution)/shard_map/ppermute | solution.py:65
  35.2 4.9 %collective-permute-start.12 = (bf16[288,1152]{1,0:T(8,128)(2,1)S(1)}, bf16[288,1152]{1,0:T(8,128)(2,1)S(1)}, u32[]{:S(2)}, u32[]{:S(2)}) collective-permute-start(bf16[288,1152]{1,0:T(8,128)(2,1)S(1)} %collective-permute-done.9.refs_1_), channel_id=1, source_target_pairs={{0,4},{4,0},{8,12},{12,8},{16,20},{20,16},{24,28},{28,24},{32,36},... | collective-permute-start | bytes 1990664 | tf_op jit(solution)/shard_map/ppermute | solution.py:65
  35.7 4.4 %collective-permute-start.13 = (bf16[288,1152]{1,0:T(8,128)(2,1)S(1)}, bf16[288,1152]{1,0:T(8,128)(2,1)S(1)}, u32[]{:S(2)}, u32[]{:S(2)}) collective-permute-start(bf16[288,1152]{1,0:T(8,128)(2,1)S(1)} %collective-permute-done.10.refs_2_), channel_id=1, source_target_pairs={{0,4},{4,0},{8,12},{12,8},{16,20},{20,16},{24,28},{28,24},{32,36},... | collective-permute-start | bytes 1990664 | tf_op jit(solution)/shard_map/ppermute | solution.py:65
  35.7 17.4 %collective-permute-start.5 = (bf16[288,640]{1,0:T(8,128)(2,1)S(1)}, bf16[288,640]{1,0:T(8,128)(2,1)S(1)}, u32[]{:S(2)}, u32[]{:S(2)}) collective-permute-start(bf16[288,640]{1,0:T(8,128)(2,1)S(1)} %get-tuple-element.45.refs_2_), channel_id=1, source_target_pairs={{0,32},{4,12},{8,40},{12,20},{16,48},{20,28},{24,56},{28,4},{32,64... | collective-permute-start | bytes 1105928 | tf_op jit(solution)/shard_map/ppermute | solution.py:65
  35.8 17.3 %collective-permute-start.6 = (bf16[288,640]{1,0:T(8,128)(2,1)S(1)}, bf16[288,640]{1,0:T(8,128)(2,1)S(1)}, u32[]{:S(2)}, u32[]{:S(2)}) collective-permute-start(bf16[288,640]{1,0:T(8,128)(2,1)S(1)} %get-tuple-element.45.refs_2_), channel_id=1, source_target_pairs={{0,64},{4,20},{8,72},{12,28},{16,80},{20,4},{24,88},{28,12},{32,96... | collective-permute-start | bytes 1105928 | tf_op jit(solution)/shard_map/ppermute | solution.py:65
  38.7 14.4 %collective-permute-start.7 = (bf16[288,640]{1,0:T(8,128)(2,1)S(1)}, bf16[288,640]{1,0:T(8,128)(2,1)S(1)}, u32[]{:S(2)}, u32[]{:S(2)}) collective-permute-start(bf16[288,640]{1,0:T(8,128)(2,1)S(1)} %get-tuple-element.45.refs_2_), channel_id=1, source_target_pairs={{0,96},{4,28},{8,104},{12,4},{16,112},{20,12},{24,120},{28,20},{32... | collective-permute-start | bytes 1105928 | tf_op jit(solution)/shard_map/ppermute | solution.py:65
  52.2 2.0 %collective-permute-start.14 = (bf16[5,128,112]{2,1,0:T(8,128)(2,1)S(1)}, bf16[5,128,112]{2,1,0:T(8,128)(2,1)S(1)}, u32[]{:S(2)}, u32[]{:S(2)}) collective-permute-start(bf16[5,128,112]{2,1,0:T(8,128)(2,1)S(1)} %get-tuple-element.51.tot_ref), channel_id=1, source_target_pairs={{0,4},{4,0},{8,12},{12,8},{16,20},{20,16},{24,28},{28,24},{32,36},... | collective-permute-start | bytes 430088 | tf_op jit(solution)/shard_map/ppermute | solution.py:65
  54.2 3.4 %collective-permute-start.18 = (bf16[288,640]{1,0:T(8,128)(2,1)S(1)}, bf16[288,640]{1,0:T(8,128)(2,1)S(1)}, u32[]{:S(2)}, u32[]{:S(2)}) collective-permute-start(bf16[288,640]{1,0:T(8,128)(2,1)S(1)} %collective-permute-done.5.refs_0_), channel_id=1, source_target_pairs={{0,4},{4,0},{8,12},{12,8},{16,20},{20,16},{24,28},{28,24},{32,36},... | collective-permute-start | bytes 1105928 | tf_op jit(solution)/shard_map/ppermute | solution.py:65
  54.5 4.6 %collective-permute-start.19 = (bf16[288,640]{1,0:T(8,128)(2,1)S(1)}, bf16[288,640]{1,0:T(8,128)(2,1)S(1)}, u32[]{:S(2)}, u32[]{:S(2)}) collective-permute-start(bf16[288,640]{1,0:T(8,128)(2,1)S(1)} %collective-permute-done.6.refs_1_), channel_id=1, source_target_pairs={{0,4},{4,0},{8,12},{12,8},{16,20},{20,16},{24,28},{28,24},{32,36},... | collective-permute-start | bytes 1105928 | tf_op jit(solution)/shard_map/ppermute | solution.py:65
  54.7 4.5 %collective-permute-start.20 = (bf16[288,640]{1,0:T(8,128)(2,1)S(1)}, bf16[288,640]{1,0:T(8,128)(2,1)S(1)}, u32[]{:S(2)}, u32[]{:S(2)}) collective-permute-start(bf16[288,640]{1,0:T(8,128)(2,1)S(1)} %collective-permute-done.7.refs_2_), channel_id=1, source_target_pairs={{0,4},{4,0},{8,12},{12,8},{16,20},{20,16},{24,28},{28,24},{32,36},... | collective-permute-start | bytes 1105928 | tf_op jit(solution)/shard_map/ppermute | solution.py:65
  55.1 9.9 %copy-start = (s32[4]{0:T(128)S(1)}, s32[4]{0:T(128)}, u32[]{:S(2)}) copy-start(s32[4]{0:T(128)} %codes.3) | copy-start | bytes 52
  55.1 12.0 %collective-permute-start.15 = (bf16[5,128,112]{2,1,0:T(8,128)(2,1)S(1)}, bf16[5,128,112]{2,1,0:T(8,128)(2,1)S(1)}, u32[]{:S(2)}, u32[]{:S(2)}) collective-permute-start(bf16[5,128,112]{2,1,0:T(8,128)(2,1)S(1)} %chip.1.a), channel_id=1, source_target_pairs={{0,8},{4,12},{8,16},{12,20},{16,24},{20,28},{24,0},{28,4},{32,40},... | collective-permute-start | bytes 430088 | tf_op jit(solution)/shard_map/ppermute | solution.py:65
  55.6 11.5 %collective-permute-start.16 = (bf16[5,128,112]{2,1,0:T(8,128)(2,1)S(1)}, bf16[5,128,112]{2,1,0:T(8,128)(2,1)S(1)}, u32[]{:S(2)}, u32[]{:S(2)}) collective-permute-start(bf16[5,128,112]{2,1,0:T(8,128)(2,1)S(1)} %chip.1.a), channel_id=1, source_target_pairs={{0,16},{4,20},{8,24},{12,28},{16,0},{20,4},{24,8},{28,12},{32,48},... | collective-permute-start | bytes 430088 | tf_op jit(solution)/shard_map/ppermute | solution.py:65
  57.6 9.5 %collective-permute-start.17 = (bf16[5,128,112]{2,1,0:T(8,128)(2,1)S(1)}, bf16[5,128,112]{2,1,0:T(8,128)(2,1)S(1)}, u32[]{:S(2)}, u32[]{:S(2)}) collective-permute-start(bf16[5,128,112]{2,1,0:T(8,128)(2,1)S(1)} %chip.1.a), channel_id=1, source_target_pairs={{0,24},{4,28},{8,0},{12,4},{16,8},{20,12},{24,16},{28,20},{32,56},... | collective-permute-start | bytes 430088 | tf_op jit(solution)/shard_map/ppermute | solution.py:65
  67.2 12.6 %copy-start.1 = (f32[5]{0:T(128)S(1)}, f32[5]{0:T(128)}, u32[]{:S(2)}) copy-start(f32[5]{0:T(128)} %scale.1) | copy-start | bytes 64
  67.2 12.5 %collective-permute-start.21 = (bf16[5,128,112]{2,1,0:T(8,128)(2,1)S(1)}, bf16[5,128,112]{2,1,0:T(8,128)(2,1)S(1)}, u32[]{:S(2)}, u32[]{:S(2)}) collective-permute-start(bf16[5,128,112]{2,1,0:T(8,128)(2,1)S(1)} %row.1), channel_id=1, source_target_pairs={{0,32},{4,36},{8,40},{12,44},{16,48},{20,52},{24,56},{28,60},{32,6... | collective-permute-start | bytes 430088 | tf_op jit(solution)/shard_map/ppermute | solution.py:65
  69.8 10.0 %collective-permute-start.22 = (bf16[5,128,112]{2,1,0:T(8,128)(2,1)S(1)}, bf16[5,128,112]{2,1,0:T(8,128)(2,1)S(1)}, u32[]{:S(2)}, u32[]{:S(2)}) collective-permute-start(bf16[5,128,112]{2,1,0:T(8,128)(2,1)S(1)} %row.1), channel_id=1, source_target_pairs={{0,64},{4,68},{8,72},{12,76},{16,80},{20,84},{24,88},{28,92},{32,9... | collective-permute-start | bytes 430088 | tf_op jit(solution)/shard_map/ppermute | solution.py:65
  73.8 6.0 %collective-permute-start.23 = (bf16[5,128,112]{2,1,0:T(8,128)(2,1)S(1)}, bf16[5,128,112]{2,1,0:T(8,128)(2,1)S(1)}, u32[]{:S(2)}, u32[]{:S(2)}) collective-permute-start(bf16[5,128,112]{2,1,0:T(8,128)(2,1)S(1)} %row.1), channel_id=1, source_target_pairs={{0,96},{4,100},{8,104},{12,108},{16,112},{20,116},{24,120},{28,124... | collective-permute-start | bytes 430088 | tf_op jit(solution)/shard_map/ppermute | solution.py:65
  82.1 6.6 %collective-permute-start.24 = (f32[1,2048]{1,0:T(1,128)S(1)}, f32[1,2048]{1,0:T(1,128)S(1)}, u32[]{:S(2)}, u32[]{:S(2)}) collective-permute-start(f32[1,2048]{1,0:T(1,128)S(1)} %get-tuple-element.69.s0), channel_id=1, source_target_pairs={{0,1},{1,2},{2,3},{3,0},{4,5},{5,6},{6,7},{7,4},{8,9},{9,10},{10,1... | collective-permute-start | bytes 24584 | tf_op jit(solution)/shard_map/ppermute | solution.py:468
  84.1 5.3 %collective-permute-start.25 = (f32[1,2048]{1,0:T(1,128)S(1)}, f32[1,2048]{1,0:T(1,128)S(1)}, u32[]{:S(2)}, u32[]{:S(2)}) collective-permute-start(f32[1,2048]{1,0:T(1,128)S(1)} %get-tuple-element.69.s0), channel_id=1, source_target_pairs={{0,2},{1,3},{2,0},{3,1},{4,6},{5,7},{6,4},{7,5},{8,10},{9,11},{10,... | collective-permute-start | bytes 24584 | tf_op jit(solution)/shard_map/ppermute | solution.py:468
  87.7 3.7 %collective-permute-start.26 = (f32[1,2048]{1,0:T(1,128)S(1)}, f32[1,2048]{1,0:T(1,128)S(1)}, u32[]{:S(2)}, u32[]{:S(2)}) collective-permute-start(f32[1,2048]{1,0:T(1,128)S(1)} %get-tuple-element.69.s0), channel_id=1, source_target_pairs={{0,3},{1,0},{2,1},{3,2},{4,7},{5,4},{6,5},{7,6},{8,11},{9,8},{10,9... | collective-permute-start | bytes 24584 | tf_op jit(solution)/shard_map/ppermute | solution.py:468
